TPU v7x, 32 devices: a whole 2x2x4 slice. The times are simulated.
32 devices in a mesh: dp: 4 (over y, x), mp: 8 (over z, core).
Axes of the slice: x: 2, y: 2, z: 4, core: 2. Of those that a mesh axis runs over, the one named last changes fastest.
Arguments:
- inputs: bfloat16 [2048, 4096], P('dp'), may hold values from -6 to 6
- out_grads: bfloat16 [2048, 4096], P('dp'), may hold values from -0.3984375 to 0.3984375
- w_gate: bfloat16 [4096, 11008], P(None, 'mp'), may hold values from -0.09375 to 0.09375
- w_up: bfloat16 [4096, 11008], P(None, 'mp'), may hold values from -0.09375 to 0.09375
- w_down: bfloat16 [11008, 4096], P('mp'), may hold values from -0.0546875 to 0.0546875
- err_down: bfloat16 [4, 11008, 4096], P('dp', 'mp'), may hold values from -3 to 3
- mom_down: float32 [11008, 4096], P('mp', 'dp'), may hold values from -0.3 to 0.3
- q_down: float32 [4096, 8], replicated, may hold values from -5 to 5
Outputs:
- in_grads: bfloat16 [2048, 4096], P('dp', 'mp')
- new_down: bfloat16 [11008, 4096], P('mp')
- next_err_down: bfloat16 [4, 11008, 4096], P('dp', 'mp')
- next_mom_down: float32 [11008, 4096], P('mp', 'dp')
All inputs are finite; a program needn't handle non-finite values.
Results may differ from a plain program's by a relative error of at most 0.005.
Values may be sent and summed in bfloat16 or wider, within the bound.
No kernel may reach another device: no remote copies, remote signals or barrier semaphores. Data moves between devices by JAX's collectives and lax.ppermute only.
A program may use at most 192 MiB of HBM per device.

v0:
```python
import jax
import jax.numpy as jnp
from jax import lax
from jax.sharding import PartitionSpec as P

R = 8


HIGH = lax.Precision.HIGHEST


def orthonormal_split(panel):
    gram = lax.psum(jnp.dot(panel.T, panel, precision=HIGH), "mp")
    lower = jnp.linalg.cholesky(gram + 1e-06 * jnp.eye(R, dtype=jnp.float32))
    return lax.linalg.triangular_solve(lower, panel, left_side=False, lower=True, transpose_a=True)


def contract_rows(left, right):
    return lax.dot_general(
        left, right, (((0,), (0,)), ((), ())), preferred_element_type=jnp.float32
    )


def contract_cols(left, right):
    return lax.dot_general(
        left, right, (((1,), (1,)), ((), ())), preferred_element_type=jnp.float32
    )


def body(inputs, out_grads, w_gate, w_up, w_down, err_down, mom_down, q_down):
    replicas = lax.axis_size("dp")
    rank_dp = lax.axis_index("dp")
    gate = jnp.dot(inputs, w_gate, preferred_element_type=jnp.float32)
    up_val = jnp.dot(inputs, w_up, preferred_element_type=jnp.float32)
    sig = jax.nn.sigmoid(gate)
    hidden = (gate * sig * up_val).astype(jnp.bfloat16)
    d_hidden = contract_cols(out_grads, w_down)
    d_gate = (d_hidden * up_val * sig * (1.0 + gate * (1.0 - sig))).astype(jnp.bfloat16)
    d_up = (d_hidden * gate * sig).astype(jnp.bfloat16)
    partial_sum = contract_cols(d_gate, w_gate) + contract_cols(d_up, w_up)
    in_grads = lax.psum_scatter(partial_sum, "mp", scatter_dimension=1, tiled=True).astype(
        jnp.bfloat16
    )
    m_down = contract_rows(hidden, out_grads) + err_down[0].astype(jnp.float32)
    left_down = lax.psum(jnp.dot(m_down, q_down, precision=HIGH), "dp")
    left_down = orthonormal_split(left_down / replicas)
    right_down = lax.psum(contract_rows(m_down, left_down), ("dp", "mp"))
    approx_down = jnp.dot(left_down, right_down.T / replicas, precision=HIGH)
    next_err_down = (m_down - approx_down).astype(jnp.bfloat16)[None]
    cols = mom_down.shape[1]
    start = rank_dp * cols
    next_mom_down = 0.9 * mom_down + lax.dynamic_slice_in_dim(approx_down, start, cols, 1)
    own_down = (
        lax.dynamic_slice_in_dim(w_down, start, cols, 1).astype(jnp.float32) - 0.1 * next_mom_down
    ).astype(jnp.bfloat16)
    new_down = lax.all_gather(own_down, "dp", axis=1, tiled=True)
    return (in_grads, new_down, next_err_down, next_mom_down)


def solution(mesh):
    in_specs = (
        P("dp", None),
        P("dp", None),
        P(None, "mp"),
        P(None, "mp"),
        P("mp", None),
        P("dp", "mp", None),
        P("mp", "dp"),
        P(),
    )
    out_specs = (P("dp", "mp"), P("mp", None), P("dp", "mp", None), P("mp", "dp"))
    return jax.shard_map(body, mesh=mesh, in_specs=in_specs, out_specs=out_specs, check_vma=False)
```

profile of v0, /device:TPU:8, one launch (start us, length us, event | category | flops | bytes accessed | tf_op | source)
XLA Modules:
  0.0 429.7 jit_solution(10809520826166647255)
XLA Ops:
  8.0 0.0 copy-start
  8.0 0.0 all-reduce.2.cloned.1.call-start
  8.1 0.0 copy-start.2
  8.1 0.0 copy-start.3
  8.1 10.2 %fusion.24 = f32[512,1376]{0,1:T(8,128)S(1)} fusion(bf16[512,4096]{1,0:T(8,128)(2,1)} %param.8, bf16[4096,1376]{0,1:T(8,128)(2,1)} %param.10), kind=kOutput, calls=%fused_computation.40 | convolution fusion | flops 5771362304 | bytes 18284544 | tf_op jit(solution)/shard_map/dot_general | solution.py:33
  18.3 0.0 copy-done.2
  18.3 0.0 copy-done.3
  18.3 0.0 copy-start.4
  18.4 6.0 %fusion.23 = f32[512,1376]{0,1:T(8,128)S(1)} fusion(bf16[512,4096]{1,0:T(8,128)(2,1)S(1)} %copy-done.3, bf16[4096,1376]{0,1:T(8,128)(2,1)S(1)} %copy-done.2), kind=kOutput, calls=%fused_computation.39 | convolution fusion | flops 5771362304 | bytes 18284544 | tf_op jit(solution)/shard_map/dot_general | solution.py:34
  24.4 0.0 copy-done.4
  24.4 0.0 copy-start.5
  24.4 14.3 %convert_add_fusion = f32[1376,4096]{1,0:T(8,128)} fusion(bf16[512,4096]{1,0:T(8,128)(2,1)S(1)} %copy-done.4, bf16[1,1376,4096]{2,1,0:T(8,128)(2,1)} %param.13, f32[512,1376]{0,1:T(8,128)S(1)} %fusion.23, f32[512,1376]{0,1:T(8,128)S(1)} %fusion.24), kind=kOutput, calls=%fused_computation | convolution fusion | flops 5786861568 | bytes 43646976 | tf_op jit(solution)/shard_map/dot_general | solution.py:19
  38.8 0.0 copy-done.5
  38.8 21.8 %fusion.25 = f32[1376,8]{0,1:T(8,128)S(1)} fusion(f32[1376,4096]{1,0:T(8,128)} %convert_add_fusion, f32[4096,8]{0,1:T(8,128)S(1)} %copy-done), kind=kOutput, calls=%fused_computation.41 | convolution fusion | flops 541065216 | bytes 22719488 | tf_op jit(solution)/shard_map/dot_general | solution.py:45
  60.5 16.7 %psum.21 = f32[1376,8]{0,1:T(8,128)S(1)} all-reduce(f32[1376,8]{0,1:T(8,128)S(1)} %fusion.25), channel_id=1, replica_groups=mesh['dp'=4,'mp'=8] {'dp'}, use_global_device_ids=true, to_apply=%region_1.0 | all-reduce | flops 11008 | bytes 88064 | tf_op jit(solution)/shard_map/psum | solution.py:45
  77.3 0.2 fusion.10
  77.4 10.0 %psum.22 = f32[8,8]{0,1:T(8,128)S(1)} all-reduce(f32[8,8]{0,1:T(8,128)S(1)} %fusion.10), channel_id=1, replica_groups=mesh['dp'=4,'mp'=8] {'mp'}, use_global_device_ids=true, to_apply=%region_2.0 | all-reduce | flops 64 | bytes 512 | tf_op jit(solution)/shard_map/psum | solution.py:13
  87.5 0.1 copy.19
  87.6 0.7 cholesky.16
  88.3 0.1 copy.20
  88.3 0.1 select_reduce_fusion
  88.5 0.6 compare_reduce_fusion
  89.1 0.6 select_select_fusion
  89.8 0.1 copy.22
  89.9 0.6 custom-call.6
  90.5 0.2 fusion.8
  90.7 9.6 %fusion.26 = f32[4096,8]{0,1:T(8,128)} fusion(f32[1376,4096]{1,0:T(8,128)} %convert_add_fusion, f32[1376,8]{0,1:T(8,128)S(1)} %fusion.8), kind=kOutput, calls=%fused_computation.42 | convolution fusion | flops 90177536 | bytes 22719488 | tf_op jit(solution)/shard_map/dot_general | solution.py:19
  100.4 0.0 all-reduce.2.cloned.1.call-update
  100.4 0.0 reduce-scatter.2.cloned.1.call-start
  100.5 0.0 copy-start.6
  100.5 0.0 slice-start
  100.5 0.0 slice-start.1
  100.5 10.5 %fusion.22 = f32[512,1376]{0,1:T(8,128)S(1)} fusion(bf16[512,4096]{1,0:T(8,128)(2,1)} %param.9, bf16[1376,4096]{1,0:T(8,128)(2,1)} %param.12), kind=kOutput, calls=%fused_computation.38 | convolution fusion | flops 5771362304 | bytes 18284544 | tf_op jit(solution)/shard_map/dot_general | solution.py:25
  111.0 0.0 copy-done.6
  111.0 0.0 slice-start.2
  111.0 13.3 %fusion.1 = f32[512,4096]{1,0:T(8,128)} fusion(bf16[4096,1376]{0,1:T(8,128)(2,1)} %param.10, f32[512,1376]{0,1:T(8,128)S(1)} %fusion.24, f32[512,1376]{0,1:T(8,128)S(1)} %fusion.22, f32[512,1376]{0,1:T(8,128)S(1)} %copy-done.6), kind=kOutput, calls=%fused_computation.10 | convolution fusion | flops 5778407424 | bytes 28114944 | tf_op jit(solution)/shard_map/dot_general | solution.py:25
  124.3 0.0 slice-done.2
  124.3 11.7 %convolution_add_fusion = f32[512,4096]{1,0:T(8,128)} fusion(f32[512,4096]{1,0:T(8,128)} %fusion.1, bf16[4096,1376]{0,1:T(8,128)(2,1)S(1)} %bitcast.29, f32[512,1376]{0,1:T(8,128)S(1)} %fusion.22, f32[512,1376]{0,1:T(8,128)S(1)} %fusion.24), kind=kOutput, calls=%fused_computation.3 | convolution fusion | flops 5777686528 | bytes 33685504 | tf_op jit(solution)/shard_map/dot_general | solution.py:25
  136.1 0.0 reduce-scatter.2.cloned.1.call-update
  136.1 0.0 all-gather.2.cloned.1.call-start
  136.1 132.9 %all-reduce.2.cloned.1.call-done = f32[4096,8]{0,1:T(8,128)} async-done(((f32[4096,8]{0,1:T(8,128)}), f32[4096,8]{0,1:T(8,128)}) %all-reduce.2.cloned.1.call-update) | async-done | bytes 131088 | tf_op jit(solution)/shard_map/psum | solution.py:47
  269.0 21.5 %fusion.5 = f32[1376,4096]{1,0:T(8,128)} fusion(f32[1376,8]{0,1:T(8,128)S(1)} %fusion.8, f32[4096,8]{0,1:T(8,128)} %all-reduce.2.cloned.1.call-done), kind=kOutput, calls=%fused_computation.14 | convolution fusion | flops 541097984 | bytes 22719488 | tf_op jit(solution)/shard_map/dot_general | solution.py:48
  290.6 10.9 %subtract_convert_fusion.1 = (bf16[1376,1024]{1,0:T(8,128)(2,1)}, f32[1376,1024]{1,0:T(8,128)}) fusion(bf16[1376,4096]{1,0:T(8,128)(2,1)} %param.12, s32[]{:T(128)S(6)} %select_n.8, f32[1376,4096]{1,0:T(8,128)} %fusion.5, f32[1376,1024]{1,0:T(8,128)} %param.14), kind=kLoop, calls=%fused_computation.4 | loop fusion | flops 8454144 | bytes 22544388 | tf_op jit(solution)/shard_map/convert_element_type | solution.py:55
  301.4 0.0 all-gather.2.cloned.1.call-update
  301.5 21.3 %fusion = bf16[1,1376,4096]{2,1,0:T(8,128)(2,1)} fusion(f32[1376,4096]{1,0:T(8,128)} %convert_add_fusion, f32[1376,4096]{1,0:T(8,128)} %fusion.5), kind=kLoop, calls=%fused_computation.2 | loop fusion | flops 11272192 | bytes 56360960 | tf_op jit(solution)/shard_map/broadcast_in_dim | solution.py:49
  322.8 2.1 convert_element_type.30
  324.9 87.4 %all-gather.2.cloned.1.call-done = bf16[1376,4096]{1,0:T(8,128)(2,1)} async-done(((bf16[1376,1024]{1,0:T(8,128)(2,1)}), bf16[1376,4096]{1,0:T(8,128)(2,1)}) %all-gather.2.cloned.1.call-update) | async-done | bytes 11272208 | tf_op jit(solution)/shard_map/all_gather | solution.py:56
  412.3 9.9 %copy.27 = bf16[1376,4096]{1,0:T(8,128)(2,1)} copy(bf16[1376,4096]{1,0:T(8,128)(2,1)} %all-gather.2.cloned.1.call-done) | data formatting | bytes 22544384
  (9 shorter events, 0.0 us)
Async XLA Ops:
  8.0 30.8 %copy-start = (f32[4096,8]{0,1:T(8,128)S(1)}, f32[4096,8]{0,1:T(8,128)}, u32[]{:S(2)}) copy-start(f32[4096,8]{0,1:T(8,128)} %param.15) | copy-start | bytes 393220
  8.0 261.0 %all-reduce.2.cloned.1.call-start = ((), (), s32[]{:S(2)}) async-start(), calls=%async_computation.2 | async-start | bytes 262144 | tf_op jit(solution)/shard_map/psum | solution.py:47
  8.1 10.3 %copy-start.2 = (bf16[4096,1376]{0,1:T(8,128)(2,1)S(1)}, bf16[4096,1376]{0,1:T(8,128)(2,1)}, u32[]{:S(2)}) copy-start(bf16[4096,1376]{0,1:T(8,128)(2,1)} %param.11) | copy-start | bytes 33816580
  8.1 10.3 %copy-start.3 = (bf16[512,4096]{1,0:T(8,128)(2,1)S(1)}, bf16[512,4096]{1,0:T(8,128)(2,1)}, u32[]{:S(2)}) copy-start(bf16[512,4096]{1,0:T(8,128)(2,1)} %param.8) | copy-start | bytes 12582916
  18.3 6.1 %copy-start.4 = (bf16[512,4096]{1,0:T(8,128)(2,1)S(1)}, bf16[512,4096]{1,0:T(8,128)(2,1)}, u32[]{:S(2)}) copy-start(bf16[512,4096]{1,0:T(8,128)(2,1)} %param.9) | copy-start | bytes 12582916
  24.4 14.3 %copy-start.5 = (f32[512,1376]{0,1:T(8,128)}, f32[512,1376]{0,1:T(8,128)S(1)}, u32[]{:S(2)}) copy-start(f32[512,1376]{0,1:T(8,128)S(1)} %fusion.23) | copy-start | bytes 8454148
  100.4 222.4 %reduce-scatter.2.cloned.1.call-start = ((), (), s32[]{:S(2)}) async-start(), calls=%async_computation.1 | async-start | bytes 9437184 | tf_op jit(solution)/shard_map/reduce_scatter | solution.py:41
  100.5 10.5 %copy-start.6 = (f32[512,1376]{0,1:T(8,128)S(1)}, f32[512,1376]{0,1:T(8,128)}, u32[]{:S(2)}) copy-start(f32[512,1376]{0,1:T(8,128)} %copy-done.5) | copy-start | bytes 8454148
  100.5 23.8 %slice-start = ((s8[11272192]{0:T(1024)(128)(4,1)}), s8[4194304]{0:T(1024)(128)(4,1)S(1)}, s32[]{:S(2)}) async-start(s8[11272192]{0:T(1024)(128)(4,1)} %bitcast.28), calls=%async_computation.4 | async-start | bytes 8388608
  100.5 23.8 %slice-start.1 = ((s8[11272192]{0:T(1024)(128)(4,1)}), s8[4194304]{0:T(1024)(128)(4,1)S(1)}, s32[]{:S(2)}) async-start(s8[11272192]{0:T(1024)(128)(4,1)} %bitcast.28), calls=%async_computation.5 | async-start | bytes 8388608
  111.0 13.3 %slice-start.2 = ((s8[11272192]{0:T(1024)(128)(4,1)}), s8[2883584]{0:T(1024)(128)(4,1)S(1)}, s32[]{:S(2)}) async-start(s8[11272192]{0:T(1024)(128)(4,1)} %bitcast.28), calls=%async_computation.6 | async-start | bytes 5767168
  136.1 276.2 %all-gather.2.cloned.1.call-start = ((), (), s32[]{:S(2)}) async-start(), calls=%async_computation.3 | async-start | bytes 14090240 | tf_op jit(solution)/shard_map/all_gather | solution.py:56
  412.3 9.9 %copy-start.1 = (f32[4096,8]{0,1:T(8,128)S(1)}, f32[4096,8]{0,1:T(8,128)}, u32[]{:S(2)}) copy-start(f32[4096,8]{0,1:T(8,128)} %param.15) | copy-start | bytes 393220
Sparse Core Ops, SparseCore 0:
  100.5 168.4 all-reduce.1
  301.6 110.6 all-gather.1
Sparse Core Ops, SparseCore 1:
  136.2 87.3 reduce-scatter.1
where the time goes:
time: 432 us; the launch traced here: 430 us
  waiting for transfers between devices  220 us (51%)
  matrix products  119 us (28%)
  other arithmetic  37.1 us (9%)
  blocking collectives  26.8 us (6%)
  between operations  15.7 us (4%)
  local copies, waits for them, and re-layouts  10.2 us (2%)
    psum x1, waiting for transfers between devices, body(): right_down = lax.psum(contract_rows(m_down, left_down), ('dp', 'mp'))  133 us
    all_gather x1, waiting for transfers between devices, body(): new_down = lax.all_gather(own_down, 'dp', axis=1, tiled=True)  87.4 us
    dot_general x3, matrix products, contract_cols(): lax.dot_general(left, right, (((1,), (1,)), ((), ())), preferred_element_...  35.5 us
    dot_general x2, matrix products, contract_rows(): lax.dot_general(left, right, (((0,), (0,)), ((), ())), preferred_element_...  24 us
    dot_general x1, matrix products, body(): left_down = lax.psum(jnp.dot(m_down, q_down, precision=HIGH), 'dp')  21.8 us
    dot_general x1, matrix products, body(): approx_down = jnp.dot(left_down, right_down.T / replicas, precision=HIGH)  21.5 us
    broadcast_in_dim x1, other arithmetic, body(): next_err_down = (m_down - approx_down).astype(jnp.bfloat16)[None]  21.3 us
    psum x1, blocking collectives, body(): left_down = lax.psum(jnp.dot(m_down, q_down, precision=HIGH), 'dp')  16.7 us
  transfers between devices with their start and end apart: 3, of which 2 were waited for; matrix products, arithmetic and copies ran while one was open for 21% of the time, Pallas kernels for 0%

commit v1 on v0

v1 whole, which is shorter than its diff:
```python
import functools

import jax
import jax.numpy as jnp
from jax import lax
from jax.experimental import pallas as pl
from jax.experimental.pallas import tpu as pltpu
from jax.sharding import PartitionSpec as P

R = 8
SPLIT = 4 * R
EPS = 1e-06
F32 = jnp.float32
BF16 = jnp.bfloat16
HIGH = lax.Precision.HIGHEST
VMEM = 48 * 2**20
ONCE = pl.Buffered(1)


def params():
    return pltpu.CompilerParams(vmem_limit_bytes=VMEM)


def cost(flops, nbytes):
    return pl.CostEstimate(flops=int(flops), bytes_accessed=int(nbytes), transcendentals=0)


def dot(left, right):
    return jnp.dot(left, right, preferred_element_type=F32)


def dot_nt(left, right):
    return lax.dot_general(left, right, (((1,), (1,)), ((), ())), preferred_element_type=F32)


def terms(rows):
    hi = rows.astype(BF16).astype(F32)
    rest = rows - hi
    mid = rest.astype(BF16).astype(F32)
    return hi, mid, rest - mid


def spread(rows):
    hi, mid, low = terms(rows)
    return jnp.concatenate([hi, mid, low, jnp.zeros_like(hi)], axis=0).astype(BF16)


def gather_terms(rows):
    return rows[:R] + rows[R : 2 * R] + rows[2 * R : 3 * R]


def whole(shape):
    return pl.BlockSpec(shape, lambda *_: (0,) * len(shape), pipeline_mode=ONCE)


def hidden_kernel(x_ref, dy_ref, wg_ref, wu_ref, wd_ref, hid_ref, dg_ref, du_ref):
    gate = dot_nt(x_ref[...], wg_ref[...])
    up = dot_nt(x_ref[...], wu_ref[...])
    dh = dot_nt(dy_ref[...], wd_ref[...])
    sig = jax.nn.sigmoid(gate)
    silu = gate * sig
    hid_ref[...] = (silu * up).T.astype(BF16)
    dg_ref[...] = (dh * up * sig * (1.0 + gate * (1.0 - sig))).astype(BF16)
    du_ref[...] = (dh * silu).astype(BF16)


def hidden_call(x, dy, wg, wu, wd):
    tok, depth = x.shape
    units = wg.shape[0]
    tile = min(256, units)
    return pl.pallas_call(
        hidden_kernel,
        grid=(pl.cdiv(units, tile),),
        in_specs=[
            whole((tok, depth)),
            whole((tok, depth)),
            pl.BlockSpec((tile, depth), lambda f: (f, 0)),
            pl.BlockSpec((tile, depth), lambda f: (f, 0)),
            pl.BlockSpec((tile, depth), lambda f: (f, 0)),
        ],
        out_specs=[
            pl.BlockSpec((tile, tok), lambda f: (f, 0)),
            pl.BlockSpec((tok, tile), lambda f: (0, f)),
            pl.BlockSpec((tok, tile), lambda f: (0, f)),
        ],
        out_shape=[
            jax.ShapeDtypeStruct((units, tok), BF16),
            jax.ShapeDtypeStruct((tok, units), BF16),
            jax.ShapeDtypeStruct((tok, units), BF16),
        ],
        compiler_params=params(),
        cost_estimate=cost(6 * tok * depth * units, 6 * depth * units + 4 * tok * depth),
        name="hidden",
    )(x, dy, wg, wu, wd)


def left_kernel(q_ref, err_ref, dy_ref, hid_ref, out_ref, err_acc, dy_acc):
    step = pl.program_id(0)

    @pl.when(step == 0)
    def _():
        err_acc[...] = jnp.zeros_like(err_acc)
        dy_acc[...] = jnp.zeros_like(dy_acc)

    q = spread(q_ref[...])
    err_acc[...] += dot_nt(q, err_ref[0])
    dy_acc[...] += dot_nt(q, dy_ref[...])

    @pl.when(step == pl.num_programs(0) - 1)
    def _():
        mixed = spread(gather_terms(dy_acc[...]))
        out_ref[...] = gather_terms(err_acc[...]) + gather_terms(dot_nt(mixed, hid_ref[...]))


def left_call(q_t, err, dy, hid):
    units, tok = hid.shape
    depth = dy.shape[1]
    tile = min(512, depth)
    return pl.pallas_call(
        left_kernel,
        grid=(depth // tile,),
        in_specs=[
            pl.BlockSpec((R, tile), lambda d: (0, d)),
            pl.BlockSpec((1, units, tile), lambda d: (0, 0, d)),
            pl.BlockSpec((tok, tile), lambda d: (0, d)),
            whole((units, tok)),
        ],
        out_specs=whole((R, units)),
        out_shape=jax.ShapeDtypeStruct((R, units), F32),
        scratch_shapes=[pltpu.VMEM((SPLIT, units), F32), pltpu.VMEM((SPLIT, tok), F32)],
        compiler_params=params(),
        cost_estimate=cost(2 * 256 * units * depth, 2 * units * depth + 2 * tok * depth),
        name="left",
    )(q_t, err, dy, hid)


def right_kernel(left_ref, hid_ref, err_ref, dy_ref, out_ref, left_terms, mixed_terms):
    step = pl.program_id(0)
    depth = dy_ref.shape[1]

    @pl.when(step == 0)
    def _():
        left = left_ref[...]
        left_terms[...] = spread(left)
        mixed_terms[...] = spread(gather_terms(dot(left_terms[...], hid_ref[...])))
        gram = lax.dot_general(
            left, left, (((1,), (1,)), ((), ())), precision=HIGH, preferred_element_type=F32
        )
        out_ref[:, out_ref.shape[1] - 128 :] = jnp.concatenate(
            [gram, jnp.zeros((R, 128 - R), F32)], axis=1
        )

    part = dot(left_terms[...], err_ref[0]) + dot(mixed_terms[...], dy_ref[...])
    out_ref[:, pl.ds(pl.multiple_of(step * depth, depth), depth)] = gather_terms(part)


def right_call(left, hid, err, dy):
    units, tok = hid.shape
    depth = dy.shape[1]
    tile = min(512, depth)
    return pl.pallas_call(
        right_kernel,
        grid=(depth // tile,),
        in_specs=[
            whole((R, units)),
            whole((units, tok)),
            pl.BlockSpec((1, units, tile), lambda d: (0, 0, d)),
            pl.BlockSpec((tok, tile), lambda d: (0, d)),
        ],
        out_specs=whole((R, depth + 128)),
        out_shape=jax.ShapeDtypeStruct((R, depth + 128), F32),
        scratch_shapes=[pltpu.VMEM((SPLIT, units), BF16), pltpu.VMEM((SPLIT, tok), BF16)],
        compiler_params=params(),
        cost_estimate=cost(2 * 256 * units * depth, 2 * units * depth + 2 * tok * depth),
        name="right",
    )(left, hid, err, dy)


def factors_kernel(replicas, sum_ref, left_ref, l_ref, r_ref):
    depth = r_ref.shape[1]
    gram = sum_ref[:, depth : depth + R] / replicas
    row = lax.broadcasted_iota(jnp.int32, (R, R), 0)
    col = lax.broadcasted_iota(jnp.int32, (R, R), 1)
    eye = (row == col).astype(F32)
    basis = jnp.zeros((R, R), F32)
    for k in range(R):
        unit = eye[k : k + 1]
        coeffs = jnp.sum(basis * gram[k : k + 1], axis=1, keepdims=True)
        rest = unit - jnp.sum(coeffs * basis, axis=0, keepdims=True)
        rest_col = jnp.sum(eye * rest, axis=1, keepdims=True)
        image = jnp.sum(rest_col * gram, axis=0, keepdims=True)
        square = jnp.sum(image * rest, axis=1, keepdims=True)
        basis = jnp.where(row == k, rest * lax.rsqrt(jnp.maximum(square, 0.0) + EPS), basis)
    left = jnp.dot(basis, left_ref[...], precision=HIGH, preferred_element_type=F32)
    right = jnp.dot(basis, sum_ref[:, :depth], precision=HIGH, preferred_element_type=F32)
    hi, mid, _ = terms(left)
    zero = jnp.zeros_like(hi)
    l_ref[...] = jnp.concatenate([hi, hi, mid, zero], axis=0).T.astype(BF16)
    hi, mid, _ = terms(right / replicas)
    zero = jnp.zeros_like(hi)
    r_ref[...] = jnp.concatenate([hi, mid, hi, zero], axis=0).astype(BF16)


def factors_call(total, left, replicas):
    units = left.shape[1]
    depth = total.shape[1] - 128
    return pl.pallas_call(
        functools.partial(factors_kernel, replicas),
        out_shape=[
            jax.ShapeDtypeStruct((units, SPLIT), BF16),
            jax.ShapeDtypeStruct((SPLIT, depth), BF16),
        ],
        compiler_params=params(),
        cost_estimate=cost(2 * 256 * 6 * R * (units + depth), 4 * R * (units + depth)),
        name="factors",
    )(total, left)


def blocks_kernel(add, where_ref, dg_ref, du_ref, wg_ref, wu_ref, *refs):
    step = pl.program_id(0)
    if add:
        added, outs = refs[: len(refs) // 2], refs[len(refs) // 2 :]
    else:
        added, outs = (None,) * len(refs), refs
    part = dot(dg_ref[...], wg_ref[...]) + dot(du_ref[...], wu_ref[...])
    for slot, (more, out) in enumerate(zip(added, outs)):

        @pl.when(step == slot)
        def _(more=more, out=out):
            out[...] = (part if more is None else part + more[...].astype(F32)).astype(BF16)


def blocks_call(pos, parity, dg, du, wg, wu, count, added=()):
    tok, units = dg.shape
    depth = wg.shape[1]
    width = depth // (2 * count)
    where = jnp.stack([pos // 2, parity]).astype(jnp.int32)
    block = pl.BlockSpec((units, width), lambda s, at: (0, 2 * (s ^ at[0]) + at[1]))
    return pl.pallas_call(
        functools.partial(blocks_kernel, bool(added)),
        grid_spec=pltpu.PrefetchScalarGridSpec(
            num_scalar_prefetch=1,
            grid=(count,),
            in_specs=[whole((tok, units)), whole((tok, units)), block, block]
            + [whole((tok, width))] * len(added),
            out_specs=[whole((tok, width))] * count,
        ),
        out_shape=[jax.ShapeDtypeStruct((tok, width), BF16)] * count,
        compiler_params=params(),
        cost_estimate=cost(2 * tok * units * depth, 2 * units * depth + tok * depth),
        name="blocks",
    )(where, dg, du, wg, wu, *added)


def error_kernel(hid_ref, dy_ref, err_ref, l_ref, r_ref, out_ref):
    grown = dot(hid_ref[...], dy_ref[...]) + err_ref[0].astype(F32)
    out_ref[0] = (grown - dot(l_ref[...], r_ref[...])).astype(BF16)


def error_call(hid, dy, err, l, r):
    units, tok = hid.shape
    depth = dy.shape[1]
    tile = min(512, depth)
    return pl.pallas_call(
        error_kernel,
        grid=(depth // tile,),
        in_specs=[
            whole((units, tok)),
            pl.BlockSpec((tok, tile), lambda d: (0, d)),
            pl.BlockSpec((1, units, tile), lambda d: (0, 0, d)),
            whole((units, SPLIT)),
            pl.BlockSpec((SPLIT, tile), lambda d: (0, d)),
        ],
        out_specs=pl.BlockSpec((1, units, tile), lambda d: (0, 0, d)),
        out_shape=jax.ShapeDtypeStruct(err.shape, BF16),
        compiler_params=params(),
        cost_estimate=cost(2 * tok * units * depth, 4 * units * depth + 2 * tok * depth),
        name="error",
    )(hid, dy, err, l, r)


def row_tile(units):
    return units // 2 if units % 32 == 0 and units > 512 else units


def updated(w, mom, approx):
    return (w.astype(F32) - 0.1 * (0.9 * mom.astype(F32) + approx)).astype(BF16)


def own_kernel(at_ref, mom_ref, w_ref, l_ref, r_ref, mom_out, w_out):
    approx = dot(l_ref[...], r_ref[...])
    mom = mom_ref[...]
    mom_out[...] = 0.9 * mom + approx
    w_out[...] = updated(w_ref[...], mom.astype(BF16), approx)


def own_call(at, mom, w, l, r, half):
    units, cols = mom.shape
    tile = row_tile(units)
    halves = cols // half
    place = pl.BlockSpec((tile, half), lambda c, f, at: (f, at[0] * halves + c))
    mine = pl.BlockSpec((tile, half), lambda c, f, at: (f, c))
    return pl.pallas_call(
        own_kernel,
        grid_spec=pltpu.PrefetchScalarGridSpec(
            num_scalar_prefetch=1,
            grid=(halves, units // tile),
            in_specs=[
                mine,
                place,
                pl.BlockSpec((tile, SPLIT), lambda c, f, at: (f, 0)),
                pl.BlockSpec((SPLIT, half), lambda c, f, at: (0, at[0] * halves + c)),
            ],
            out_specs=[mine, place],
        ),
        out_shape=[jax.ShapeDtypeStruct(mom.shape, F32), jax.ShapeDtypeStruct(w.shape, BF16)],
        compiler_params=params(),
        cost_estimate=cost(512 * units * cols, 12 * units * cols),
        name="own",
    )(at, mom, w, l, r)


def others_kernel(count, at_ref, *refs):
    pieces = refs[:count]
    w_ref, l_ref, r_ref, _, w_out = refs[count:]
    for slot, piece in enumerate(pieces):

        @pl.when(pl.program_id(0) == slot)
        def _(piece=piece):
            w_out[...] = updated(w_ref[...], piece[...], dot(l_ref[...], r_ref[...]))


def others_call(at, pieces, w, l, r, new):
    units, half = pieces[0].shape
    tile = row_tile(units)
    steps = units // tile
    count = len(pieces)

    def piece_spec(slot):
        def index(c, f, at):
            return (jnp.where(c == slot, f, jnp.where(c < slot, 0, steps - 1)), 0)

        return pl.BlockSpec((tile, half), index)

    place = pl.BlockSpec((tile, half), lambda c, f, at: (f, at[c]))
    return pl.pallas_call(
        functools.partial(others_kernel, count),
        grid_spec=pltpu.PrefetchScalarGridSpec(
            num_scalar_prefetch=1,
            grid=(count, steps),
            in_specs=[piece_spec(slot) for slot in range(count)]
            + [
                place,
                pl.BlockSpec((tile, SPLIT), lambda c, f, at: (f, 0)),
                pl.BlockSpec((SPLIT, half), lambda c, f, at: (0, at[c])),
                pl.BlockSpec(memory_space=pl.ANY),
            ],
            out_specs=place,
        ),
        out_shape=jax.ShapeDtypeStruct(w.shape, BF16),
        input_output_aliases={count + 4: 0},
        compiler_params=params(),
        cost_estimate=cost(512 * units * half * count, 6 * units * half * count),
        name="others",
    )(at, *pieces, w, l, r, new)


def exchange(value, axis, mask):
    size = lax.axis_size(axis)
    return lax.ppermute(value, axis, [(i, i ^ mask) for i in range(size)])


def after(value, *earlier):
    return lax.optimization_barrier((value, *earlier))[0]


def masks(size):
    return [1 << bit for bit in range(size.bit_length() - 1)]


def body(inputs, out_grads, w_gate, w_up, w_down, err_down, mom_down, q_down):
    replicas = lax.axis_size("dp")
    shards = lax.axis_size("mp")
    rank_dp = lax.axis_index("dp")
    rank_mp = lax.axis_index("mp")
    cols = mom_down.shape[1]
    half = cols // 2
    w_gate, w_up = w_gate.T, w_up.T

    mom_low = [mom_down[:, :half].astype(BF16), mom_down[:, half:].astype(BF16)]
    far = replicas == 4
    got = {}
    got[2, 0] = exchange(mom_low[0], "dp", 2)
    got[1, 1] = exchange(mom_low[1], "dp", 1)

    hid, d_gate, d_up = hidden_call(inputs, out_grads, w_gate, w_up, w_down)
    late = after(mom_low[0], hid), after(mom_low[1], hid)
    got[1, 0] = exchange(late[0], "dp", 1)
    got[2, 1] = exchange(late[1], "dp", 2)
    for mask in range(3, replicas):
        if not far:
            got[mask, 0] = exchange(late[0], "dp", mask)
            got[mask, 1] = exchange(late[1], "dp", mask)

    left = left_call(q_down.T, err_down, out_grads, hid)
    left = left / replicas
    if far:
        parts = [exchange(left, "dp", mask) for mask in (1, 2, 3)]
    count = shards // 2
    other = blocks_call(rank_mp, 1 - rank_mp % 2, d_gate, d_up, w_gate, w_up, count)
    if far:
        left = (left + parts[0]) + (parts[1] + parts[2])
    else:
        for mask in masks(replicas):
            left = left + exchange(left, "dp", mask)
    left = after(left, other[0])
    other = [exchange(block, "mp", 1) for block in other]
    total = right_call(left, hid, err_down, out_grads)

    if far:
        got[3, 0] = exchange(after(got[2, 0], total), "dp", 1)
        got[3, 1] = exchange(after(got[1, 1], total), "dp", 2)

    mine = blocks_call(rank_mp, rank_mp % 2, d_gate, d_up, w_gate, w_up, count, tuple(other))
    for mask in masks(shards):
        total = total + exchange(total, "mp", mask)
    for mask in masks(replicas):
        total = total + exchange(total, "dp", mask)
    landed = [exchange(mine[slot], "mp", 2 * slot) for slot in range(1, count)]

    l, r = factors_call(total, left, replicas)
    next_err = error_call(hid, out_grads, err_down, l, r)
    at = jnp.reshape(rank_dp, (1,)).astype(jnp.int32)
    next_mom, new = own_call(at, mom_down, w_down, l, r, half)

    in_grads = mine[0].astype(F32)
    for block in landed:
        in_grads = in_grads + block.astype(F32)
    in_grads = in_grads.astype(BF16)

    def place(keys):
        return jnp.stack([2 * (rank_dp ^ mask) + side for mask, side in keys]).astype(jnp.int32)

    first = [(2, 0), (1, 1)]
    second = [key for key in sorted(got) if key not in first]
    for keys in (first, second):
        new = others_call(place(keys), [got[key] for key in keys], w_down, l, r, new)
    return (in_grads, new, next_err, next_mom)


def solution(mesh):
    in_specs = (
        P("dp", None),
        P("dp", None),
        P(None, "mp"),
        P(None, "mp"),
        P("mp", None),
        P("dp", "mp", None),
        P("mp", "dp"),
        P(),
    )
    out_specs = (P("dp", "mp"), P("mp", None), P("dp", "mp", None), P("mp", "dp"))
    return jax.shard_map(body, mesh=mesh, in_specs=in_specs, out_specs=out_specs, check_vma=False)
```

time: 432 us -> 197 us (0.46)
  waiting for transfers between devices: 220 us -> 49.5 us
  matrix products: 119 us -> 0 us
  Pallas kernels: 0 us -> 109 us
  other arithmetic: 37.1 us -> 6.71 us
  blocking collectives: 26.8 us -> 0 us
  starting transfers between devices: 0.12 us -> 24.6 us
  between operations: 15.7 us -> 0.82 us
  local copies, waits for them, and re-layouts: 10.2 us -> 3.99 us
    psum x1 -> x0, waiting for transfers between devices: 133 us -> none  [body(): right_down = lax.psum(contract_rows(m_down, left_down), ('dp', 'mp'))]
    dot_general x10 -> x0, matrix products: 119 us -> none  [the longest x3 35.5 us: contract_cols(): lax.dot_general(left, right, (((1,), (1,)), ((), ())), preferred_element_...]
    pallas_call x0 -> x10, Pallas kernels: none -> 109 us  [the longest x1 27.6 us: hidden_call(): pl.pallas_call(hidden_kernel, grid=(pl.cdiv(units, tile),), in_specs=[who...]
    all_gather x1 -> x0, waiting for transfers between devices: 87.4 us -> none  [body(): new_down = lax.all_gather(own_down, 'dp', axis=1, tiled=True)]
    ppermute x0 -> x21, waiting for transfers between devices: none -> 49.5 us  [exchange(): return lax.ppermute(value, axis, [(i, i ^ mask) for i in range(size)])]
    psum x2 -> x0, blocking collectives: 26.8 us -> none  [the longest x1 16.7 us: body(): left_down = lax.psum(jnp.dot(m_down, q_down, precision=HIGH), 'dp')]
    ppermute x0 -> x21, starting transfers between devices: none -> 24.6 us  [exchange(): return lax.ppermute(value, axis, [(i, i ^ mask) for i in range(size)])]
    broadcast_in_dim x1 -> x0, other arithmetic: 21.3 us -> none  [body(): next_err_down = (m_down - approx_down).astype(jnp.bfloat16)[None]]
  transfers between devices with their start and end apart: 3 -> 21, of which waited for: 2 -> 5; matrix products, arithmetic and copies ran while one was open for 21% -> 4% of each run, Pallas kernels for 0% -> 31%
where the time goes in v1:
time: 197 us; the launch traced here: 195 us
  Pallas kernels  109 us (55%)
  waiting for transfers between devices  49.5 us (25%)
  starting transfers between devices  24.6 us (12%)
  other arithmetic  6.71 us (3%)
  local copies, waits for them, and re-layouts  3.99 us (2%)
    ppermute x21, waiting for transfers between devices, exchange(): return lax.ppermute(value, axis, [(i, i ^ mask) for i in range(size)])  49.5 us
    pallas_call x1, Pallas kernels, hidden_call(): pl.pallas_call(hidden_kernel, grid=(pl.cdiv(units, tile),), in_specs=[who...  27.6 us
    ppermute x21, starting transfers between devices, exchange(): return lax.ppermute(value, axis, [(i, i ^ mask) for i in range(size)])  24.6 us
    pallas_call x2, Pallas kernels, blocks_call(): pl.pallas_call(functools.partial(blocks_kernel, bool(added)), grid_spec=p...  21 us
    pallas_call x2, Pallas kernels, others_call(): pl.pallas_call(functools.partial(others_kernel, count), grid_spec=pltpu.P...  16.3 us
    pallas_call x1, Pallas kernels, error_call(): pl.pallas_call(error_kernel, grid=(depth // tile,), in_specs=[whole((unit...  14.8 us
    pallas_call x1, Pallas kernels, left_call(): pl.pallas_call(left_kernel, grid=(depth // tile,), in_specs=[pl.BlockSpec...  10.1 us
    pallas_call x1, Pallas kernels, right_call(): pl.pallas_call(right_kernel, grid=(depth // tile,), in_specs=[whole((R, u...  8.46 us
  transfers between devices with their start and end apart: 21, of which 5 were waited for; matrix products, arithmetic and copies ran while one was open for 4% of the time, Pallas kernels for 31%

profile of v1, /device:TPU:8, one launch (start us, length us, event | category | flops | bytes accessed | tf_op | source)
XLA Modules:
  0.0 194.7 jit_solution(15269142634900679329)
XLA Ops:
  0.6 0.0 copy-start
  0.7 27.6 %hidden.1 = (bf16[1376,512]{1,0:T(8,128)(2,1)S(1)}, bf16[512,1376]{1,0:T(8,128)(2,1)S(1)}, bf16[512,1376]{1,0:T(8,128)(2,1)S(1)}) custom-call(bf16[512,4096]{1,0:T(8,128)(2,1)} %x_ref.1, bf16[512,4096]{1,0:T(8,128)(2,1)} %dy_ref.7, bf16[1376,4096]{1,0:T(8,128)(2,1)} %bitcast.14, bf16[1376,4096]{1,0:T(8,128)(2,1)} %bitcast.17, bf16[1376,4096]{1,0:T(8,128)(2,1)} %refs_4_.1), custom_call_target="tpu_custom_call" | custom-call | flops 17314086912 | bytes 42205184 | tf_op jit(solution)/shard_map/hidden/pallas_call | solution.py:71
  28.3 0.0 copy-start.3
  28.3 10.1 %left.1 = f32[8,1376]{1,0:T(8,128)S(1)} custom-call(f32[8,4096]{1,0:T(8,128)S(1)} %bitcast.13, bf16[1,1376,4096]{2,1,0:T(8,128)(2,1)} %err_ref.5, bf16[512,4096]{1,0:T(8,128)(2,1)S(1)} %copy-done, bf16[1376,512]{1,0:T(8,128)(2,1)S(1)} %get-tuple-element.34.hid_ref), custom_call_target="tpu_custom_call" | custom-call | flops 2885681152 | bytes 15466496 | tf_op jit(solution)/shard_map/left/pallas_call | solution.py:119
  38.4 1.6 collective-permute-start.11
  40.0 1.4 collective-permute-start.12
  41.5 0.5 collective-permute-start.10
  42.0 0.1 pad_add_fusion.1.where_ref
  42.1 1.4 copy-done.4
  43.4 9.8 %blocks.2 = (bf16[512,512]{1,0:T(8,128)(2,1)S(1)}, bf16[512,512]{1,0:T(8,128)(2,1)S(1)}, bf16[512,512]{1,0:T(8,128)(2,1)S(1)}, bf16[512,512]{1,0:T(8,128)(2,1)S(1)}) custom-call(s32[2]{0:T(128)S(1)} %pad_add_fusion.1.where_ref, bf16[512,1376]{1,0:T(8,128)(2,1)S(1)} %get-tuple-element.24.dg_ref, bf16[512,1376]{1,0:T(8,128)(2,1)S(1)} %copy-done.4, ...), custom_call_target="tpu_custom_call" | custom-call | flops 5771362304 | bytes 13369344 | tf_op jit(solution)/shard_map/blocks/pallas_call | solution.py:239
  53.2 0.1 collective-permute-start
  53.3 0.5 collective-permute-start.1
  53.8 3.3 %convert.4 = bf16[1376,1024]{1,0:T(8,128)(2,1)S(1)} convert(f32[1376,1024]{1,0:T(8,128)} %mom_ref.1) | non-fusion elementwise | flops 1409024 | bytes 8454144 | tf_op jit(solution)/shard_map/convert.1
  57.1 0.1 collective-permute-start.2
  57.2 0.5 collective-permute-start.3
  57.7 8.5 %right.1 = f32[8,4224]{1,0:T(8,128)S(1)} custom-call(f32[8,1376]{1,0:T(8,128)S(1)} %add_add_fusion.left_ref, bf16[1376,512]{1,0:T(8,128)(2,1)S(1)} %get-tuple-element.34.hid_ref, bf16[1,1376,4096]{2,1,0:T(8,128)(2,1)} %err_ref.5, bf16[512,4096]{1,0:T(8,128)(2,1)S(1)} %copy-done.1), custom_call_target="tpu_custom_call" | custom-call | flops 2885681152 | bytes 15466496 | tf_op jit(solution)/shard_map/right/pallas_call | solution.py:161
  66.2 0.1 collective-permute-start.16
  66.3 1.8 fusion
  68.1 1.5 collective-permute-start.9
  69.7 1.5 collective-permute-start.14
  71.1 0.1 pad_add_fusion.where_ref
  71.2 0.5 collective-permute-start.17
  71.8 11.2 %blocks.3 = (bf16[512,512]{1,0:T(8,128)(2,1)S(1)}, bf16[512,512]{1,0:T(8,128)(2,1)S(1)}, bf16[512,512]{1,0:T(8,128)(2,1)}, bf16[512,512]{1,0:T(8,128)(2,1)S(1)}) custom-call(s32[2]{0:T(128)S(1)} %pad_add_fusion.where_ref, bf16[512,1376]{1,0:T(8,128)(2,1)S(1)} %get-tuple-element.24.dg_ref, bf16[512,1376]{1,0:T(8,128)(2,1)} %copy-done.3, ...), custom_call_target="tpu_custom_call" | custom-call | flops 5771362304 | bytes 13369344 | tf_op jit(solution)/shard_map/blocks/pallas_call | solution.py:239
  83.0 2.7 %collective-permute-start.6 = (bf16[512,512]{1,0:T(8,128)(2,1)S(1)}, bf16[512,512]{1,0:T(8,128)(2,1)S(1)}, u32[]{:S(2)}, u32[]{:S(2)}) collective-permute-start(bf16[512,512]{1,0:T(8,128)(2,1)S(1)} %get-tuple-element.33), channel_id=1, source_target_pairs={{0,6},{1,7},{2,4},{3,5},{4,2},{5,3},{6,0},{7,1},{8,14},{9,15},{10,... | collective-permute-start | bytes 1572872 | tf_op jit(solution)/shard_map/ppermute | solution.py:370
  85.7 1.3 collective-permute-start.18
  87.0 26.7 %collective-permute-done.18 = f32[8,4224]{1,0:T(8,128)S(1)} collective-permute-done((f32[8,4224]{1,0:T(8,128)S(1)}, f32[8,4224]{1,0:T(8,128)S(1)}, u32[]{:S(2)}, u32[]{:S(2)}) %collective-permute-start.18) | collective-permute-done | bytes 135200 | tf_op jit(solution)/shard_map/ppermute | solution.py:370
  113.7 0.6 collective-permute-start.19
  114.3 4.5 %collective-permute-done.19 = f32[8,4224]{1,0:T(8,128)S(1)} collective-permute-done((f32[8,4224]{1,0:T(8,128)S(1)}, f32[8,4224]{1,0:T(8,128)S(1)}, u32[]{:S(2)}, u32[]{:S(2)}) %collective-permute-start.19) | collective-permute-done | bytes 135200 | tf_op jit(solution)/shard_map/ppermute | solution.py:370
  118.8 0.6 collective-permute-start.20
  119.3 3.4 %collective-permute-start.5 = (bf16[512,512]{1,0:T(8,128)(2,1)}, bf16[512,512]{1,0:T(8,128)(2,1)}, u32[]{:S(2)}, u32[]{:S(2)}) collective-permute-start(bf16[512,512]{1,0:T(8,128)(2,1)} %get-tuple-element.32), channel_id=1, source_target_pairs={{0,4},{1,5},{2,6},{3,7},{4,0},{5,1},{6,2},{7,3},{8,12},{9,13},{10,... | collective-permute-start | bytes 1572872 | tf_op jit(solution)/shard_map/ppermute | solution.py:370
  122.7 0.5 collective-permute-start.7
  123.3 1.5 collective-permute-start.8
  124.8 1.5 collective-permute-start.13
  126.3 0.8 copy-done.8
  127.1 0.5 collective-permute-start.15
  127.6 0.1 pad_add_fusion.3.at_ref
  127.7 0.1 pad_add_fusion.2.at_ref
  127.8 0.9 add.61.sum_ref
  128.7 2.5 %factors.1 = (bf16[1376,32]{1,0:T(8,128)(2,1)S(1)}, bf16[32,4096]{1,0:T(8,128)(2,1)S(1)}) custom-call(f32[8,4224]{1,0:T(8,128)S(1)} %add.61.sum_ref, f32[8,1376]{1,0:T(8,128)S(1)} %add_add_fusion.left_ref), custom_call_target="tpu_custom_call" | custom-call | flops 134479872 | bytes 175104 | tf_op jit(solution)/shard_map/factors/pallas_call | solution.py:207
  131.2 8.3 %own.1 = (f32[1376,1024]{1,0:T(8,128)}, bf16[1376,4096]{1,0:T(8,128)(2,1)}) custom-call(s32[1]{0:T(128)} %bitcast.12.at_ref, f32[1376,1024]{1,0:T(8,128)} %mom_ref.1, bf16[1376,4096]{1,0:T(8,128)(2,1)} %refs_4_.1, bf16[1376,32]{1,0:T(8,128)(2,1)S(1)} %get-tuple-element.40.l_ref.refs_3_.refs_5_, bf16[32,4096]{1,0:T(8,128)(2,1)S(1)} %get-tuple-element.41.r_ref.refs_4_.refs_6_), custom_call_target="tpu_custom_call" | custom-call | flops 721420288 | bytes 16908288 | tf_op jit(solution)/shard_map/own/pallas_call | solution.py:303
  139.5 2.3 %collective-permute-done.5 = bf16[512,512]{1,0:T(8,128)(2,1)} collective-permute-done((bf16[512,512]{1,0:T(8,128)(2,1)}, bf16[512,512]{1,0:T(8,128)(2,1)}, u32[]{:S(2)}, u32[]{:S(2)}) %collective-permute-start.5) | collective-permute-done | bytes 524320 | tf_op jit(solution)/shard_map/ppermute | solution.py:370
  141.8 3.7 %collective-permute-start.4 = (bf16[512,512]{1,0:T(8,128)(2,1)S(1)}, bf16[512,512]{1,0:T(8,128)(2,1)S(1)}, u32[]{:S(2)}, u32[]{:S(2)}) collective-permute-start(bf16[512,512]{1,0:T(8,128)(2,1)S(1)} %copy-done.7), channel_id=1, source_target_pairs={{0,2},{1,3},{2,0},{3,1},{4,6},{5,7},{6,4},{7,5},{8,10},{9,11},{10,... | collective-permute-start | bytes 1572872 | tf_op jit(solution)/shard_map/ppermute | solution.py:370
  145.4 14.8 %error.1 = bf16[1,1376,4096]{2,1,0:T(8,128)(2,1)} custom-call(bf16[1376,512]{1,0:T(8,128)(2,1)S(1)} %get-tuple-element.34.hid_ref, bf16[512,4096]{1,0:T(8,128)(2,1)S(1)} %copy-done.2, bf16[1,1376,4096]{2,1,0:T(8,128)(2,1)} %err_ref.5, bf16[1376,32]{1,0:T(8,128)(2,1)S(1)} %get-tuple-element.40.l_ref.refs_3_.refs_5_, ...), custom_call_target="tpu_custom_call" | custom-call | flops 5771362304 | bytes 26738688 | tf_op jit(solution)/shard_map/error/pallas_call | solution.py:264
  160.2 2.1 %add_convert_fusion = bf16[512,512]{1,0:T(8,128)(2,1)} fusion(bf16[512,512]{1,0:T(8,128)(2,1)S(1)} %copy-done.9, bf16[512,512]{1,0:T(8,128)(2,1)} %collective-permute-done.5, bf16[512,512]{1,0:T(8,128)(2,1)S(1)} %collective-permute-done.4, bf16[512,512]{1,0:T(8,128)(2,1)S(1)} %get-tuple-element.30), kind=kLoop, calls=%fused_computation | loop fusion | flops 2097152 | bytes 2621440 | tf_op jit(solution)/shard_map/convert_element_type | solution.py:439
  162.3 6.0 %others.2.refs_7_ = bf16[1376,4096]{1,0:T(8,128)(2,1)} custom-call(s32[2]{0:T(128)S(1)} %pad_add_fusion.3.at_ref, bf16[1376,512]{1,0:T(8,128)(2,1)} %collective-permute-done.9.refs_0_, bf16[1376,512]{1,0:T(8,128)(2,1)} %collective-permute-done.14.refs_1_, bf16[1376,4096]{1,0:T(8,128)(2,1)} %refs_4_.1, ...), custom_call_target="tpu_custom_call", output_to_operand_aliasing={{}: (6, {})} | custom-call | flops 721420288 | bytes 8454144 | tf_op jit(solution)/shard_map/others/pallas_call | solution.py:346
  168.3 15.2 %collective-permute-done.13.refs_2_ = bf16[1376,512]{1,0:T(8,128)(2,1)} collective-permute-done((bf16[1376,512]{1,0:T(8,128)(2,1)}, bf16[1376,512]{1,0:T(8,128)(2,1)}, u32[]{:S(2)}, u32[]{:S(2)}) %collective-permute-start.13) | collective-permute-done | bytes 1409056 | tf_op jit(solution)/shard_map/ppermute | solution.py:370
  183.5 0.9 collective-permute-done.15.refs_3_
  184.3 10.3 %others.3 = bf16[1376,4096]{1,0:T(8,128)(2,1)} custom-call(s32[4]{0:T(128)S(1)} %pad_add_fusion.2.at_ref, bf16[1376,512]{1,0:T(8,128)(2,1)S(1)} %collective-permute-done.7.refs_0_, bf16[1376,512]{1,0:T(8,128)(2,1)} %collective-permute-done.8.refs_1_, bf16[1376,512]{1,0:T(8,128)(2,1)} %collective-permute-done.13.refs_2_, ...), custom_call_target="tpu_custom_call", output_to_operand_aliasing={{}: (8, {})} | custom-call | flops 1442840576 | bytes 16908288 | tf_op jit(solution)/shard_map/others/pallas_call | solution.py:346
  (40 shorter events, 0.2 us)
Async XLA Ops:
  0.6 27.7 %copy-start = (bf16[512,4096]{1,0:T(8,128)(2,1)S(1)}, bf16[512,4096]{1,0:T(8,128)(2,1)}, u32[]{:S(2)}) copy-start(bf16[512,4096]{1,0:T(8,128)(2,1)} %dy_ref.7) | copy-start | bytes 12582916
  0.6 27.7 %copy-start.5 = (f32[4096,8]{0,1:T(8,128)S(1)}, f32[4096,8]{0,1:T(8,128)}, u32[]{:S(2)}) copy-start(f32[4096,8]{0,1:T(8,128)} %param.15) | copy-start | bytes 393220
  28.3 10.2 %copy-start.3 = (bf16[512,1376]{1,0:T(8,128)(2,1)}, bf16[512,1376]{1,0:T(8,128)(2,1)S(1)}, u32[]{:S(2)}) copy-start(bf16[512,1376]{1,0:T(8,128)(2,1)S(1)} %get-tuple-element.25.du_ref) | copy-start | bytes 4227076
  38.4 18.7 %collective-permute-start.11 = (f32[8,1376]{1,0:T(8,128)S(1)}, f32[8,1376]{1,0:T(8,128)S(1)}, u32[]{:S(2)}, u32[]{:S(2)}) collective-permute-start(f32[8,1376]{1,0:T(8,128)S(1)} %broadcast_multiply_fusion), channel_id=1, source_target_pairs={{0,16},{8,24},{16,0},{24,8},{1,17},{9,25},{17,1},{25,9},{2,18},{10... | collective-permute-start | bytes 132104 | tf_op jit(solution)/shard_map/ppermute | solution.py:370
  40.0 17.2 %collective-permute-start.12 = (f32[8,1376]{1,0:T(8,128)S(1)}, f32[8,1376]{1,0:T(8,128)S(1)}, u32[]{:S(2)}, u32[]{:S(2)}) collective-permute-start(f32[8,1376]{1,0:T(8,128)S(1)} %broadcast_multiply_fusion), channel_id=1, source_target_pairs={{0,24},{8,16},{16,8},{24,0},{1,25},{9,17},{17,9},{25,1},{2,26},{10... | collective-permute-start | bytes 132104 | tf_op jit(solution)/shard_map/ppermute | solution.py:370
  41.5 16.2 %collective-permute-start.10 = (f32[8,1376]{1,0:T(8,128)S(1)}, f32[8,1376]{1,0:T(8,128)S(1)}, u32[]{:S(2)}, u32[]{:S(2)}) collective-permute-start(f32[8,1376]{1,0:T(8,128)S(1)} %broadcast_multiply_fusion), channel_id=1, source_target_pairs={{0,8},{8,0},{16,24},{24,16},{1,9},{9,1},{17,25},{25,17},{2,10},{10... | collective-permute-start | bytes 132104 | tf_op jit(solution)/shard_map/ppermute | solution.py:370
  42.1 1.4 copy-start.4
  53.2 16.4 %collective-permute-start = (bf16[512,512]{1,0:T(8,128)(2,1)S(1)}, bf16[512,512]{1,0:T(8,128)(2,1)S(1)}, u32[]{:S(2)}, u32[]{:S(2)}) collective-permute-start(bf16[512,512]{1,0:T(8,128)(2,1)S(1)} %get-tuple-element.26), channel_id=1, source_target_pairs={{0,1},{1,0},{2,3},{3,2},{4,5},{5,4},{6,7},{7,6},{8,9},{9,8},{10,11... | collective-permute-start | bytes 1572872 | tf_op jit(solution)/shard_map/ppermute | solution.py:370
  53.3 4.4 %copy-start.1 = (bf16[512,4096]{1,0:T(8,128)(2,1)S(1)}, bf16[512,4096]{1,0:T(8,128)(2,1)}, u32[]{:S(2)}) copy-start(bf16[512,4096]{1,0:T(8,128)(2,1)} %dy_ref.7) | copy-start | bytes 12582916
  53.3 17.9 %collective-permute-start.1 = (bf16[512,512]{1,0:T(8,128)(2,1)S(1)}, bf16[512,512]{1,0:T(8,128)(2,1)S(1)}, u32[]{:S(2)}, u32[]{:S(2)}) collective-permute-start(bf16[512,512]{1,0:T(8,128)(2,1)S(1)} %get-tuple-element.27), channel_id=1, source_target_pairs={{0,1},{1,0},{2,3},{3,2},{4,5},{5,4},{6,7},{7,6},{8,9},{9,8},{10,11... | collective-permute-start | bytes 1572872 | tf_op jit(solution)/shard_map/ppermute | solution.py:370
  57.1 14.6 %collective-permute-start.2 = (bf16[512,512]{1,0:T(8,128)(2,1)S(1)}, bf16[512,512]{1,0:T(8,128)(2,1)S(1)}, u32[]{:S(2)}, u32[]{:S(2)}) collective-permute-start(bf16[512,512]{1,0:T(8,128)(2,1)S(1)} %get-tuple-element.28), channel_id=1, source_target_pairs={{0,1},{1,0},{2,3},{3,2},{4,5},{5,4},{6,7},{7,6},{8,9},{9,8},{10,11... | collective-permute-start | bytes 1572872 | tf_op jit(solution)/shard_map/ppermute | solution.py:370
  57.2 14.6 %collective-permute-start.3 = (bf16[512,512]{1,0:T(8,128)(2,1)S(1)}, bf16[512,512]{1,0:T(8,128)(2,1)S(1)}, u32[]{:S(2)}, u32[]{:S(2)}) collective-permute-start(bf16[512,512]{1,0:T(8,128)(2,1)S(1)} %get-tuple-element.29), channel_id=1, source_target_pairs={{0,1},{1,0},{2,3},{3,2},{4,5},{5,4},{6,7},{7,6},{8,9},{9,8},{10,11... | collective-permute-start | bytes 1572872 | tf_op jit(solution)/shard_map/ppermute | solution.py:370
  66.2 1.9 collective-permute-start.16
  68.1 54.6 %collective-permute-start.9 = (bf16[1376,512]{1,0:T(8,128)(2,1)}, bf16[1376,512]{1,0:T(8,128)(2,1)}, u32[]{:S(2)}, u32[]{:S(2)}) collective-permute-start(bf16[1376,512]{1,0:T(8,128)(2,1)} %get-tuple-element.35), channel_id=1, source_target_pairs={{0,16},{8,24},{16,0},{24,8},{1,17},{9,25},{17,1},{25,9},{2,18},{10... | collective-permute-start | bytes 4227080 | tf_op jit(solution)/shard_map/ppermute | solution.py:370
  69.7 53.6 %collective-permute-start.14 = (bf16[1376,512]{1,0:T(8,128)(2,1)}, bf16[1376,512]{1,0:T(8,128)(2,1)}, u32[]{:S(2)}, u32[]{:S(2)}) collective-permute-start(bf16[1376,512]{1,0:T(8,128)(2,1)} %get-tuple-element.36), channel_id=1, source_target_pairs={{0,8},{8,0},{16,24},{24,16},{1,9},{9,1},{17,25},{25,17},{2,10},{10... | collective-permute-start | bytes 4227080 | tf_op jit(solution)/shard_map/ppermute | solution.py:370
  71.2 14.4 %collective-permute-start.17 = (f32[8,4224]{1,0:T(8,128)S(1)}, f32[8,4224]{1,0:T(8,128)S(1)}, u32[]{:S(2)}, u32[]{:S(2)}) collective-permute-start(f32[8,4224]{1,0:T(8,128)S(1)} %add.57), channel_id=1, source_target_pairs={{0,2},{1,3},{2,0},{3,1},{4,6},{5,7},{6,4},{7,5},{8,10},{9,11},{10,... | collective-permute-start | bytes 405512 | tf_op jit(solution)/shard_map/ppermute | solution.py:370
  83.0 39.7 %copy-start.6 = (bf16[512,512]{1,0:T(8,128)(2,1)}, bf16[512,512]{1,0:T(8,128)(2,1)S(1)}, u32[]{:S(2)}) copy-start(bf16[512,512]{1,0:T(8,128)(2,1)S(1)} %get-tuple-element.31) | copy-start | bytes 1572868
  83.0 43.3 %collective-permute-start.6 = (bf16[512,512]{1,0:T(8,128)(2,1)S(1)}, bf16[512,512]{1,0:T(8,128)(2,1)S(1)}, u32[]{:S(2)}, u32[]{:S(2)}) collective-permute-start(bf16[512,512]{1,0:T(8,128)(2,1)S(1)} %get-tuple-element.33), channel_id=1, source_target_pairs={{0,6},{1,7},{2,4},{3,5},{4,2},{5,3},{6,0},{7,1},{8,14},{9,15},{10,... | collective-permute-start | bytes 1572872 | tf_op jit(solution)/shard_map/ppermute | solution.py:370
  85.7 28.0 %collective-permute-start.18 = (f32[8,4224]{1,0:T(8,128)S(1)}, f32[8,4224]{1,0:T(8,128)S(1)}, u32[]{:S(2)}, u32[]{:S(2)}) collective-permute-start(f32[8,4224]{1,0:T(8,128)S(1)} %add.58), channel_id=1, source_target_pairs={{0,4},{1,5},{2,6},{3,7},{4,0},{5,1},{6,2},{7,3},{8,12},{9,13},{10,... | collective-permute-start | bytes 405512 | tf_op jit(solution)/shard_map/ppermute | solution.py:370
  113.7 5.1 %collective-permute-start.19 = (f32[8,4224]{1,0:T(8,128)S(1)}, f32[8,4224]{1,0:T(8,128)S(1)}, u32[]{:S(2)}, u32[]{:S(2)}) collective-permute-start(f32[8,4224]{1,0:T(8,128)S(1)} %add.59), channel_id=1, source_target_pairs={{0,8},{8,0},{16,24},{24,16},{1,9},{9,1},{17,25},{25,17},{2,10},{10... | collective-permute-start | bytes 405512 | tf_op jit(solution)/shard_map/ppermute | solution.py:370
  118.8 6.0 %collective-permute-start.20 = (f32[8,4224]{1,0:T(8,128)S(1)}, f32[8,4224]{1,0:T(8,128)S(1)}, u32[]{:S(2)}, u32[]{:S(2)}) collective-permute-start(f32[8,4224]{1,0:T(8,128)S(1)} %add.60), channel_id=1, source_target_pairs={{0,16},{8,24},{16,0},{24,8},{1,17},{9,25},{17,1},{25,9},{2,18},{10... | collective-permute-start | bytes 405512 | tf_op jit(solution)/shard_map/ppermute | solution.py:370
  119.3 22.4 %collective-permute-start.5 = (bf16[512,512]{1,0:T(8,128)(2,1)}, bf16[512,512]{1,0:T(8,128)(2,1)}, u32[]{:S(2)}, u32[]{:S(2)}) collective-permute-start(bf16[512,512]{1,0:T(8,128)(2,1)} %get-tuple-element.32), channel_id=1, source_target_pairs={{0,4},{1,5},{2,6},{3,7},{4,0},{5,1},{6,2},{7,3},{8,12},{9,13},{10,... | collective-permute-start | bytes 1572872 | tf_op jit(solution)/shard_map/ppermute | solution.py:370
  122.7 45.6 %collective-permute-start.7 = (bf16[1376,512]{1,0:T(8,128)(2,1)}, bf16[1376,512]{1,0:T(8,128)(2,1)S(1)}, u32[]{:S(2)}, u32[]{:S(2)}) collective-permute-start(bf16[1376,512]{1,0:T(8,128)(2,1)} %get-tuple-element.35), channel_id=1, source_target_pairs={{0,8},{8,0},{16,24},{24,16},{1,9},{9,1},{17,25},{25,17},{2,10},{10... | collective-permute-start | bytes 4227080 | tf_op jit(solution)/shard_map/ppermute | solution.py:370
  123.3 45.1 %collective-permute-start.8 = (bf16[1376,512]{1,0:T(8,128)(2,1)}, bf16[1376,512]{1,0:T(8,128)(2,1)}, u32[]{:S(2)}, u32[]{:S(2)}) collective-permute-start(bf16[1376,512]{1,0:T(8,128)(2,1)} %get-tuple-element.36), channel_id=1, source_target_pairs={{0,16},{8,24},{16,0},{24,8},{1,17},{9,25},{17,1},{25,9},{2,18},{10... | collective-permute-start | bytes 4227080 | tf_op jit(solution)/shard_map/ppermute | solution.py:370
  124.8 1.5 copy-start.10
  124.8 58.7 %collective-permute-start.13 = (bf16[1376,512]{1,0:T(8,128)(2,1)}, bf16[1376,512]{1,0:T(8,128)(2,1)}, u32[]{:S(2)}, u32[]{:S(2)}) collective-permute-start(bf16[1376,512]{1,0:T(8,128)(2,1)} %collective-permute-done.9.refs_0_), channel_id=1, source_target_pairs={{0,8},{8,0},{16,24},{24,16},{1,9},{9,1},{17,25},{25,17},{2,10},{10... | collective-permute-start | bytes 4227080 | tf_op jit(solution)/shard_map/ppermute | solution.py:370
  126.3 0.8 copy-start.8
  127.1 57.2 %collective-permute-start.15 = (bf16[1376,512]{1,0:T(8,128)(2,1)}, bf16[1376,512]{1,0:T(8,128)(2,1)}, u32[]{:S(2)}, u32[]{:S(2)}) collective-permute-start(bf16[1376,512]{1,0:T(8,128)(2,1)} %collective-permute-done.14.refs_1_), channel_id=1, source_target_pairs={{0,16},{8,24},{16,0},{24,8},{1,17},{9,25},{17,1},{25,9},{2,18},{10... | collective-permute-start | bytes 4227080 | tf_op jit(solution)/shard_map/ppermute | solution.py:370
  131.2 10.6 %copy-start.7 = (bf16[512,512]{1,0:T(8,128)(2,1)S(1)}, bf16[512,512]{1,0:T(8,128)(2,1)}, u32[]{:S(2)}) copy-start(bf16[512,512]{1,0:T(8,128)(2,1)} %copy-done.6) | copy-start | bytes 1572868
  131.2 14.2 %copy-start.2 = (bf16[512,4096]{1,0:T(8,128)(2,1)S(1)}, bf16[512,4096]{1,0:T(8,128)(2,1)}, u32[]{:S(2)}) copy-start(bf16[512,4096]{1,0:T(8,128)(2,1)} %dy_ref.7) | copy-start | bytes 12582916
  141.8 18.4 %copy-start.9 = (bf16[512,512]{1,0:T(8,128)(2,1)S(1)}, bf16[512,512]{1,0:T(8,128)(2,1)}, u32[]{:S(2)}) copy-start(bf16[512,512]{1,0:T(8,128)(2,1)} %copy-done.8) | copy-start | bytes 1572868
  141.8 18.4 %collective-permute-start.4 = (bf16[512,512]{1,0:T(8,128)(2,1)S(1)}, bf16[512,512]{1,0:T(8,128)(2,1)S(1)}, u32[]{:S(2)}, u32[]{:S(2)}) collective-permute-start(bf16[512,512]{1,0:T(8,128)(2,1)S(1)} %copy-done.7), channel_id=1, source_target_pairs={{0,2},{1,3},{2,0},{3,1},{4,6},{5,7},{6,4},{7,5},{8,10},{9,11},{10,... | collective-permute-start | bytes 1572872 | tf_op jit(solution)/shard_map/ppermute | solution.py:370

commit v2 on v0

v2 whole, which is shorter than its diff:
```python
import functools

import jax
import jax.numpy as jnp
from jax import lax
from jax.experimental import pallas as pl
from jax.experimental.pallas import tpu as pltpu
from jax.sharding import PartitionSpec as P

R = 8
SPLIT = 4 * R
EPS = 1e-06
F32 = jnp.float32
BF16 = jnp.bfloat16
HIGH = lax.Precision.HIGHEST
VMEM = 48 * 2**20
ONCE = pl.Buffered(1)
HELD = pl.BlockSpec(memory_space=pl.ANY)


def launch(kernel, name, grid, args, in_specs, out_specs, out_shape, *, places=(), held=(),
           through=(), scratch=(), aliases=None):
    n_in, n_out = len(args), len(out_shape)
    n_held, n_through, n_place = len(held), len(through), len(places)
    first = n_place + n_in

    def inner(*refs):
        outs = first + n_held + n_through
        kernel(*refs[:first], *refs[outs : outs + n_out], *refs[outs + n_out + n_through :])

    links = {first + n_held + i: n_out + i for i in range(n_through)}
    return pl.pallas_call(
        inner,
        grid_spec=pltpu.PrefetchScalarGridSpec(
            num_scalar_prefetch=n_place,
            grid=grid,
            in_specs=list(in_specs) + [HELD] * (n_held + n_through),
            out_specs=list(out_specs) + [HELD] * n_through,
            scratch_shapes=list(scratch),
        ),
        out_shape=list(out_shape)
        + [jax.ShapeDtypeStruct(array.shape, array.dtype) for array in through],
        input_output_aliases={**links, **(aliases or {})},
        compiler_params=pltpu.CompilerParams(vmem_limit_bytes=VMEM),
        cost_estimate=pl.CostEstimate(flops=1, bytes_accessed=1, transcendentals=0),
        name=name,
    )(*places, *args, *held, *through)


def shaped(shape, dtype):
    return jax.ShapeDtypeStruct(shape, dtype)


def dot(left, right):
    return jnp.dot(left, right, preferred_element_type=F32)


def dot_nt(left, right):
    return lax.dot_general(left, right, (((1,), (1,)), ((), ())), preferred_element_type=F32)


def terms(rows):
    hi = rows.astype(BF16).astype(F32)
    rest = rows - hi
    mid = rest.astype(BF16).astype(F32)
    return hi, mid, rest - mid


def spread(rows):
    hi, mid, low = terms(rows)
    return jnp.concatenate([hi, mid, low, jnp.zeros_like(hi)], axis=0).astype(BF16)


def gather_terms(rows):
    return rows[:R] + rows[R : 2 * R] + rows[2 * R : 3 * R]


def tree(parts):
    while len(parts) > 1:
        odd = parts[len(parts) // 2 * 2 :]
        parts = [left + right for left, right in zip(parts[::2], parts[1::2])] + odd
    return parts[0]


def whole(shape):
    return pl.BlockSpec(shape, lambda *_: (0,) * len(shape), pipeline_mode=ONCE)


def row_tile(units):
    return units // 2 if units % 32 == 0 and units > 512 else units


def cast_kernel(mom_ref, *halves):
    half = halves[0].shape[1]
    low, high = mom_ref[:, :half].astype(BF16), mom_ref[:, half:].astype(BF16)
    halves[0][...] = low
    halves[1][...] = high
    halves[2][...] = low
    halves[3][...] = high


def cast_call(mom):
    units, cols = mom.shape
    tile = row_tile(units)
    part = pl.BlockSpec((tile, cols // 2), lambda f: (f, 0))
    return launch(
        cast_kernel,
        "cast",
        (units // tile,),
        [mom],
        [pl.BlockSpec((tile, cols), lambda f: (f, 0))],
        [part] * 4,
        [shaped((units, cols // 2), BF16)] * 4,
    )


def hidden_kernel(x_ref, wg_ref, wu_ref, hid_ref, fac_ref, silu_ref):
    gate = dot_nt(x_ref[...], wg_ref[...])
    up = dot_nt(x_ref[...], wu_ref[...])
    sig = jax.nn.sigmoid(gate)
    silu = gate * sig
    hid_ref[...] = (silu * up).T.astype(BF16)
    fac_ref[...] = up * sig * (1.0 + gate * (1.0 - sig))
    silu_ref[...] = silu


def hidden_call(x, wg, wu, **links):
    tok, depth = x.shape
    units = wg.shape[0]
    tile = min(256, units)
    rows = pl.BlockSpec((tile, depth), lambda f: (f, 0))
    part = pl.BlockSpec((tok, tile), lambda f: (0, f))
    return launch(
        hidden_kernel,
        "hidden",
        (pl.cdiv(units, tile),),
        [x, wg, wu],
        [whole((tok, depth)), rows, rows],
        [pl.BlockSpec((tile, tok), lambda f: (f, 0)), part, part],
        [shaped((units, tok), BF16), shaped((tok, units), F32), shaped((tok, units), F32)],
        **links,
    )


def slopes_kernel(dy_ref, wd_ref, fac_ref, silu_ref, dg_ref, du_ref):
    dh = dot_nt(dy_ref[...], wd_ref[...])
    dg_ref[...] = (dh * fac_ref[...]).astype(BF16)
    du_ref[...] = (dh * silu_ref[...]).astype(BF16)


def slopes_call(dy, wd, fac, silu, **links):
    tok, depth = dy.shape
    units = wd.shape[0]
    tile = min(256, units)
    part = pl.BlockSpec((tok, tile), lambda f: (0, f))
    return launch(
        slopes_kernel,
        "slopes",
        (pl.cdiv(units, tile),),
        [dy, wd, fac, silu],
        [whole((tok, depth)), pl.BlockSpec((tile, depth), lambda f: (f, 0)), part, part],
        [part, part],
        [shaped((tok, units), BF16)] * 2,
        **links,
    )


def left_kernel(replicas, q_ref, err_ref, dy_ref, hid_ref, out_ref, err_acc, dy_acc):
    step = pl.program_id(0)

    @pl.when(step == 0)
    def _():
        err_acc[...] = jnp.zeros_like(err_acc)
        dy_acc[...] = jnp.zeros_like(dy_acc)

    q = spread(q_ref[...])
    err_acc[...] += dot_nt(err_ref[0], q)
    dy_acc[...] += dot_nt(dy_ref[...], q)

    @pl.when(step == pl.num_programs(0) - 1)
    def _():
        mixed = spread(gather_terms(dy_acc[...].T))
        both = gather_terms((err_acc[...] + dot_nt(hid_ref[...], mixed)).T)
        out_ref[...] = both / replicas


def left_call(q_t, err, dy, hid, replicas, **links):
    units, tok = hid.shape
    depth = dy.shape[1]
    tile = min(512, depth)
    return launch(
        functools.partial(left_kernel, replicas),
        "left",
        (depth // tile,),
        [q_t, err, dy, hid],
        [
            pl.BlockSpec((R, tile), lambda d: (0, d)),
            pl.BlockSpec((1, units, tile), lambda d: (0, 0, d)),
            pl.BlockSpec((tok, tile), lambda d: (0, d)),
            whole((units, tok)),
        ],
        [whole((R, units))],
        [shaped((R, units), F32)],
        scratch=[pltpu.VMEM((units, SPLIT), F32), pltpu.VMEM((tok, SPLIT), F32)],
        **links,
    )


def right_kernel(parts, *refs):
    lefts, (hid_ref, err_ref, dy_ref, out_ref, left_ref, left_terms, mixed_terms) = (
        refs[:parts],
        refs[parts:],
    )
    step = pl.program_id(0)
    depth = dy_ref.shape[1]

    @pl.when(step == 0)
    def _():
        left = tree([ref[...] for ref in lefts])
        left_ref[...] = left
        left_terms[...] = spread(left)
        mixed_terms[...] = spread(gather_terms(dot(left_terms[...], hid_ref[...])))
        gram = lax.dot_general(
            left, left, (((1,), (1,)), ((), ())), precision=HIGH, preferred_element_type=F32
        )
        out_ref[:, out_ref.shape[1] - 128 :] = jnp.concatenate(
            [gram, jnp.zeros((R, 128 - R), F32)], axis=1
        )

    part = dot(left_terms[...], err_ref[0]) + dot(mixed_terms[...], dy_ref[...])
    out_ref[:, pl.ds(pl.multiple_of(step * depth, depth), depth)] = gather_terms(part)


def right_call(lefts, hid, err, dy, **links):
    units, tok = hid.shape
    depth = dy.shape[1]
    tile = min(512, depth)
    return launch(
        functools.partial(right_kernel, len(lefts)),
        "right",
        (depth // tile,),
        [*lefts, hid, err, dy],
        [whole((R, units))] * len(lefts)
        + [
            whole((units, tok)),
            pl.BlockSpec((1, units, tile), lambda d: (0, 0, d)),
            pl.BlockSpec((tok, tile), lambda d: (0, d)),
        ],
        [whole((R, depth + 128)), whole((R, units))],
        [shaped((R, depth + 128), F32), shaped((R, units), F32)],
        scratch=[pltpu.VMEM((SPLIT, units), BF16), pltpu.VMEM((SPLIT, tok), BF16)],
        **links,
    )


def sum_kernel(one_ref, two_ref, out_ref):
    out_ref[...] = one_ref[...] + two_ref[...]


def sum_call(one, two, **links):
    return launch(
        sum_kernel,
        "sum",
        (1,),
        [one, two],
        [whole(one.shape)] * 2,
        [whole(one.shape)],
        [shaped(one.shape, one.dtype)],
        **links,
    )


def join_kernel(*refs):
    refs[-1][...] = tree([ref[...].astype(F32) for ref in refs[:-1]]).astype(BF16)


def join_call(parts, **links):
    shape = parts[0].shape
    return launch(
        join_kernel,
        "join",
        (1,),
        parts,
        [whole(shape)] * len(parts),
        [whole(shape)],
        [shaped(shape, BF16)],
        **links,
    )


def factors_kernel(replicas, sum_ref, left_ref, l_ref, r_ref):
    depth = r_ref.shape[1]
    gram = sum_ref[:, depth : depth + R] / replicas
    row = lax.broadcasted_iota(jnp.int32, (R, R), 0)
    col = lax.broadcasted_iota(jnp.int32, (R, R), 1)
    eye = (row == col).astype(F32)
    basis = jnp.zeros((R, R), F32)
    for k in range(R):
        unit = eye[k : k + 1]
        coeffs = jnp.sum(basis * gram[k : k + 1], axis=1, keepdims=True)
        rest = unit - jnp.sum(coeffs * basis, axis=0, keepdims=True)
        rest_col = jnp.sum(eye * rest, axis=1, keepdims=True)
        image = jnp.sum(rest_col * gram, axis=0, keepdims=True)
        square = jnp.sum(image * rest, axis=1, keepdims=True)
        basis = jnp.where(row == k, rest * lax.rsqrt(jnp.maximum(square, 0.0) + EPS), basis)
    left = jnp.dot(basis, left_ref[...], precision=HIGH, preferred_element_type=F32)
    right = jnp.dot(basis, sum_ref[:, :depth], precision=HIGH, preferred_element_type=F32)
    hi, mid, _ = terms(left)
    zero = jnp.zeros_like(hi)
    l_ref[...] = jnp.concatenate([hi, hi, mid, zero], axis=0).T.astype(BF16)
    hi, mid, _ = terms(right / replicas)
    zero = jnp.zeros_like(hi)
    r_ref[...] = jnp.concatenate([hi, mid, hi, zero], axis=0).astype(BF16)


def factors_call(total, left, replicas, **links):
    units = left.shape[1]
    depth = total.shape[1] - 128
    return launch(
        functools.partial(factors_kernel, replicas),
        "factors",
        (1,),
        [total, left],
        [whole(total.shape), whole(left.shape)],
        [whole((units, SPLIT)), whole((SPLIT, depth))],
        [shaped((units, SPLIT), BF16), shaped((SPLIT, depth), BF16)],
        **links,
    )


def other_kernel(where_ref, dg_ref, du_ref, wg_ref, wu_ref, out_ref):
    out_ref[0] = (dot(dg_ref[...], wg_ref[...]) + dot(du_ref[...], wu_ref[...])).astype(BF16)


def mine_kernel(where_ref, dg_ref, du_ref, wg_ref, wu_ref, add_ref, *outs):
    part = dot(dg_ref[...], wg_ref[...]) + dot(du_ref[...], wu_ref[...])
    part = (part + add_ref[0].astype(F32)).astype(BF16)
    for slot, out in enumerate(outs):

        @pl.when(pl.program_id(0) == slot)
        def _(out=out):
            out[...] = part


def blocks_call(pos, parity, slots, count, dg, du, wg, wu, add=None, **links):
    tok, units = dg.shape
    depth = wg.shape[1]
    width = depth // (2 * count)
    where = jnp.stack([pos // 2, parity]).astype(jnp.int32)
    first, steps = slots
    block = pl.BlockSpec((units, width), lambda s, at: (0, 2 * ((s + first) ^ at[0]) + at[1]))
    slot = pl.BlockSpec((1, tok, width), lambda s, at: (s, 0, 0))
    in_specs = [whole((tok, units)), whole((tok, units)), block, block]
    args = [dg, du, wg, wu]
    if add is None:
        kernel = other_kernel
        out_specs = [slot]
        out_shape = [shaped((steps, tok, width), BF16)]
    else:
        kernel = mine_kernel
        in_specs.append(slot)
        args.append(add)
        out_specs = [whole((tok, width))] * steps
        out_shape = [shaped((tok, width), BF16)] * steps
    return launch(
        kernel, "blocks", (steps,), args, in_specs, out_specs, out_shape, places=[where], **links
    )


def updated(w, mom, approx):
    return (w.astype(F32) - 0.1 * (0.9 * mom.astype(F32) + approx)).astype(BF16)


def final_kernel(early, own, at_ref, hid_ref, dy_ref, err_ref, l_ref, r_ref, w_ref, mom_ref, *refs):
    pieces, (err_out, w_out, mom_out) = refs[:-3], refs[-3:]
    step = pl.program_id(0)
    approx = dot(l_ref[...], r_ref[...])
    grown = dot(hid_ref[...], dy_ref[...]) + err_ref[0].astype(F32)
    err_out[0] = (grown - approx).astype(BF16)

    @pl.when((step >= early) & (step < early + own))
    def _():
        mom = mom_ref[...]
        mom_out[...] = 0.9 * mom + approx
        w_out[...] = updated(w_ref[...], mom.astype(BF16), approx)

    for slot, piece in enumerate(pieces):

        @pl.when(step == early + own + slot)
        def _(piece=piece):
            w_out[...] = updated(w_ref[...], piece[...], approx)


def final_call(at, early, hid, dy, err, l, r, w, mom, pieces, **links):
    units, tok = hid.shape
    cols = mom.shape[1]
    half = pieces[0].shape[1]
    own = cols // half
    tile = row_tile(units)
    tiles = units // tile
    count = dy.shape[1] // half

    def held_to(low, high, column):
        def index(c, f, at):
            row = jnp.where(c < low, 0, jnp.where(c > high, tiles - 1, f))
            return row, column(jnp.clip(c, low, high), at)

        return pl.BlockSpec((tile, half), index)

    weights = held_to(early, count - 1, lambda c, at: at[c])
    momenta = held_to(early, early + own - 1, lambda c, at: c - early)
    arrived = [held_to(early + own + s, early + own + s, lambda c, at: 0) for s in range(len(pieces))]
    error = pl.BlockSpec((1, tile, half), lambda c, f, at: (0, f, at[c]))
    return launch(
        functools.partial(final_kernel, early, own),
        "final",
        (count, tiles),
        [hid, dy, err, l, r, w, mom, *pieces],
        [
            pl.BlockSpec((tile, tok), lambda c, f, at: (f, 0)),
            pl.BlockSpec((tok, half), lambda c, f, at: (0, at[c])),
            error,
            pl.BlockSpec((tile, SPLIT), lambda c, f, at: (f, 0)),
            pl.BlockSpec((SPLIT, half), lambda c, f, at: (0, at[c])),
            weights,
            momenta,
            *arrived,
        ],
        [error, weights, momenta],
        [shaped(err.shape, BF16), shaped(w.shape, BF16), shaped(mom.shape, F32)],
        places=[at],
        **links,
    )


def last_kernel(at_ref, low_ref, high_ref, w_ref, l_ref, r_ref, _, w_out):
    half = low_ref.shape[1]
    approx = dot(l_ref[...], r_ref[...])
    w_out[:, :half] = updated(w_ref[:, :half], low_ref[...], approx[:, :half])
    w_out[:, half:] = updated(w_ref[:, half:], high_ref[...], approx[:, half:])


def last_call(at, low, high, w, l, r, new):
    units, half = low.shape
    tile = min(256, units)
    part = pl.BlockSpec((tile, half), lambda f, at: (f, 0))
    place = pl.BlockSpec((tile, 2 * half), lambda f, at: (f, at[0]))
    return launch(
        last_kernel,
        "last",
        (pl.cdiv(units, tile),),
        [low, high, w, l, r, new],
        [
            part,
            part,
            place,
            pl.BlockSpec((tile, SPLIT), lambda f, at: (f, 0)),
            pl.BlockSpec((SPLIT, 2 * half), lambda f, at: (0, at[0])),
            HELD,
        ],
        [place],
        [shaped(w.shape, BF16)],
        places=[at],
        aliases={6: 0},
    )


def exchange(value, axis, mask):
    size = lax.axis_size(axis)
    return lax.ppermute(value, axis, [(i, i ^ mask) for i in range(size)])


def masks(size):
    return [1 << bit for bit in range(size.bit_length() - 1)]


def body(inputs, out_grads, w_gate, w_up, w_down, err_down, mom_down, q_down):
    replicas = lax.axis_size("dp")
    shards = lax.axis_size("mp")
    rank_dp = lax.axis_index("dp")
    rank_mp = lax.axis_index("mp")
    w_gate, w_up = w_gate.T, w_up.T
    count = shards // 2
    split = max(1, count // 2)
    got = {}

    low, high, later_low, later_high = cast_call(mom_down)
    got[2, 0] = exchange(low, "dp", 2)
    got[1, 1] = exchange(high, "dp", 1)

    hid, fac, silu = hidden_call(inputs, w_gate, w_up, held=[low])
    (left,) = left_call(q_down.T, err_down, out_grads, hid, replicas)
    lefts = [left] + [exchange(left, "dp", mask) for mask in range(1, replicas)]
    d_gate, d_up = slopes_call(out_grads, w_down, fac, silu, held=[left])

    def blocks(parity, slots, add=None, **links):
        return blocks_call(
            rank_mp, parity, slots, count, d_gate, d_up, w_gate, w_up, add, **links
        )

    here, there = rank_mp % 2, 1 - rank_mp % 2
    early, late = (0, split), (split, count - split)
    other, later_low, later_high = blocks(
        there,
        early,
        held=[got[2, 0], got[1, 1], *lefts[1:]],
        through=[later_low, later_high],
    )
    got[1, 0] = exchange(later_low, "dp", 1)
    got[2, 1] = exchange(later_high, "dp", 2)

    total, left, other = right_call(lefts, hid, err_down, out_grads, through=[other])

    others = [exchange(other, "mp", 1)]
    mine = []
    for index, mask in enumerate(masks(shards)):
        more = exchange(total, "mp", mask)
        held = []
        if index == 0 and late[1]:
            (other,) = blocks(there, late, held=[total])
            others.append(exchange(other, "mp", 1))
            held = [other]
        elif index == 1 or (index == 0 and not late[1]):
            mine = list(blocks(here, early, others[0], held=[total]))
            held = [mine[0]]
        elif index == 2 and late[1]:
            mine = list(blocks(here, late, others[1], held=[total], through=mine))
            mine = mine[late[1] :] + mine[: late[1]]
            held = [mine[-1]]
        if index == len(masks(shards)) - 1:
            held += [got[1, 0], got[2, 1]]
        (total,) = sum_call(total, more, held=held)
    for mask in masks(replicas):
        (total,) = sum_call(total, exchange(total, "dp", mask))

    l, r, low, high = factors_call(total, left, replicas, through=[got[2, 0], got[1, 1]])
    got[3, 0] = exchange(low, "dp", 1)
    got[3, 1] = exchange(high, "dp", 2)
    got[2, 0], got[1, 1] = low, high
    landed = [exchange(mine[slot], "mp", 2 * slot) for slot in range(1, count)]

    keys = [(1, 1), (2, 0), (1, 0), (2, 1)]
    order = [(3, 0), (3, 1), (0, 0), (0, 1)] + keys
    at = jnp.stack([2 * (rank_dp ^ mask) + side for mask, side in order]).astype(jnp.int32)
    next_err, new, next_mom = final_call(
        at, 2, hid, out_grads, err_down, l, r, w_down, mom_down, [got[key] for key in keys]
    )

    (in_grads,) = join_call([mine[0]] + landed, held=[next_err])

    last = jnp.reshape(rank_dp ^ 3, (1,)).astype(jnp.int32)
    (new,) = last_call(last, got[3, 0], got[3, 1], w_down, l, r, new)
    return (in_grads, new, next_err, next_mom)


def solution(mesh):
    in_specs = (
        P("dp", None),
        P("dp", None),
        P(None, "mp"),
        P(None, "mp"),
        P("mp", None),
        P("dp", "mp", None),
        P("mp", "dp"),
        P(),
    )
    out_specs = (P("dp", "mp"), P("mp", None), P("dp", "mp", None), P("mp", "dp"))
    return jax.shard_map(body, mesh=mesh, in_specs=in_specs, out_specs=out_specs, check_vma=False)
```

time: 432 us -> 179 us (0.41)
  waiting for transfers between devices: 220 us -> 19.6 us
  Pallas kernels: 0 us -> 126 us
  matrix products: 119 us -> 0 us
  other arithmetic: 37.1 us -> 0.15 us
  blocking collectives: 26.8 us -> 0 us
  starting transfers between devices: 0.12 us -> 21.1 us
  between operations: 15.7 us -> 0.81 us
    psum x1 -> x0, waiting for transfers between devices: 133 us -> none  [body(): right_down = lax.psum(contract_rows(m_down, left_down), ('dp', 'mp'))]
    pallas_call x0 -> x18, Pallas kernels: none -> 126 us  [launch(): pl.pallas_call(inner, grid_spec=pltpu.PrefetchScalarGridSpec(num_scalar_p...]
    dot_general x10 -> x0, matrix products: 119 us -> none  [the longest x3 35.5 us: contract_cols(): lax.dot_general(left, right, (((1,), (1,)), ((), ())), preferred_element_...]
    all_gather x1 -> x0, waiting for transfers between devices: 87.4 us -> none  [body(): new_down = lax.all_gather(own_down, 'dp', axis=1, tiled=True)]
    psum x2 -> x0, blocking collectives: 26.8 us -> none  [the longest x1 16.7 us: body(): left_down = lax.psum(jnp.dot(m_down, q_down, precision=HIGH), 'dp')]
    broadcast_in_dim x1 -> x0, other arithmetic: 21.3 us -> none  [body(): next_err_down = (m_down - approx_down).astype(jnp.bfloat16)[None]]
    ppermute x0 -> x19, starting transfers between devices: none -> 21.1 us  [exchange(): return lax.ppermute(value, axis, [(i, i ^ mask) for i in range(size)])]
    ppermute x0 -> x19, waiting for transfers between devices: none -> 19.6 us  [exchange(): return lax.ppermute(value, axis, [(i, i ^ mask) for i in range(size)])]
  transfers between devices with their start and end apart: 3 -> 19, of which waited for: 2 -> 5; matrix products, arithmetic and copies ran while one was open for 21% -> 0% of each run, Pallas kernels for 0% -> 59%
where the time goes in v2:
time: 179 us; the launch traced here: 178 us
  Pallas kernels  126 us (70%)
  starting transfers between devices  21.1 us (12%)
  waiting for transfers between devices  19.6 us (11%)
  local copies, waits for them, and re-layouts  10.1 us (6%)
    pallas_call x18, Pallas kernels, launch(): pl.pallas_call(inner, grid_spec=pltpu.PrefetchScalarGridSpec(num_scalar_p...  126 us
    ppermute x19, starting transfers between devices, exchange(): return lax.ppermute(value, axis, [(i, i ^ mask) for i in range(size)])  21.1 us
    ppermute x19, waiting for transfers between devices, exchange(): return lax.ppermute(value, axis, [(i, i ^ mask) for i in range(size)])  19.6 us
    unnamed x34, local copies, waits for them, and re-layouts  10.1 us
  transfers between devices with their start and end apart: 19, of which 5 were waited for; matrix products, arithmetic and copies ran while one was open for 0% of the time, Pallas kernels for 59%

profile of v2, /device:TPU:8, one launch (start us, length us, event | category | flops | bytes accessed | tf_op | source)
XLA Modules:
  0.0 178.0 jit_solution(2010289276002196118)
XLA Ops:
  0.6 4.5 %cast.1 = (bf16[1376,512]{1,0:T(8,128)(2,1)}, bf16[1376,512]{1,0:T(8,128)(2,1)}, bf16[1376,512]{1,0:T(8,128)(2,1)}, bf16[1376,512]{1,0:T(8,128)(2,1)}) custom-call(f32[1376,1024]{1,0:T(8,128)} %refs_7_.1), custom_call_target="tpu_custom_call" | custom-call | flops 1 | bytes 1 | tf_op jit(solution)/shard_map/cast/pallas_call | solution.py:32
  5.1 1.5 collective-permute-start.4
  6.6 1.5 collective-permute-start.3
  8.1 20.0 %hidden.1 = (bf16[1376,512]{1,0:T(8,128)(2,1)S(1)}, f32[512,1376]{1,0:T(8,128)S(1)}, f32[512,1376]{1,0:T(8,128)}) custom-call(bf16[512,4096]{1,0:T(8,128)(2,1)} %refs_0_.4, bf16[1376,4096]{1,0:T(8,128)(2,1)} %bitcast.16, bf16[1376,4096]{1,0:T(8,128)(2,1)} %bitcast.21, bf16[1376,512]{1,0:T(8,128)(2,1)} %get-tuple-element.32.refs_3_), custom_call_target="tpu_custom_call" | custom-call | flops 1 | bytes 1 | tf_op jit(solution)/shard_map/hidden/pallas_call | solution.py:32
  28.1 10.7 %left.1.refs_4_.refs_0_ = f32[8,1376]{1,0:T(8,128)S(1)} custom-call(f32[8,4096]{1,0:T(8,128)S(1)} %bitcast.15, bf16[1,1376,4096]{2,1,0:T(8,128)(2,1)} %refs_3_.2, bf16[512,4096]{1,0:T(8,128)(2,1)S(1)} %copy-done, bf16[1376,512]{1,0:T(8,128)(2,1)S(1)} %get-tuple-element.35.refs_3_.refs_4_.refs_1_), custom_call_target="tpu_custom_call" | custom-call | flops 1 | bytes 1 | tf_op jit(solution)/shard_map/left/pallas_call | solution.py:32
  38.9 0.5 collective-permute-start.2
  39.4 1.5 collective-permute-start.1
  40.9 1.5 collective-permute-start
  42.4 0.1 pad_add_fusion.1.refs_0_
  42.5 1.8 %copy-done.10 = f32[512,1376]{1,0:T(8,128)S(1)} copy-done((f32[512,1376]{1,0:T(8,128)S(1)}, f32[512,1376]{1,0:T(8,128)}, u32[]{:S(2)}) %copy-start.10) | copy-done | bytes 2818072
  44.3 11.9 %slopes.1 = (bf16[512,1376]{1,0:T(8,128)(2,1)S(1)}, bf16[512,1376]{1,0:T(8,128)(2,1)S(1)}) custom-call(bf16[512,4096]{1,0:T(8,128)(2,1)} %refs_2_.3, bf16[1376,4096]{1,0:T(8,128)(2,1)} %refs_3_.3, f32[512,1376]{1,0:T(8,128)S(1)} %copy-done.10, f32[512,1376]{1,0:T(8,128)} %get-tuple-element.34.refs_3_, f32[8,1376]{1,0:T(8,128)S(1)} %left.1.refs_4_.refs_0_), custom_call_target="tpu_custom_call" | custom-call | flops 1 | bytes 1 | tf_op jit(solution)/shard_map/slopes/pallas_call | solution.py:32
  56.2 1.1 copy-done.1
  57.3 1.1 copy-done.3
  58.4 1.1 copy-done.5
  59.5 7.6 %blocks.4 = (bf16[2,512,512]{2,1,0:T(8,128)(2,1)}, bf16[1376,512]{1,0:T(8,128)(2,1)}, bf16[1376,512]{1,0:T(8,128)(2,1)}) custom-call(s32[2]{0:T(128)S(1)} %pad_add_fusion.1.refs_0_, bf16[512,1376]{1,0:T(8,128)(2,1)} %copy-done.1, bf16[512,1376]{1,0:T(8,128)(2,1)} %copy-done.3, ...), custom_call_target="tpu_custom_call", output_to_operand_aliasing={{1}: (10, {}), {2}: (11, {})} | custom-call | flops 1 | bytes 1 | tf_op jit(solution)/shard_map/blocks/pallas_call | solution.py:32
  67.2 0.5 collective-permute-start.13
  67.7 0.5 collective-permute-start.14
  68.2 9.3 %right.1 = (f32[8,4224]{1,0:T(8,128)S(1)}, f32[8,1376]{1,0:T(8,128)S(1)}, bf16[2,512,512]{2,1,0:T(8,128)(2,1)}) custom-call(f32[8,1376]{1,0:T(8,128)S(1)} %left.1.refs_4_.refs_0_, f32[8,1376]{1,0:T(8,128)S(1)} %collective-permute-done.refs_7_.refs_1_, f32[8,1376]{1,0:T(8,128)S(1)} %collective-permute-done.1.refs_8_.refs_2_, ...), custom_call_target="tpu_custom_call", output_to_operand_aliasing={{2}: (7, {})} | custom-call | flops 1 | bytes 1 | tf_op jit(solution)/shard_map/right/pallas_call | solution.py:32
  77.6 6.0 %blocks.5.refs_2_ = bf16[2,512,512]{2,1,0:T(8,128)(2,1)S(1)} custom-call(s32[2]{0:T(128)S(1)} %pad_add_fusion.1.refs_0_, bf16[512,1376]{1,0:T(8,128)(2,1)S(1)} %copy-done.2, bf16[512,1376]{1,0:T(8,128)(2,1)S(1)} %copy-done.4, bf16[1376,4096]{1,0:T(8,128)(2,1)} %bitcast.18, bf16[1376,4096]{1,0:T(8,128)(2,1)} %bitcast.23, ...), custom_call_target="tpu_custom_call" | custom-call | flops 1 | bytes 1 | tf_op jit(solution)/shard_map/blocks/pallas_call | solution.py:32
  83.6 0.5 collective-permute-start.5
  84.1 0.1 collective-permute-start.6
  84.2 2.4 %collective-permute-done.6.refs_1_ = f32[8,4224]{1,0:T(8,128)S(1)} collective-permute-done((f32[8,4224]{1,0:T(8,128)S(1)}, f32[8,4224]{1,0:T(8,128)S(1)}, u32[]{:S(2)}, u32[]{:S(2)}) %collective-permute-start.6) | collective-permute-done | bytes 135200 | tf_op jit(solution)/shard_map/ppermute | solution.py:470
  86.6 0.1 collective-permute-start.7
  86.8 6.8 %blocks.6 = (bf16[512,512]{1,0:T(8,128)(2,1)S(1)}, bf16[512,512]{1,0:T(8,128)(2,1)}) custom-call(s32[2]{0:T(128)S(1)} %pad_add_fusion.refs_0_, bf16[512,1376]{1,0:T(8,128)(2,1)S(1)} %copy-done.2, bf16[512,1376]{1,0:T(8,128)(2,1)S(1)} %copy-done.4, bf16[1376,4096]{1,0:T(8,128)(2,1)} %bitcast.19, bf16[1376,4096]{1,0:T(8,128)(2,1)} %bitcast.24, ...), custom_call_target="tpu_custom_call" | custom-call | flops 1 | bytes 1 | tf_op jit(solution)/shard_map/blocks/pallas_call | solution.py:32
  93.7 3.1 %collective-permute-start.12 = (f32[8,4224]{1,0:T(8,128)S(1)}, f32[8,4224]{1,0:T(8,128)S(1)}, u32[]{:S(2)}, u32[]{:S(2)}) collective-permute-start(f32[8,4224]{1,0:T(8,128)S(1)} %sum.6.refs_6_.refs_0_), channel_id=1, source_target_pairs={{0,4},{1,5},{2,6},{3,7},{4,0},{5,1},{6,2},{7,3},{8,12},{9,13},{10,... | collective-permute-start | bytes 405512 | tf_op jit(solution)/shard_map/ppermute | solution.py:470
  96.8 7.1 %blocks.7 = (bf16[512,512]{1,0:T(8,128)(2,1)}, bf16[512,512]{1,0:T(8,128)(2,1)}, bf16[512,512]{1,0:T(8,128)(2,1)S(1)}, bf16[512,512]{1,0:T(8,128)(2,1)}) custom-call(s32[2]{0:T(128)S(1)} %pad_add_fusion.refs_0_, bf16[512,1376]{1,0:T(8,128)(2,1)S(1)} %copy-done.2, bf16[512,1376]{1,0:T(8,128)(2,1)S(1)} %copy-done.4, ...), custom_call_target="tpu_custom_call", output_to_operand_aliasing={{2}: (7, {}), {3}: (8, {})} | custom-call | flops 1 | bytes 1 | tf_op jit(solution)/shard_map/blocks/pallas_call | solution.py:32
  104.0 1.0 copy-done.7
  105.0 0.5 copy-done.8
  105.5 1.5 collective-permute-start.15
  107.0 3.8 %collective-permute-done.15.refs_1_ = f32[8,4224]{1,0:T(8,128)S(1)} collective-permute-done((f32[8,4224]{1,0:T(8,128)S(1)}, f32[8,4224]{1,0:T(8,128)S(1)}, u32[]{:S(2)}, u32[]{:S(2)}) %collective-permute-start.15) | collective-permute-done | bytes 135200 | tf_op jit(solution)/shard_map/ppermute | solution.py:470
  110.8 1.6 collective-permute-start.16
  112.4 3.5 %collective-permute-done.16.refs_1_ = f32[8,4224]{1,0:T(8,128)S(1)} collective-permute-done((f32[8,4224]{1,0:T(8,128)S(1)}, f32[8,4224]{1,0:T(8,128)S(1)}, u32[]{:S(2)}, u32[]{:S(2)}) %collective-permute-start.16) | collective-permute-done | bytes 135200 | tf_op jit(solution)/shard_map/ppermute | solution.py:470
  115.9 2.5 %factors.1 = (bf16[1376,32]{1,0:T(8,128)(2,1)S(1)}, bf16[32,4096]{1,0:T(8,128)(2,1)S(1)}, bf16[1376,512]{1,0:T(8,128)(2,1)}, bf16[1376,512]{1,0:T(8,128)(2,1)S(1)}) custom-call(f32[8,4224]{1,0:T(8,128)S(1)} %sum.9.refs_0_, f32[8,1376]{1,0:T(8,128)S(1)} %get-tuple-element.52.refs_1_, ...), custom_call_target="tpu_custom_call", output_to_operand_aliasing={{2}: (2, {}), {3}: (3, {})} | custom-call | flops 1 | bytes 1 | tf_op jit(solution)/shard_map/factors/pallas_call | solution.py:32
  118.4 0.7 copy-done.11
  119.1 0.7 copy-done.13
  119.8 1.5 collective-permute-start.18
  121.4 1.5 collective-permute-start.17
  122.9 1.6 collective-permute-start.9
  124.4 0.4 collective-permute-start.10
  124.8 1.5 collective-permute-start.11
  126.4 0.1 stack.62.refs_0_
  126.4 1.0 copy-done.12
  127.4 0.9 copy-done.14
  128.4 30.9 %final.1 = (bf16[1,1376,4096]{2,1,0:T(8,128)(2,1)}, bf16[1376,4096]{1,0:T(8,128)(2,1)}, f32[1376,1024]{1,0:T(8,128)}) custom-call(s32[8]{0:T(128)S(1)} %stack.62.refs_0_, bf16[1376,512]{1,0:T(8,128)(2,1)S(1)} %get-tuple-element.35.refs_3_.refs_4_.refs_1_, bf16[512,4096]{1,0:T(8,128)(2,1)} %refs_2_.3, bf16[1,1376,4096]{2,1,0:T(8,128)(2,1)} %refs_3_.2, ...), custom_call_target="tpu_custom_call" | custom-call | flops 1 | bytes 1 | tf_op jit(solution)/shard_map/final/pallas_call | solution.py:32
  159.3 0.7 collective-permute-done.10.refs_2_
  160.0 9.2 %collective-permute-done.11.refs_3_ = bf16[512,512]{1,0:T(8,128)(2,1)} collective-permute-done((bf16[512,512]{1,0:T(8,128)(2,1)}, bf16[512,512]{1,0:T(8,128)(2,1)}, u32[]{:S(2)}, u32[]{:S(2)}) %collective-permute-start.11) | collective-permute-done | bytes 524320 | tf_op jit(solution)/shard_map/ppermute | solution.py:470
  169.2 2.4 %join.1 = bf16[512,512]{1,0:T(8,128)(2,1)} custom-call(bf16[512,512]{1,0:T(8,128)(2,1)S(1)} %get-tuple-element.46.refs_0_, bf16[512,512]{1,0:T(8,128)(2,1)} %collective-permute-done.9.refs_1_, bf16[512,512]{1,0:T(8,128)(2,1)} %collective-permute-done.10.refs_2_, bf16[512,512]{1,0:T(8,128)(2,1)} %collective-permute-done.11.refs_3_, ...), custom_call_target="tpu_custom_call" | custom-call | flops 1 | bytes 1 | tf_op jit(solution)/shard_map/join/pallas_call | solution.py:32
  171.6 6.4 %last.1 = bf16[1376,4096]{1,0:T(8,128)(2,1)} custom-call(s32[1]{0:T(128)} %bitcast.14.refs_0_, bf16[1376,512]{1,0:T(8,128)(2,1)} %collective-permute-done.17.refs_1_, bf16[1376,512]{1,0:T(8,128)(2,1)} %collective-permute-done.18.refs_2_, bf16[1376,4096]{1,0:T(8,128)(2,1)} %refs_3_.3, ...), custom_call_target="tpu_custom_call", output_to_operand_aliasing={{}: (6, {})} | custom-call | flops 1 | bytes 1 | tf_op jit(solution)/shard_map/last/pallas_call | solution.py:32
  (45 shorter events, 0.3 us)
Async XLA Ops:
  5.1 53.3 %collective-permute-start.4 = (bf16[1376,512]{1,0:T(8,128)(2,1)}, bf16[1376,512]{1,0:T(8,128)(2,1)S(1)}, u32[]{:S(2)}, u32[]{:S(2)}) collective-permute-start(bf16[1376,512]{1,0:T(8,128)(2,1)} %get-tuple-element.38), channel_id=1, source_target_pairs={{0,8},{8,0},{16,24},{24,16},{1,9},{9,1},{17,25},{25,17},{2,10},{10... | collective-permute-start | bytes 4227080 | tf_op jit(solution)/shard_map/ppermute | solution.py:470
  6.6 51.8 %collective-permute-start.3 = (bf16[1376,512]{1,0:T(8,128)(2,1)}, bf16[1376,512]{1,0:T(8,128)(2,1)}, u32[]{:S(2)}, u32[]{:S(2)}) collective-permute-start(bf16[1376,512]{1,0:T(8,128)(2,1)} %get-tuple-element.32.refs_3_), channel_id=1, source_target_pairs={{0,16},{8,24},{16,0},{24,8},{1,17},{9,25},{17,1},{25,9},{2,18},{10... | collective-permute-start | bytes 4227080 | tf_op jit(solution)/shard_map/ppermute | solution.py:470
  8.1 20.0 %copy-start = (bf16[512,4096]{1,0:T(8,128)(2,1)S(1)}, bf16[512,4096]{1,0:T(8,128)(2,1)}, u32[]{:S(2)}) copy-start(bf16[512,4096]{1,0:T(8,128)(2,1)} %refs_2_.3) | copy-start | bytes 12582916
  8.1 20.0 %copy-start.16 = (f32[4096,8]{0,1:T(8,128)S(1)}, f32[4096,8]{0,1:T(8,128)}, u32[]{:S(2)}) copy-start(f32[4096,8]{0,1:T(8,128)} %param.15) | copy-start | bytes 393220
  28.1 10.8 %copy-start.9 = (f32[512,1376]{1,0:T(8,128)}, f32[512,1376]{1,0:T(8,128)S(1)}, u32[]{:S(2)}) copy-start(f32[512,1376]{1,0:T(8,128)S(1)} %get-tuple-element.33.refs_2_) | copy-start | bytes 8454148
  38.9 19.5 %collective-permute-start.2 = (f32[8,1376]{1,0:T(8,128)S(1)}, f32[8,1376]{1,0:T(8,128)S(1)}, u32[]{:S(2)}, u32[]{:S(2)}) collective-permute-start(f32[8,1376]{1,0:T(8,128)S(1)} %left.1.refs_4_.refs_0_), channel_id=1, source_target_pairs={{0,24},{8,16},{16,8},{24,0},{1,25},{9,17},{17,9},{25,1},{2,26},{10... | collective-permute-start | bytes 132104 | tf_op jit(solution)/shard_map/ppermute | solution.py:470
  39.4 19.0 %collective-permute-start.1 = (f32[8,1376]{1,0:T(8,128)S(1)}, f32[8,1376]{1,0:T(8,128)S(1)}, u32[]{:S(2)}, u32[]{:S(2)}) collective-permute-start(f32[8,1376]{1,0:T(8,128)S(1)} %left.1.refs_4_.refs_0_), channel_id=1, source_target_pairs={{0,16},{8,24},{16,0},{24,8},{1,17},{9,25},{17,1},{25,9},{2,18},{10... | collective-permute-start | bytes 132104 | tf_op jit(solution)/shard_map/ppermute | solution.py:470
  40.9 17.5 %collective-permute-start = (f32[8,1376]{1,0:T(8,128)S(1)}, f32[8,1376]{1,0:T(8,128)S(1)}, u32[]{:S(2)}, u32[]{:S(2)}) collective-permute-start(f32[8,1376]{1,0:T(8,128)S(1)} %left.1.refs_4_.refs_0_), channel_id=1, source_target_pairs={{0,8},{8,0},{16,24},{24,16},{1,9},{9,1},{17,25},{25,17},{2,10},{10... | collective-permute-start | bytes 132104 | tf_op jit(solution)/shard_map/ppermute | solution.py:470
  42.5 1.8 %copy-start.10 = (f32[512,1376]{1,0:T(8,128)S(1)}, f32[512,1376]{1,0:T(8,128)}, u32[]{:S(2)}) copy-start(f32[512,1376]{1,0:T(8,128)} %copy-done.9) | copy-start | bytes 8454148
  56.2 1.1 copy-start.1
  57.3 1.1 copy-start.3
  58.4 1.1 copy-start.5
  67.2 36.7 %collective-permute-start.13 = (bf16[1376,512]{1,0:T(8,128)(2,1)}, bf16[1376,512]{1,0:T(8,128)(2,1)S(1)}, u32[]{:S(2)}, u32[]{:S(2)}) collective-permute-start(bf16[1376,512]{1,0:T(8,128)(2,1)} %get-tuple-element.50), channel_id=1, source_target_pairs={{0,8},{8,0},{16,24},{24,16},{1,9},{9,1},{17,25},{25,17},{2,10},{10... | collective-permute-start | bytes 4227080 | tf_op jit(solution)/shard_map/ppermute | solution.py:470
  67.7 36.2 %collective-permute-start.14 = (bf16[1376,512]{1,0:T(8,128)(2,1)}, bf16[1376,512]{1,0:T(8,128)(2,1)S(1)}, u32[]{:S(2)}, u32[]{:S(2)}) collective-permute-start(bf16[1376,512]{1,0:T(8,128)(2,1)} %get-tuple-element.51), channel_id=1, source_target_pairs={{0,16},{8,24},{16,0},{24,8},{1,17},{9,25},{17,1},{25,9},{2,18},{10... | collective-permute-start | bytes 4227080 | tf_op jit(solution)/shard_map/ppermute | solution.py:470
  68.2 9.4 %copy-start.2 = (bf16[512,1376]{1,0:T(8,128)(2,1)S(1)}, bf16[512,1376]{1,0:T(8,128)(2,1)}, u32[]{:S(2)}) copy-start(bf16[512,1376]{1,0:T(8,128)(2,1)} %copy-done.1) | copy-start | bytes 4227076
  68.2 9.4 %copy-start.4 = (bf16[512,1376]{1,0:T(8,128)(2,1)S(1)}, bf16[512,1376]{1,0:T(8,128)(2,1)}, u32[]{:S(2)}) copy-start(bf16[512,1376]{1,0:T(8,128)(2,1)} %copy-done.3) | copy-start | bytes 4227076
  77.5 9.3 %collective-permute-start.8 = (bf16[2,512,512]{2,1,0:T(8,128)(2,1)}, bf16[2,512,512]{2,1,0:T(8,128)(2,1)S(1)}, u32[]{:S(2)}, u32[]{:S(2)}) collective-permute-start(bf16[2,512,512]{2,1,0:T(8,128)(2,1)} %get-tuple-element.43), channel_id=1, source_target_pairs={{0,1},{1,0},{2,3},{3,2},{4,5},{5,4},{6,7},{7,6},{8,9},{9,8},{10,11... | collective-permute-start | bytes 3145736 | tf_op jit(solution)/shard_map/ppermute | solution.py:470
  83.6 13.2 %collective-permute-start.5 = (bf16[2,512,512]{2,1,0:T(8,128)(2,1)S(1)}, bf16[2,512,512]{2,1,0:T(8,128)(2,1)S(1)}, u32[]{:S(2)}, u32[]{:S(2)}) collective-permute-start(bf16[2,512,512]{2,1,0:T(8,128)(2,1)S(1)} %blocks.5.refs_2_), channel_id=1, source_target_pairs={{0,1},{1,0},{2,3},{3,2},{4,5},{5,4},{6,7},{7,6},{8,9},{9,8},{10,11... | collective-permute-start | bytes 3145736 | tf_op jit(solution)/shard_map/ppermute | solution.py:470
  84.1 2.5 %collective-permute-start.6 = (f32[8,4224]{1,0:T(8,128)S(1)}, f32[8,4224]{1,0:T(8,128)S(1)}, u32[]{:S(2)}, u32[]{:S(2)}) collective-permute-start(f32[8,4224]{1,0:T(8,128)S(1)} %get-tuple-element.42.refs_5_.refs_0_), channel_id=1, source_target_pairs={{0,1},{1,0},{2,3},{3,2},{4,5},{5,4},{6,7},{7,6},{8,9},{9,8},{10,11... | collective-permute-start | bytes 405512 | tf_op jit(solution)/shard_map/ppermute | solution.py:470
  86.6 7.0 %collective-permute-start.7 = (f32[8,4224]{1,0:T(8,128)S(1)}, f32[8,4224]{1,0:T(8,128)S(1)}, u32[]{:S(2)}, u32[]{:S(2)}) collective-permute-start(f32[8,4224]{1,0:T(8,128)S(1)} %sum.5.refs_6_.refs_0_), channel_id=1, source_target_pairs={{0,2},{1,3},{2,0},{3,1},{4,6},{5,7},{6,4},{7,5},{8,10},{9,11},{10,... | collective-permute-start | bytes 405512 | tf_op jit(solution)/shard_map/ppermute | solution.py:470
  93.7 10.2 %collective-permute-start.12 = (f32[8,4224]{1,0:T(8,128)S(1)}, f32[8,4224]{1,0:T(8,128)S(1)}, u32[]{:S(2)}, u32[]{:S(2)}) collective-permute-start(f32[8,4224]{1,0:T(8,128)S(1)} %sum.6.refs_6_.refs_0_), channel_id=1, source_target_pairs={{0,4},{1,5},{2,6},{3,7},{4,0},{5,1},{6,2},{7,3},{8,12},{9,13},{10,... | collective-permute-start | bytes 405512 | tf_op jit(solution)/shard_map/ppermute | solution.py:470
  103.9 1.1 copy-start.7
  103.9 1.6 copy-start.8
  103.9 12.0 %copy-start.6 = (bf16[1376,512]{1,0:T(8,128)(2,1)S(1)}, bf16[1376,512]{1,0:T(8,128)(2,1)}, u32[]{:S(2)}) copy-start(bf16[1376,512]{1,0:T(8,128)(2,1)} %copy-done.5) | copy-start | bytes 4227076
  105.5 5.3 %collective-permute-start.15 = (f32[8,4224]{1,0:T(8,128)S(1)}, f32[8,4224]{1,0:T(8,128)S(1)}, u32[]{:S(2)}, u32[]{:S(2)}) collective-permute-start(f32[8,4224]{1,0:T(8,128)S(1)} %sum.7.refs_0_), channel_id=1, source_target_pairs={{0,8},{8,0},{16,24},{24,16},{1,9},{9,1},{17,25},{25,17},{2,10},{10... | collective-permute-start | bytes 405512 | tf_op jit(solution)/shard_map/ppermute | solution.py:470
  110.8 5.1 %collective-permute-start.16 = (f32[8,4224]{1,0:T(8,128)S(1)}, f32[8,4224]{1,0:T(8,128)S(1)}, u32[]{:S(2)}, u32[]{:S(2)}) collective-permute-start(f32[8,4224]{1,0:T(8,128)S(1)} %sum.8.refs_0_), channel_id=1, source_target_pairs={{0,16},{8,24},{16,0},{24,8},{1,17},{9,25},{17,1},{25,9},{2,18},{10... | collective-permute-start | bytes 405512 | tf_op jit(solution)/shard_map/ppermute | solution.py:470
  118.4 0.7 copy-start.11
  119.1 0.7 copy-start.13
  119.8 51.8 %collective-permute-start.18 = (bf16[1376,512]{1,0:T(8,128)(2,1)S(1)}, bf16[1376,512]{1,0:T(8,128)(2,1)}, u32[]{:S(2)}, u32[]{:S(2)}) collective-permute-start(bf16[1376,512]{1,0:T(8,128)(2,1)S(1)} %get-tuple-element.55.refs_8_), channel_id=1, source_target_pairs={{0,16},{8,24},{16,0},{24,8},{1,17},{9,25},{17,1},{25,9},{2,18},{10... | collective-permute-start | bytes 4227080 | tf_op jit(solution)/shard_map/ppermute | solution.py:470
  121.4 50.2 %collective-permute-start.17 = (bf16[1376,512]{1,0:T(8,128)(2,1)}, bf16[1376,512]{1,0:T(8,128)(2,1)}, u32[]{:S(2)}, u32[]{:S(2)}) collective-permute-start(bf16[1376,512]{1,0:T(8,128)(2,1)} %get-tuple-element.56.refs_9_), channel_id=1, source_target_pairs={{0,8},{8,0},{16,24},{24,16},{1,9},{9,1},{17,25},{25,17},{2,10},{10... | collective-permute-start | bytes 4227080 | tf_op jit(solution)/shard_map/ppermute | solution.py:470
  122.9 36.4 %collective-permute-start.9 = (bf16[512,512]{1,0:T(8,128)(2,1)}, bf16[512,512]{1,0:T(8,128)(2,1)}, u32[]{:S(2)}, u32[]{:S(2)}) collective-permute-start(bf16[512,512]{1,0:T(8,128)(2,1)} %get-tuple-element.47), channel_id=1, source_target_pairs={{0,2},{1,3},{2,0},{3,1},{4,6},{5,7},{6,4},{7,5},{8,10},{9,11},{10,... | collective-permute-start | bytes 1572872 | tf_op jit(solution)/shard_map/ppermute | solution.py:470
  124.4 35.6 %collective-permute-start.10 = (bf16[512,512]{1,0:T(8,128)(2,1)}, bf16[512,512]{1,0:T(8,128)(2,1)}, u32[]{:S(2)}, u32[]{:S(2)}) collective-permute-start(bf16[512,512]{1,0:T(8,128)(2,1)} %get-tuple-element.48), channel_id=1, source_target_pairs={{0,4},{1,5},{2,6},{3,7},{4,0},{5,1},{6,2},{7,3},{8,12},{9,13},{10,... | collective-permute-start | bytes 1572872 | tf_op jit(solution)/shard_map/ppermute | solution.py:470
  124.8 44.3 %collective-permute-start.11 = (bf16[512,512]{1,0:T(8,128)(2,1)}, bf16[512,512]{1,0:T(8,128)(2,1)}, u32[]{:S(2)}, u32[]{:S(2)}) collective-permute-start(bf16[512,512]{1,0:T(8,128)(2,1)} %get-tuple-element.49.refs_2_), channel_id=1, source_target_pairs={{0,6},{1,7},{2,4},{3,5},{4,2},{5,3},{6,0},{7,1},{8,14},{9,15},{10,... | collective-permute-start | bytes 1572872 | tf_op jit(solution)/shard_map/ppermute | solution.py:470
  126.4 1.0 copy-start.12
  127.4 0.9 copy-start.14
  169.2 2.5 %copy-start.15 = (bf16[32,4096]{1,0:T(8,128)(2,1)S(1)}, bf16[32,4096]{1,0:T(8,128)(2,1)}, u32[]{:S(2)}) copy-start(bf16[32,4096]{1,0:T(8,128)(2,1)} %copy-done.13) | copy-start | bytes 786436

commit v3 on v0

v3 whole, which is shorter than its diff:
```python
import functools

import jax
import jax.numpy as jnp
from jax import lax
from jax.experimental import pallas as pl
from jax.experimental.pallas import tpu as pltpu
from jax.sharding import PartitionSpec as P

R = 8
SPLIT = 4 * R
EPS = 1e-06
F32 = jnp.float32
BF16 = jnp.bfloat16
HIGH = lax.Precision.HIGHEST
VMEM = 62 * 2**20
ONCE = pl.Buffered(1)
HELD = pl.BlockSpec(memory_space=pl.ANY)


def launch(kernel, name, grid, args, in_specs, out_specs, out_shape, *, places=(), held=(),
           through=(), scratch=(), aliases=None):
    n_in, n_out = len(args), len(out_shape)
    n_held, n_through, n_place = len(held), len(through), len(places)
    first = n_place + n_in

    def inner(*refs):
        outs = first + n_held + n_through
        kernel(*refs[:first], *refs[outs : outs + n_out], *refs[outs + n_out + n_through :])

    links = {first + n_held + i: n_out + i for i in range(n_through)}
    return pl.pallas_call(
        inner,
        grid_spec=pltpu.PrefetchScalarGridSpec(
            num_scalar_prefetch=n_place,
            grid=grid,
            in_specs=list(in_specs) + [HELD] * (n_held + n_through),
            out_specs=list(out_specs) + [HELD] * n_through,
            scratch_shapes=list(scratch),
        ),
        out_shape=list(out_shape)
        + [jax.ShapeDtypeStruct(array.shape, array.dtype) for array in through],
        input_output_aliases={**links, **(aliases or {})},
        compiler_params=pltpu.CompilerParams(vmem_limit_bytes=VMEM),
        cost_estimate=pl.CostEstimate(flops=1, bytes_accessed=1, transcendentals=0),
        name=name,
    )(*places, *args, *held, *through)


def shaped(shape, dtype):
    return jax.ShapeDtypeStruct(shape, dtype)


def dot(left, right):
    return jnp.dot(left, right, preferred_element_type=F32)


def dot_nt(left, right):
    return lax.dot_general(left, right, (((1,), (1,)), ((), ())), preferred_element_type=F32)


def terms(rows):
    hi = rows.astype(BF16).astype(F32)
    rest = rows - hi
    mid = rest.astype(BF16).astype(F32)
    return hi, mid, rest - mid


def spread(rows):
    hi, mid, low = terms(rows)
    return jnp.concatenate([hi, mid, low, jnp.zeros_like(hi)], axis=0).astype(BF16)


def gather_terms(rows):
    return rows[:R] + rows[R : 2 * R] + rows[2 * R : 3 * R]


def tree(parts):
    while len(parts) > 1:
        odd = parts[len(parts) // 2 * 2 :]
        parts = [left + right for left, right in zip(parts[::2], parts[1::2])] + odd
    return parts[0]


def whole(shape):
    return pl.BlockSpec(shape, lambda *_: (0,) * len(shape), pipeline_mode=ONCE)


def unit_tile(units):
    return 256 if units > 512 and units % 16 == 0 else units


def cast_kernel(mom_ref, out_ref):
    out_ref[...] = mom_ref[...].astype(BF16)


def cast_call(mom):
    units, cols = mom.shape
    tile = unit_tile(units)
    part = pl.BlockSpec((tile, cols), lambda f: (f, 0))
    return launch(
        cast_kernel, "cast", (pl.cdiv(units, tile),), [mom], [part], [part], [shaped(mom.shape, BF16)]
    )


def hidden_kernel(
    x_ref, wg_ref, wu_ref, wd_ref, q_ref, dy_any, hid_ref, dg_ref, du_ref, dyq_ref, dy_ref, sem
):
    fetch = pltpu.make_async_copy(dy_any, dy_ref, sem)

    @pl.when(pl.program_id(0) == 0)
    def _():
        fetch.start()

    gate = dot_nt(x_ref[...], wg_ref[...])
    up = dot_nt(x_ref[...], wu_ref[...])

    @pl.when(pl.program_id(0) == 0)
    def _():
        fetch.wait()
        dyq_ref[...] = gather_terms(dot_nt(spread(q_ref[...]), dy_ref[...]))

    dh = dot_nt(dy_ref[...], wd_ref[...])
    sig = jax.nn.sigmoid(gate)
    silu = gate * sig
    hid_ref[...] = (silu * up).T.astype(BF16)
    dg_ref[0] = (dh * up * sig * (1.0 + gate * (1.0 - sig))).astype(BF16)
    du_ref[0] = (dh * silu).astype(BF16)


def hidden_call(x, dy, wg, wu, wd, q_t, **links):
    tok, depth = x.shape
    units = wg.shape[0]
    tile = unit_tile(units)
    tiles = pl.cdiv(units, tile)
    rows = pl.BlockSpec((tile, depth), lambda f: (f, 0))
    part = pl.BlockSpec((1, tok, tile), lambda f: (f, 0, 0))
    return launch(
        hidden_kernel,
        "hidden",
        (tiles,),
        [x, wg, wu, wd, q_t, dy],
        [whole((tok, depth)), rows, rows, rows, whole(q_t.shape), HELD],
        [pl.BlockSpec((tile, tok), lambda f: (f, 0)), part, part, whole((R, tok))],
        [
            shaped((units, tok), BF16),
            shaped((tiles, tok, tile), BF16),
            shaped((tiles, tok, tile), BF16),
            shaped((R, tok), F32),
        ],
        scratch=[pltpu.VMEM((tok, depth), BF16), pltpu.SemaphoreType.DMA(())],
        **links,
    )


def left_kernel(replicas, q_ref, dyq_ref, err_ref, hid_ref, out_ref, q_terms, dyq_terms):
    @pl.when(pl.program_id(0) == 0)
    def _():
        q_terms[...] = spread(q_ref[...])
        dyq_terms[...] = spread(dyq_ref[...])

    both = dot_nt(err_ref[0], q_terms[...]) + dot_nt(hid_ref[...], dyq_terms[...])
    out_ref[...] = gather_terms(both.T) / replicas


def left_call(q_t, dyq, err, hid, replicas, **links):
    units, tok = hid.shape
    depth = q_t.shape[1]
    tile = unit_tile(units)
    return launch(
        functools.partial(left_kernel, replicas),
        "left",
        (pl.cdiv(units, tile),),
        [q_t, dyq, err, hid],
        [
            whole(q_t.shape),
            whole(dyq.shape),
            pl.BlockSpec((1, tile, depth), lambda f: (0, f, 0)),
            pl.BlockSpec((tile, tok), lambda f: (f, 0)),
        ],
        [pl.BlockSpec((R, tile), lambda f: (0, f))],
        [shaped((R, units), F32)],
        scratch=[pltpu.VMEM((SPLIT, depth), BF16), pltpu.VMEM((SPLIT, tok), BF16)],
        **links,
    )


def columns(ref, step, tile):
    if ref.shape[1] == tile:
        return ref[...]
    return ref[:, pl.ds(pl.multiple_of(step * tile, tile), tile)]


def right_kernel(parts, dy_steps, *refs):
    lefts = refs[:parts]
    hid_ref, err_ref, dy_ref, out_ref, left_ref, left_terms, mixed_terms, total = refs[parts:]
    step = pl.program_id(0)
    units = left_ref.shape[1]
    tile, depth = err_ref.shape[1:]
    dy_tile = dy_ref.shape[0]
    tail = units % tile
    last = pl.num_programs(0) - 1

    @pl.when(step == 0)
    def _():
        left = tree([ref[...] for ref in lefts])
        left_ref[...] = left
        left_terms[:, :units] = spread(left)
        mixed_terms[...] = spread(gather_terms(dot(left_terms[:, :units], hid_ref[...])))
        gram = lax.dot_general(
            left, left, (((1,), (1,)), ((), ())), precision=HIGH, preferred_element_type=F32
        )
        out_ref[:, depth:] = jnp.concatenate([gram, jnp.zeros((R, 128 - R), F32)], axis=1)
        total[...] = jnp.zeros_like(total)

    @pl.when(step < dy_steps)
    def _():
        total[...] += dot(columns(mixed_terms, step, dy_tile), dy_ref[...])

    if tail:

        @pl.when(step < last)
        def _():
            total[...] += dot(columns(left_terms, step, tile), err_ref[0])

        @pl.when(step == last)
        def _():
            total[...] += dot(left_terms[:, units - tail : units], err_ref[0, :tail])

    else:
        total[...] += dot(columns(left_terms, step, tile), err_ref[0])

    @pl.when(step == last)
    def _():
        out_ref[:, :depth] = gather_terms(total[...])


def right_call(lefts, hid, err, dy, **links):
    units, tok = hid.shape
    depth = dy.shape[1]
    tile = unit_tile(units)
    tiles = pl.cdiv(units, tile)
    dy_steps = 2 if tiles > 1 else 1
    return launch(
        functools.partial(right_kernel, len(lefts), dy_steps),
        "right",
        (tiles,),
        [*lefts, hid, err, dy],
        [whole((R, units))] * len(lefts)
        + [
            whole((units, tok)),
            pl.BlockSpec((1, tile, depth), lambda f: (0, f, 0)),
            pl.BlockSpec((tok // dy_steps, depth), lambda f: (jnp.minimum(f, dy_steps - 1), 0)),
        ],
        [whole((R, depth + 128)), whole((R, units))],
        [shaped((R, depth + 128), F32), shaped((R, units), F32)],
        scratch=[
            pltpu.VMEM((SPLIT, tiles * tile), BF16),
            pltpu.VMEM((SPLIT, tok), BF16),
            pltpu.VMEM((SPLIT, depth), F32),
        ],
        **links,
    )


def sum_kernel(one_ref, two_ref, out_ref):
    out_ref[...] = one_ref[...] + two_ref[...]


def sum_call(one, two, **links):
    return launch(
        sum_kernel,
        "sum",
        (1,),
        [one, two],
        [whole(one.shape)] * 2,
        [whole(one.shape)],
        [shaped(one.shape, one.dtype)],
        **links,
    )


def join_kernel(*refs):
    refs[-1][...] = tree([ref[...].astype(F32) for ref in refs[:-1]]).astype(BF16)


def join_call(parts, **links):
    shape = parts[0].shape
    return launch(
        join_kernel,
        "join",
        (1,),
        parts,
        [whole(shape)] * len(parts),
        [whole(shape)],
        [shaped(shape, BF16)],
        **links,
    )


def factors_kernel(replicas, sum_ref, left_ref, l_ref, r_ref):
    depth = r_ref.shape[1]
    gram = sum_ref[:, depth : depth + R] / replicas
    row = lax.broadcasted_iota(jnp.int32, (R, R), 0)
    col = lax.broadcasted_iota(jnp.int32, (R, R), 1)
    eye = (row == col).astype(F32)
    basis = jnp.zeros((R, R), F32)
    for k in range(R):
        unit = eye[k : k + 1]
        coeffs = jnp.sum(basis * gram[k : k + 1], axis=1, keepdims=True)
        rest = unit - jnp.sum(coeffs * basis, axis=0, keepdims=True)
        rest_col = jnp.sum(eye * rest, axis=1, keepdims=True)
        image = jnp.sum(rest_col * gram, axis=0, keepdims=True)
        square = jnp.sum(image * rest, axis=1, keepdims=True)
        basis = jnp.where(row == k, rest * lax.rsqrt(jnp.maximum(square, 0.0) + EPS), basis)
    left = jnp.dot(basis, left_ref[...], precision=HIGH, preferred_element_type=F32)
    right = jnp.dot(basis, sum_ref[:, :depth], precision=HIGH, preferred_element_type=F32)
    hi, mid, _ = terms(left)
    zero = jnp.zeros_like(hi)
    l_ref[...] = jnp.concatenate([hi, hi, mid, zero], axis=0).T.astype(BF16)
    hi, mid, _ = terms(right / replicas)
    zero = jnp.zeros_like(hi)
    r_ref[...] = jnp.concatenate([hi, mid, hi, zero], axis=0).astype(BF16)


def factors_call(total, left, replicas, **links):
    units = left.shape[1]
    depth = total.shape[1] - 128
    return launch(
        functools.partial(factors_kernel, replicas),
        "factors",
        (1,),
        [total, left],
        [whole(total.shape), whole(left.shape)],
        [whole((units, SPLIT)), whole((SPLIT, depth))],
        [shaped((units, SPLIT), BF16), shaped((SPLIT, depth), BF16)],
        **links,
    )


def blocks_kernel(width, tail, where_ref, dg_ref, du_ref, wg_ref, wu_ref, other_ref, mine_ref, acc):
    step = pl.program_id(0)
    last = pl.num_programs(0) - 1
    pairs = acc.shape[1] // width

    def add(units, first):
        for block in range(pairs):
            cols = slice(block * width, (block + 1) * width)
            part = dot(dg_ref[0, :, :units], wg_ref[:units, cols])
            part += dot(du_ref[0, :, :units], wu_ref[:units, cols])
            acc[:, cols] = part if first else acc[:, cols] + part

    full = dg_ref.shape[2]

    @pl.when(step == 0)
    def _():
        add(full, True)

    @pl.when((step > 0) & ((step < last) | (tail == full)))
    def _():
        add(full, False)

    if tail != full:

        @pl.when((step > 0) & (step == last))
        def _():
            add(tail, False)

    @pl.when(step == last)
    def _():
        for block in range(pairs):
            cols = slice(block * width, (block + 1) * width)
            slot = (block // 2) ^ lax.rem(where_ref[0], pairs // 2)

            @pl.when(where_ref[1] == block % 2)
            def _(cols=cols, slot=slot):
                mine_ref[slot] = acc[:, cols]

            @pl.when(where_ref[1] != block % 2)
            def _(cols=cols, slot=slot):
                other_ref[slot] = acc[:, cols].astype(BF16)


def blocks_call(pos, side, count, dg, du, wg, wu, **links):
    tiles, tok, tile = dg.shape
    units, depth = wg.shape
    width = depth // (2 * count)
    split = count // 2
    tail = units - (tiles - 1) * tile
    where = jnp.stack([pos // 2, pos % 2]).astype(jnp.int32)
    part = pl.BlockSpec((1, tok, tile), lambda f, at: (f, 0, 0))
    rows = pl.BlockSpec((tile, depth // 2), lambda f, at: (f, (at[0] // split) ^ side))
    return launch(
        functools.partial(blocks_kernel, width, tail),
        "blocks",
        (tiles,),
        [dg, du, wg, wu],
        [part, part, rows, rows],
        [whole((split, tok, width))] * 2,
        [shaped((split, tok, width), BF16), shaped((split, tok, width), F32)],
        places=[where],
        scratch=[pltpu.VMEM((tok, depth // 2), F32)],
        **links,
    )


def add_kernel(one_ref, two_ref, *outs):
    for slot, out in enumerate(outs):

        @pl.when(pl.program_id(0) == slot)
        def _(out=out):
            out[...] = (one_ref[0] + two_ref[0].astype(F32)).astype(BF16)


def add_call(one, two, **links):
    slots, tok, width = one.shape
    slot = pl.BlockSpec((1, tok, width), lambda s: (s, 0, 0))
    return launch(
        add_kernel,
        "add",
        (slots,),
        [one, two],
        [slot, slot],
        [whole((tok, width))] * slots,
        [shaped((tok, width), BF16)] * slots,
        **links,
    )


def error_kernel(hid_ref, dy_ref, err_ref, l_ref, r_ref, out_ref):
    grown = dot(hid_ref[...], dy_ref[...]) + err_ref[0].astype(F32)
    out_ref[0] = (grown - dot(l_ref[...], r_ref[...])).astype(BF16)


def error_call(hid, dy, err, l, r, **links):
    units, tok = hid.shape
    depth = dy.shape[1]
    tile = 352 if units > 512 else units
    rows = pl.BlockSpec((1, tile, depth), lambda f: (0, f, 0))
    return launch(
        error_kernel,
        "error",
        (pl.cdiv(units, tile),),
        [hid, dy, err, l, r],
        [
            pl.BlockSpec((tile, tok), lambda f: (f, 0)),
            whole(dy.shape),
            rows,
            pl.BlockSpec((tile, SPLIT), lambda f: (f, 0)),
            whole(r.shape),
        ],
        [rows],
        [shaped(err.shape, BF16)],
        **links,
    )


def update_kernel(at_ref, mom_ref, all_ref, w_ref, l_ref, r_ref, mine_ref, mom_out, w_out):
    cols = mom_ref.shape[1]
    mom_out[...] = 0.9 * mom_ref[...] + dot(l_ref[...], mine_ref[...])
    for part in range(all_ref.shape[0]):
        at = slice(part * cols, (part + 1) * cols)
        mom = 0.9 * all_ref[part].astype(F32) + dot(l_ref[...], r_ref[:, at])
        w_out[:, at] = (w_ref[:, at].astype(F32) - 0.1 * mom).astype(BF16)


def update_call(at, mom, everyone, w, l, r, **links):
    units, cols = mom.shape
    depth = w.shape[1]
    tile = 176 if units > 512 else units
    rows = pl.BlockSpec((tile, depth), lambda f, at: (f, 0))
    mine = pl.BlockSpec((tile, cols), lambda f, at: (f, 0))
    return launch(
        update_kernel,
        "update",
        (pl.cdiv(units, tile),),
        [mom, everyone, w, l, r, r],
        [
            mine,
            pl.BlockSpec((everyone.shape[0], tile, cols), lambda f, at: (0, f, 0)),
            rows,
            pl.BlockSpec((tile, SPLIT), lambda f, at: (f, 0)),
            whole(r.shape),
            pl.BlockSpec((SPLIT, cols), lambda f, at: (0, at[0])),
        ],
        [mine, rows],
        [shaped(mom.shape, F32), shaped(w.shape, BF16)],
        places=[at],
        **links,
    )


def exchange(value, axis, mask):
    size = lax.axis_size(axis)
    return lax.ppermute(value, axis, [(i, i ^ mask) for i in range(size)])


def masks(size):
    return [1 << bit for bit in range(size.bit_length() - 1)]


def body(inputs, out_grads, w_gate, w_up, w_down, err_down, mom_down, q_down):
    replicas = lax.axis_size("dp")
    shards = lax.axis_size("mp")
    rank_dp = lax.axis_index("dp")
    rank_mp = lax.axis_index("mp")
    w_gate, w_up, q_t = w_gate.T, w_up.T, q_down.T
    count = shards // 2

    (low,) = cast_call(mom_down)
    everyone = lax.all_gather(low, "dp")

    hid, d_gate, d_up, dyq = hidden_call(
        inputs, out_grads, w_gate, w_up, w_down, q_t, held=[low]
    )
    (left,) = left_call(q_t, dyq, err_down, hid, replicas)
    lefts = [left] + [exchange(left, "dp", mask) for mask in range(1, replicas)]

    def blocks(side, **links):
        return blocks_call(rank_mp, side, count, d_gate, d_up, w_gate, w_up, **links)

    other, first = blocks(0, held=[left])
    total, left, other = right_call(lefts, hid, err_down, out_grads, through=[other])

    others = [exchange(other, "mp", 1)]
    steps = masks(shards)
    for index, mask in enumerate(steps):
        more = exchange(total, "mp", mask)
        held, through = [], []
        if index == 0:
            other, second = blocks(1, held=[total])
            others.append(exchange(other, "mp", 1))
            held = [other]
        elif index == 1:
            mine = list(add_call(first, others[0], held=[total]))
            held = [mine[0]]
        elif index == 2:
            mine += list(add_call(second, others[1], held=[total]))
            held = [mine[-1]]
        if index == len(steps) - 1:
            through = mine
        total, *mine_now = sum_call(total, more, held=held, through=through)
        if through:
            mine = mine_now
    landed = [exchange(mine[slot], "mp", 2 * slot) for slot in range(1, count)]
    for mask in masks(replicas):
        (total,) = sum_call(total, exchange(total, "dp", mask))

    l, r = factors_call(total, left, replicas)
    (next_err,) = error_call(hid, out_grads, err_down, l, r)
    (in_grads,) = join_call([mine[0]] + landed, held=[next_err])
    at = jnp.reshape(rank_dp, (1,)).astype(jnp.int32)
    next_mom, new = update_call(at, mom_down, everyone, w_down, l, r, held=[in_grads])
    return (in_grads, new, next_err, next_mom)


def solution(mesh):
    in_specs = (
        P("dp", None),
        P("dp", None),
        P(None, "mp"),
        P(None, "mp"),
        P("mp", None),
        P("dp", "mp", None),
        P("mp", "dp"),
        P(),
    )
    out_specs = (P("dp", "mp"), P("mp", None), P("dp", "mp", None), P("mp", "dp"))
    return jax.shard_map(body, mesh=mesh, in_specs=in_specs, out_specs=out_specs, check_vma=False)
```

time: 432 us -> 195 us (0.45)
  waiting for transfers between devices: 220 us -> 24 us
  Pallas kernels: 0 us -> 135 us
  matrix products: 119 us -> 0 us
  other arithmetic: 37.1 us -> 0.56 us
  blocking collectives: 26.8 us -> 0 us
  starting transfers between devices: 0.12 us -> 13.3 us
    pallas_call x0 -> x17, Pallas kernels: none -> 135 us  [launch(): pl.pallas_call(inner, grid_spec=pltpu.PrefetchScalarGridSpec(num_scalar_p...]
    psum x1 -> x0, waiting for transfers between devices: 133 us -> none  [body(): right_down = lax.psum(contract_rows(m_down, left_down), ('dp', 'mp'))]
    dot_general x10 -> x0, matrix products: 119 us -> none  [the longest x3 35.5 us: contract_cols(): lax.dot_general(left, right, (((1,), (1,)), ((), ())), preferred_element_...]
    all_gather x1, waiting for transfers between devices: 87.4 us -> 0.01 us  [body(): everyone = lax.all_gather(low, 'dp')]
    psum x2 -> x0, blocking collectives: 26.8 us -> none  [the longest x1 16.7 us: body(): left_down = lax.psum(jnp.dot(m_down, q_down, precision=HIGH), 'dp')]
    ppermute x0 -> x13, waiting for transfers between devices: none -> 24 us  [exchange(): return lax.ppermute(value, axis, [(i, i ^ mask) for i in range(size)])]
    broadcast_in_dim x1 -> x0, other arithmetic: 21.3 us -> none  [body(): next_err_down = (m_down - approx_down).astype(jnp.bfloat16)[None]]
    ppermute x0 -> x13, starting transfers between devices: none -> 13.2 us  [exchange(): return lax.ppermute(value, axis, [(i, i ^ mask) for i in range(size)])]
  transfers between devices with their start and end apart: 3 -> 14, of which waited for: 2 -> 5; matrix products, arithmetic and copies ran while one was open for 21% -> 1% of each run, Pallas kernels for 0% -> 57%
where the time goes in v3:
time: 195 us; the launch traced here: 194 us
  Pallas kernels  135 us (69%)
  waiting for transfers between devices  24 us (12%)
  between operations  14.1 us (7%)
  starting transfers between devices  13.3 us (7%)
  local copies, waits for them, and re-layouts  7.53 us (4%)
    pallas_call x17, Pallas kernels, launch(): pl.pallas_call(inner, grid_spec=pltpu.PrefetchScalarGridSpec(num_scalar_p...  135 us
    ppermute x13, waiting for transfers between devices, exchange(): return lax.ppermute(value, axis, [(i, i ^ mask) for i in range(size)])  24 us
    ppermute x13, starting transfers between devices, exchange(): return lax.ppermute(value, axis, [(i, i ^ mask) for i in range(size)])  13.2 us
    unnamed x27, local copies, waits for them, and re-layouts  7.53 us
  transfers between devices with their start and end apart: 14, of which 5 were waited for; matrix products, arithmetic and copies ran while one was open for 1% of the time, Pallas kernels for 57%

profile of v3, /device:TPU:8, one launch (start us, length us, event | category | flops | bytes accessed | tf_op | source)
XLA Modules:
  0.0 194.1 jit_solution(14006844705491724347)
XLA Ops:
  7.2 0.0 all-gather.3.cloned.1.call-start
  7.2 5.6 %cast.1.refs_6_ = bf16[1376,1024]{1,0:T(8,128)(2,1)} custom-call(f32[1376,1024]{1,0:T(8,128)} %refs_1_.3), custom_call_target="tpu_custom_call" | custom-call | flops 1 | bytes 1 | tf_op jit(solution)/shard_map/cast/pallas_call | solution.py:32
  12.8 0.0 all-gather.3.cloned.1.call-update
  12.9 30.1 %hidden.1 = (bf16[1376,512]{1,0:T(8,128)(2,1)}, bf16[6,512,256]{2,1,0:T(8,128)(2,1)}, bf16[6,512,256]{2,1,0:T(8,128)(2,1)}, f32[8,512]{1,0:T(8,128)}) custom-call(bf16[512,4096]{1,0:T(8,128)(2,1)} %refs_0_.3, bf16[1376,4096]{1,0:T(8,128)(2,1)} %bitcast.7, bf16[1376,4096]{1,0:T(8,128)(2,1)} %bitcast.10, bf16[1376,4096]{1,0:T(8,128)(2,1)} %refs_3_.3, ...), custom_call_target="tpu_custom_call" | custom-call | flops 1 | bytes 1 | tf_op jit(solution)/shard_map/hidden/pallas_call | solution.py:32
  42.9 8.7 %left.1.refs_5_.refs_0_ = f32[8,1376]{1,0:T(8,128)} custom-call(f32[8,4096]{1,0:T(8,128)} %bitcast.15, f32[8,512]{1,0:T(8,128)} %get-tuple-element.28.refs_1_, bf16[1,1376,4096]{2,1,0:T(8,128)(2,1)} %refs_2_.3, bf16[1376,512]{1,0:T(8,128)(2,1)} %get-tuple-element.29.refs_3_.refs_4_.refs_0_), custom_call_target="tpu_custom_call" | custom-call | flops 1 | bytes 1 | tf_op jit(solution)/shard_map/left/pallas_call | solution.py:32
  51.7 2.5 %collective-permute-start.2 = (f32[8,1376]{1,0:T(8,128)}, f32[8,1376]{1,0:T(8,128)S(1)}, u32[]{:S(2)}, u32[]{:S(2)}) collective-permute-start(f32[8,1376]{1,0:T(8,128)} %left.1.refs_5_.refs_0_), channel_id=1, source_target_pairs={{0,24},{8,16},{16,8},{24,0},{1,25},{9,17},{17,9},{25,1},{2,26},{10... | collective-permute-start | bytes 132104 | tf_op jit(solution)/shard_map/ppermute | solution.py:495
  54.1 0.5 collective-permute-start.1
  54.6 0.5 collective-permute-start
  55.1 0.6 pad_add_fusion.refs_0_
  55.7 13.0 %blocks.2 = (bf16[2,512,512]{2,1,0:T(8,128)(2,1)}, f32[2,512,512]{2,1,0:T(8,128)}) custom-call(s32[2]{0:T(128)} %pad_add_fusion.refs_0_, bf16[6,512,256]{2,1,0:T(8,128)(2,1)} %get-tuple-element.30.refs_1_, bf16[6,512,256]{2,1,0:T(8,128)(2,1)} %get-tuple-element.31.refs_2_, bf16[1376,4096]{1,0:T(8,128)(2,1)} %bitcast.8, bf16[1376,4096]{1,0:T(8,128)(2,1)} %bitcast.11, ...), custom_call_target="tpu_custom_call" | custom-call | flops 1 | bytes 1 | tf_op jit(solution)/shard_map/blocks/pallas_call | solution.py:32
  68.7 0.6 copy-done.10
  69.3 0.0 copy-done.11
  69.3 0.0 copy-done.12
  69.4 9.5 %right.1 = (f32[8,4224]{1,0:T(8,128)}, f32[8,1376]{1,0:T(8,128)}, bf16[2,512,512]{2,1,0:T(8,128)(2,1)}) custom-call(f32[8,1376]{1,0:T(8,128)} %left.1.refs_5_.refs_0_, f32[8,1376]{1,0:T(8,128)} %copy-done.12, f32[8,1376]{1,0:T(8,128)} %copy-done.11, f32[8,1376]{1,0:T(8,128)} %copy-done.10, ...), custom_call_target="tpu_custom_call", output_to_operand_aliasing={{2}: (7, {})} | custom-call | flops 1 | bytes 1 | tf_op jit(solution)/shard_map/right/pallas_call | solution.py:32
  78.9 13.1 %blocks.3 = (bf16[2,512,512]{2,1,0:T(8,128)(2,1)}, f32[2,512,512]{2,1,0:T(8,128)}) custom-call(s32[2]{0:T(128)} %pad_add_fusion.refs_0_, bf16[6,512,256]{2,1,0:T(8,128)(2,1)} %get-tuple-element.30.refs_1_, bf16[6,512,256]{2,1,0:T(8,128)(2,1)} %get-tuple-element.31.refs_2_, bf16[1376,4096]{1,0:T(8,128)(2,1)} %bitcast.9, bf16[1376,4096]{1,0:T(8,128)(2,1)} %bitcast.12, ...), custom_call_target="tpu_custom_call" | custom-call | flops 1 | bytes 1 | tf_op jit(solution)/shard_map/blocks/pallas_call | solution.py:32
  91.9 0.5 collective-permute-start.7
  92.4 0.1 collective-permute-start.3
  92.5 2.3 %collective-permute-done.3.refs_1_ = f32[8,4224]{1,0:T(8,128)S(1)} collective-permute-done((f32[8,4224]{1,0:T(8,128)S(1)}, f32[8,4224]{1,0:T(8,128)S(1)}, u32[]{:S(2)}, u32[]{:S(2)}) %collective-permute-start.3) | collective-permute-done | bytes 135200 | tf_op jit(solution)/shard_map/ppermute | solution.py:495
  94.8 0.6 copy-done.9
  95.4 1.6 sum.5.refs_2_.refs_0_
  97.1 0.1 collective-permute-start.4
  97.1 3.0 %add.11 = (bf16[512,512]{1,0:T(8,128)(2,1)}, bf16[512,512]{1,0:T(8,128)(2,1)}) custom-call(f32[2,512,512]{2,1,0:T(8,128)} %get-tuple-element.35.refs_0_, bf16[2,512,512]{2,1,0:T(8,128)(2,1)} %collective-permute-done.5.refs_1_, f32[8,4224]{1,0:T(8,128)} %sum.5.refs_2_.refs_0_), custom_call_target="tpu_custom_call" | custom-call | flops 1 | bytes 1 | tf_op jit(solution)/shard_map/add/pallas_call | solution.py:32
  100.2 2.7 %collective-permute-done.4.refs_1_ = f32[8,4224]{1,0:T(8,128)S(1)} collective-permute-done((f32[8,4224]{1,0:T(8,128)}, f32[8,4224]{1,0:T(8,128)S(1)}, u32[]{:S(2)}, u32[]{:S(2)}) %collective-permute-start.4) | collective-permute-done | bytes 135200 | tf_op jit(solution)/shard_map/ppermute | solution.py:495
  102.9 0.7 copy-done.6
  103.6 1.6 sum.6.refs_2_.refs_0_
  105.2 2.5 %collective-permute-start.6 = (f32[8,4224]{1,0:T(8,128)}, f32[8,4224]{1,0:T(8,128)S(1)}, u32[]{:S(2)}, u32[]{:S(2)}) collective-permute-start(f32[8,4224]{1,0:T(8,128)} %sum.6.refs_2_.refs_0_), channel_id=1, source_target_pairs={{0,4},{1,5},{2,6},{3,7},{4,0},{5,1},{6,2},{7,3},{8,12},{9,13},{10,... | collective-permute-start | bytes 405512 | tf_op jit(solution)/shard_map/ppermute | solution.py:495
  107.7 1.0 copy-done
  108.7 3.0 %add.12 = (bf16[512,512]{1,0:T(8,128)(2,1)}, bf16[512,512]{1,0:T(8,128)(2,1)}) custom-call(f32[2,512,512]{2,1,0:T(8,128)} %get-tuple-element.38.refs_0_, bf16[2,512,512]{2,1,0:T(8,128)(2,1)} %copy-done, f32[8,4224]{1,0:T(8,128)} %sum.6.refs_2_.refs_0_), custom_call_target="tpu_custom_call" | custom-call | flops 1 | bytes 1 | tf_op jit(solution)/shard_map/add/pallas_call | solution.py:32
  111.7 1.9 copy.21.refs_6_
  113.5 0.7 copy-done.5
  114.2 1.6 sum.7
  115.8 1.1 collective-permute-start.8
  116.9 1.9 collective-permute-start.9
  118.8 0.6 collective-permute-start.10
  119.4 1.5 collective-permute-start.11
  120.9 7.5 %collective-permute-done.11.refs_1_ = f32[8,4224]{1,0:T(8,128)S(1)} collective-permute-done((f32[8,4224]{1,0:T(8,128)}, f32[8,4224]{1,0:T(8,128)S(1)}, u32[]{:S(2)}, u32[]{:S(2)}) %collective-permute-start.11) | collective-permute-done | bytes 135200 | tf_op jit(solution)/shard_map/ppermute | solution.py:495
  128.4 0.7 copy-done.8
  129.1 1.6 sum.8.refs_0_
  130.7 1.5 collective-permute-start.12
  132.2 3.7 %collective-permute-done.12.refs_1_ = f32[8,4224]{1,0:T(8,128)S(1)} collective-permute-done((f32[8,4224]{1,0:T(8,128)}, f32[8,4224]{1,0:T(8,128)S(1)}, u32[]{:S(2)}, u32[]{:S(2)}) %collective-permute-start.12) | collective-permute-done | bytes 135200 | tf_op jit(solution)/shard_map/ppermute | solution.py:495
  135.9 0.7 copy-done.7
  136.6 1.6 sum.9.refs_0_
  138.2 4.2 %factors.1 = (bf16[1376,32]{1,0:T(8,128)(2,1)}, bf16[32,4096]{1,0:T(8,128)(2,1)}) custom-call(f32[8,4224]{1,0:T(8,128)} %sum.9.refs_0_, f32[8,1376]{1,0:T(8,128)} %get-tuple-element.47.refs_1_), custom_call_target="tpu_custom_call" | custom-call | flops 1 | bytes 1 | tf_op jit(solution)/shard_map/factors/pallas_call | solution.py:32
  142.4 15.0 %error.1.refs_4_ = bf16[1,1376,4096]{2,1,0:T(8,128)(2,1)} custom-call(bf16[1376,512]{1,0:T(8,128)(2,1)} %get-tuple-element.29.refs_3_.refs_4_.refs_0_, bf16[512,4096]{1,0:T(8,128)(2,1)} %refs_1_.2, bf16[1,1376,4096]{2,1,0:T(8,128)(2,1)} %refs_2_.3, bf16[1376,32]{1,0:T(8,128)(2,1)} %get-tuple-element.48.refs_3_.refs_4_, ...), custom_call_target="tpu_custom_call" | custom-call | flops 1 | bytes 1 | tf_op jit(solution)/shard_map/error/pallas_call | solution.py:32
  157.5 7.7 %collective-permute-done.10.refs_3_ = bf16[512,512]{1,0:T(8,128)(2,1)S(1)} collective-permute-done((bf16[512,512]{1,0:T(8,128)(2,1)}, bf16[512,512]{1,0:T(8,128)(2,1)S(1)}, u32[]{:S(2)}, u32[]{:S(2)}) %collective-permute-start.10) | collective-permute-done | bytes 524320 | tf_op jit(solution)/shard_map/ppermute | solution.py:495
  165.2 0.8 copy-done.4
  166.0 2.6 %join.1.refs_7_ = bf16[512,512]{1,0:T(8,128)(2,1)} custom-call(bf16[512,512]{1,0:T(8,128)(2,1)} %get-tuple-element.42.refs_0_, bf16[512,512]{1,0:T(8,128)(2,1)} %copy-done.2, bf16[512,512]{1,0:T(8,128)(2,1)} %copy-done.3, bf16[512,512]{1,0:T(8,128)(2,1)} %copy-done.4, bf16[1,1376,4096]{2,1,0:T(8,128)(2,1)} %error.1.refs_4_), custom_call_target="tpu_custom_call" | custom-call | flops 1 | bytes 1 | tf_op jit(solution)/shard_map/join/pallas_call | solution.py:32
  168.5 18.7 %update.1 = (f32[1376,1024]{1,0:T(8,128)}, bf16[1376,4096]{1,0:T(8,128)(2,1)}) custom-call(s32[1]{0:T(128)} %bitcast.5.refs_0_, f32[1376,1024]{1,0:T(8,128)} %refs_1_.3, bf16[4,1376,1024]{2,1,0:T(8,128)(2,1)} %bitcast.13, bf16[1376,4096]{1,0:T(8,128)(2,1)} %refs_3_.3, bf16[1376,32]{1,0:T(8,128)(2,1)} %get-tuple-element.48.refs_3_.refs_4_, ...), custom_call_target="tpu_custom_call" | custom-call | flops 1 | bytes 1 | tf_op jit(solution)/shard_map/update/pallas_call | solution.py:32
  (26 shorter events, 0.1 us)
Async XLA Ops:
  7.2 161.4 %all-gather.3.cloned.1.call-start = ((), (), s32[]{:S(2)}) async-start(), calls=%async_computation | async-start | bytes 14090240 | tf_op jit(solution)/shard_map/all_gather | solution.py:511
  51.7 17.0 %collective-permute-start.2 = (f32[8,1376]{1,0:T(8,128)}, f32[8,1376]{1,0:T(8,128)S(1)}, u32[]{:S(2)}, u32[]{:S(2)}) collective-permute-start(f32[8,1376]{1,0:T(8,128)} %left.1.refs_5_.refs_0_), channel_id=1, source_target_pairs={{0,24},{8,16},{16,8},{24,0},{1,25},{9,17},{17,9},{25,1},{2,26},{10... | collective-permute-start | bytes 132104 | tf_op jit(solution)/shard_map/ppermute | solution.py:495
  54.1 14.6 %collective-permute-start.1 = (f32[8,1376]{1,0:T(8,128)}, f32[8,1376]{1,0:T(8,128)S(1)}, u32[]{:S(2)}, u32[]{:S(2)}) collective-permute-start(f32[8,1376]{1,0:T(8,128)} %left.1.refs_5_.refs_0_), channel_id=1, source_target_pairs={{0,16},{8,24},{16,0},{24,8},{1,17},{9,25},{17,1},{25,9},{2,18},{10... | collective-permute-start | bytes 132104 | tf_op jit(solution)/shard_map/ppermute | solution.py:495
  54.6 14.1 %collective-permute-start = (f32[8,1376]{1,0:T(8,128)}, f32[8,1376]{1,0:T(8,128)S(1)}, u32[]{:S(2)}, u32[]{:S(2)}) collective-permute-start(f32[8,1376]{1,0:T(8,128)} %left.1.refs_5_.refs_0_), channel_id=1, source_target_pairs={{0,8},{8,0},{16,24},{24,16},{1,9},{9,1},{17,25},{25,17},{2,10},{10... | collective-permute-start | bytes 132104 | tf_op jit(solution)/shard_map/ppermute | solution.py:495
  68.7 0.6 copy-start.10
  68.7 0.6 copy-start.11
  68.7 0.6 copy-start.12
  78.8 18.3 %collective-permute-start.5 = (bf16[2,512,512]{2,1,0:T(8,128)(2,1)}, bf16[2,512,512]{2,1,0:T(8,128)(2,1)}, u32[]{:S(2)}, u32[]{:S(2)}) collective-permute-start(bf16[2,512,512]{2,1,0:T(8,128)(2,1)} %get-tuple-element.36), channel_id=1, source_target_pairs={{0,1},{1,0},{2,3},{3,2},{4,5},{5,4},{6,7},{7,6},{8,9},{9,8},{10,11... | collective-permute-start | bytes 3145736 | tf_op jit(solution)/shard_map/ppermute | solution.py:495
  78.8 13.6 %copy-start.1 = (f32[8,4224]{1,0:T(8,128)S(1)}, f32[8,4224]{1,0:T(8,128)}, u32[]{:S(2)}) copy-start(f32[8,4224]{1,0:T(8,128)} %get-tuple-element.33.refs_5_.refs_0_) | copy-start | bytes 405508
  91.9 15.8 %collective-permute-start.7 = (bf16[2,512,512]{2,1,0:T(8,128)(2,1)}, bf16[2,512,512]{2,1,0:T(8,128)(2,1)S(1)}, u32[]{:S(2)}, u32[]{:S(2)}) collective-permute-start(bf16[2,512,512]{2,1,0:T(8,128)(2,1)} %get-tuple-element.34.refs_2_), channel_id=1, source_target_pairs={{0,1},{1,0},{2,3},{3,2},{4,5},{5,4},{6,7},{7,6},{8,9},{9,8},{10,11... | collective-permute-start | bytes 3145736 | tf_op jit(solution)/shard_map/ppermute | solution.py:495
  92.4 2.4 %collective-permute-start.3 = (f32[8,4224]{1,0:T(8,128)S(1)}, f32[8,4224]{1,0:T(8,128)S(1)}, u32[]{:S(2)}, u32[]{:S(2)}) collective-permute-start(f32[8,4224]{1,0:T(8,128)S(1)} %copy-done.1), channel_id=1, source_target_pairs={{0,1},{1,0},{2,3},{3,2},{4,5},{5,4},{6,7},{7,6},{8,9},{9,8},{10,11... | collective-permute-start | bytes 405512 | tf_op jit(solution)/shard_map/ppermute | solution.py:495
  94.8 0.7 copy-start.9
  97.1 5.8 %collective-permute-start.4 = (f32[8,4224]{1,0:T(8,128)}, f32[8,4224]{1,0:T(8,128)S(1)}, u32[]{:S(2)}, u32[]{:S(2)}) collective-permute-start(f32[8,4224]{1,0:T(8,128)} %sum.5.refs_2_.refs_0_), channel_id=1, source_target_pairs={{0,2},{1,3},{2,0},{3,1},{4,6},{5,7},{6,4},{7,5},{8,10},{9,11},{10,... | collective-permute-start | bytes 405512 | tf_op jit(solution)/shard_map/ppermute | solution.py:495
  102.9 0.7 copy-start.6
  105.2 8.3 %collective-permute-start.6 = (f32[8,4224]{1,0:T(8,128)}, f32[8,4224]{1,0:T(8,128)S(1)}, u32[]{:S(2)}, u32[]{:S(2)}) collective-permute-start(f32[8,4224]{1,0:T(8,128)} %sum.6.refs_2_.refs_0_), channel_id=1, source_target_pairs={{0,4},{1,5},{2,6},{3,7},{4,0},{5,1},{6,2},{7,3},{8,12},{9,13},{10,... | collective-permute-start | bytes 405512 | tf_op jit(solution)/shard_map/ppermute | solution.py:495
  107.7 1.0 copy-start
  113.5 0.7 copy-start.5
  115.8 41.6 %collective-permute-start.8 = (bf16[512,512]{1,0:T(8,128)(2,1)}, bf16[512,512]{1,0:T(8,128)(2,1)S(1)}, u32[]{:S(2)}, u32[]{:S(2)}) collective-permute-start(bf16[512,512]{1,0:T(8,128)(2,1)} %get-tuple-element.43), channel_id=1, source_target_pairs={{0,2},{1,3},{2,0},{3,1},{4,6},{5,7},{6,4},{7,5},{8,10},{9,11},{10,... | collective-permute-start | bytes 1572872 | tf_op jit(solution)/shard_map/ppermute | solution.py:495
  116.9 40.6 %collective-permute-start.9 = (bf16[512,512]{1,0:T(8,128)(2,1)}, bf16[512,512]{1,0:T(8,128)(2,1)S(1)}, u32[]{:S(2)}, u32[]{:S(2)}) collective-permute-start(bf16[512,512]{1,0:T(8,128)(2,1)} %get-tuple-element.44), channel_id=1, source_target_pairs={{0,4},{1,5},{2,6},{3,7},{4,0},{5,1},{6,2},{7,3},{8,12},{9,13},{10,... | collective-permute-start | bytes 1572872 | tf_op jit(solution)/shard_map/ppermute | solution.py:495
  118.8 46.3 %collective-permute-start.10 = (bf16[512,512]{1,0:T(8,128)(2,1)}, bf16[512,512]{1,0:T(8,128)(2,1)S(1)}, u32[]{:S(2)}, u32[]{:S(2)}) collective-permute-start(bf16[512,512]{1,0:T(8,128)(2,1)} %get-tuple-element.45), channel_id=1, source_target_pairs={{0,6},{1,7},{2,4},{3,5},{4,2},{5,3},{6,0},{7,1},{8,14},{9,15},{10,... | collective-permute-start | bytes 1572872 | tf_op jit(solution)/shard_map/ppermute | solution.py:495
  119.4 9.0 %collective-permute-start.11 = (f32[8,4224]{1,0:T(8,128)}, f32[8,4224]{1,0:T(8,128)S(1)}, u32[]{:S(2)}, u32[]{:S(2)}) collective-permute-start(f32[8,4224]{1,0:T(8,128)} %get-tuple-element.46.refs_0_), channel_id=1, source_target_pairs={{0,8},{8,0},{16,24},{24,16},{1,9},{9,1},{17,25},{25,17},{2,10},{10... | collective-permute-start | bytes 405512 | tf_op jit(solution)/shard_map/ppermute | solution.py:495
  128.4 0.7 copy-start.8
  130.7 5.2 %collective-permute-start.12 = (f32[8,4224]{1,0:T(8,128)}, f32[8,4224]{1,0:T(8,128)S(1)}, u32[]{:S(2)}, u32[]{:S(2)}) collective-permute-start(f32[8,4224]{1,0:T(8,128)} %sum.8.refs_0_), channel_id=1, source_target_pairs={{0,16},{8,24},{16,0},{24,8},{1,17},{9,25},{17,1},{25,9},{2,18},{10... | collective-permute-start | bytes 405512 | tf_op jit(solution)/shard_map/ppermute | solution.py:495
  135.9 0.7 copy-start.7
  157.5 7.7 %copy-start.2 = (bf16[512,512]{1,0:T(8,128)(2,1)}, bf16[512,512]{1,0:T(8,128)(2,1)S(1)}, u32[]{:S(2)}) copy-start(bf16[512,512]{1,0:T(8,128)(2,1)S(1)} %collective-permute-done.8.refs_1_) | copy-start | bytes 1572868
  157.5 7.7 %copy-start.3 = (bf16[512,512]{1,0:T(8,128)(2,1)}, bf16[512,512]{1,0:T(8,128)(2,1)S(1)}, u32[]{:S(2)}) copy-start(bf16[512,512]{1,0:T(8,128)(2,1)S(1)} %collective-permute-done.9.refs_2_) | copy-start | bytes 1572868
  165.2 0.8 copy-start.4
Sparse Core Ops, SparseCore 0:
  13.0 117.5 all-gather.2

commit v4 on v3

--- a/solution.py
+++ b/solution.py
@@ -13,13 +13,16 @@
 F32 = jnp.float32
 BF16 = jnp.bfloat16
 HIGH = lax.Precision.HIGHEST
-VMEM = 62 * 2**20
+VMEM = 48 * 2**20
+SMALL = 12 * 2**20
+LARGE = 62 * 2**20
 ONCE = pl.Buffered(1)
+STREAMS = 4
 HELD = pl.BlockSpec(memory_space=pl.ANY)
 
 
 def launch(kernel, name, grid, args, in_specs, out_specs, out_shape, *, places=(), held=(),
-           through=(), scratch=(), aliases=None):
+           through=(), scratch=(), vmem=VMEM):
     n_in, n_out = len(args), len(out_shape)
     n_held, n_through, n_place = len(held), len(through), len(places)
     first = n_place + n_in
@@ -40,8 +43,8 @@
         ),
         out_shape=list(out_shape)
         + [jax.ShapeDtypeStruct(array.shape, array.dtype) for array in through],
-        input_output_aliases={**links, **(aliases or {})},
-        compiler_params=pltpu.CompilerParams(vmem_limit_bytes=VMEM),
+        input_output_aliases=links,
+        compiler_params=pltpu.CompilerParams(vmem_limit_bytes=vmem),
         cost_estimate=pl.CostEstimate(flops=1, bytes_accessed=1, transcendentals=0),
         name=name,
     )(*places, *args, *held, *through)
@@ -96,31 +99,48 @@
 
 def cast_call(mom):
     units, cols = mom.shape
-    tile = unit_tile(units)
+    tile = 352 if units > 512 else units
     part = pl.BlockSpec((tile, cols), lambda f: (f, 0))
     return launch(
-        cast_kernel, "cast", (pl.cdiv(units, tile),), [mom], [part], [part], [shaped(mom.shape, BF16)]
-    )
+        cast_kernel,
+        "cast",
+        (pl.cdiv(units, tile),),
+        [mom],
+        [part],
+        [part],
+        [shaped(mom.shape, BF16)],
+    )
+
+
+def dot_parts(left_ref, parts):
+    width = parts[0].shape[-1]
+    total = None
+    for at, part in enumerate(parts):
+        more = dot_nt(left_ref[:, at * width : (at + 1) * width], part[...])
+        total = more if total is None else total + more
+    return total
 
 
 def hidden_kernel(
-    x_ref, wg_ref, wu_ref, wd_ref, q_ref, dy_any, hid_ref, dg_ref, du_ref, dyq_ref, dy_ref, sem
+    x_ref, q_ref, dy_any, *refs
 ):
+    weights, (hid_ref, dg_ref, du_ref, dyq_ref, dy_ref, sem) = refs[:-6], refs[-6:]
+    ways = len(weights) // 3
     fetch = pltpu.make_async_copy(dy_any, dy_ref, sem)
 
     @pl.when(pl.program_id(0) == 0)
     def _():
         fetch.start()
 
-    gate = dot_nt(x_ref[...], wg_ref[...])
-    up = dot_nt(x_ref[...], wu_ref[...])
+    gate = dot_parts(x_ref, weights[:ways])
+    up = dot_parts(x_ref, weights[ways : 2 * ways])
 
     @pl.when(pl.program_id(0) == 0)
     def _():
         fetch.wait()
         dyq_ref[...] = gather_terms(dot_nt(spread(q_ref[...]), dy_ref[...]))
 
-    dh = dot_nt(dy_ref[...], wd_ref[...])
+    dh = dot_parts(dy_ref, weights[2 * ways :])
     sig = jax.nn.sigmoid(gate)
     silu = gate * sig
     hid_ref[...] = (silu * up).T.astype(BF16)
@@ -133,14 +153,15 @@
     units = wg.shape[0]
     tile = unit_tile(units)
     tiles = pl.cdiv(units, tile)
-    rows = pl.BlockSpec((tile, depth), lambda f: (f, 0))
+    ways = 2
+    rows = [pl.BlockSpec((tile, depth // ways), lambda f, c=c: (f, c)) for c in range(ways)]
     part = pl.BlockSpec((1, tok, tile), lambda f: (f, 0, 0))
     return launch(
         hidden_kernel,
         "hidden",
         (tiles,),
-        [x, wg, wu, wd, q_t, dy],
-        [whole((tok, depth)), rows, rows, rows, whole(q_t.shape), HELD],
+        [x, q_t, dy] + [wg] * ways + [wu] * ways + [wd] * ways,
+        [whole((tok, depth)), whole(q_t.shape), HELD] + rows * 3,
         [pl.BlockSpec((tile, tok), lambda f: (f, 0)), part, part, whole((R, tok))],
         [
             shaped((units, tok), BF16),
@@ -153,14 +174,24 @@
     )
 
 
-def left_kernel(replicas, q_ref, dyq_ref, err_ref, hid_ref, out_ref, q_terms, dyq_terms):
+def left_kernel(replicas, q_ref, dyq_ref, hid_ref, *refs):
+    errs, (out_ref, q_terms, dyq_terms) = refs[:-3], refs[-3:]
+    width = errs[0].shape[2]
+
     @pl.when(pl.program_id(0) == 0)
     def _():
         q_terms[...] = spread(q_ref[...])
         dyq_terms[...] = spread(dyq_ref[...])
 
-    both = dot_nt(err_ref[0], q_terms[...]) + dot_nt(hid_ref[...], dyq_terms[...])
+    both = dot_nt(hid_ref[...], dyq_terms[...])
+    for at, err_ref in enumerate(errs):
+        both += dot_nt(err_ref[0], q_terms[:, at * width : (at + 1) * width])
     out_ref[...] = gather_terms(both.T) / replicas
+
+
+def error_streams(tile, depth):
+    shape = (1, tile, depth // STREAMS)
+    return [pl.BlockSpec(shape, lambda f, c=c: (0, f, c)) for c in range(STREAMS)]
 
 
 def left_call(q_t, dyq, err, hid, replicas, **links):
@@ -171,13 +202,9 @@
         functools.partial(left_kernel, replicas),
         "left",
         (pl.cdiv(units, tile),),
-        [q_t, dyq, err, hid],
-        [
-            whole(q_t.shape),
-            whole(dyq.shape),
-            pl.BlockSpec((1, tile, depth), lambda f: (0, f, 0)),
-            pl.BlockSpec((tile, tok), lambda f: (f, 0)),
-        ],
+        [q_t, dyq, hid] + [err] * STREAMS,
+        [whole(q_t.shape), whole(dyq.shape), pl.BlockSpec((tile, tok), lambda f: (f, 0))]
+        + error_streams(tile, depth),
         [pl.BlockSpec((R, tile), lambda f: (0, f))],
         [shaped((R, units), F32)],
         scratch=[pltpu.VMEM((SPLIT, depth), BF16), pltpu.VMEM((SPLIT, tok), BF16)],
@@ -193,10 +220,14 @@
 
 def right_kernel(parts, dy_steps, *refs):
     lefts = refs[:parts]
-    hid_ref, err_ref, dy_ref, out_ref, left_ref, left_terms, mixed_terms, total = refs[parts:]
+    errs, (hid_ref, dy_ref, out_ref, left_ref, left_terms, mixed_terms, total) = (
+        refs[parts:-7],
+        refs[-7:],
+    )
     step = pl.program_id(0)
     units = left_ref.shape[1]
-    tile, depth = err_ref.shape[1:]
+    tile, width = errs[0].shape[1:]
+    depth = width * len(errs)
     dy_tile = dy_ref.shape[0]
     tail = units % tile
     last = pl.num_programs(0) - 1
@@ -221,14 +252,20 @@
 
         @pl.when(step < last)
         def _():
-            total[...] += dot(columns(left_terms, step, tile), err_ref[0])
+            left = columns(left_terms, step, tile)
+            for at, err_ref in enumerate(errs):
+                total[:, at * width : (at + 1) * width] += dot(left, err_ref[0])
 
         @pl.when(step == last)
         def _():
-            total[...] += dot(left_terms[:, units - tail : units], err_ref[0, :tail])
+            left = left_terms[:, units - tail : units]
+            for at, err_ref in enumerate(errs):
+                total[:, at * width : (at + 1) * width] += dot(left, err_ref[0, :tail])
 
     else:
-        total[...] += dot(columns(left_terms, step, tile), err_ref[0])
+        left = columns(left_terms, step, tile)
+        for at, err_ref in enumerate(errs):
+            total[:, at * width : (at + 1) * width] += dot(left, err_ref[0])
 
     @pl.when(step == last)
     def _():
@@ -245,11 +282,11 @@
         functools.partial(right_kernel, len(lefts), dy_steps),
         "right",
         (tiles,),
-        [*lefts, hid, err, dy],
+        [*lefts] + [err] * STREAMS + [hid, dy],
         [whole((R, units))] * len(lefts)
+        + error_streams(tile, depth)
         + [
             whole((units, tok)),
-            pl.BlockSpec((1, tile, depth), lambda f: (0, f, 0)),
             pl.BlockSpec((tok // dy_steps, depth), lambda f: (jnp.minimum(f, dy_steps - 1), 0)),
         ],
         [whole((R, depth + 128)), whole((R, units))],
@@ -276,6 +313,7 @@
         [whole(one.shape)] * 2,
         [whole(one.shape)],
         [shaped(one.shape, one.dtype)],
+        vmem=SMALL,
         **links,
     )
 
@@ -294,6 +332,7 @@
         [whole(shape)] * len(parts),
         [whole(shape)],
         [shaped(shape, BF16)],
+        vmem=SMALL,
         **links,
     )
 
@@ -334,6 +373,7 @@
         [whole(total.shape), whole(left.shape)],
         [whole((units, SPLIT)), whole((SPLIT, depth))],
         [shaped((units, SPLIT), BF16), shaped((SPLIT, depth), BF16)],
+        vmem=SMALL,
         **links,
     )
 
@@ -389,7 +429,8 @@
     tail = units - (tiles - 1) * tile
     where = jnp.stack([pos // 2, pos % 2]).astype(jnp.int32)
     part = pl.BlockSpec((1, tok, tile), lambda f, at: (f, 0, 0))
-    rows = pl.BlockSpec((tile, depth // 2), lambda f, at: (f, (at[0] // split) ^ side))
+    half = depth // 2
+    rows = pl.BlockSpec((tile, half), lambda f, at: (f, (at[0] // split) ^ side))
     return launch(
         functools.partial(blocks_kernel, width, tail),
         "blocks",
@@ -399,7 +440,7 @@
         [whole((split, tok, width))] * 2,
         [shaped((split, tok, width), BF16), shaped((split, tok, width), F32)],
         places=[where],
-        scratch=[pltpu.VMEM((tok, depth // 2), F32)],
+        scratch=[pltpu.VMEM((tok, half), F32)],
         **links,
     )
 
@@ -423,33 +464,37 @@
         [slot, slot],
         [whole((tok, width))] * slots,
         [shaped((tok, width), BF16)] * slots,
-        **links,
-    )
-
-
-def error_kernel(hid_ref, dy_ref, err_ref, l_ref, r_ref, out_ref):
-    grown = dot(hid_ref[...], dy_ref[...]) + err_ref[0].astype(F32)
-    out_ref[0] = (grown - dot(l_ref[...], r_ref[...])).astype(BF16)
+        vmem=SMALL,
+        **links,
+    )
+
+
+def error_kernel(hid_ref, dy_ref, l_ref, r_ref, *refs):
+    errs, out_ref = refs[:-1], refs[-1]
+    width = errs[0].shape[2]
+    for part, err_ref in enumerate(errs):
+        at = slice(part * width, (part + 1) * width)
+        grown = dot(hid_ref[...], dy_ref[:, at]) + err_ref[0].astype(F32)
+        out_ref[0, :, at] = (grown - dot(l_ref[...], r_ref[:, at])).astype(BF16)
 
 
 def error_call(hid, dy, err, l, r, **links):
     units, tok = hid.shape
     depth = dy.shape[1]
     tile = 352 if units > 512 else units
-    rows = pl.BlockSpec((1, tile, depth), lambda f: (0, f, 0))
     return launch(
         error_kernel,
         "error",
         (pl.cdiv(units, tile),),
-        [hid, dy, err, l, r],
+        [hid, dy, l, r] + [err] * STREAMS,
         [
             pl.BlockSpec((tile, tok), lambda f: (f, 0)),
             whole(dy.shape),
-            rows,
             pl.BlockSpec((tile, SPLIT), lambda f: (f, 0)),
             whole(r.shape),
+            *error_streams(tile, depth),
         ],
-        [rows],
+        [pl.BlockSpec((1, tile, depth), lambda f: (0, f, 0))],
         [shaped(err.shape, BF16)],
         **links,
     )
@@ -470,6 +515,7 @@
     tile = 176 if units > 512 else units
     rows = pl.BlockSpec((tile, depth), lambda f, at: (f, 0))
     mine = pl.BlockSpec((tile, cols), lambda f, at: (f, 0))
+    parts = everyone.shape[0]
     return launch(
         update_kernel,
         "update",
@@ -477,7 +523,7 @@
         [mom, everyone, w, l, r, r],
         [
             mine,
-            pl.BlockSpec((everyone.shape[0], tile, cols), lambda f, at: (0, f, 0)),
+            pl.BlockSpec((parts, tile, cols), lambda f, at: (0, f, 0)),
             rows,
             pl.BlockSpec((tile, SPLIT), lambda f, at: (f, 0)),
             whole(r.shape),
@@ -486,6 +532,7 @@
         [mine, rows],
         [shaped(mom.shape, F32), shaped(w.shape, BF16)],
         places=[at],
+        vmem=LARGE,
         **links,
     )
 
@@ -548,9 +595,9 @@
 
     l, r = factors_call(total, left, replicas)
     (next_err,) = error_call(hid, out_grads, err_down, l, r)
-    (in_grads,) = join_call([mine[0]] + landed, held=[next_err])
     at = jnp.reshape(rank_dp, (1,)).astype(jnp.int32)
-    next_mom, new = update_call(at, mom_down, everyone, w_down, l, r, held=[in_grads])
+    next_mom, new = update_call(at, mom_down, everyone, w_down, l, r, held=[next_err])
+    (in_grads,) = join_call([mine[0]] + landed, held=[next_mom])
     return (in_grads, new, next_err, next_mom)
 
 

time: 195 us -> 180 us (0.923)
  Pallas kernels: 135 us -> 115 us
    pallas_call x17, Pallas kernels: 135 us -> 115 us  [launch(): pl.pallas_call(inner, grid_spec=pltpu.PrefetchScalarGridSpec(num_scalar_p...]
    unnamed x27 -> x21, local copies, waits for them, and re-layouts: 7.53 us -> 7.61 us
  transfers between devices with their start and end apart: 14 -> 14, of which waited for: 5 -> 5; matrix products, arithmetic and copies ran while one was open for 1% -> 0% of each run, Pallas kernels for 57% -> 61%
where the time goes in v4:
time: 180 us; the launch traced here: 177 us
  Pallas kernels  115 us (64%)
  waiting for transfers between devices  25.8 us (14%)
  starting transfers between devices  14.4 us (8%)
  between operations  14.2 us (8%)
  local copies, waits for them, and re-layouts  7.61 us (4%)
    pallas_call x17, Pallas kernels, launch(): pl.pallas_call(inner, grid_spec=pltpu.PrefetchScalarGridSpec(num_scalar_p...  115 us
    ppermute x13, waiting for transfers between devices, exchange(): return lax.ppermute(value, axis, [(i, i ^ mask) for i in range(size)])  25.7 us
    ppermute x13, starting transfers between devices, exchange(): return lax.ppermute(value, axis, [(i, i ^ mask) for i in range(size)])  14.4 us
    unnamed x21, local copies, waits for them, and re-layouts  7.61 us
  transfers between devices with their start and end apart: 14, of which 5 were waited for; matrix products, arithmetic and copies ran while one was open for 0% of the time, Pallas kernels for 61%

profile of v4, /device:TPU:8, one launch (start us, length us, event | category | flops | bytes accessed | tf_op | source)
XLA Modules:
  0.0 177.2 jit_solution(3396243624703291854)
XLA Ops:
  7.2 0.0 all-gather.3.cloned.1.call-start
  7.2 4.7 %cast.1.refs_9_ = bf16[1376,1024]{1,0:T(8,128)(2,1)} custom-call(f32[1376,1024]{1,0:T(8,128)} %refs_1_.3), custom_call_target="tpu_custom_call" | custom-call | flops 1 | bytes 1 | tf_op jit(solution)/shard_map/cast/pallas_call | solution.py:35
  11.9 0.0 all-gather.3.cloned.1.call-update
  12.0 30.7 %hidden.1 = (bf16[1376,512]{1,0:T(8,128)(2,1)S(1)}, bf16[6,512,256]{2,1,0:T(8,128)(2,1)S(1)}, bf16[6,512,256]{2,1,0:T(8,128)(2,1)S(1)}, f32[8,512]{1,0:T(8,128)S(1)}) custom-call(bf16[512,4096]{1,0:T(8,128)(2,1)} %refs_0_.3, f32[8,4096]{1,0:T(8,128)S(1)} %bitcast.7, bf16[512,4096]{1,0:T(8,128)(2,1)} %refs_1_.2, bf16[1376,4096]{1,0:T(8,128)(2,1)} %bitcast.9, ...), custom_call_target="tpu_custom_call" | custom-call | flops 1 | bytes 1 | tf_op jit(solution)/shard_map/hidden/pallas_call | solution.py:35
  42.6 0.0 copy-start.1
  42.6 1.1 copy-done.1
  43.8 7.9 %left.1.refs_5_.refs_0_ = f32[8,1376]{1,0:T(8,128)S(1)} custom-call(f32[8,4096]{1,0:T(8,128)S(1)} %bitcast.8, f32[8,512]{1,0:T(8,128)S(1)} %get-tuple-element.28.refs_1_, bf16[1376,512]{1,0:T(8,128)(2,1)S(1)} %get-tuple-element.29.refs_2_.refs_8_.refs_0_, bf16[1,1376,4096]{2,1,0:T(8,128)(2,1)} %refs_7_.5, bf16[1,1376,4096]{2,1,0:T(8,128)(2,1)} %refs_7_.5, ...), custom_call_target="tpu_custom_call" | custom-call | flops 1 | bytes 1 | tf_op jit(solution)/shard_map/left/pallas_call | solution.py:35
  51.7 2.6 %collective-permute-start.2 = (f32[8,1376]{1,0:T(8,128)S(1)}, f32[8,1376]{1,0:T(8,128)S(1)}, u32[]{:S(2)}, u32[]{:S(2)}) collective-permute-start(f32[8,1376]{1,0:T(8,128)S(1)} %left.1.refs_5_.refs_0_), channel_id=1, source_target_pairs={{0,24},{8,16},{16,8},{24,0},{1,25},{9,17},{17,9},{25,1},{2,26},{10... | collective-permute-start | bytes 132104 | tf_op jit(solution)/shard_map/ppermute | solution.py:542
  54.2 0.4 collective-permute-start.1
  54.7 0.6 collective-permute-start
  55.2 0.1 pad_add_fusion.refs_0_
  55.3 1.4 copy-done.2
  56.7 12.0 %blocks.2 = (bf16[2,512,512]{2,1,0:T(8,128)(2,1)S(1)}, f32[2,512,512]{2,1,0:T(8,128)}) custom-call(s32[2]{0:T(128)S(1)} %pad_add_fusion.refs_0_, bf16[6,512,256]{2,1,0:T(8,128)(2,1)S(1)} %get-tuple-element.30.refs_1_, bf16[6,512,256]{2,1,0:T(8,128)(2,1)S(1)} %copy-done.2, bf16[1376,4096]{1,0:T(8,128)(2,1)} %bitcast.11, bf16[1376,4096]{1,0:T(8,128)(2,1)} %bitcast.15, ...), custom_call_target="tpu_custom_call" | custom-call | flops 1 | bytes 1 | tf_op jit(solution)/shard_map/blocks/pallas_call | solution.py:35
  68.7 0.0 collective-permute-done.2.refs_3_
  68.7 0.0 collective-permute-done.1.refs_2_
  68.7 0.0 copy-start.3
  68.7 8.4 %right.1 = (f32[8,4224]{1,0:T(8,128)S(1)}, f32[8,1376]{1,0:T(8,128)S(1)}, bf16[2,512,512]{2,1,0:T(8,128)(2,1)S(1)}) custom-call(f32[8,1376]{1,0:T(8,128)S(1)} %left.1.refs_5_.refs_0_, f32[8,1376]{1,0:T(8,128)S(1)} %collective-permute-done.refs_1_, f32[8,1376]{1,0:T(8,128)S(1)} %collective-permute-done.1.refs_2_, ...), custom_call_target="tpu_custom_call", output_to_operand_aliasing={{2}: (10, {})} | custom-call | flops 1 | bytes 1 | tf_op jit(solution)/shard_map/right/pallas_call | solution.py:35
  77.2 0.1 collective-permute-start.5
  77.3 0.0 copy-start.6
  77.3 12.1 %blocks.3 = (bf16[2,512,512]{2,1,0:T(8,128)(2,1)S(1)}, f32[2,512,512]{2,1,0:T(8,128)}) custom-call(s32[2]{0:T(128)S(1)} %pad_add_fusion.refs_0_, bf16[6,512,256]{2,1,0:T(8,128)(2,1)S(1)} %get-tuple-element.30.refs_1_, bf16[6,512,256]{2,1,0:T(8,128)(2,1)S(1)} %copy-done.3, bf16[1376,4096]{1,0:T(8,128)(2,1)} %bitcast.12, bf16[1376,4096]{1,0:T(8,128)(2,1)} %bitcast.16, ...), custom_call_target="tpu_custom_call" | custom-call | flops 1 | bytes 1 | tf_op jit(solution)/shard_map/blocks/pallas_call | solution.py:35
  89.4 0.5 collective-permute-start.7
  89.8 0.0 collective-permute-start.3
  89.9 2.5 %collective-permute-done.3.refs_1_ = f32[8,4224]{1,0:T(8,128)S(1)} collective-permute-done((f32[8,4224]{1,0:T(8,128)S(1)}, f32[8,4224]{1,0:T(8,128)S(1)}, u32[]{:S(2)}, u32[]{:S(2)}) %collective-permute-start.3) | collective-permute-done | bytes 135200 | tf_op jit(solution)/shard_map/ppermute | solution.py:542
  92.3 0.1 collective-permute-start.4
  92.4 1.2 add.11
  93.7 4.6 %collective-permute-done.4.refs_1_ = f32[8,4224]{1,0:T(8,128)S(1)} collective-permute-done((f32[8,4224]{1,0:T(8,128)S(1)}, f32[8,4224]{1,0:T(8,128)S(1)}, u32[]{:S(2)}, u32[]{:S(2)}) %collective-permute-start.4) | collective-permute-done | bytes 135200 | tf_op jit(solution)/shard_map/ppermute | solution.py:542
  98.3 3.1 %collective-permute-start.6 = (f32[8,4224]{1,0:T(8,128)S(1)}, f32[8,4224]{1,0:T(8,128)S(1)}, u32[]{:S(2)}, u32[]{:S(2)}) collective-permute-start(f32[8,4224]{1,0:T(8,128)S(1)} %sum.6.refs_2_.refs_0_), channel_id=1, source_target_pairs={{0,4},{1,5},{2,6},{3,7},{4,0},{5,1},{6,2},{7,3},{8,12},{9,13},{10,... | collective-permute-start | bytes 405512 | tf_op jit(solution)/shard_map/ppermute | solution.py:542
  101.4 0.0 collective-permute-done.7.refs_1_
  101.4 1.0 add.12
  102.4 4.3 %collective-permute-done.6.refs_1_ = f32[8,4224]{1,0:T(8,128)S(1)} collective-permute-done((f32[8,4224]{1,0:T(8,128)S(1)}, f32[8,4224]{1,0:T(8,128)S(1)}, u32[]{:S(2)}, u32[]{:S(2)}) %collective-permute-start.6) | collective-permute-done | bytes 135200 | tf_op jit(solution)/shard_map/ppermute | solution.py:542
  106.7 1.4 collective-permute-start.8
  108.1 2.2 %collective-permute-start.9 = (bf16[512,512]{1,0:T(8,128)(2,1)}, bf16[512,512]{1,0:T(8,128)(2,1)}, u32[]{:S(2)}, u32[]{:S(2)}) collective-permute-start(bf16[512,512]{1,0:T(8,128)(2,1)} %get-tuple-element.44), channel_id=1, source_target_pairs={{0,4},{1,5},{2,6},{3,7},{4,0},{5,1},{6,2},{7,3},{8,12},{9,13},{10,... | collective-permute-start | bytes 1572872 | tf_op jit(solution)/shard_map/ppermute | solution.py:542
  110.3 0.5 collective-permute-start.10
  110.8 1.5 collective-permute-start.11
  112.3 7.3 %collective-permute-done.11.refs_1_ = f32[8,4224]{1,0:T(8,128)S(1)} collective-permute-done((f32[8,4224]{1,0:T(8,128)S(1)}, f32[8,4224]{1,0:T(8,128)S(1)}, u32[]{:S(2)}, u32[]{:S(2)}) %collective-permute-start.11) | collective-permute-done | bytes 135200 | tf_op jit(solution)/shard_map/ppermute | solution.py:542
  119.6 1.6 collective-permute-start.12
  121.2 7.1 %collective-permute-done.12.refs_1_ = f32[8,4224]{1,0:T(8,128)S(1)} collective-permute-done((f32[8,4224]{1,0:T(8,128)S(1)}, f32[8,4224]{1,0:T(8,128)S(1)}, u32[]{:S(2)}, u32[]{:S(2)}) %collective-permute-start.12) | collective-permute-done | bytes 135200 | tf_op jit(solution)/shard_map/ppermute | solution.py:542
  128.2 2.5 %factors.1 = (bf16[1376,32]{1,0:T(8,128)(2,1)S(1)}, bf16[32,4096]{1,0:T(8,128)(2,1)S(1)}) custom-call(f32[8,4224]{1,0:T(8,128)S(1)} %sum.9.refs_0_, f32[8,1376]{1,0:T(8,128)S(1)} %get-tuple-element.47.refs_1_), custom_call_target="tpu_custom_call" | custom-call | flops 1 | bytes 1 | tf_op jit(solution)/shard_map/factors/pallas_call | solution.py:35
  130.7 0.0 copy-start
  130.8 2.4 %copy-done = bf16[512,4096]{1,0:T(8,128)(2,1)S(1)} copy-done((bf16[512,4096]{1,0:T(8,128)(2,1)S(1)}, bf16[512,4096]{1,0:T(8,128)(2,1)}, u32[]{:S(2)}) %copy-start) | copy-done | bytes 4194328
  133.2 13.4 %error.1.refs_7_ = bf16[1,1376,4096]{2,1,0:T(8,128)(2,1)} custom-call(bf16[1376,512]{1,0:T(8,128)(2,1)S(1)} %get-tuple-element.29.refs_2_.refs_8_.refs_0_, bf16[512,4096]{1,0:T(8,128)(2,1)S(1)} %copy-done, bf16[1376,32]{1,0:T(8,128)(2,1)S(1)} %get-tuple-element.48.refs_2_.refs_4_, bf16[32,4096]{1,0:T(8,128)(2,1)S(1)} %get-tuple-element.49.refs_3_.refs_5_.refs_6_, ...), custom_call_target="tpu_custom_call" | custom-call | flops 1 | bytes 1 | tf_op jit(solution)/shard_map/error/pallas_call | solution.py:35
  146.6 0.0 all-gather.3.cloned.1.call-done
  146.6 18.7 %update.1 = (f32[1376,1024]{1,0:T(8,128)}, bf16[1376,4096]{1,0:T(8,128)(2,1)}) custom-call(s32[1]{0:T(128)} %bitcast.5.refs_0_, f32[1376,1024]{1,0:T(8,128)} %refs_1_.3, bf16[4,1376,1024]{2,1,0:T(8,128)(2,1)} %bitcast.17, bf16[1376,4096]{1,0:T(8,128)(2,1)} %refs_3_.3, bf16[1376,32]{1,0:T(8,128)(2,1)} %copy-done.8, bf16[32,4096]{1,0:T(8,128)(2,1)} %copy-done.5, ...), custom_call_target="tpu_custom_call" | custom-call | flops 1 | bytes 1 | tf_op jit(solution)/shard_map/update/pallas_call | solution.py:35
  165.4 0.0 collective-permute-done.8.refs_1_
  165.4 0.0 collective-permute-done.10.refs_3_
  165.4 0.0 copy-start.4
  165.4 2.6 %copy-done.4 = f32[1376,1024]{1,0:T(8,128)S(1)} copy-done((f32[1376,1024]{1,0:T(8,128)S(1)}, f32[1376,1024]{1,0:T(8,128)}, u32[]{:S(2)}) %copy-start.4) | copy-done | bytes 5636120
  168.0 2.4 %join.1 = bf16[512,512]{1,0:T(8,128)(2,1)} custom-call(bf16[512,512]{1,0:T(8,128)(2,1)S(1)} %get-tuple-element.42.refs_0_, bf16[512,512]{1,0:T(8,128)(2,1)} %collective-permute-done.8.refs_1_, bf16[512,512]{1,0:T(8,128)(2,1)} %collective-permute-done.9.refs_2_, bf16[512,512]{1,0:T(8,128)(2,1)} %collective-permute-done.10.refs_3_, f32[1376,1024]{1,0:T(8,128)S(1)} %copy-done.4), custom_call_target="tpu_custom_call" | custom-call | flops 1 | bytes 1 | tf_op jit(solution)/shard_map/join/pallas_call | solution.py:35
  (20 shorter events, 0.1 us)
Async XLA Ops:
  7.2 4.8 %copy-start.9 = (f32[4096,8]{0,1:T(8,128)S(1)}, f32[4096,8]{0,1:T(8,128)}, u32[]{:S(2)}) copy-start(f32[4096,8]{0,1:T(8,128)} %param.15) | copy-start | bytes 393220
  7.2 139.5 %all-gather.3.cloned.1.call-start = ((), (), s32[]{:S(2)}) async-start(), calls=%async_computation | async-start | bytes 14090240 | tf_op jit(solution)/shard_map/all_gather | solution.py:558
  42.6 1.1 copy-start.1
  51.7 17.0 %collective-permute-start.2 = (f32[8,1376]{1,0:T(8,128)S(1)}, f32[8,1376]{1,0:T(8,128)S(1)}, u32[]{:S(2)}, u32[]{:S(2)}) collective-permute-start(f32[8,1376]{1,0:T(8,128)S(1)} %left.1.refs_5_.refs_0_), channel_id=1, source_target_pairs={{0,24},{8,16},{16,8},{24,0},{1,25},{9,17},{17,9},{25,1},{2,26},{10... | collective-permute-start | bytes 132104 | tf_op jit(solution)/shard_map/ppermute | solution.py:542
  54.2 14.5 %collective-permute-start.1 = (f32[8,1376]{1,0:T(8,128)S(1)}, f32[8,1376]{1,0:T(8,128)S(1)}, u32[]{:S(2)}, u32[]{:S(2)}) collective-permute-start(f32[8,1376]{1,0:T(8,128)S(1)} %left.1.refs_5_.refs_0_), channel_id=1, source_target_pairs={{0,16},{8,24},{16,0},{24,8},{1,17},{9,25},{17,1},{25,9},{2,18},{10... | collective-permute-start | bytes 132104 | tf_op jit(solution)/shard_map/ppermute | solution.py:542
  54.7 14.0 %collective-permute-start = (f32[8,1376]{1,0:T(8,128)S(1)}, f32[8,1376]{1,0:T(8,128)S(1)}, u32[]{:S(2)}, u32[]{:S(2)}) collective-permute-start(f32[8,1376]{1,0:T(8,128)S(1)} %left.1.refs_5_.refs_0_), channel_id=1, source_target_pairs={{0,8},{8,0},{16,24},{24,16},{1,9},{9,1},{17,25},{25,17},{2,10},{10... | collective-permute-start | bytes 132104 | tf_op jit(solution)/shard_map/ppermute | solution.py:542
  55.3 1.4 copy-start.2
  68.7 8.5 %copy-start.3 = (bf16[6,512,256]{2,1,0:T(8,128)(2,1)S(1)}, bf16[6,512,256]{2,1,0:T(8,128)(2,1)}, u32[]{:S(2)}) copy-start(bf16[6,512,256]{2,1,0:T(8,128)(2,1)} %copy-done.1) | copy-start | bytes 4718596
  77.2 15.2 %collective-permute-start.5 = (bf16[2,512,512]{2,1,0:T(8,128)(2,1)S(1)}, bf16[2,512,512]{2,1,0:T(8,128)(2,1)S(1)}, u32[]{:S(2)}, u32[]{:S(2)}) collective-permute-start(bf16[2,512,512]{2,1,0:T(8,128)(2,1)S(1)} %get-tuple-element.36), channel_id=1, source_target_pairs={{0,1},{1,0},{2,3},{3,2},{4,5},{5,4},{6,7},{7,6},{8,9},{9,8},{10,11... | collective-permute-start | bytes 3145736 | tf_op jit(solution)/shard_map/ppermute | solution.py:542
  77.3 15.2 %copy-start.6 = (f32[2,512,512]{2,1,0:T(8,128)S(1)}, f32[2,512,512]{2,1,0:T(8,128)}, u32[]{:S(2)}) copy-start(f32[2,512,512]{2,1,0:T(8,128)} %get-tuple-element.35.refs_0_) | copy-start | bytes 6291460
  89.4 12.0 %copy-start.7 = (f32[2,512,512]{2,1,0:T(8,128)S(1)}, f32[2,512,512]{2,1,0:T(8,128)}, u32[]{:S(2)}) copy-start(f32[2,512,512]{2,1,0:T(8,128)} %get-tuple-element.38.refs_0_) | copy-start | bytes 6291460
  89.4 12.0 %collective-permute-start.7 = (bf16[2,512,512]{2,1,0:T(8,128)(2,1)S(1)}, bf16[2,512,512]{2,1,0:T(8,128)(2,1)S(1)}, u32[]{:S(2)}, u32[]{:S(2)}) collective-permute-start(bf16[2,512,512]{2,1,0:T(8,128)(2,1)S(1)} %get-tuple-element.34.refs_2_), channel_id=1, source_target_pairs={{0,1},{1,0},{2,3},{3,2},{4,5},{5,4},{6,7},{7,6},{8,9},{9,8},{10,11... | collective-permute-start | bytes 3145736 | tf_op jit(solution)/shard_map/ppermute | solution.py:542
  89.8 2.5 %collective-permute-start.3 = (f32[8,4224]{1,0:T(8,128)S(1)}, f32[8,4224]{1,0:T(8,128)S(1)}, u32[]{:S(2)}, u32[]{:S(2)}) collective-permute-start(f32[8,4224]{1,0:T(8,128)S(1)} %get-tuple-element.33.refs_5_.refs_0_), channel_id=1, source_target_pairs={{0,1},{1,0},{2,3},{3,2},{4,5},{5,4},{6,7},{7,6},{8,9},{9,8},{10,11... | collective-permute-start | bytes 405512 | tf_op jit(solution)/shard_map/ppermute | solution.py:542
  92.3 5.9 %collective-permute-start.4 = (f32[8,4224]{1,0:T(8,128)S(1)}, f32[8,4224]{1,0:T(8,128)S(1)}, u32[]{:S(2)}, u32[]{:S(2)}) collective-permute-start(f32[8,4224]{1,0:T(8,128)S(1)} %sum.5.refs_2_.refs_0_), channel_id=1, source_target_pairs={{0,2},{1,3},{2,0},{3,1},{4,6},{5,7},{6,4},{7,5},{8,10},{9,11},{10,... | collective-permute-start | bytes 405512 | tf_op jit(solution)/shard_map/ppermute | solution.py:542
  98.3 8.4 %collective-permute-start.6 = (f32[8,4224]{1,0:T(8,128)S(1)}, f32[8,4224]{1,0:T(8,128)S(1)}, u32[]{:S(2)}, u32[]{:S(2)}) collective-permute-start(f32[8,4224]{1,0:T(8,128)S(1)} %sum.6.refs_2_.refs_0_), channel_id=1, source_target_pairs={{0,4},{1,5},{2,6},{3,7},{4,0},{5,1},{6,2},{7,3},{8,12},{9,13},{10,... | collective-permute-start | bytes 405512 | tf_op jit(solution)/shard_map/ppermute | solution.py:542
  106.7 58.6 %collective-permute-start.8 = (bf16[512,512]{1,0:T(8,128)(2,1)}, bf16[512,512]{1,0:T(8,128)(2,1)}, u32[]{:S(2)}, u32[]{:S(2)}) collective-permute-start(bf16[512,512]{1,0:T(8,128)(2,1)} %get-tuple-element.43), channel_id=1, source_target_pairs={{0,2},{1,3},{2,0},{3,1},{4,6},{5,7},{6,4},{7,5},{8,10},{9,11},{10,... | collective-permute-start | bytes 1572872 | tf_op jit(solution)/shard_map/ppermute | solution.py:542
  108.1 57.3 %collective-permute-start.9 = (bf16[512,512]{1,0:T(8,128)(2,1)}, bf16[512,512]{1,0:T(8,128)(2,1)}, u32[]{:S(2)}, u32[]{:S(2)}) collective-permute-start(bf16[512,512]{1,0:T(8,128)(2,1)} %get-tuple-element.44), channel_id=1, source_target_pairs={{0,4},{1,5},{2,6},{3,7},{4,0},{5,1},{6,2},{7,3},{8,12},{9,13},{10,... | collective-permute-start | bytes 1572872 | tf_op jit(solution)/shard_map/ppermute | solution.py:542
  110.3 55.1 %collective-permute-start.10 = (bf16[512,512]{1,0:T(8,128)(2,1)S(1)}, bf16[512,512]{1,0:T(8,128)(2,1)}, u32[]{:S(2)}, u32[]{:S(2)}) collective-permute-start(bf16[512,512]{1,0:T(8,128)(2,1)S(1)} %get-tuple-element.45), channel_id=1, source_target_pairs={{0,6},{1,7},{2,4},{3,5},{4,2},{5,3},{6,0},{7,1},{8,14},{9,15},{10,... | collective-permute-start | bytes 1572872 | tf_op jit(solution)/shard_map/ppermute | solution.py:542
  110.8 8.8 %collective-permute-start.11 = (f32[8,4224]{1,0:T(8,128)S(1)}, f32[8,4224]{1,0:T(8,128)S(1)}, u32[]{:S(2)}, u32[]{:S(2)}) collective-permute-start(f32[8,4224]{1,0:T(8,128)S(1)} %get-tuple-element.46.refs_0_), channel_id=1, source_target_pairs={{0,8},{8,0},{16,24},{24,16},{1,9},{9,1},{17,25},{25,17},{2,10},{10... | collective-permute-start | bytes 405512 | tf_op jit(solution)/shard_map/ppermute | solution.py:542
  119.6 8.6 %collective-permute-start.12 = (f32[8,4224]{1,0:T(8,128)S(1)}, f32[8,4224]{1,0:T(8,128)S(1)}, u32[]{:S(2)}, u32[]{:S(2)}) collective-permute-start(f32[8,4224]{1,0:T(8,128)S(1)} %sum.8.refs_0_), channel_id=1, source_target_pairs={{0,16},{8,24},{16,0},{24,8},{1,17},{9,25},{17,1},{25,9},{2,18},{10... | collective-permute-start | bytes 405512 | tf_op jit(solution)/shard_map/ppermute | solution.py:542
  130.7 15.9 %copy-start.5 = (bf16[32,4096]{1,0:T(8,128)(2,1)}, bf16[32,4096]{1,0:T(8,128)(2,1)S(1)}, u32[]{:S(2)}) copy-start(bf16[32,4096]{1,0:T(8,128)(2,1)S(1)} %get-tuple-element.49.refs_3_.refs_5_.refs_6_) | copy-start | bytes 786436
  130.7 15.9 %copy-start.8 = (bf16[1376,32]{1,0:T(8,128)(2,1)}, bf16[1376,32]{1,0:T(8,128)(2,1)S(1)}, u32[]{:S(2)}) copy-start(bf16[1376,32]{1,0:T(8,128)(2,1)S(1)} %get-tuple-element.48.refs_2_.refs_4_) | copy-start | bytes 264196
  130.7 2.4 %copy-start = (bf16[512,4096]{1,0:T(8,128)(2,1)S(1)}, bf16[512,4096]{1,0:T(8,128)(2,1)}, u32[]{:S(2)}) copy-start(bf16[512,4096]{1,0:T(8,128)(2,1)} %refs_1_.2) | copy-start | bytes 12582916
  165.4 2.6 %copy-start.4 = (f32[1376,1024]{1,0:T(8,128)S(1)}, f32[1376,1024]{1,0:T(8,128)}, u32[]{:S(2)}) copy-start(f32[1376,1024]{1,0:T(8,128)} %get-tuple-element.27.refs_4_) | copy-start | bytes 16908292
Sparse Core Ops, SparseCore 0:
  12.1 117.9 all-gather.2

commit v5 on v4

--- a/solution.py
+++ b/solution.py
@@ -22,7 +22,7 @@
 
 
 def launch(kernel, name, grid, args, in_specs, out_specs, out_shape, *, places=(), held=(),
-           through=(), scratch=(), vmem=VMEM):
+           through=(), scratch=(), vmem=VMEM, aliases=None):
     n_in, n_out = len(args), len(out_shape)
     n_held, n_through, n_place = len(held), len(through), len(places)
     first = n_place + n_in
@@ -43,7 +43,7 @@
         ),
         out_shape=list(out_shape)
         + [jax.ShapeDtypeStruct(array.shape, array.dtype) for array in through],
-        input_output_aliases=links,
+        input_output_aliases={**links, **(aliases or {})},
         compiler_params=pltpu.CompilerParams(vmem_limit_bytes=vmem),
         cost_estimate=pl.CostEstimate(flops=1, bytes_accessed=1, transcendentals=0),
         name=name,
@@ -93,80 +93,71 @@
     return 256 if units > 512 and units % 16 == 0 else units
 
 
-def cast_kernel(mom_ref, out_ref):
-    out_ref[...] = mom_ref[...].astype(BF16)
-
-
-def cast_call(mom):
+def cast_kernel(mom_ref, *outs):
+    half = mom_ref.shape[1] // 2
+    low, high = mom_ref[:, :half].astype(BF16), mom_ref[:, half:].astype(BF16)
+    for out, part in zip(outs, (low, high, low, high)):
+        out[...] = part
+
+
+def cast_call(mom, **links):
     units, cols = mom.shape
-    tile = 352 if units > 512 else units
-    part = pl.BlockSpec((tile, cols), lambda f: (f, 0))
+    tile = units // 2 if units % 32 == 0 and units > 512 else units
+    part = pl.BlockSpec((tile, cols // 2), lambda f: (f, 0))
     return launch(
         cast_kernel,
         "cast",
-        (pl.cdiv(units, tile),),
+        (units // tile,),
         [mom],
-        [part],
-        [part],
-        [shaped(mom.shape, BF16)],
-    )
-
-
-def dot_parts(left_ref, parts):
-    width = parts[0].shape[-1]
-    total = None
-    for at, part in enumerate(parts):
-        more = dot_nt(left_ref[:, at * width : (at + 1) * width], part[...])
-        total = more if total is None else total + more
-    return total
+        [pl.BlockSpec((tile, cols), lambda f: (f, 0))],
+        [part] * 4,
+        [shaped((units, cols // 2), BF16)] * 4,
+        **links,
+    )
 
 
 def hidden_kernel(
-    x_ref, q_ref, dy_any, *refs
+    x_ref, wg_ref, wu_ref, wd_ref, q_ref, dy_any, hid_ref, dg_ref, du_ref, dyq_ref, dy_ref, sem
 ):
-    weights, (hid_ref, dg_ref, du_ref, dyq_ref, dy_ref, sem) = refs[:-6], refs[-6:]
-    ways = len(weights) // 3
     fetch = pltpu.make_async_copy(dy_any, dy_ref, sem)
 
     @pl.when(pl.program_id(0) == 0)
     def _():
         fetch.start()
 
-    gate = dot_parts(x_ref, weights[:ways])
-    up = dot_parts(x_ref, weights[ways : 2 * ways])
+    gate = dot_nt(x_ref[...], wg_ref[...])
+    up = dot_nt(x_ref[...], wu_ref[...])
 
     @pl.when(pl.program_id(0) == 0)
     def _():
         fetch.wait()
-        dyq_ref[...] = gather_terms(dot_nt(spread(q_ref[...]), dy_ref[...]))
-
-    dh = dot_parts(dy_ref, weights[2 * ways :])
+        dyq_ref[...] = gather_terms(dot_nt(dy_ref[...], spread(q_ref[...])).T)
+
+    dh = dot_nt(dy_ref[...], wd_ref[...])
     sig = jax.nn.sigmoid(gate)
     silu = gate * sig
     hid_ref[...] = (silu * up).T.astype(BF16)
-    dg_ref[0] = (dh * up * sig * (1.0 + gate * (1.0 - sig))).astype(BF16)
-    du_ref[0] = (dh * silu).astype(BF16)
+    dg_ref[...] = (dh * up * sig * (1.0 + gate * (1.0 - sig))).astype(BF16)
+    du_ref[...] = (dh * silu).astype(BF16)
 
 
 def hidden_call(x, dy, wg, wu, wd, q_t, **links):
     tok, depth = x.shape
     units = wg.shape[0]
     tile = unit_tile(units)
-    tiles = pl.cdiv(units, tile)
-    ways = 2
-    rows = [pl.BlockSpec((tile, depth // ways), lambda f, c=c: (f, c)) for c in range(ways)]
-    part = pl.BlockSpec((1, tok, tile), lambda f: (f, 0, 0))
+    rows = pl.BlockSpec((tile, depth), lambda f: (f, 0))
+    part = pl.BlockSpec((tok, tile), lambda f: (0, f))
     return launch(
         hidden_kernel,
         "hidden",
-        (tiles,),
-        [x, q_t, dy] + [wg] * ways + [wu] * ways + [wd] * ways,
-        [whole((tok, depth)), whole(q_t.shape), HELD] + rows * 3,
+        (pl.cdiv(units, tile),),
+        [x, wg, wu, wd, q_t, dy],
+        [whole((tok, depth)), rows, rows, rows, whole(q_t.shape), HELD],
         [pl.BlockSpec((tile, tok), lambda f: (f, 0)), part, part, whole((R, tok))],
         [
             shaped((units, tok), BF16),
-            shaped((tiles, tok, tile), BF16),
-            shaped((tiles, tok, tile), BF16),
+            shaped((tok, units), BF16),
+            shaped((tok, units), BF16),
             shaped((R, tok), F32),
         ],
         scratch=[pltpu.VMEM((tok, depth), BF16), pltpu.SemaphoreType.DMA(())],
@@ -373,99 +364,47 @@
         [whole(total.shape), whole(left.shape)],
         [whole((units, SPLIT)), whole((SPLIT, depth))],
         [shaped((units, SPLIT), BF16), shaped((SPLIT, depth), BF16)],
-        vmem=SMALL,
-        **links,
-    )
-
-
-def blocks_kernel(width, tail, where_ref, dg_ref, du_ref, wg_ref, wu_ref, other_ref, mine_ref, acc):
-    step = pl.program_id(0)
-    last = pl.num_programs(0) - 1
-    pairs = acc.shape[1] // width
-
-    def add(units, first):
-        for block in range(pairs):
-            cols = slice(block * width, (block + 1) * width)
-            part = dot(dg_ref[0, :, :units], wg_ref[:units, cols])
-            part += dot(du_ref[0, :, :units], wu_ref[:units, cols])
-            acc[:, cols] = part if first else acc[:, cols] + part
-
-    full = dg_ref.shape[2]
-
-    @pl.when(step == 0)
-    def _():
-        add(full, True)
-
-    @pl.when((step > 0) & ((step < last) | (tail == full)))
-    def _():
-        add(full, False)
-
-    if tail != full:
-
-        @pl.when((step > 0) & (step == last))
-        def _():
-            add(tail, False)
-
-    @pl.when(step == last)
-    def _():
-        for block in range(pairs):
-            cols = slice(block * width, (block + 1) * width)
-            slot = (block // 2) ^ lax.rem(where_ref[0], pairs // 2)
-
-            @pl.when(where_ref[1] == block % 2)
-            def _(cols=cols, slot=slot):
-                mine_ref[slot] = acc[:, cols]
-
-            @pl.when(where_ref[1] != block % 2)
-            def _(cols=cols, slot=slot):
-                other_ref[slot] = acc[:, cols].astype(BF16)
-
-
-def blocks_call(pos, side, count, dg, du, wg, wu, **links):
-    tiles, tok, tile = dg.shape
-    units, depth = wg.shape
-    width = depth // (2 * count)
-    split = count // 2
-    tail = units - (tiles - 1) * tile
-    where = jnp.stack([pos // 2, pos % 2]).astype(jnp.int32)
-    part = pl.BlockSpec((1, tok, tile), lambda f, at: (f, 0, 0))
-    half = depth // 2
-    rows = pl.BlockSpec((tile, half), lambda f, at: (f, (at[0] // split) ^ side))
-    return launch(
-        functools.partial(blocks_kernel, width, tail),
-        "blocks",
-        (tiles,),
-        [dg, du, wg, wu],
-        [part, part, rows, rows],
-        [whole((split, tok, width))] * 2,
-        [shaped((split, tok, width), BF16), shaped((split, tok, width), F32)],
-        places=[where],
-        scratch=[pltpu.VMEM((tok, half), F32)],
-        **links,
-    )
-
-
-def add_kernel(one_ref, two_ref, *outs):
+        vmem=LARGE,
+        **links,
+    )
+
+
+def other_kernel(where_ref, dg_ref, du_ref, wg_ref, wu_ref, out_ref):
+    out_ref[0] = (dot(dg_ref[...], wg_ref[...]) + dot(du_ref[...], wu_ref[...])).astype(BF16)
+
+
+def mine_kernel(where_ref, dg_ref, du_ref, wg_ref, wu_ref, add_ref, *outs):
+    part = dot(dg_ref[...], wg_ref[...]) + dot(du_ref[...], wu_ref[...])
+    part = (part + add_ref[0].astype(F32)).astype(BF16)
     for slot, out in enumerate(outs):
 
         @pl.when(pl.program_id(0) == slot)
         def _(out=out):
-            out[...] = (one_ref[0] + two_ref[0].astype(F32)).astype(BF16)
-
-
-def add_call(one, two, **links):
-    slots, tok, width = one.shape
-    slot = pl.BlockSpec((1, tok, width), lambda s: (s, 0, 0))
-    return launch(
-        add_kernel,
-        "add",
-        (slots,),
-        [one, two],
-        [slot, slot],
-        [whole((tok, width))] * slots,
-        [shaped((tok, width), BF16)] * slots,
-        vmem=SMALL,
-        **links,
+            out[...] = part
+
+
+def blocks_call(pos, parity, slots, count, dg, du, wg, wu, add=None, **links):
+    tok, units = dg.shape
+    depth = wg.shape[1]
+    width = depth // (2 * count)
+    where = jnp.stack([pos // 2, parity]).astype(jnp.int32)
+    first, steps = slots
+    block = pl.BlockSpec((units, width), lambda s, at: (0, 2 * ((s + first) ^ at[0]) + at[1]))
+    slot = pl.BlockSpec((1, tok, width), lambda s, at: (s, 0, 0))
+    in_specs = [whole((tok, units)), whole((tok, units)), block, block]
+    args = [dg, du, wg, wu]
+    if add is None:
+        kernel = other_kernel
+        out_specs = [slot]
+        out_shape = [shaped((steps, tok, width), BF16)]
+    else:
+        kernel = mine_kernel
+        in_specs.append(slot)
+        args.append(add)
+        out_specs = [whole((tok, width))] * steps
+        out_shape = [shaped((tok, width), BF16)] * steps
+    return launch(
+        kernel, "blocks", (steps,), args, in_specs, out_specs, out_shape, places=[where], **links
     )
 
 
@@ -500,39 +439,92 @@
     )
 
 
-def update_kernel(at_ref, mom_ref, all_ref, w_ref, l_ref, r_ref, mine_ref, mom_out, w_out):
-    cols = mom_ref.shape[1]
-    mom_out[...] = 0.9 * mom_ref[...] + dot(l_ref[...], mine_ref[...])
-    for part in range(all_ref.shape[0]):
-        at = slice(part * cols, (part + 1) * cols)
-        mom = 0.9 * all_ref[part].astype(F32) + dot(l_ref[...], r_ref[:, at])
-        w_out[:, at] = (w_ref[:, at].astype(F32) - 0.1 * mom).astype(BF16)
-
-
-def update_call(at, mom, everyone, w, l, r, **links):
+def updated(w, mom, approx):
+    return (w.astype(F32) - 0.1 * (0.9 * mom.astype(F32) + approx)).astype(BF16)
+
+
+def update_kernel(own, at_ref, mom_ref, l_ref, r_ref, w_ref, *refs):
+    pieces, (mom_out, w_out) = refs[:-2], refs[-2:]
+    step = pl.program_id(0)
+
+    @pl.when(step < own)
+    def _():
+        approx = dot(l_ref[...], r_ref[...])
+        mom = mom_ref[...]
+        mom_out[...] = 0.9 * mom + approx
+        w_out[...] = updated(w_ref[...], mom.astype(BF16), approx)
+
+    for slot, piece in enumerate(pieces):
+
+        @pl.when(step == own + slot)
+        def _(piece=piece):
+            w_out[...] = updated(w_ref[...], piece[...], dot(l_ref[...], r_ref[...]))
+
+
+def update_call(at, mom, pieces, w, l, r, **links):
     units, cols = mom.shape
-    depth = w.shape[1]
-    tile = 176 if units > 512 else units
-    rows = pl.BlockSpec((tile, depth), lambda f, at: (f, 0))
-    mine = pl.BlockSpec((tile, cols), lambda f, at: (f, 0))
-    parts = everyone.shape[0]
-    return launch(
-        update_kernel,
+    half = pieces[0].shape[1]
+    own = cols // half
+    tile = units // 2 if units % 32 == 0 and units > 512 else units
+    tiles = units // tile
+
+    def during(low, high, column):
+        def index(c, f, at):
+            row = jnp.where(c < low, 0, jnp.where(c > high, tiles - 1, f))
+            return row, column(jnp.clip(c, low, high))
+
+        return pl.BlockSpec((tile, half), index)
+
+    momenta = during(0, own - 1, lambda c: c)
+    weights = pl.BlockSpec((tile, half), lambda c, f, at: (f, at[c]))
+    return launch(
+        functools.partial(update_kernel, own),
         "update",
-        (pl.cdiv(units, tile),),
-        [mom, everyone, w, l, r, r],
+        (own + len(pieces), tiles),
+        [mom, l, r, w, *pieces],
         [
-            mine,
-            pl.BlockSpec((parts, tile, cols), lambda f, at: (0, f, 0)),
-            rows,
-            pl.BlockSpec((tile, SPLIT), lambda f, at: (f, 0)),
-            whole(r.shape),
-            pl.BlockSpec((SPLIT, cols), lambda f, at: (0, at[0])),
+            momenta,
+            pl.BlockSpec((tile, SPLIT), lambda c, f, at: (f, 0)),
+            pl.BlockSpec((SPLIT, half), lambda c, f, at: (0, at[c])),
+            weights,
+            *[during(own + s, own + s, lambda c: 0) for s in range(len(pieces))],
         ],
-        [mine, rows],
+        [momenta, weights],
         [shaped(mom.shape, F32), shaped(w.shape, BF16)],
         places=[at],
-        vmem=LARGE,
+        **links,
+    )
+
+
+def last_kernel(at_ref, low_ref, high_ref, w_ref, l_ref, r_ref, _, w_out):
+    half = low_ref.shape[1]
+    approx = dot(l_ref[...], r_ref[...])
+    w_out[:, :half] = updated(w_ref[:, :half], low_ref[...], approx[:, :half])
+    w_out[:, half:] = updated(w_ref[:, half:], high_ref[...], approx[:, half:])
+
+
+def last_call(at, low, high, w, l, r, new, **links):
+    units, half = low.shape
+    tile = 352 if units > 512 else units
+    part = pl.BlockSpec((tile, half), lambda f, at: (f, 0))
+    place = pl.BlockSpec((tile, 2 * half), lambda f, at: (f, at[0]))
+    return launch(
+        last_kernel,
+        "last",
+        (pl.cdiv(units, tile),),
+        [low, high, w, l, r, new],
+        [
+            part,
+            part,
+            place,
+            pl.BlockSpec((tile, SPLIT), lambda f, at: (f, 0)),
+            pl.BlockSpec((SPLIT, 2 * half), lambda f, at: (0, at[0])),
+            HELD,
+        ],
+        [place],
+        [shaped(w.shape, BF16)],
+        places=[at],
+        aliases={6: 0},
         **links,
     )
 
@@ -540,6 +532,10 @@
 def exchange(value, axis, mask):
     size = lax.axis_size(axis)
     return lax.ppermute(value, axis, [(i, i ^ mask) for i in range(size)])
+
+
+def arrived(one, two):
+    return one[:16, :128] + two[:16, :128]
 
 
 def masks(size):
@@ -553,9 +549,11 @@
     rank_mp = lax.axis_index("mp")
     w_gate, w_up, q_t = w_gate.T, w_up.T, q_down.T
     count = shards // 2
-
-    (low,) = cast_call(mom_down)
-    everyone = lax.all_gather(low, "dp")
+    split = max(1, count // 2)
+    early, late = (0, split), (split, count - split)
+
+    low, high, later_low, later_high = cast_call(mom_down)
+    got = {(2, 0): exchange(low, "dp", 2), (1, 1): exchange(high, "dp", 1)}
 
     hid, d_gate, d_up, dyq = hidden_call(
         inputs, out_grads, w_gate, w_up, w_down, q_t, held=[low]
@@ -563,41 +561,68 @@
     (left,) = left_call(q_t, dyq, err_down, hid, replicas)
     lefts = [left] + [exchange(left, "dp", mask) for mask in range(1, replicas)]
 
-    def blocks(side, **links):
-        return blocks_call(rank_mp, side, count, d_gate, d_up, w_gate, w_up, **links)
-
-    other, first = blocks(0, held=[left])
-    total, left, other = right_call(lefts, hid, err_down, out_grads, through=[other])
-
-    others = [exchange(other, "mp", 1)]
-    steps = masks(shards)
-    for index, mask in enumerate(steps):
-        more = exchange(total, "mp", mask)
-        held, through = [], []
-        if index == 0:
-            other, second = blocks(1, held=[total])
-            others.append(exchange(other, "mp", 1))
-            held = [other]
-        elif index == 1:
-            mine = list(add_call(first, others[0], held=[total]))
-            held = [mine[0]]
-        elif index == 2:
-            mine += list(add_call(second, others[1], held=[total]))
-            held = [mine[-1]]
-        if index == len(steps) - 1:
-            through = mine
-        total, *mine_now = sum_call(total, more, held=held, through=through)
+    here, there = rank_mp % 2, 1 - rank_mp % 2
+    others, mine = [], []
+
+    def blocks(turn, order, held=()):
+        parity, slots = (there, here)[turn // 2], (early, late)[turn % 2]
+        if slots[1] == 0:
+            return order
+        add = others[turn % 2] if turn > 1 else None
+        *outs, order = blocks_call(
+            rank_mp, parity, slots, count, d_gate, d_up, w_gate, w_up, add, held=held, through=[order]
+        )
+        (mine if turn > 1 else others).extend(outs)
+        return order
+
+    def send_other(through):
         if through:
-            mine = mine_now
+            others[-1] = exchange(through[0], "mp", 1)
+
+    order = blocks(0, dyq, [left, arrived(got[2, 0], got[1, 1])])
+    total, left, order, later_low, later_high, *fresh = right_call(
+        lefts,
+        hid,
+        err_down,
+        out_grads,
+        through=[order, later_low, later_high, others[0]],
+    )
+    send_other(fresh)
+    got[1, 0] = exchange(later_low, "dp", 1)
+    got[2, 1] = exchange(later_high, "dp", 2)
+
+    rounds = [("mp", mask) for mask in masks(shards)] + [("dp", mask) for mask in masks(replicas)]
+    for index, (axis, mask) in enumerate(rounds):
+        more = exchange(total, axis, mask)
+        if index < 3:
+            order = blocks(index + 1, order, [total])
+        through = others[1:] if index == 0 else []
+        held = [arrived(got[1, 0], got[2, 1])] if index == 2 else []
+        total, order, *fresh = sum_call(total, more, held=held, through=[order, *through])
+        send_other(fresh)
+    l, r, got[2, 0], got[1, 1] = factors_call(
+        total, left, replicas, through=[got[2, 0], got[1, 1]]
+    )
+    got[3, 0] = exchange(got[2, 0], "dp", 1)
+    got[3, 1] = exchange(got[1, 1], "dp", 2)
     landed = [exchange(mine[slot], "mp", 2 * slot) for slot in range(1, count)]
-    for mask in masks(replicas):
-        (total,) = sum_call(total, exchange(total, "dp", mask))
-
-    l, r = factors_call(total, left, replicas)
+
     (next_err,) = error_call(hid, out_grads, err_down, l, r)
-    at = jnp.reshape(rank_dp, (1,)).astype(jnp.int32)
-    next_mom, new = update_call(at, mom_down, everyone, w_down, l, r, held=[next_err])
-    (in_grads,) = join_call([mine[0]] + landed, held=[next_mom])
+    keys = [(1, 0), (1, 1), (2, 0), (2, 1)]
+    at = jnp.stack([2 * (rank_dp ^ mask) + side for mask, side in [(0, 0), (0, 1)] + keys])
+    next_mom, new, order = update_call(
+        at.astype(jnp.int32),
+        mom_down,
+        [got[key] for key in keys],
+        w_down,
+        l,
+        r,
+        held=[next_err],
+        through=[order],
+    )
+    far = jnp.reshape(rank_dp ^ 3, (1,)).astype(jnp.int32)
+    new, order = last_call(far, got[3, 0], got[3, 1], w_down, l, r, new, through=[order])
+    (in_grads,) = join_call([mine[0]] + landed, held=[order])
     return (in_grads, new, next_err, next_mom)
 
 

time: 180 us -> 165 us (0.917)
  between operations: 14.2 us -> 0.91 us
  waiting for transfers between devices: 25.8 us -> 16.4 us
  starting transfers between devices: 14.4 us -> 19 us
  Pallas kernels: 115 us -> 118 us
    ppermute x13 -> x19, waiting for transfers between devices: 25.7 us -> 16.4 us  [exchange(): return lax.ppermute(value, axis, [(i, i ^ mask) for i in range(size)])]
    ppermute x13 -> x19, starting transfers between devices: 14.4 us -> 19 us  [exchange(): return lax.ppermute(value, axis, [(i, i ^ mask) for i in range(size)])]
    pallas_call x17 -> x18, Pallas kernels: 115 us -> 118 us  [launch(): pl.pallas_call(inner, grid_spec=pltpu.PrefetchScalarGridSpec(num_scalar_p...]
    unnamed x21 -> x42, local copies, waits for them, and re-layouts: 7.61 us -> 7.06 us
  transfers between devices with their start and end apart: 14 -> 19, of which waited for: 5 -> 4; matrix products, arithmetic and copies ran while one was open for 0% -> 1% of each run, Pallas kernels for 61% -> 61%
where the time goes in v5:
time: 165 us; the launch traced here: 162 us
  Pallas kernels  118 us (72%)
  starting transfers between devices  19 us (12%)
  waiting for transfers between devices  16.4 us (10%)
  local copies, waits for them, and re-layouts  7.14 us (4%)
    pallas_call x18, Pallas kernels, launch(): pl.pallas_call(inner, grid_spec=pltpu.PrefetchScalarGridSpec(num_scalar_p...  118 us
    ppermute x19, starting transfers between devices, exchange(): return lax.ppermute(value, axis, [(i, i ^ mask) for i in range(size)])  19 us
    ppermute x19, waiting for transfers between devices, exchange(): return lax.ppermute(value, axis, [(i, i ^ mask) for i in range(size)])  16.4 us
    unnamed x42, local copies, waits for them, and re-layouts  7.06 us
  transfers between devices with their start and end apart: 19, of which 4 were waited for; matrix products, arithmetic and copies ran while one was open for 1% of the time, Pallas kernels for 61%

profile of v5, /device:TPU:8, one launch (start us, length us, event | category | flops | bytes accessed | tf_op | source)
XLA Modules:
  0.0 162.1 jit_solution(12486737120878711418)
XLA Ops:
  0.6 4.0 %cast.1 = (bf16[1376,512]{1,0:T(8,128)(2,1)}, bf16[1376,512]{1,0:T(8,128)(2,1)}, bf16[1376,512]{1,0:T(8,128)(2,1)S(1)}, bf16[1376,512]{1,0:T(8,128)(2,1)S(1)}) custom-call(f32[1376,1024]{1,0:T(8,128)} %refs_1_.3), custom_call_target="tpu_custom_call" | custom-call | flops 1 | bytes 1 | tf_op jit(solution)/shard_map/cast/pallas_call | solution.py:35
  4.6 1.1 copy-done.10
  5.8 1.5 collective-permute-start.4
  7.2 1.5 collective-permute-start.3
  8.8 29.6 %hidden.1 = (bf16[1376,512]{1,0:T(8,128)(2,1)S(1)}, bf16[512,1376]{1,0:T(8,128)(2,1)S(1)}, bf16[512,1376]{1,0:T(8,128)(2,1)S(1)}, f32[8,512]{1,0:T(8,128)S(1)}) custom-call(bf16[512,4096]{1,0:T(8,128)(2,1)} %refs_0_.3, bf16[1376,4096]{1,0:T(8,128)(2,1)} %bitcast.15, bf16[1376,4096]{1,0:T(8,128)(2,1)} %bitcast.20, bf16[1376,4096]{1,0:T(8,128)(2,1)} %refs_3_.5, ...), custom_call_target="tpu_custom_call" | custom-call | flops 1 | bytes 1 | tf_op jit(solution)/shard_map/hidden/pallas_call | solution.py:35
  38.4 0.0 copy-start.1
  38.4 8.4 %left.1.refs_5_.refs_0_ = f32[8,1376]{1,0:T(8,128)S(1)} custom-call(f32[8,4096]{1,0:T(8,128)S(1)} %bitcast.14, f32[8,512]{1,0:T(8,128)S(1)} %get-tuple-element.51.refs_1_.refs_7_, bf16[1376,512]{1,0:T(8,128)(2,1)S(1)} %get-tuple-element.52.refs_2_.refs_8_.refs_0_, bf16[1,1376,4096]{2,1,0:T(8,128)(2,1)} %refs_7_.3, bf16[1,1376,4096]{2,1,0:T(8,128)(2,1)} %refs_7_.3, ...), custom_call_target="tpu_custom_call" | custom-call | flops 1 | bytes 1 | tf_op jit(solution)/shard_map/left/pallas_call | solution.py:35
  46.8 0.5 collective-permute-start.2
  47.4 1.5 collective-permute-start.1
  48.9 1.5 collective-permute-start
  50.4 0.1 pad_add_fusion.1.refs_0_
  50.4 0.0 collective-permute-done.4.refs_3_
  50.4 0.7 slice_add_fusion.1.refs_6_
  51.1 6.2 %blocks.4 = (bf16[2,512,512]{2,1,0:T(8,128)(2,1)S(1)}, f32[8,512]{1,0:T(8,128)S(1)}) custom-call(s32[2]{0:T(128)S(1)} %pad_add_fusion.1.refs_0_, bf16[512,1376]{1,0:T(8,128)(2,1)S(1)} %get-tuple-element.49.refs_1_, bf16[512,1376]{1,0:T(8,128)(2,1)S(1)} %get-tuple-element.50.refs_2_, bf16[1376,4096]{1,0:T(8,128)(2,1)} %bitcast.16, ...), custom_call_target="tpu_custom_call", output_to_operand_aliasing={{1}: (7, {})} | custom-call | flops 1 | bytes 1 | tf_op jit(solution)/shard_map/blocks/pallas_call | solution.py:35
  57.4 8.4 %right.1 = (f32[8,4224]{1,0:T(8,128)S(1)}, f32[8,1376]{1,0:T(8,128)S(1)}, f32[8,512]{1,0:T(8,128)S(1)}, bf16[1376,512]{1,0:T(8,128)(2,1)S(1)}, bf16[1376,512]{1,...) custom-call(f32[8,1376]{1,0:T(8,128)S(1)} %left.1.refs_5_.refs_0_, ...), custom_call_target="tpu_custom_call", output_to_operand_aliasing={{2}: (10, {}), {3}: (11, {}), {4}: (12, {}), {5}: (13, {})} | custom-call | flops 1 | bytes 1 | tf_op jit(solution)/shard_map/right/pallas_call | solution.py:35
  65.8 0.6 collective-permute-start.13
  66.4 0.5 collective-permute-start.14
  66.9 0.5 collective-permute-start.5
  67.4 6.0 %blocks.5 = (bf16[2,512,512]{2,1,0:T(8,128)(2,1)S(1)}, f32[8,512]{1,0:T(8,128)S(1)}) custom-call(s32[2]{0:T(128)S(1)} %pad_add_fusion.1.refs_0_, bf16[512,1376]{1,0:T(8,128)(2,1)S(1)} %get-tuple-element.49.refs_1_, bf16[512,1376]{1,0:T(8,128)(2,1)S(1)} %get-tuple-element.50.refs_2_, bf16[1376,4096]{1,0:T(8,128)(2,1)} %bitcast.17, ...), custom_call_target="tpu_custom_call", output_to_operand_aliasing={{1}: (6, {})} | custom-call | flops 1 | bytes 1 | tf_op jit(solution)/shard_map/blocks/pallas_call | solution.py:35
  73.4 0.1 collective-permute-start.8
  73.5 0.1 collective-permute-start.9
  73.6 0.1 pad_add_fusion.refs_0_
  73.7 6.1 %blocks.6 = (bf16[512,512]{1,0:T(8,128)(2,1)S(1)}, bf16[512,512]{1,0:T(8,128)(2,1)S(1)}, f32[8,512]{1,0:T(8,128)S(1)}) custom-call(s32[2]{0:T(128)S(1)} %pad_add_fusion.refs_0_, bf16[512,1376]{1,0:T(8,128)(2,1)S(1)} %get-tuple-element.49.refs_1_, bf16[512,1376]{1,0:T(8,128)(2,1)S(1)} %get-tuple-element.50.refs_2_, ...), custom_call_target="tpu_custom_call", output_to_operand_aliasing={{2}: (7, {})} | custom-call | flops 1 | bytes 1 | tf_op jit(solution)/shard_map/blocks/pallas_call | solution.py:35
  79.8 0.0 copy-start.17
  79.8 3.1 %collective-permute-start.12 = (f32[8,4224]{1,0:T(8,128)S(1)}, f32[8,4224]{1,0:T(8,128)S(1)}, u32[]{:S(2)}, u32[]{:S(2)}) collective-permute-start(f32[8,4224]{1,0:T(8,128)S(1)} %get-tuple-element.69.refs_6_.refs_0_), channel_id=1, source_target_pairs={{0,4},{1,5},{2,6},{3,7},{4,0},{5,1},{6,2},{7,3},{8,12},{9,13},{10,... | collective-permute-start | bytes 405512 | tf_op jit(solution)/shard_map/ppermute | solution.py:534
  82.9 6.1 %blocks.7 = (bf16[512,512]{1,0:T(8,128)(2,1)S(1)}, bf16[512,512]{1,0:T(8,128)(2,1)S(1)}, f32[8,512]{1,0:T(8,128)S(1)}) custom-call(s32[2]{0:T(128)S(1)} %pad_add_fusion.refs_0_, bf16[512,1376]{1,0:T(8,128)(2,1)S(1)} %get-tuple-element.49.refs_1_, bf16[512,1376]{1,0:T(8,128)(2,1)S(1)} %get-tuple-element.50.refs_2_, ...), custom_call_target="tpu_custom_call", output_to_operand_aliasing={{2}: (7, {})} | custom-call | flops 1 | bytes 1 | tf_op jit(solution)/shard_map/blocks/pallas_call | solution.py:35
  89.0 8.1 %collective-permute-done.13.refs_5_ = bf16[1376,512]{1,0:T(8,128)(2,1)S(1)} collective-permute-done((bf16[1376,512]{1,0:T(8,128)(2,1)S(1)}, bf16[1376,512]{1,0:T(8,128)(2,1)S(1)}, u32[]{:S(2)}, u32[]{:S(2)}) %collective-permute-start.13) | collective-permute-done | bytes 1409056 | tf_op jit(solution)/shard_map/ppermute | solution.py:534
  97.1 0.2 collective-permute-done.14.refs_8_
  97.4 1.1 copy-done.8
  98.5 1.6 collective-permute-start.15
  100.1 3.5 %collective-permute-done.15.refs_1_ = f32[8,4224]{1,0:T(8,128)S(1)} collective-permute-done((f32[8,4224]{1,0:T(8,128)S(1)}, f32[8,4224]{1,0:T(8,128)S(1)}, u32[]{:S(2)}, u32[]{:S(2)}) %collective-permute-start.15) | collective-permute-done | bytes 135200 | tf_op jit(solution)/shard_map/ppermute | solution.py:534
  103.6 0.6 collective-permute-start.16
  104.2 4.5 %collective-permute-done.16.refs_1_ = f32[8,4224]{1,0:T(8,128)S(1)} collective-permute-done((f32[8,4224]{1,0:T(8,128)S(1)}, f32[8,4224]{1,0:T(8,128)S(1)}, u32[]{:S(2)}, u32[]{:S(2)}) %collective-permute-start.16) | collective-permute-done | bytes 135200 | tf_op jit(solution)/shard_map/ppermute | solution.py:534
  108.7 0.6 copy-done.15
  109.4 4.3 %factors.1 = (bf16[1376,32]{1,0:T(8,128)(2,1)}, bf16[32,4096]{1,0:T(8,128)(2,1)}, bf16[1376,512]{1,0:T(8,128)(2,1)}, bf16[1376,512]{1,0:T(8,128)(2,1)}) custom-call(f32[8,4224]{1,0:T(8,128)} %copy-done.15, f32[8,1376]{1,0:T(8,128)} %copy-done.16, bf16[1376,512]{1,0:T(8,128)(2,1)} %collective-permute-done.3.refs_2_, ...), custom_call_target="tpu_custom_call", output_to_operand_aliasing={{2}: (2, {}), {3}: (3, {})} | custom-call | flops 1 | bytes 1 | tf_op jit(solution)/shard_map/factors/pallas_call | solution.py:35
  113.7 1.5 collective-permute-start.17
  115.2 0.5 collective-permute-start.18
  115.7 0.4 collective-permute-start.7
  116.1 2.6 %collective-permute-start.10 = (bf16[512,512]{1,0:T(8,128)(2,1)}, bf16[512,512]{1,0:T(8,128)(2,1)}, u32[]{:S(2)}, u32[]{:S(2)}) collective-permute-start(bf16[512,512]{1,0:T(8,128)(2,1)} %copy-done.19), channel_id=1, source_target_pairs={{0,4},{1,5},{2,6},{3,7},{4,0},{5,1},{6,2},{7,3},{8,12},{9,13},{10,... | collective-permute-start | bytes 1572872 | tf_op jit(solution)/shard_map/ppermute | solution.py:534
  118.7 0.4 collective-permute-start.11
  119.2 0.1 stack.54.refs_0_
  119.2 2.2 %copy-done = bf16[512,4096]{1,0:T(8,128)(2,1)S(1)} copy-done((bf16[512,4096]{1,0:T(8,128)(2,1)S(1)}, bf16[512,4096]{1,0:T(8,128)(2,1)}, u32[]{:S(2)}) %copy-start) | copy-done | bytes 4194328
  121.4 1.0 copy-done.4
  122.4 0.9 copy-done.6
  123.4 13.7 %error.1.refs_9_ = bf16[1,1376,4096]{2,1,0:T(8,128)(2,1)} custom-call(bf16[1376,512]{1,0:T(8,128)(2,1)S(1)} %copy-done.3, bf16[512,4096]{1,0:T(8,128)(2,1)S(1)} %copy-done, bf16[1376,32]{1,0:T(8,128)(2,1)S(1)} %copy-done.4, bf16[32,4096]{1,0:T(8,128)(2,1)S(1)} %copy-done.6, bf16[1,1376,4096]{2,1,0:T(8,128)(2,1)} %refs_7_.3, bf16[1,1376,4096]{2,1,0:T(8,128)(2,1)} %refs_7_.3, ...), custom_call_target="tpu_custom_call" | custom-call | flops 1 | bytes 1 | tf_op jit(solution)/shard_map/error/pallas_call | solution.py:35
  137.1 17.4 %update.1 = (f32[1376,1024]{1,0:T(8,128)}, bf16[1376,4096]{1,0:T(8,128)(2,1)}, f32[8,512]{1,0:T(8,128)S(1)}) custom-call(s32[6]{0:T(128)S(1)} %stack.54.refs_0_, f32[1376,1024]{1,0:T(8,128)} %refs_1_.3, bf16[1376,32]{1,0:T(8,128)(2,1)S(1)} %copy-done.5, bf16[32,4096]{1,0:T(8,128)(2,1)S(1)} %copy-done.7, ...), custom_call_target="tpu_custom_call", output_to_operand_aliasing={{2}: (10, {})} | custom-call | flops 1 | bytes 1 | tf_op jit(solution)/shard_map/update/pallas_call | solution.py:35
  154.5 5.1 %last.1 = (bf16[1376,4096]{1,0:T(8,128)(2,1)}, f32[8,512]{1,0:T(8,128)S(1)}) custom-call(s32[1]{0:T(128)} %bitcast.6.refs_0_, bf16[1376,512]{1,0:T(8,128)(2,1)S(1)} %collective-permute-done.17.refs_1_, bf16[1376,512]{1,0:T(8,128)(2,1)} %collective-permute-done.18.refs_2_, bf16[1376,4096]{1,0:T(8,128)(2,1)} %refs_3_.5, ...), custom_call_target="tpu_custom_call", output_to_operand_aliasing={{1}: (7, {}), {0}: (6, {})} | custom-call | flops 1 | bytes 1 | tf_op jit(solution)/shard_map/last/pallas_call | solution.py:35
  159.7 2.4 %join.1 = bf16[512,512]{1,0:T(8,128)(2,1)} custom-call(bf16[512,512]{1,0:T(8,128)(2,1)S(1)} %get-tuple-element.65.refs_0_, bf16[512,512]{1,0:T(8,128)(2,1)} %collective-permute-done.7.refs_1_, bf16[512,512]{1,0:T(8,128)(2,1)} %collective-permute-done.10.refs_2_, bf16[512,512]{1,0:T(8,128)(2,1)} %collective-permute-done.11.refs_3_, ...), custom_call_target="tpu_custom_call" | custom-call | flops 1 | bytes 1 | tf_op jit(solution)/shard_map/join/pallas_call | solution.py:35
  (55 shorter events, 0.2 us)
Async XLA Ops:
  0.6 8.1 %copy-start.14 = (f32[4096,8]{0,1:T(8,128)S(1)}, f32[4096,8]{0,1:T(8,128)}, u32[]{:S(2)}) copy-start(f32[4096,8]{0,1:T(8,128)} %param.15) | copy-start | bytes 393220
  4.6 1.1 copy-start.10
  5.8 32.6 %copy-start.12 = (bf16[1376,512]{1,0:T(8,128)(2,1)}, bf16[1376,512]{1,0:T(8,128)(2,1)S(1)}, u32[]{:S(2)}) copy-start(bf16[1376,512]{1,0:T(8,128)(2,1)S(1)} %get-tuple-element.56.refs_12_) | copy-start | bytes 4227076
  5.8 44.7 %collective-permute-start.4 = (bf16[1376,512]{1,0:T(8,128)(2,1)}, bf16[1376,512]{1,0:T(8,128)(2,1)}, u32[]{:S(2)}, u32[]{:S(2)}) collective-permute-start(bf16[1376,512]{1,0:T(8,128)(2,1)} %get-tuple-element.53), channel_id=1, source_target_pairs={{0,8},{8,0},{16,24},{24,16},{1,9},{9,1},{17,25},{25,17},{2,10},{10... | collective-permute-start | bytes 4227080 | tf_op jit(solution)/shard_map/ppermute | solution.py:534
  7.2 43.2 %collective-permute-start.3 = (bf16[1376,512]{1,0:T(8,128)(2,1)}, bf16[1376,512]{1,0:T(8,128)(2,1)}, u32[]{:S(2)}, u32[]{:S(2)}) collective-permute-start(bf16[1376,512]{1,0:T(8,128)(2,1)} %get-tuple-element.48.refs_6_), channel_id=1, source_target_pairs={{0,16},{8,24},{16,0},{24,8},{1,17},{9,25},{17,1},{25,9},{2,18},{10... | collective-permute-start | bytes 4227080 | tf_op jit(solution)/shard_map/ppermute | solution.py:534
  38.4 8.4 %copy-start.1 = (bf16[1376,512]{1,0:T(8,128)(2,1)}, bf16[1376,512]{1,0:T(8,128)(2,1)S(1)}, u32[]{:S(2)}) copy-start(bf16[1376,512]{1,0:T(8,128)(2,1)S(1)} %get-tuple-element.52.refs_2_.refs_8_.refs_0_) | copy-start | bytes 4227076
  46.8 10.6 %collective-permute-start.2 = (f32[8,1376]{1,0:T(8,128)S(1)}, f32[8,1376]{1,0:T(8,128)S(1)}, u32[]{:S(2)}, u32[]{:S(2)}) collective-permute-start(f32[8,1376]{1,0:T(8,128)S(1)} %left.1.refs_5_.refs_0_), channel_id=1, source_target_pairs={{0,24},{8,16},{16,8},{24,0},{1,25},{9,17},{17,9},{25,1},{2,26},{10... | collective-permute-start | bytes 132104 | tf_op jit(solution)/shard_map/ppermute | solution.py:534
  47.4 10.0 %collective-permute-start.1 = (f32[8,1376]{1,0:T(8,128)S(1)}, f32[8,1376]{1,0:T(8,128)S(1)}, u32[]{:S(2)}, u32[]{:S(2)}) collective-permute-start(f32[8,1376]{1,0:T(8,128)S(1)} %left.1.refs_5_.refs_0_), channel_id=1, source_target_pairs={{0,16},{8,24},{16,0},{24,8},{1,17},{9,25},{17,1},{25,9},{2,18},{10... | collective-permute-start | bytes 132104 | tf_op jit(solution)/shard_map/ppermute | solution.py:534
  48.9 8.5 %collective-permute-start = (f32[8,1376]{1,0:T(8,128)S(1)}, f32[8,1376]{1,0:T(8,128)S(1)}, u32[]{:S(2)}, u32[]{:S(2)}) collective-permute-start(f32[8,1376]{1,0:T(8,128)S(1)} %left.1.refs_5_.refs_0_), channel_id=1, source_target_pairs={{0,8},{8,0},{16,24},{24,16},{1,9},{9,1},{17,25},{25,17},{2,10},{10... | collective-permute-start | bytes 132104 | tf_op jit(solution)/shard_map/ppermute | solution.py:534
  51.1 6.3 %copy-start.2 = (bf16[1376,512]{1,0:T(8,128)(2,1)S(1)}, bf16[1376,512]{1,0:T(8,128)(2,1)}, u32[]{:S(2)}) copy-start(bf16[1376,512]{1,0:T(8,128)(2,1)} %copy-done.1) | copy-start | bytes 4227076
  51.1 6.3 %copy-start.11 = (bf16[1376,512]{1,0:T(8,128)(2,1)S(1)}, bf16[1376,512]{1,0:T(8,128)(2,1)}, u32[]{:S(2)}) copy-start(bf16[1376,512]{1,0:T(8,128)(2,1)} %copy-done.10) | copy-start | bytes 4227076
  51.1 6.3 %copy-start.13 = (bf16[1376,512]{1,0:T(8,128)(2,1)S(1)}, bf16[1376,512]{1,0:T(8,128)(2,1)}, u32[]{:S(2)}) copy-start(bf16[1376,512]{1,0:T(8,128)(2,1)} %copy-done.12) | copy-start | bytes 4227076
  65.8 7.6 %copy-start.16 = (f32[8,1376]{1,0:T(8,128)}, f32[8,1376]{1,0:T(8,128)S(1)}, u32[]{:S(2)}) copy-start(f32[8,1376]{1,0:T(8,128)S(1)} %get-tuple-element.81.refs_1_) | copy-start | bytes 132100
  65.8 31.3 %collective-permute-start.13 = (bf16[1376,512]{1,0:T(8,128)(2,1)S(1)}, bf16[1376,512]{1,0:T(8,128)(2,1)S(1)}, u32[]{:S(2)}, u32[]{:S(2)}) collective-permute-start(bf16[1376,512]{1,0:T(8,128)(2,1)S(1)} %get-tuple-element.73), channel_id=1, source_target_pairs={{0,8},{8,0},{16,24},{24,16},{1,9},{9,1},{17,25},{25,17},{2,10},{10... | collective-permute-start | bytes 4227080 | tf_op jit(solution)/shard_map/ppermute | solution.py:534
  66.4 30.9 %collective-permute-start.14 = (bf16[1376,512]{1,0:T(8,128)(2,1)S(1)}, bf16[1376,512]{1,0:T(8,128)(2,1)S(1)}, u32[]{:S(2)}, u32[]{:S(2)}) collective-permute-start(bf16[1376,512]{1,0:T(8,128)(2,1)S(1)} %get-tuple-element.74), channel_id=1, source_target_pairs={{0,16},{8,24},{16,0},{24,8},{1,17},{9,25},{17,1},{25,9},{2,18},{10... | collective-permute-start | bytes 4227080 | tf_op jit(solution)/shard_map/ppermute | solution.py:534
  66.9 6.5 %collective-permute-start.6 = (f32[8,4224]{1,0:T(8,128)S(1)}, f32[8,4224]{1,0:T(8,128)S(1)}, u32[]{:S(2)}, u32[]{:S(2)}) collective-permute-start(f32[8,4224]{1,0:T(8,128)S(1)} %get-tuple-element.59.refs_5_.refs_0_), channel_id=1, source_target_pairs={{0,1},{1,0},{2,3},{3,2},{4,5},{5,4},{6,7},{7,6},{8,9},{9,8},{10,11... | collective-permute-start | bytes 405512 | tf_op jit(solution)/shard_map/ppermute | solution.py:534
  66.9 6.8 %collective-permute-start.5 = (bf16[2,512,512]{2,1,0:T(8,128)(2,1)S(1)}, bf16[2,512,512]{2,1,0:T(8,128)(2,1)S(1)}, u32[]{:S(2)}, u32[]{:S(2)}) collective-permute-start(bf16[2,512,512]{2,1,0:T(8,128)(2,1)S(1)} %get-tuple-element.58), channel_id=1, source_target_pairs={{0,1},{1,0},{2,3},{3,2},{4,5},{5,4},{6,7},{7,6},{8,9},{9,8},{10,11... | collective-permute-start | bytes 3145736 | tf_op jit(solution)/shard_map/ppermute | solution.py:534
  73.4 9.4 %collective-permute-start.8 = (bf16[2,512,512]{2,1,0:T(8,128)(2,1)S(1)}, bf16[2,512,512]{2,1,0:T(8,128)(2,1)S(1)}, u32[]{:S(2)}, u32[]{:S(2)}) collective-permute-start(bf16[2,512,512]{2,1,0:T(8,128)(2,1)S(1)} %get-tuple-element.67), channel_id=1, source_target_pairs={{0,1},{1,0},{2,3},{3,2},{4,5},{5,4},{6,7},{7,6},{8,9},{9,8},{10,11... | collective-permute-start | bytes 3145736 | tf_op jit(solution)/shard_map/ppermute | solution.py:534
  73.5 6.3 %collective-permute-start.9 = (f32[8,4224]{1,0:T(8,128)S(1)}, f32[8,4224]{1,0:T(8,128)S(1)}, u32[]{:S(2)}, u32[]{:S(2)}) collective-permute-start(f32[8,4224]{1,0:T(8,128)S(1)} %get-tuple-element.63.refs_6_.refs_0_), channel_id=1, source_target_pairs={{0,2},{1,3},{2,0},{3,1},{4,6},{5,7},{6,4},{7,5},{8,10},{9,11},{10,... | collective-permute-start | bytes 405512 | tf_op jit(solution)/shard_map/ppermute | solution.py:534
  79.8 9.2 %copy-start.17 = (bf16[512,512]{1,0:T(8,128)(2,1)}, bf16[512,512]{1,0:T(8,128)(2,1)S(1)}, u32[]{:S(2)}) copy-start(bf16[512,512]{1,0:T(8,128)(2,1)S(1)} %get-tuple-element.66) | copy-start | bytes 1572868
  79.8 18.7 %collective-permute-start.12 = (f32[8,4224]{1,0:T(8,128)S(1)}, f32[8,4224]{1,0:T(8,128)S(1)}, u32[]{:S(2)}, u32[]{:S(2)}) collective-permute-start(f32[8,4224]{1,0:T(8,128)S(1)} %get-tuple-element.69.refs_6_.refs_0_), channel_id=1, source_target_pairs={{0,4},{1,5},{2,6},{3,7},{4,0},{5,1},{6,2},{7,3},{8,12},{9,13},{10,... | collective-permute-start | bytes 405512 | tf_op jit(solution)/shard_map/ppermute | solution.py:534
  89.0 9.5 %copy-start.19 = (bf16[512,512]{1,0:T(8,128)(2,1)}, bf16[512,512]{1,0:T(8,128)(2,1)S(1)}, u32[]{:S(2)}) copy-start(bf16[512,512]{1,0:T(8,128)(2,1)S(1)} %get-tuple-element.71) | copy-start | bytes 1572868
  89.0 20.4 %copy-start.18 = (bf16[512,512]{1,0:T(8,128)(2,1)}, bf16[512,512]{1,0:T(8,128)(2,1)S(1)}, u32[]{:S(2)}) copy-start(bf16[512,512]{1,0:T(8,128)(2,1)S(1)} %get-tuple-element.72) | copy-start | bytes 1572868
  97.4 12.0 %copy-start.20 = (bf16[1376,512]{1,0:T(8,128)(2,1)}, bf16[1376,512]{1,0:T(8,128)(2,1)S(1)}, u32[]{:S(2)}) copy-start(bf16[1376,512]{1,0:T(8,128)(2,1)S(1)} %collective-permute-done.14.refs_8_) | copy-start | bytes 4227076
  97.4 1.1 copy-start.8
  98.5 5.1 %collective-permute-start.15 = (f32[8,4224]{1,0:T(8,128)S(1)}, f32[8,4224]{1,0:T(8,128)S(1)}, u32[]{:S(2)}, u32[]{:S(2)}) collective-permute-start(f32[8,4224]{1,0:T(8,128)S(1)} %get-tuple-element.76.refs_0_), channel_id=1, source_target_pairs={{0,8},{8,0},{16,24},{24,16},{1,9},{9,1},{17,25},{25,17},{2,10},{10... | collective-permute-start | bytes 405512 | tf_op jit(solution)/shard_map/ppermute | solution.py:534
  103.6 5.1 %collective-permute-start.16 = (f32[8,4224]{1,0:T(8,128)S(1)}, f32[8,4224]{1,0:T(8,128)S(1)}, u32[]{:S(2)}, u32[]{:S(2)}) collective-permute-start(f32[8,4224]{1,0:T(8,128)S(1)} %get-tuple-element.78.refs_0_), channel_id=1, source_target_pairs={{0,16},{8,24},{16,0},{24,8},{1,17},{9,25},{17,1},{25,9},{2,18},{10... | collective-permute-start | bytes 405512 | tf_op jit(solution)/shard_map/ppermute | solution.py:534
  108.7 0.6 copy-start.15
  109.4 9.9 %copy-start.3 = (bf16[1376,512]{1,0:T(8,128)(2,1)S(1)}, bf16[1376,512]{1,0:T(8,128)(2,1)}, u32[]{:S(2)}) copy-start(bf16[1376,512]{1,0:T(8,128)(2,1)} %copy-done.1) | copy-start | bytes 4227076
  113.7 40.9 %collective-permute-start.17 = (bf16[1376,512]{1,0:T(8,128)(2,1)}, bf16[1376,512]{1,0:T(8,128)(2,1)S(1)}, u32[]{:S(2)}, u32[]{:S(2)}) collective-permute-start(bf16[1376,512]{1,0:T(8,128)(2,1)} %get-tuple-element.82.refs_7_), channel_id=1, source_target_pairs={{0,8},{8,0},{16,24},{24,16},{1,9},{9,1},{17,25},{25,17},{2,10},{10... | collective-permute-start | bytes 4227080 | tf_op jit(solution)/shard_map/ppermute | solution.py:534
  115.2 39.4 %collective-permute-start.18 = (bf16[1376,512]{1,0:T(8,128)(2,1)}, bf16[1376,512]{1,0:T(8,128)(2,1)}, u32[]{:S(2)}, u32[]{:S(2)}) collective-permute-start(bf16[1376,512]{1,0:T(8,128)(2,1)} %get-tuple-element.83.refs_6_), channel_id=1, source_target_pairs={{0,16},{8,24},{16,0},{24,8},{1,17},{9,25},{17,1},{25,9},{2,18},{10... | collective-permute-start | bytes 4227080 | tf_op jit(solution)/shard_map/ppermute | solution.py:534
  115.7 44.0 %collective-permute-start.7 = (bf16[512,512]{1,0:T(8,128)(2,1)}, bf16[512,512]{1,0:T(8,128)(2,1)}, u32[]{:S(2)}, u32[]{:S(2)}) collective-permute-start(bf16[512,512]{1,0:T(8,128)(2,1)} %copy-done.17), channel_id=1, source_target_pairs={{0,2},{1,3},{2,0},{3,1},{4,6},{5,7},{6,4},{7,5},{8,10},{9,11},{10,... | collective-permute-start | bytes 1572872 | tf_op jit(solution)/shard_map/ppermute | solution.py:534
  116.1 43.6 %collective-permute-start.10 = (bf16[512,512]{1,0:T(8,128)(2,1)}, bf16[512,512]{1,0:T(8,128)(2,1)}, u32[]{:S(2)}, u32[]{:S(2)}) collective-permute-start(bf16[512,512]{1,0:T(8,128)(2,1)} %copy-done.19), channel_id=1, source_target_pairs={{0,4},{1,5},{2,6},{3,7},{4,0},{5,1},{6,2},{7,3},{8,12},{9,13},{10,... | collective-permute-start | bytes 1572872 | tf_op jit(solution)/shard_map/ppermute | solution.py:534
  118.7 41.0 %collective-permute-start.11 = (bf16[512,512]{1,0:T(8,128)(2,1)}, bf16[512,512]{1,0:T(8,128)(2,1)}, u32[]{:S(2)}, u32[]{:S(2)}) collective-permute-start(bf16[512,512]{1,0:T(8,128)(2,1)} %copy-done.18), channel_id=1, source_target_pairs={{0,6},{1,7},{2,4},{3,5},{4,2},{5,3},{6,0},{7,1},{8,14},{9,15},{10,... | collective-permute-start | bytes 1572872 | tf_op jit(solution)/shard_map/ppermute | solution.py:534
  119.2 2.2 %copy-start = (bf16[512,4096]{1,0:T(8,128)(2,1)S(1)}, bf16[512,4096]{1,0:T(8,128)(2,1)}, u32[]{:S(2)}) copy-start(bf16[512,4096]{1,0:T(8,128)(2,1)} %refs_1_.2) | copy-start | bytes 12582916
  121.4 1.0 copy-start.4
  122.4 0.9 copy-start.6
  123.4 13.8 %copy-start.5 = (bf16[1376,32]{1,0:T(8,128)(2,1)S(1)}, bf16[1376,32]{1,0:T(8,128)(2,1)}, u32[]{:S(2)}) copy-start(bf16[1376,32]{1,0:T(8,128)(2,1)} %get-tuple-element.84.refs_2_.refs_4_) | copy-start | bytes 264196
  123.4 13.8 %copy-start.7 = (bf16[32,4096]{1,0:T(8,128)(2,1)S(1)}, bf16[32,4096]{1,0:T(8,128)(2,1)}, u32[]{:S(2)}) copy-start(bf16[32,4096]{1,0:T(8,128)(2,1)} %get-tuple-element.85.refs_3_.refs_5_) | copy-start | bytes 786436
  123.4 13.8 %copy-start.9 = (bf16[1376,512]{1,0:T(8,128)(2,1)S(1)}, bf16[1376,512]{1,0:T(8,128)(2,1)}, u32[]{:S(2)}) copy-start(bf16[1376,512]{1,0:T(8,128)(2,1)} %copy-done.8) | copy-start | bytes 4227076

commit v6 on v5

--- a/solution.py
+++ b/solution.py
@@ -18,6 +18,7 @@
 LARGE = 62 * 2**20
 ONCE = pl.Buffered(1)
 STREAMS = 4
+MEDIUM = 48 * 2**20
 HELD = pl.BlockSpec(memory_space=pl.ANY)
 
 
@@ -112,95 +113,93 @@
         [pl.BlockSpec((tile, cols), lambda f: (f, 0))],
         [part] * 4,
         [shaped((units, cols // 2), BF16)] * 4,
+        vmem=MEDIUM,
         **links,
     )
 
 
 def hidden_kernel(
-    x_ref, wg_ref, wu_ref, wd_ref, q_ref, dy_any, hid_ref, dg_ref, du_ref, dyq_ref, dy_ref, sem
+    replicas,
+    x_ref, wg_ref, wu_ref, wd_ref, err_ref, q_ref, dy_any,
+    hid_ref, dg_ref, du_ref, left_ref, dyq_ref,
+    dy_ref, q_terms, dyq_terms, sem,
 ):
     fetch = pltpu.make_async_copy(dy_any, dy_ref, sem)
 
     @pl.when(pl.program_id(0) == 0)
     def _():
         fetch.start()
+        q_terms[...] = spread(q_ref[...])
 
     gate = dot_nt(x_ref[...], wg_ref[...])
     up = dot_nt(x_ref[...], wu_ref[...])
+    both = dot_nt(err_ref[0], q_terms[...])
 
     @pl.when(pl.program_id(0) == 0)
     def _():
         fetch.wait()
-        dyq_ref[...] = gather_terms(dot_nt(dy_ref[...], spread(q_ref[...])).T)
+        dyq = gather_terms(dot_nt(dy_ref[...], q_terms[...]).T)
+        dyq_ref[...] = dyq
+        dyq_terms[...] = spread(dyq)
 
     dh = dot_nt(dy_ref[...], wd_ref[...])
     sig = jax.nn.sigmoid(gate)
     silu = gate * sig
-    hid_ref[...] = (silu * up).T.astype(BF16)
+    hid = (silu * up).T.astype(BF16)
+    hid_ref[...] = hid
     dg_ref[...] = (dh * up * sig * (1.0 + gate * (1.0 - sig))).astype(BF16)
     du_ref[...] = (dh * silu).astype(BF16)
-
-
-def hidden_call(x, dy, wg, wu, wd, q_t, **links):
+    both += dot_nt(hid, dyq_terms[...])
+    left_ref[...] = gather_terms(both.T) / replicas
+
+
+def hidden_call(x, dy, wg, wu, wd, err, q_t, replicas, **links):
     tok, depth = x.shape
     units = wg.shape[0]
     tile = unit_tile(units)
     rows = pl.BlockSpec((tile, depth), lambda f: (f, 0))
     part = pl.BlockSpec((tok, tile), lambda f: (0, f))
     return launch(
-        hidden_kernel,
+        functools.partial(hidden_kernel, replicas),
         "hidden",
         (pl.cdiv(units, tile),),
-        [x, wg, wu, wd, q_t, dy],
-        [whole((tok, depth)), rows, rows, rows, whole(q_t.shape), HELD],
-        [pl.BlockSpec((tile, tok), lambda f: (f, 0)), part, part, whole((R, tok))],
+        [x, wg, wu, wd, err, q_t, dy],
+        [
+            whole((tok, depth)),
+            rows,
+            rows,
+            rows,
+            pl.BlockSpec((1, tile, depth), lambda f: (0, f, 0)),
+            whole(q_t.shape),
+            HELD,
+        ],
+        [
+            pl.BlockSpec((tile, tok), lambda f: (f, 0)),
+            part,
+            part,
+            pl.BlockSpec((R, tile), lambda f: (0, f)),
+            whole((R, tok)),
+        ],
         [
             shaped((units, tok), BF16),
             shaped((tok, units), BF16),
             shaped((tok, units), BF16),
+            shaped((R, units), F32),
             shaped((R, tok), F32),
         ],
-        scratch=[pltpu.VMEM((tok, depth), BF16), pltpu.SemaphoreType.DMA(())],
-        **links,
-    )
-
-
-def left_kernel(replicas, q_ref, dyq_ref, hid_ref, *refs):
-    errs, (out_ref, q_terms, dyq_terms) = refs[:-3], refs[-3:]
-    width = errs[0].shape[2]
-
-    @pl.when(pl.program_id(0) == 0)
-    def _():
-        q_terms[...] = spread(q_ref[...])
-        dyq_terms[...] = spread(dyq_ref[...])
-
-    both = dot_nt(hid_ref[...], dyq_terms[...])
-    for at, err_ref in enumerate(errs):
-        both += dot_nt(err_ref[0], q_terms[:, at * width : (at + 1) * width])
-    out_ref[...] = gather_terms(both.T) / replicas
+        scratch=[
+            pltpu.VMEM((tok, depth), BF16),
+            pltpu.VMEM((SPLIT, depth), BF16),
+            pltpu.VMEM((SPLIT, tok), BF16),
+            pltpu.SemaphoreType.DMA(()),
+        ],
+        **links,
+    )
 
 
 def error_streams(tile, depth):
     shape = (1, tile, depth // STREAMS)
     return [pl.BlockSpec(shape, lambda f, c=c: (0, f, c)) for c in range(STREAMS)]
-
-
-def left_call(q_t, dyq, err, hid, replicas, **links):
-    units, tok = hid.shape
-    depth = q_t.shape[1]
-    tile = unit_tile(units)
-    return launch(
-        functools.partial(left_kernel, replicas),
-        "left",
-        (pl.cdiv(units, tile),),
-        [q_t, dyq, hid] + [err] * STREAMS,
-        [whole(q_t.shape), whole(dyq.shape), pl.BlockSpec((tile, tok), lambda f: (f, 0))]
-        + error_streams(tile, depth),
-        [pl.BlockSpec((R, tile), lambda f: (0, f))],
-        [shaped((R, units), F32)],
-        scratch=[pltpu.VMEM((SPLIT, depth), BF16), pltpu.VMEM((SPLIT, tok), BF16)],
-        **links,
-    )
 
 
 def columns(ref, step, tile):
@@ -287,6 +286,7 @@
             pltpu.VMEM((SPLIT, tok), BF16),
             pltpu.VMEM((SPLIT, depth), F32),
         ],
+        vmem=MEDIUM,
         **links,
     )
 
@@ -404,7 +404,7 @@
         out_specs = [whole((tok, width))] * steps
         out_shape = [shaped((tok, width), BF16)] * steps
     return launch(
-        kernel, "blocks", (steps,), args, in_specs, out_specs, out_shape, places=[where], **links
+        kernel, "blocks", (steps,), args, in_specs, out_specs, out_shape, places=[where], vmem=MEDIUM, **links
     )
 
 
@@ -435,6 +435,7 @@
         ],
         [pl.BlockSpec((1, tile, depth), lambda f: (0, f, 0))],
         [shaped(err.shape, BF16)],
+        vmem=LARGE,
         **links,
     )
 
@@ -492,6 +493,7 @@
         [momenta, weights],
         [shaped(mom.shape, F32), shaped(w.shape, BF16)],
         places=[at],
+        vmem=LARGE,
         **links,
     )
 
@@ -525,6 +527,7 @@
         [shaped(w.shape, BF16)],
         places=[at],
         aliases={6: 0},
+        vmem=LARGE,
         **links,
     )
 
@@ -550,62 +553,78 @@
     w_gate, w_up, q_t = w_gate.T, w_up.T, q_down.T
     count = shards // 2
     split = max(1, count // 2)
-    early, late = (0, split), (split, count - split)
+    turns = [(split, count - split), (0, split)] if count > split else [(0, split)]
 
     low, high, later_low, later_high = cast_call(mom_down)
     got = {(2, 0): exchange(low, "dp", 2), (1, 1): exchange(high, "dp", 1)}
 
-    hid, d_gate, d_up, dyq = hidden_call(
-        inputs, out_grads, w_gate, w_up, w_down, q_t, held=[low]
-    )
-    (left,) = left_call(q_t, dyq, err_down, hid, replicas)
+    hid, d_gate, d_up, left, dyq = hidden_call(
+        inputs, out_grads, w_gate, w_up, w_down, err_down, q_t, replicas, held=[low]
+    )
     lefts = [left] + [exchange(left, "dp", mask) for mask in range(1, replicas)]
 
     here, there = rank_mp % 2, 1 - rank_mp % 2
-    others, mine = [], []
-
-    def blocks(turn, order, held=()):
-        parity, slots = (there, here)[turn // 2], (early, late)[turn % 2]
-        if slots[1] == 0:
-            return order
-        add = others[turn % 2] if turn > 1 else None
-        *outs, order = blocks_call(
-            rank_mp, parity, slots, count, d_gate, d_up, w_gate, w_up, add, held=held, through=[order]
+    others, mine = [], [None] * count
+
+    def blocks(turn, order, held=(), through=()):
+        side, part = divmod(turn, len(turns))
+        parity, slots = (there, here)[side], turns[part]
+        add = others[part] if side else None
+        size = slots[1] if side else 1
+        outs = blocks_call(
+            rank_mp,
+            parity,
+            slots,
+            count,
+            d_gate,
+            d_up,
+            w_gate,
+            w_up,
+            add,
+            held=held,
+            through=[order, *through],
         )
-        (mine if turn > 1 else others).extend(outs)
-        return order
-
-    def send_other(through):
-        if through:
-            others[-1] = exchange(through[0], "mp", 1)
-
-    order = blocks(0, dyq, [left, arrived(got[2, 0], got[1, 1])])
-    total, left, order, later_low, later_high, *fresh = right_call(
+        if side:
+            mine[slots[0] : slots[0] + size] = outs[:size]
+        else:
+            others.append(outs[0])
+        return outs[size:]
+
+    total, left, order, later_low, later_high = right_call(
         lefts,
         hid,
         err_down,
         out_grads,
-        through=[order, later_low, later_high, others[0]],
-    )
-    send_other(fresh)
+        held=[arrived(got[2, 0], got[1, 1])],
+        through=[dyq, later_low, later_high],
+    )
     got[1, 0] = exchange(later_low, "dp", 1)
     got[2, 1] = exchange(later_high, "dp", 2)
 
     rounds = [("mp", mask) for mask in masks(shards)] + [("dp", mask) for mask in masks(replicas)]
     for index, (axis, mask) in enumerate(rounds):
         more = exchange(total, axis, mask)
-        if index < 3:
-            order = blocks(index + 1, order, [total])
-        through = others[1:] if index == 0 else []
-        held = [arrived(got[1, 0], got[2, 1])] if index == 2 else []
+        if index < 2 * len(turns):
+            (order,) = blocks(index, order, [total])
+        relay = index == 2 and count == 4
+        through = others[index:] if index < len(turns) else [mine[3]] if relay else []
+        held = [arrived(got[1, 0], got[2, 1])] if index == 3 else []
         total, order, *fresh = sum_call(total, more, held=held, through=[order, *through])
-        send_other(fresh)
+        if relay:
+            relayed = exchange(fresh[0], "mp", 2)
+        elif fresh:
+            others[index] = exchange(fresh[0], "mp", 1)
+    if count == 4:
+        relayed, order = join_call([mine[2], relayed], held=[total], through=[order])
     l, r, got[2, 0], got[1, 1] = factors_call(
-        total, left, replicas, through=[got[2, 0], got[1, 1]]
+        total, left, replicas, held=[order], through=[got[2, 0], got[1, 1]]
     )
     got[3, 0] = exchange(got[2, 0], "dp", 1)
     got[3, 1] = exchange(got[1, 1], "dp", 2)
-    landed = [exchange(mine[slot], "mp", 2 * slot) for slot in range(1, count)]
+    if count == 4:
+        landed = [exchange(relayed, "mp", 4), exchange(mine[1], "mp", 2)]
+    else:
+        landed = [exchange(mine[slot], "mp", 2 * slot) for slot in range(1, count)]
 
     (next_err,) = error_call(hid, out_grads, err_down, l, r)
     keys = [(1, 0), (1, 1), (2, 0), (2, 1)]

time: 165 us -> 152 us (0.921)
  waiting for transfers between devices: 16.4 us -> 6.2 us
  local copies, waits for them, and re-layouts: 7.14 us -> 2.6 us
  starting transfers between devices: 19 us -> 23 us
    ppermute x19, waiting for transfers between devices: 16.4 us -> 6.2 us  [exchange(): return lax.ppermute(value, axis, [(i, i ^ mask) for i in range(size)])]
    unnamed x42 -> x18, local copies, waits for them, and re-layouts: 7.06 us -> 1.94 us
    ppermute x19, starting transfers between devices: 19 us -> 23 us  [exchange(): return lax.ppermute(value, axis, [(i, i ^ mask) for i in range(size)])]
  transfers between devices with their start and end apart: 19 -> 19, of which waited for: 4 -> 4; matrix products, arithmetic and copies ran while one was open for 1% -> 1% of each run, Pallas kernels for 61% -> 66%
where the time goes in v6:
time: 152 us; the launch traced here: 150 us
  Pallas kernels  117 us (77%)
  starting transfers between devices  23 us (15%)
  waiting for transfers between devices  6.2 us (4%)
  local copies, waits for them, and re-layouts  2.6 us (2%)
    pallas_call x18, Pallas kernels, launch(): pl.pallas_call(inner, grid_spec=pltpu.PrefetchScalarGridSpec(num_scalar_p...  117 us
    ppermute x19, starting transfers between devices, exchange(): return lax.ppermute(value, axis, [(i, i ^ mask) for i in range(size)])  23 us
    ppermute x19, waiting for transfers between devices, exchange(): return lax.ppermute(value, axis, [(i, i ^ mask) for i in range(size)])  6.2 us
  transfers between devices with their start and end apart: 19, of which 4 were waited for; matrix products, arithmetic and copies ran while one was open for 1% of the time, Pallas kernels for 66%

profile of v6, /device:TPU:8, one launch (start us, length us, event | category | flops | bytes accessed | tf_op | source)
XLA Modules:
  0.0 150.0 jit_solution(6365970230667079860)
XLA Ops:
  0.6 4.0 %cast.1 = (bf16[1376,512]{1,0:T(8,128)(2,1)S(1)}, bf16[1376,512]{1,0:T(8,128)(2,1)S(1)}, bf16[1376,512]{1,0:T(8,128)(2,1)}, bf16[1376,512]{1,0:T(8,128)(2,1)}) custom-call(f32[1376,1024]{1,0:T(8,128)} %refs_1_.3), custom_call_target="tpu_custom_call" | custom-call | flops 1 | bytes 1 | tf_op jit(solution)/shard_map/cast/pallas_call | solution.py:36
  4.6 1.5 collective-permute-start.4
  6.1 1.5 %collective-permute-start.3 = (bf16[1376,512]{1,0:T(8,128)(2,1)S(1)}, bf16[1376,512]{1,0:T(8,128)(2,1)S(1)}, u32[]{:S(2)}, u32[]{:S(2)}) collective-permute-start(bf16[1376,512]{1,0:T(8,128)(2,1)S(1)} %get-tuple-element.52.refs_7_), channel_id=1, source_target_pairs={{0,16},{8,24},{16,0},{24,8},{1,17},{9,25},{17,1},{25,9},{2,18},{10... | collective-permute-start | bytes 4227080 | tf_op jit(solution)/shard_map/ppermute | solution.py:537
  7.6 35.1 %hidden.1 = (bf16[1376,512]{1,0:T(8,128)(2,1)S(1)}, bf16[512,1376]{1,0:T(8,128)(2,1)S(1)}, bf16[512,1376]{1,0:T(8,128)(2,1)S(1)}, f32[8,1376]{1,0:T(8,128)S(1)}, f32[8,512]{1,0:T(8,128)S(1)}) custom-call(bf16[512,4096]{1,0:T(8,128)(2,1)} %refs_0_.3, bf16[1376,4096]{1,0:T(8,128)(2,1)} %bitcast.14, bf16[1376,4096]{1,0:T(8,128)(2,1)} %bitcast.19, ...), custom_call_target="tpu_custom_call" | custom-call | flops 1 | bytes 1 | tf_op jit(solution)/shard_map/hidden/pallas_call | solution.py:36
  42.8 0.6 collective-permute-start.2
  43.3 1.5 %collective-permute-start.1 = (f32[8,1376]{1,0:T(8,128)S(1)}, f32[8,1376]{1,0:T(8,128)S(1)}, u32[]{:S(2)}, u32[]{:S(2)}) collective-permute-start(f32[8,1376]{1,0:T(8,128)S(1)} %get-tuple-element.55.refs_0_), channel_id=1, source_target_pairs={{0,16},{8,24},{16,0},{24,8},{1,17},{9,25},{17,1},{25,9},{2,18},{10... | collective-permute-start | bytes 132104 | tf_op jit(solution)/shard_map/ppermute | solution.py:537
  44.8 1.5 collective-permute-start
  46.3 0.0 collective-permute-done.4.refs_4_
  46.3 1.5 collective-permute-done.2.refs_3_
  47.8 0.0 collective-permute-done.1.refs_2_
  47.8 1.0 collective-permute-done.refs_1_
  48.9 8.3 %right.1 = (f32[8,4224]{1,0:T(8,128)S(1)}, f32[8,1376]{1,0:T(8,128)S(1)}, f32[8,512]{1,0:T(8,128)S(1)}, bf16[1376,512]{1,0:T(8,128)(2,1)}, bf16[1376,512]{1,0:T(8,128)(2,1)}) custom-call(f32[8,1376]{1,0:T(8,128)S(1)} %get-tuple-element.55.refs_0_, ...), custom_call_target="tpu_custom_call", output_to_operand_aliasing={{2}: (11, {}), {3}: (12, {}), {4}: (13, {})} | custom-call | flops 1 | bytes 1 | tf_op jit(solution)/shard_map/right/pallas_call | solution.py:36
  57.2 0.0 copy-start.5
  57.2 0.6 copy-done.5
  57.8 1.5 collective-permute-start.12
  59.3 0.5 collective-permute-start.13
  59.8 0.0 collective-permute-start.5
  59.8 0.1 pad_add_fusion.1.refs_0_
  59.9 6.0 %blocks.4 = (bf16[2,512,512]{2,1,0:T(8,128)(2,1)S(1)}, f32[8,512]{1,0:T(8,128)S(1)}) custom-call(s32[2]{0:T(128)S(1)} %pad_add_fusion.1.refs_0_, bf16[512,1376]{1,0:T(8,128)(2,1)S(1)} %get-tuple-element.53.refs_1_, bf16[512,1376]{1,0:T(8,128)(2,1)S(1)} %get-tuple-element.54.refs_2_, bf16[1376,4096]{1,0:T(8,128)(2,1)} %bitcast.15, ...), custom_call_target="tpu_custom_call", output_to_operand_aliasing={{1}: (6, {})} | custom-call | flops 1 | bytes 1 | tf_op jit(solution)/shard_map/blocks/pallas_call | solution.py:36
  65.9 0.6 collective-permute-start.9
  66.5 0.4 collective-permute-start.6
  66.9 6.0 %blocks.5 = (bf16[2,512,512]{2,1,0:T(8,128)(2,1)S(1)}, f32[8,512]{1,0:T(8,128)S(1)}) custom-call(s32[2]{0:T(128)S(1)} %pad_add_fusion.1.refs_0_, bf16[512,1376]{1,0:T(8,128)(2,1)S(1)} %get-tuple-element.53.refs_1_, bf16[512,1376]{1,0:T(8,128)(2,1)S(1)} %get-tuple-element.54.refs_2_, bf16[1376,4096]{1,0:T(8,128)(2,1)} %bitcast.16, ...), custom_call_target="tpu_custom_call", output_to_operand_aliasing={{1}: (6, {})} | custom-call | flops 1 | bytes 1 | tf_op jit(solution)/shard_map/blocks/pallas_call | solution.py:36
  72.9 0.0 collective-permute-done.6.refs_1_
  72.9 0.1 collective-permute-start.7
  73.0 2.7 %collective-permute-start.8 = (f32[8,4224]{1,0:T(8,128)S(1)}, f32[8,4224]{1,0:T(8,128)S(1)}, u32[]{:S(2)}, u32[]{:S(2)}) collective-permute-start(f32[8,4224]{1,0:T(8,128)S(1)} %get-tuple-element.70.refs_6_.refs_0_), channel_id=1, source_target_pairs={{0,4},{1,5},{2,6},{3,7},{4,0},{5,1},{6,2},{7,3},{8,12},{9,13},{10,... | collective-permute-start | bytes 405512 | tf_op jit(solution)/shard_map/ppermute | solution.py:537
  75.7 0.1 pad_add_fusion.refs_0_
  75.7 6.1 %blocks.6 = (bf16[512,512]{1,0:T(8,128)(2,1)S(1)}, bf16[512,512]{1,0:T(8,128)(2,1)S(1)}, f32[8,512]{1,0:T(8,128)S(1)}) custom-call(s32[2]{0:T(128)S(1)} %pad_add_fusion.refs_0_, bf16[512,1376]{1,0:T(8,128)(2,1)S(1)} %get-tuple-element.53.refs_1_, bf16[512,1376]{1,0:T(8,128)(2,1)S(1)} %get-tuple-element.54.refs_2_, ...), custom_call_target="tpu_custom_call", output_to_operand_aliasing={{2}: (7, {})} | custom-call | flops 1 | bytes 1 | tf_op jit(solution)/shard_map/blocks/pallas_call | solution.py:36
  81.8 0.2 collective-permute-done.8.refs_1_
  82.0 2.3 %collective-permute-start.10 = (bf16[512,512]{1,0:T(8,128)(2,1)S(1)}, bf16[512,512]{1,0:T(8,128)(2,1)S(1)}, u32[]{:S(2)}, u32[]{:S(2)}) collective-permute-start(bf16[512,512]{1,0:T(8,128)(2,1)S(1)} %get-tuple-element.79), channel_id=1, source_target_pairs={{0,2},{1,3},{2,0},{3,1},{4,6},{5,7},{6,4},{7,5},{8,10},{9,11},{10,... | collective-permute-start | bytes 1572872 | tf_op jit(solution)/shard_map/ppermute | solution.py:537
  84.4 0.5 collective-permute-start.11
  84.8 6.8 %blocks.7 = (bf16[512,512]{1,0:T(8,128)(2,1)S(1)}, bf16[512,512]{1,0:T(8,128)(2,1)}, f32[8,512]{1,0:T(8,128)S(1)}) custom-call(s32[2]{0:T(128)S(1)} %pad_add_fusion.refs_0_, bf16[512,1376]{1,0:T(8,128)(2,1)S(1)} %get-tuple-element.53.refs_1_, bf16[512,1376]{1,0:T(8,128)(2,1)S(1)} %get-tuple-element.54.refs_2_, ...), custom_call_target="tpu_custom_call", output_to_operand_aliasing={{2}: (7, {})} | custom-call | flops 1 | bytes 1 | tf_op jit(solution)/shard_map/blocks/pallas_call | solution.py:36
  91.7 0.7 slice_add_fusion.refs_2_
  92.4 1.6 %collective-permute-start.14 = (f32[8,4224]{1,0:T(8,128)S(1)}, f32[8,4224]{1,0:T(8,128)S(1)}, u32[]{:S(2)}, u32[]{:S(2)}) collective-permute-start(f32[8,4224]{1,0:T(8,128)S(1)} %get-tuple-element.83.refs_0_), channel_id=1, source_target_pairs={{0,16},{8,24},{16,0},{24,8},{1,17},{9,25},{17,1},{25,9},{2,18},{10... | collective-permute-start | bytes 405512 | tf_op jit(solution)/shard_map/ppermute | solution.py:537
  94.0 3.4 %collective-permute-done.14.refs_1_ = f32[8,4224]{1,0:T(8,128)S(1)} collective-permute-done((f32[8,4224]{1,0:T(8,128)S(1)}, f32[8,4224]{1,0:T(8,128)S(1)}, u32[]{:S(2)}, u32[]{:S(2)}) %collective-permute-start.14) | collective-permute-done | bytes 135200 | tf_op jit(solution)/shard_map/ppermute | solution.py:537
  97.5 0.0 copy-start.3
  97.5 0.1 join.2
  97.7 0.6 copy-done.1
  98.2 4.3 %factors.1 = (bf16[1376,32]{1,0:T(8,128)(2,1)}, bf16[32,4096]{1,0:T(8,128)(2,1)}, bf16[1376,512]{1,0:T(8,128)(2,1)}, bf16[1376,512]{1,0:T(8,128)(2,1)}) custom-call(f32[8,4224]{1,0:T(8,128)} %copy-done.3, f32[8,1376]{1,0:T(8,128)} %copy-done.5, f32[8,512]{1,0:T(8,128)} %copy-done.1, ...), custom_call_target="tpu_custom_call", output_to_operand_aliasing={{2}: (3, {}), {3}: (4, {})} | custom-call | flops 1 | bytes 1 | tf_op jit(solution)/shard_map/factors/pallas_call | solution.py:36
  102.6 1.6 %collective-permute-start.17 = (bf16[1376,512]{1,0:T(8,128)(2,1)}, bf16[1376,512]{1,0:T(8,128)(2,1)}, u32[]{:S(2)}, u32[]{:S(2)}) collective-permute-start(bf16[1376,512]{1,0:T(8,128)(2,1)} %get-tuple-element.91.refs_7_), channel_id=1, source_target_pairs={{0,8},{8,0},{16,24},{24,16},{1,9},{9,1},{17,25},{25,17},{2,10},{10... | collective-permute-start | bytes 4227080 | tf_op jit(solution)/shard_map/ppermute | solution.py:537
  104.1 1.5 %collective-permute-start.18 = (bf16[1376,512]{1,0:T(8,128)(2,1)}, bf16[1376,512]{1,0:T(8,128)(2,1)}, u32[]{:S(2)}, u32[]{:S(2)}) collective-permute-start(bf16[1376,512]{1,0:T(8,128)(2,1)} %get-tuple-element.92.refs_6_), channel_id=1, source_target_pairs={{0,16},{8,24},{16,0},{24,8},{1,17},{9,25},{17,1},{25,9},{2,18},{10... | collective-permute-start | bytes 4227080 | tf_op jit(solution)/shard_map/ppermute | solution.py:537
  105.6 0.3 collective-permute-start.16
  106.0 2.8 %collective-permute-start.15 = (bf16[512,512]{1,0:T(8,128)(2,1)}, bf16[512,512]{1,0:T(8,128)(2,1)S(1)}, u32[]{:S(2)}, u32[]{:S(2)}) collective-permute-start(bf16[512,512]{1,0:T(8,128)(2,1)} %copy-done.6), channel_id=1, source_target_pairs={{0,4},{1,5},{2,6},{3,7},{4,0},{5,1},{6,2},{7,3},{8,12},{9,13},{10,... | collective-permute-start | bytes 1572872 | tf_op jit(solution)/shard_map/ppermute | solution.py:537
  108.8 0.7 stack.54.refs_0_
  109.5 15.1 %error.1.refs_9_ = bf16[1,1376,4096]{2,1,0:T(8,128)(2,1)} custom-call(bf16[1376,512]{1,0:T(8,128)(2,1)} %copy-done, bf16[512,4096]{1,0:T(8,128)(2,1)} %refs_1_.2, bf16[1376,32]{1,0:T(8,128)(2,1)} %get-tuple-element.93.refs_2_.refs_4_, bf16[32,4096]{1,0:T(8,128)(2,1)} %get-tuple-element.94.refs_3_.refs_5_, bf16[1,1376,4096]{2,1,0:T(8,128)(2,1)} %refs_7_.3, ...), custom_call_target="tpu_custom_call" | custom-call | flops 1 | bytes 1 | tf_op jit(solution)/shard_map/error/pallas_call | solution.py:36
  124.6 18.3 %update.1 = (f32[1376,1024]{1,0:T(8,128)}, bf16[1376,4096]{1,0:T(8,128)(2,1)}, f32[8,512]{1,0:T(8,128)}) custom-call(s32[6]{0:T(128)} %stack.54.refs_0_, f32[1376,1024]{1,0:T(8,128)} %refs_1_.3, bf16[1376,32]{1,0:T(8,128)(2,1)} %get-tuple-element.93.refs_2_.refs_4_, ...), custom_call_target="tpu_custom_call", output_to_operand_aliasing={{2}: (10, {})} | custom-call | flops 1 | bytes 1 | tf_op jit(solution)/shard_map/update/pallas_call | solution.py:36
  142.9 5.4 %last.1 = (bf16[1376,4096]{1,0:T(8,128)(2,1)}, f32[8,512]{1,0:T(8,128)}) custom-call(s32[1]{0:T(128)} %bitcast.6.refs_0_, bf16[1376,512]{1,0:T(8,128)(2,1)} %collective-permute-done.17.refs_1_, bf16[1376,512]{1,0:T(8,128)(2,1)} %collective-permute-done.18.refs_2_, bf16[1376,4096]{1,0:T(8,128)(2,1)} %refs_3_.3, ...), custom_call_target="tpu_custom_call", output_to_operand_aliasing={{1}: (7, {}), {0}: (6, {})} | custom-call | flops 1 | bytes 1 | tf_op jit(solution)/shard_map/last/pallas_call | solution.py:36
  148.3 0.7 copy-done.2
  149.0 1.0 join.3
  (31 shorter events, 0.2 us)
Async XLA Ops:
  0.6 7.0 %copy-start.4 = (f32[4096,8]{0,1:T(8,128)S(1)}, f32[4096,8]{0,1:T(8,128)}, u32[]{:S(2)}) copy-start(f32[4096,8]{0,1:T(8,128)} %param.15) | copy-start | bytes 393220
  4.6 41.7 %collective-permute-start.4 = (bf16[1376,512]{1,0:T(8,128)(2,1)S(1)}, bf16[1376,512]{1,0:T(8,128)(2,1)S(1)}, u32[]{:S(2)}, u32[]{:S(2)}) collective-permute-start(bf16[1376,512]{1,0:T(8,128)(2,1)S(1)} %get-tuple-element.57), channel_id=1, source_target_pairs={{0,8},{8,0},{16,24},{24,16},{1,9},{9,1},{17,25},{25,17},{2,10},{10... | collective-permute-start | bytes 4227080 | tf_op jit(solution)/shard_map/ppermute | solution.py:537
  6.1 40.2 %collective-permute-start.3 = (bf16[1376,512]{1,0:T(8,128)(2,1)S(1)}, bf16[1376,512]{1,0:T(8,128)(2,1)S(1)}, u32[]{:S(2)}, u32[]{:S(2)}) collective-permute-start(bf16[1376,512]{1,0:T(8,128)(2,1)S(1)} %get-tuple-element.52.refs_7_), channel_id=1, source_target_pairs={{0,16},{8,24},{16,0},{24,8},{1,17},{9,25},{17,1},{25,9},{2,18},{10... | collective-permute-start | bytes 4227080 | tf_op jit(solution)/shard_map/ppermute | solution.py:537
  42.7 14.5 %copy-start = (bf16[1376,512]{1,0:T(8,128)(2,1)}, bf16[1376,512]{1,0:T(8,128)(2,1)S(1)}, u32[]{:S(2)}) copy-start(bf16[1376,512]{1,0:T(8,128)(2,1)S(1)} %get-tuple-element.56.refs_8_.refs_0_) | copy-start | bytes 4227076
  42.8 5.1 %collective-permute-start.2 = (f32[8,1376]{1,0:T(8,128)S(1)}, f32[8,1376]{1,0:T(8,128)S(1)}, u32[]{:S(2)}, u32[]{:S(2)}) collective-permute-start(f32[8,1376]{1,0:T(8,128)S(1)} %get-tuple-element.55.refs_0_), channel_id=1, source_target_pairs={{0,24},{8,16},{16,8},{24,0},{1,25},{9,17},{17,9},{25,1},{2,26},{10... | collective-permute-start | bytes 132104 | tf_op jit(solution)/shard_map/ppermute | solution.py:537
  43.3 4.5 %collective-permute-start.1 = (f32[8,1376]{1,0:T(8,128)S(1)}, f32[8,1376]{1,0:T(8,128)S(1)}, u32[]{:S(2)}, u32[]{:S(2)}) collective-permute-start(f32[8,1376]{1,0:T(8,128)S(1)} %get-tuple-element.55.refs_0_), channel_id=1, source_target_pairs={{0,16},{8,24},{16,0},{24,8},{1,17},{9,25},{17,1},{25,9},{2,18},{10... | collective-permute-start | bytes 132104 | tf_op jit(solution)/shard_map/ppermute | solution.py:537
  44.8 4.0 %collective-permute-start = (f32[8,1376]{1,0:T(8,128)S(1)}, f32[8,1376]{1,0:T(8,128)S(1)}, u32[]{:S(2)}, u32[]{:S(2)}) collective-permute-start(f32[8,1376]{1,0:T(8,128)S(1)} %get-tuple-element.55.refs_0_), channel_id=1, source_target_pairs={{0,8},{8,0},{16,24},{24,16},{1,9},{9,1},{17,25},{25,17},{2,10},{10... | collective-permute-start | bytes 132104 | tf_op jit(solution)/shard_map/ppermute | solution.py:537
  46.3 2.6 %copy-start.7 = (bf16[1376,512]{1,0:T(8,128)(2,1)}, bf16[1376,512]{1,0:T(8,128)(2,1)S(1)}, u32[]{:S(2)}) copy-start(bf16[1376,512]{1,0:T(8,128)(2,1)S(1)} %collective-permute-done.4.refs_4_) | copy-start | bytes 4227076
  46.3 10.9 %copy-start.8 = (bf16[1376,512]{1,0:T(8,128)(2,1)}, bf16[1376,512]{1,0:T(8,128)(2,1)S(1)}, u32[]{:S(2)}) copy-start(bf16[1376,512]{1,0:T(8,128)(2,1)S(1)} %collective-permute-done.3.refs_3_) | copy-start | bytes 4227076
  57.2 0.6 copy-start.5
  57.8 33.8 %collective-permute-start.12 = (bf16[1376,512]{1,0:T(8,128)(2,1)}, bf16[1376,512]{1,0:T(8,128)(2,1)}, u32[]{:S(2)}, u32[]{:S(2)}) collective-permute-start(bf16[1376,512]{1,0:T(8,128)(2,1)} %get-tuple-element.80), channel_id=1, source_target_pairs={{0,8},{8,0},{16,24},{24,16},{1,9},{9,1},{17,25},{25,17},{2,10},{10... | collective-permute-start | bytes 4227080 | tf_op jit(solution)/shard_map/ppermute | solution.py:537
  59.3 32.3 %collective-permute-start.13 = (bf16[1376,512]{1,0:T(8,128)(2,1)}, bf16[1376,512]{1,0:T(8,128)(2,1)}, u32[]{:S(2)}, u32[]{:S(2)}) collective-permute-start(bf16[1376,512]{1,0:T(8,128)(2,1)} %get-tuple-element.81), channel_id=1, source_target_pairs={{0,16},{8,24},{16,0},{24,8},{1,17},{9,25},{17,1},{25,9},{2,18},{10... | collective-permute-start | bytes 4227080 | tf_op jit(solution)/shard_map/ppermute | solution.py:537
  59.8 6.0 %collective-permute-start.5 = (f32[8,4224]{1,0:T(8,128)S(1)}, f32[8,4224]{1,0:T(8,128)S(1)}, u32[]{:S(2)}, u32[]{:S(2)}) collective-permute-start(f32[8,4224]{1,0:T(8,128)S(1)} %get-tuple-element.61.refs_5_.refs_0_), channel_id=1, source_target_pairs={{0,1},{1,0},{2,3},{3,2},{4,5},{5,4},{6,7},{7,6},{8,9},{9,8},{10,11... | collective-permute-start | bytes 405512 | tf_op jit(solution)/shard_map/ppermute | solution.py:537
  65.9 9.8 %collective-permute-start.9 = (bf16[2,512,512]{2,1,0:T(8,128)(2,1)S(1)}, bf16[2,512,512]{2,1,0:T(8,128)(2,1)S(1)}, u32[]{:S(2)}, u32[]{:S(2)}) collective-permute-start(bf16[2,512,512]{2,1,0:T(8,128)(2,1)S(1)} %get-tuple-element.71), channel_id=1, source_target_pairs={{0,1},{1,0},{2,3},{3,2},{4,5},{5,4},{6,7},{7,6},{8,9},{9,8},{10,11... | collective-permute-start | bytes 3145736 | tf_op jit(solution)/shard_map/ppermute | solution.py:537
  66.5 6.4 %collective-permute-start.6 = (f32[8,4224]{1,0:T(8,128)S(1)}, f32[8,4224]{1,0:T(8,128)S(1)}, u32[]{:S(2)}, u32[]{:S(2)}) collective-permute-start(f32[8,4224]{1,0:T(8,128)S(1)} %get-tuple-element.65.refs_5_.refs_0_), channel_id=1, source_target_pairs={{0,2},{1,3},{2,0},{3,1},{4,6},{5,7},{6,4},{7,5},{8,10},{9,11},{10,... | collective-permute-start | bytes 405512 | tf_op jit(solution)/shard_map/ppermute | solution.py:537
  72.9 11.9 %collective-permute-start.7 = (bf16[2,512,512]{2,1,0:T(8,128)(2,1)S(1)}, bf16[2,512,512]{2,1,0:T(8,128)(2,1)S(1)}, u32[]{:S(2)}, u32[]{:S(2)}) collective-permute-start(bf16[2,512,512]{2,1,0:T(8,128)(2,1)S(1)} %get-tuple-element.69), channel_id=1, source_target_pairs={{0,1},{1,0},{2,3},{3,2},{4,5},{5,4},{6,7},{7,6},{8,9},{9,8},{10,11... | collective-permute-start | bytes 3145736 | tf_op jit(solution)/shard_map/ppermute | solution.py:537
  73.0 9.0 %collective-permute-start.8 = (f32[8,4224]{1,0:T(8,128)S(1)}, f32[8,4224]{1,0:T(8,128)S(1)}, u32[]{:S(2)}, u32[]{:S(2)}) collective-permute-start(f32[8,4224]{1,0:T(8,128)S(1)} %get-tuple-element.70.refs_6_.refs_0_), channel_id=1, source_target_pairs={{0,4},{1,5},{2,6},{3,7},{4,0},{5,1},{6,2},{7,3},{8,12},{9,13},{10,... | collective-permute-start | bytes 405512 | tf_op jit(solution)/shard_map/ppermute | solution.py:537
  82.0 15.5 %collective-permute-start.10 = (bf16[512,512]{1,0:T(8,128)(2,1)S(1)}, bf16[512,512]{1,0:T(8,128)(2,1)S(1)}, u32[]{:S(2)}, u32[]{:S(2)}) collective-permute-start(bf16[512,512]{1,0:T(8,128)(2,1)S(1)} %get-tuple-element.79), channel_id=1, source_target_pairs={{0,2},{1,3},{2,0},{3,1},{4,6},{5,7},{6,4},{7,5},{8,10},{9,11},{10,... | collective-permute-start | bytes 1572872 | tf_op jit(solution)/shard_map/ppermute | solution.py:537
  84.4 8.0 %collective-permute-start.11 = (f32[8,4224]{1,0:T(8,128)S(1)}, f32[8,4224]{1,0:T(8,128)S(1)}, u32[]{:S(2)}, u32[]{:S(2)}) collective-permute-start(f32[8,4224]{1,0:T(8,128)S(1)} %get-tuple-element.75.refs_6_.refs_0_), channel_id=1, source_target_pairs={{0,8},{8,0},{16,24},{24,16},{1,9},{9,1},{17,25},{25,17},{2,10},{10... | collective-permute-start | bytes 405512 | tf_op jit(solution)/shard_map/ppermute | solution.py:537
  92.4 5.1 %collective-permute-start.14 = (f32[8,4224]{1,0:T(8,128)S(1)}, f32[8,4224]{1,0:T(8,128)S(1)}, u32[]{:S(2)}, u32[]{:S(2)}) collective-permute-start(f32[8,4224]{1,0:T(8,128)S(1)} %get-tuple-element.83.refs_0_), channel_id=1, source_target_pairs={{0,16},{8,24},{16,0},{24,8},{1,17},{9,25},{17,1},{25,9},{2,18},{10... | collective-permute-start | bytes 405512 | tf_op jit(solution)/shard_map/ppermute | solution.py:537
  97.5 0.8 copy-start.3
  97.6 0.6 copy-start.1
  98.2 4.3 %copy-start.6 = (bf16[512,512]{1,0:T(8,128)(2,1)}, bf16[512,512]{1,0:T(8,128)(2,1)S(1)}, u32[]{:S(2)}) copy-start(bf16[512,512]{1,0:T(8,128)(2,1)S(1)} %get-tuple-element.87) | copy-start | bytes 1572868
  102.6 40.3 %collective-permute-start.17 = (bf16[1376,512]{1,0:T(8,128)(2,1)}, bf16[1376,512]{1,0:T(8,128)(2,1)}, u32[]{:S(2)}, u32[]{:S(2)}) collective-permute-start(bf16[1376,512]{1,0:T(8,128)(2,1)} %get-tuple-element.91.refs_7_), channel_id=1, source_target_pairs={{0,8},{8,0},{16,24},{24,16},{1,9},{9,1},{17,25},{25,17},{2,10},{10... | collective-permute-start | bytes 4227080 | tf_op jit(solution)/shard_map/ppermute | solution.py:537
  104.1 38.8 %collective-permute-start.18 = (bf16[1376,512]{1,0:T(8,128)(2,1)}, bf16[1376,512]{1,0:T(8,128)(2,1)}, u32[]{:S(2)}, u32[]{:S(2)}) collective-permute-start(bf16[1376,512]{1,0:T(8,128)(2,1)} %get-tuple-element.92.refs_6_), channel_id=1, source_target_pairs={{0,16},{8,24},{16,0},{24,8},{1,17},{9,25},{17,1},{25,9},{2,18},{10... | collective-permute-start | bytes 4227080 | tf_op jit(solution)/shard_map/ppermute | solution.py:537
  105.6 42.7 %collective-permute-start.16 = (bf16[512,512]{1,0:T(8,128)(2,1)}, bf16[512,512]{1,0:T(8,128)(2,1)S(1)}, u32[]{:S(2)}, u32[]{:S(2)}) collective-permute-start(bf16[512,512]{1,0:T(8,128)(2,1)} %get-tuple-element.88), channel_id=1, source_target_pairs={{0,2},{1,3},{2,0},{3,1},{4,6},{5,7},{6,4},{7,5},{8,10},{9,11},{10,... | collective-permute-start | bytes 1572872 | tf_op jit(solution)/shard_map/ppermute | solution.py:537
  106.0 42.3 %collective-permute-start.15 = (bf16[512,512]{1,0:T(8,128)(2,1)}, bf16[512,512]{1,0:T(8,128)(2,1)S(1)}, u32[]{:S(2)}, u32[]{:S(2)}) collective-permute-start(bf16[512,512]{1,0:T(8,128)(2,1)} %copy-done.6), channel_id=1, source_target_pairs={{0,4},{1,5},{2,6},{3,7},{4,0},{5,1},{6,2},{7,3},{8,12},{9,13},{10,... | collective-permute-start | bytes 1572872 | tf_op jit(solution)/shard_map/ppermute | solution.py:537
  148.3 0.7 copy-start.2

commit v7 on v6

--- a/solution.py
+++ b/solution.py
@@ -323,7 +323,6 @@
         [whole(shape)] * len(parts),
         [whole(shape)],
         [shaped(shape, BF16)],
-        vmem=SMALL,
         **links,
     )
 
@@ -408,11 +407,27 @@
     )
 
 
-def error_kernel(hid_ref, dy_ref, l_ref, r_ref, *refs):
-    errs, out_ref = refs[:-1], refs[-1]
+def error_kernel(hid_ref, l_ref, r_ref, dy_any, *refs):
+    errs, (out_ref, dy_ref, sems) = refs[:-3], refs[-3:]
     width = errs[0].shape[2]
-    for part, err_ref in enumerate(errs):
-        at = slice(part * width, (part + 1) * width)
+    first = pl.program_id(0) == 0
+    cuts = [slice(part * width, (part + 1) * width) for part in range(len(errs))]
+    fetches = [
+        pltpu.make_async_copy(dy_any.at[:, at], dy_ref.at[:, at], sems.at[part])
+        for part, at in enumerate(cuts)
+    ]
+
+    @pl.when(first)
+    def _():
+        for fetch in fetches:
+            fetch.start()
+
+    for at, err_ref, fetch in zip(cuts, errs, fetches):
+
+        @pl.when(first)
+        def _(fetch=fetch):
+            fetch.wait()
+
         grown = dot(hid_ref[...], dy_ref[:, at]) + err_ref[0].astype(F32)
         out_ref[0, :, at] = (grown - dot(l_ref[...], r_ref[:, at])).astype(BF16)
 
@@ -425,16 +440,17 @@
         error_kernel,
         "error",
         (pl.cdiv(units, tile),),
-        [hid, dy, l, r] + [err] * STREAMS,
+        [hid, l, r, dy] + [err] * STREAMS,
         [
             pl.BlockSpec((tile, tok), lambda f: (f, 0)),
-            whole(dy.shape),
             pl.BlockSpec((tile, SPLIT), lambda f: (f, 0)),
             whole(r.shape),
+            HELD,
             *error_streams(tile, depth),
         ],
         [pl.BlockSpec((1, tile, depth), lambda f: (0, f, 0))],
         [shaped(err.shape, BF16)],
+        scratch=[pltpu.VMEM(dy.shape, BF16), pltpu.SemaphoreType.DMA((STREAMS,))],
         vmem=LARGE,
         **links,
     )
@@ -444,53 +460,53 @@
     return (w.astype(F32) - 0.1 * (0.9 * mom.astype(F32) + approx)).astype(BF16)
 
 
-def update_kernel(own, at_ref, mom_ref, l_ref, r_ref, w_ref, *refs):
+def update_kernel(at_ref, mom_ref, l_ref, r_ref, w_ref, *refs):
     pieces, (mom_out, w_out) = refs[:-2], refs[-2:]
-    step = pl.program_id(0)
-
-    @pl.when(step < own)
+    half = pieces[0].shape[1]
+    group = pl.program_id(0)
+    approx = dot(l_ref[...], r_ref[...])
+
+    @pl.when(group == 0)
     def _():
-        approx = dot(l_ref[...], r_ref[...])
         mom = mom_ref[...]
         mom_out[...] = 0.9 * mom + approx
         w_out[...] = updated(w_ref[...], mom.astype(BF16), approx)
 
-    for slot, piece in enumerate(pieces):
-
-        @pl.when(step == own + slot)
-        def _(piece=piece):
-            w_out[...] = updated(w_ref[...], piece[...], dot(l_ref[...], r_ref[...]))
+    for pair in range(len(pieces) // 2):
+
+        @pl.when(group == 1 + pair)
+        def _(pair=pair):
+            for side, piece in enumerate(pieces[2 * pair : 2 * pair + 2]):
+                at = slice(side * half, (side + 1) * half)
+                w_out[:, at] = updated(w_ref[:, at], piece[...], approx[:, at])
 
 
 def update_call(at, mom, pieces, w, l, r, **links):
     units, cols = mom.shape
     half = pieces[0].shape[1]
-    own = cols // half
-    tile = units // 2 if units % 32 == 0 and units > 512 else units
-    tiles = units // tile
-
-    def during(low, high, column):
+    tile = 352 if units > 512 else units
+    tiles = pl.cdiv(units, tile)
+
+    def during(group, width):
         def index(c, f, at):
-            row = jnp.where(c < low, 0, jnp.where(c > high, tiles - 1, f))
-            return row, column(jnp.clip(c, low, high))
-
-        return pl.BlockSpec((tile, half), index)
-
-    momenta = during(0, own - 1, lambda c: c)
-    weights = pl.BlockSpec((tile, half), lambda c, f, at: (f, at[c]))
-    return launch(
-        functools.partial(update_kernel, own),
+            return jnp.where(c < group, 0, jnp.where(c > group, tiles - 1, f)), 0
+
+        return pl.BlockSpec((tile, width), index)
+
+    weights = pl.BlockSpec((tile, cols), lambda c, f, at: (f, at[c]))
+    return launch(
+        update_kernel,
         "update",
-        (own + len(pieces), tiles),
+        (1 + len(pieces) // 2, tiles),
         [mom, l, r, w, *pieces],
         [
-            momenta,
+            during(0, cols),
             pl.BlockSpec((tile, SPLIT), lambda c, f, at: (f, 0)),
-            pl.BlockSpec((SPLIT, half), lambda c, f, at: (0, at[c])),
+            pl.BlockSpec((SPLIT, cols), lambda c, f, at: (0, at[c])),
             weights,
-            *[during(own + s, own + s, lambda c: 0) for s in range(len(pieces))],
-        ],
-        [momenta, weights],
+            *[during(1 + slot // 2, half) for slot in range(len(pieces))],
+        ],
+        [during(0, cols), weights],
         [shaped(mom.shape, F32), shaped(w.shape, BF16)],
         places=[at],
         vmem=LARGE,
@@ -615,7 +631,9 @@
         elif fresh:
             others[index] = exchange(fresh[0], "mp", 1)
     if count == 4:
-        relayed, order = join_call([mine[2], relayed], held=[total], through=[order])
+        relayed, order = join_call(
+            [mine[2], relayed], held=[total], through=[order], vmem=SMALL
+        )
     l, r, got[2, 0], got[1, 1] = factors_call(
         total, left, replicas, held=[order], through=[got[2, 0], got[1, 1]]
     )
@@ -628,7 +646,7 @@
 
     (next_err,) = error_call(hid, out_grads, err_down, l, r)
     keys = [(1, 0), (1, 1), (2, 0), (2, 1)]
-    at = jnp.stack([2 * (rank_dp ^ mask) + side for mask, side in [(0, 0), (0, 1)] + keys])
+    at = jnp.stack([rank_dp, rank_dp ^ 1, rank_dp ^ 2])
     next_mom, new, order = update_call(
         at.astype(jnp.int32),
         mom_down,
@@ -639,9 +657,9 @@
         held=[next_err],
         through=[order],
     )
-    far = jnp.reshape(rank_dp ^ 3, (1,)).astype(jnp.int32)
-    new, order = last_call(far, got[3, 0], got[3, 1], w_down, l, r, new, through=[order])
-    (in_grads,) = join_call([mine[0]] + landed, held=[order])
+    corner = jnp.reshape(rank_dp ^ 3, (1,)).astype(jnp.int32)
+    new, order = last_call(corner, got[3, 0], got[3, 1], w_down, l, r, new, through=[order])
+    (in_grads,) = join_call([mine[0]] + landed, held=[order], vmem=SMALL)
     return (in_grads, new, next_err, next_mom)
 
 

time: 152 us -> 155 us (1.020)
  Pallas kernels: 117 us -> 119 us
    pallas_call x18, Pallas kernels: 117 us -> 119 us  [launch(): pl.pallas_call(inner, grid_spec=pltpu.PrefetchScalarGridSpec(num_scalar_p...]
where the time goes in v7:
time: 155 us; the launch traced here: 153 us
  Pallas kernels  119 us (77%)
  starting transfers between devices  23 us (15%)
  waiting for transfers between devices  5.54 us (4%)
  local copies, waits for them, and re-layouts  2.74 us (2%)
  other arithmetic  2.17 us (1%)
    pallas_call x18, Pallas kernels, launch(): pl.pallas_call(inner, grid_spec=pltpu.PrefetchScalarGridSpec(num_scalar_p...  119 us
    ppermute x19, starting transfers between devices, exchange(): return lax.ppermute(value, axis, [(i, i ^ mask) for i in range(size)])  23 us
    ppermute x19, waiting for transfers between devices, exchange(): return lax.ppermute(value, axis, [(i, i ^ mask) for i in range(size)])  5.54 us
  transfers between devices with their start and end apart: 19, of which 4 were waited for; matrix products, arithmetic and copies ran while one was open for 1% of the time, Pallas kernels for 66%

profile of v7, /device:TPU:8, one launch (start us, length us, event | category | flops | bytes accessed | tf_op | source)
XLA Modules:
  0.0 153.4 jit_solution(7543113579627607048)
XLA Ops:
  0.6 4.0 %cast.1 = (bf16[1376,512]{1,0:T(8,128)(2,1)S(1)}, bf16[1376,512]{1,0:T(8,128)(2,1)S(1)}, bf16[1376,512]{1,0:T(8,128)(2,1)}, bf16[1376,512]{1,0:T(8,128)(2,1)}) custom-call(f32[1376,1024]{1,0:T(8,128)} %refs_1_.1), custom_call_target="tpu_custom_call" | custom-call | flops 1 | bytes 1 | tf_op jit(solution)/shard_map/cast/pallas_call | solution.py:36
  4.6 1.5 collective-permute-start.4
  6.1 1.5 collective-permute-start.3
  7.6 35.1 %hidden.1 = (bf16[1376,512]{1,0:T(8,128)(2,1)S(1)}, bf16[512,1376]{1,0:T(8,128)(2,1)S(1)}, bf16[512,1376]{1,0:T(8,128)(2,1)S(1)}, f32[8,1376]{1,0:T(8,128)S(1)}, f32[8,512]{1,0:T(8,128)S(1)}) custom-call(bf16[512,4096]{1,0:T(8,128)(2,1)} %refs_0_.3, bf16[1376,4096]{1,0:T(8,128)(2,1)} %bitcast.11, bf16[1376,4096]{1,0:T(8,128)(2,1)} %bitcast.16, ...), custom_call_target="tpu_custom_call" | custom-call | flops 1 | bytes 1 | tf_op jit(solution)/shard_map/hidden/pallas_call | solution.py:36
  42.8 0.6 collective-permute-start.2
  43.3 1.5 collective-permute-start.1
  44.8 1.5 collective-permute-start
  46.3 0.0 collective-permute-done.4.refs_4_
  46.3 0.0 collective-permute-done.3.refs_3_
  46.3 0.7 slice_add_fusion.1.refs_10_
  47.0 0.8 collective-permute-done.2.refs_3_
  47.8 1.0 collective-permute-done.refs_1_
  48.9 8.3 %right.1 = (f32[8,4224]{1,0:T(8,128)S(1)}, f32[8,1376]{1,0:T(8,128)S(1)}, f32[8,512]{1,0:T(8,128)S(1)}, bf16[1376,512]{1,0:T(8,128)(2,1)}, bf16[1376,512]{1,0:T(8,128)(2,1)}) custom-call(f32[8,1376]{1,0:T(8,128)S(1)} %get-tuple-element.55.refs_0_, ...), custom_call_target="tpu_custom_call", output_to_operand_aliasing={{2}: (11, {}), {3}: (12, {}), {4}: (13, {})} | custom-call | flops 1 | bytes 1 | tf_op jit(solution)/shard_map/right/pallas_call | solution.py:36
  57.2 0.0 copy-start.5
  57.2 0.6 copy-done.5
  57.8 1.5 collective-permute-start.12
  59.3 0.5 collective-permute-start.13
  59.8 0.1 pad_add_fusion.1.refs_0_
  59.9 6.0 %blocks.4 = (bf16[2,512,512]{2,1,0:T(8,128)(2,1)S(1)}, f32[8,512]{1,0:T(8,128)S(1)}) custom-call(s32[2]{0:T(128)S(1)} %pad_add_fusion.1.refs_0_, bf16[512,1376]{1,0:T(8,128)(2,1)S(1)} %get-tuple-element.53.refs_1_, bf16[512,1376]{1,0:T(8,128)(2,1)S(1)} %get-tuple-element.54.refs_2_, bf16[1376,4096]{1,0:T(8,128)(2,1)} %bitcast.12, ...), custom_call_target="tpu_custom_call", output_to_operand_aliasing={{1}: (6, {})} | custom-call | flops 1 | bytes 1 | tf_op jit(solution)/shard_map/blocks/pallas_call | solution.py:36
  65.9 0.6 collective-permute-start.9
  66.5 0.4 collective-permute-start.6
  66.9 6.0 %blocks.5 = (bf16[2,512,512]{2,1,0:T(8,128)(2,1)S(1)}, f32[8,512]{1,0:T(8,128)S(1)}) custom-call(s32[2]{0:T(128)S(1)} %pad_add_fusion.1.refs_0_, bf16[512,1376]{1,0:T(8,128)(2,1)S(1)} %get-tuple-element.53.refs_1_, bf16[512,1376]{1,0:T(8,128)(2,1)S(1)} %get-tuple-element.54.refs_2_, bf16[1376,4096]{1,0:T(8,128)(2,1)} %bitcast.13, ...), custom_call_target="tpu_custom_call", output_to_operand_aliasing={{1}: (6, {})} | custom-call | flops 1 | bytes 1 | tf_op jit(solution)/shard_map/blocks/pallas_call | solution.py:36
  72.9 0.1 collective-permute-start.7
  73.0 2.7 %collective-permute-start.8 = (f32[8,4224]{1,0:T(8,128)S(1)}, f32[8,4224]{1,0:T(8,128)S(1)}, u32[]{:S(2)}, u32[]{:S(2)}) collective-permute-start(f32[8,4224]{1,0:T(8,128)S(1)} %get-tuple-element.70.refs_6_.refs_0_), channel_id=1, source_target_pairs={{0,4},{1,5},{2,6},{3,7},{4,0},{5,1},{6,2},{7,3},{8,12},{9,13},{10,... | collective-permute-start | bytes 405512 | tf_op jit(solution)/shard_map/ppermute | solution.py:553
  75.7 0.1 pad_add_fusion.refs_0_
  75.7 6.1 %blocks.6 = (bf16[512,512]{1,0:T(8,128)(2,1)S(1)}, bf16[512,512]{1,0:T(8,128)(2,1)S(1)}, f32[8,512]{1,0:T(8,128)S(1)}) custom-call(s32[2]{0:T(128)S(1)} %pad_add_fusion.refs_0_, bf16[512,1376]{1,0:T(8,128)(2,1)S(1)} %get-tuple-element.53.refs_1_, bf16[512,1376]{1,0:T(8,128)(2,1)S(1)} %get-tuple-element.54.refs_2_, ...), custom_call_target="tpu_custom_call", output_to_operand_aliasing={{2}: (7, {})} | custom-call | flops 1 | bytes 1 | tf_op jit(solution)/shard_map/blocks/pallas_call | solution.py:36
  81.8 0.2 collective-permute-done.8.refs_1_
  82.0 2.3 %collective-permute-start.10 = (bf16[512,512]{1,0:T(8,128)(2,1)S(1)}, bf16[512,512]{1,0:T(8,128)(2,1)S(1)}, u32[]{:S(2)}, u32[]{:S(2)}) collective-permute-start(bf16[512,512]{1,0:T(8,128)(2,1)S(1)} %get-tuple-element.79), channel_id=1, source_target_pairs={{0,2},{1,3},{2,0},{3,1},{4,6},{5,7},{6,4},{7,5},{8,10},{9,11},{10,... | collective-permute-start | bytes 1572872 | tf_op jit(solution)/shard_map/ppermute | solution.py:553
  84.3 0.5 collective-permute-start.11
  84.8 6.8 %blocks.7 = (bf16[512,512]{1,0:T(8,128)(2,1)S(1)}, bf16[512,512]{1,0:T(8,128)(2,1)}, f32[8,512]{1,0:T(8,128)S(1)}) custom-call(s32[2]{0:T(128)S(1)} %pad_add_fusion.refs_0_, bf16[512,1376]{1,0:T(8,128)(2,1)S(1)} %get-tuple-element.53.refs_1_, bf16[512,1376]{1,0:T(8,128)(2,1)S(1)} %get-tuple-element.54.refs_2_, ...), custom_call_target="tpu_custom_call", output_to_operand_aliasing={{2}: (7, {})} | custom-call | flops 1 | bytes 1 | tf_op jit(solution)/shard_map/blocks/pallas_call | solution.py:36
  91.7 0.7 slice_add_fusion.refs_2_
  92.4 1.6 %collective-permute-start.14 = (f32[8,4224]{1,0:T(8,128)S(1)}, f32[8,4224]{1,0:T(8,128)S(1)}, u32[]{:S(2)}, u32[]{:S(2)}) collective-permute-start(f32[8,4224]{1,0:T(8,128)S(1)} %get-tuple-element.83.refs_0_), channel_id=1, source_target_pairs={{0,16},{8,24},{16,0},{24,8},{1,17},{9,25},{17,1},{25,9},{2,18},{10... | collective-permute-start | bytes 405512 | tf_op jit(solution)/shard_map/ppermute | solution.py:553
  94.0 3.4 %collective-permute-done.14.refs_1_ = f32[8,4224]{1,0:T(8,128)S(1)} collective-permute-done((f32[8,4224]{1,0:T(8,128)S(1)}, f32[8,4224]{1,0:T(8,128)S(1)}, u32[]{:S(2)}, u32[]{:S(2)}) %collective-permute-start.14) | collective-permute-done | bytes 135200 | tf_op jit(solution)/shard_map/ppermute | solution.py:553
  97.5 0.0 copy-start.3
  97.5 0.1 join.2
  97.6 0.6 copy-done.1
  98.2 0.8 copy-done.6
  99.0 4.2 %factors.1 = (bf16[1376,32]{1,0:T(8,128)(2,1)}, bf16[32,4096]{1,0:T(8,128)(2,1)}, bf16[1376,512]{1,0:T(8,128)(2,1)}, bf16[1376,512]{1,0:T(8,128)(2,1)}) custom-call(f32[8,4224]{1,0:T(8,128)} %copy-done.3, f32[8,1376]{1,0:T(8,128)} %copy-done.5, f32[8,512]{1,0:T(8,128)} %copy-done.1, ...), custom_call_target="tpu_custom_call", output_to_operand_aliasing={{2}: (3, {}), {3}: (4, {})} | custom-call | flops 1 | bytes 1 | tf_op jit(solution)/shard_map/factors/pallas_call | solution.py:36
  103.2 1.6 %collective-permute-start.17 = (bf16[1376,512]{1,0:T(8,128)(2,1)}, bf16[1376,512]{1,0:T(8,128)(2,1)}, u32[]{:S(2)}, u32[]{:S(2)}) collective-permute-start(bf16[1376,512]{1,0:T(8,128)(2,1)} %get-tuple-element.91.refs_7_), channel_id=1, source_target_pairs={{0,8},{8,0},{16,24},{24,16},{1,9},{9,1},{17,25},{25,17},{2,10},{10... | collective-permute-start | bytes 4227080 | tf_op jit(solution)/shard_map/ppermute | solution.py:553
  104.8 1.5 collective-permute-start.18
  106.3 0.3 collective-permute-start.16
  106.6 2.8 %collective-permute-start.15 = (bf16[512,512]{1,0:T(8,128)(2,1)}, bf16[512,512]{1,0:T(8,128)(2,1)S(1)}, u32[]{:S(2)}, u32[]{:S(2)}) collective-permute-start(bf16[512,512]{1,0:T(8,128)(2,1)} %copy-done.6), channel_id=1, source_target_pairs={{0,4},{1,5},{2,6},{3,7},{4,0},{5,1},{6,2},{7,3},{8,12},{9,13},{10,... | collective-permute-start | bytes 1572872 | tf_op jit(solution)/shard_map/ppermute | solution.py:553
  109.4 0.6 pad_add_fusion.2.refs_0_
  110.1 17.0 %error.1.refs_9_ = bf16[1,1376,4096]{2,1,0:T(8,128)(2,1)} custom-call(bf16[1376,512]{1,0:T(8,128)(2,1)} %copy-done, bf16[1376,32]{1,0:T(8,128)(2,1)} %get-tuple-element.93.refs_1_.refs_2_.refs_4_, bf16[32,4096]{1,0:T(8,128)(2,1)} %get-tuple-element.94.refs_2_.refs_3_.refs_5_, bf16[512,4096]{1,0:T(8,128)(2,1)} %refs_3_.4, bf16[1,1376,4096]{2,1,0:T(8,128)(2,1)} %refs_7_.3, ...), custom_call_target="tpu_custom_call" | custom-call | flops 1 | bytes 1 | tf_op jit(solution)/shard_map/error/pallas_call | solution.py:36
  127.1 19.2 %update.1 = (f32[1376,1024]{1,0:T(8,128)}, bf16[1376,4096]{1,0:T(8,128)(2,1)}, f32[8,512]{1,0:T(8,128)}) custom-call(s32[3]{0:T(128)} %pad_add_fusion.2.refs_0_, f32[1376,1024]{1,0:T(8,128)} %refs_1_.1, bf16[1376,32]{1,0:T(8,128)(2,1)} %get-tuple-element.93.refs_1_.refs_2_.refs_4_, ...), custom_call_target="tpu_custom_call", output_to_operand_aliasing={{2}: (10, {})} | custom-call | flops 1 | bytes 1 | tf_op jit(solution)/shard_map/update/pallas_call | solution.py:36
  146.3 5.4 %last.1 = (bf16[1376,4096]{1,0:T(8,128)(2,1)}, f32[8,512]{1,0:T(8,128)}) custom-call(s32[1]{0:T(128)} %bitcast.6.refs_0_, bf16[1376,512]{1,0:T(8,128)(2,1)} %collective-permute-done.17.refs_1_, bf16[1376,512]{1,0:T(8,128)(2,1)} %collective-permute-done.18.refs_2_, bf16[1376,4096]{1,0:T(8,128)(2,1)} %refs_3_.5, ...), custom_call_target="tpu_custom_call", output_to_operand_aliasing={{1}: (7, {}), {0}: (6, {})} | custom-call | flops 1 | bytes 1 | tf_op jit(solution)/shard_map/last/pallas_call | solution.py:36
  151.8 0.7 copy-done.2
  152.5 1.0 join.3
  (27 shorter events, 0.1 us)
Async XLA Ops:
  0.6 7.0 %copy-start.4 = (f32[4096,8]{0,1:T(8,128)S(1)}, f32[4096,8]{0,1:T(8,128)}, u32[]{:S(2)}) copy-start(f32[4096,8]{0,1:T(8,128)} %param.15) | copy-start | bytes 393220
  4.6 41.7 %collective-permute-start.4 = (bf16[1376,512]{1,0:T(8,128)(2,1)S(1)}, bf16[1376,512]{1,0:T(8,128)(2,1)}, u32[]{:S(2)}, u32[]{:S(2)}) collective-permute-start(bf16[1376,512]{1,0:T(8,128)(2,1)S(1)} %get-tuple-element.57), channel_id=1, source_target_pairs={{0,8},{8,0},{16,24},{24,16},{1,9},{9,1},{17,25},{25,17},{2,10},{10... | collective-permute-start | bytes 4227080 | tf_op jit(solution)/shard_map/ppermute | solution.py:553
  6.1 40.2 %collective-permute-start.3 = (bf16[1376,512]{1,0:T(8,128)(2,1)S(1)}, bf16[1376,512]{1,0:T(8,128)(2,1)}, u32[]{:S(2)}, u32[]{:S(2)}) collective-permute-start(bf16[1376,512]{1,0:T(8,128)(2,1)S(1)} %get-tuple-element.52.refs_7_), channel_id=1, source_target_pairs={{0,16},{8,24},{16,0},{24,8},{1,17},{9,25},{17,1},{25,9},{2,18},{10... | collective-permute-start | bytes 4227080 | tf_op jit(solution)/shard_map/ppermute | solution.py:553
  42.7 14.4 %copy-start = (bf16[1376,512]{1,0:T(8,128)(2,1)}, bf16[1376,512]{1,0:T(8,128)(2,1)S(1)}, u32[]{:S(2)}) copy-start(bf16[1376,512]{1,0:T(8,128)(2,1)S(1)} %get-tuple-element.56.refs_8_.refs_0_) | copy-start | bytes 4227076
  42.8 5.1 %collective-permute-start.2 = (f32[8,1376]{1,0:T(8,128)S(1)}, f32[8,1376]{1,0:T(8,128)S(1)}, u32[]{:S(2)}, u32[]{:S(2)}) collective-permute-start(f32[8,1376]{1,0:T(8,128)S(1)} %get-tuple-element.55.refs_0_), channel_id=1, source_target_pairs={{0,24},{8,16},{16,8},{24,0},{1,25},{9,17},{17,9},{25,1},{2,26},{10... | collective-permute-start | bytes 132104 | tf_op jit(solution)/shard_map/ppermute | solution.py:553
  43.3 4.5 %collective-permute-start.1 = (f32[8,1376]{1,0:T(8,128)S(1)}, f32[8,1376]{1,0:T(8,128)S(1)}, u32[]{:S(2)}, u32[]{:S(2)}) collective-permute-start(f32[8,1376]{1,0:T(8,128)S(1)} %get-tuple-element.55.refs_0_), channel_id=1, source_target_pairs={{0,16},{8,24},{16,0},{24,8},{1,17},{9,25},{17,1},{25,9},{2,18},{10... | collective-permute-start | bytes 132104 | tf_op jit(solution)/shard_map/ppermute | solution.py:553
  44.8 4.0 %collective-permute-start = (f32[8,1376]{1,0:T(8,128)S(1)}, f32[8,1376]{1,0:T(8,128)S(1)}, u32[]{:S(2)}, u32[]{:S(2)}) collective-permute-start(f32[8,1376]{1,0:T(8,128)S(1)} %get-tuple-element.55.refs_0_), channel_id=1, source_target_pairs={{0,8},{8,0},{16,24},{24,16},{1,9},{9,1},{17,25},{25,17},{2,10},{10... | collective-permute-start | bytes 132104 | tf_op jit(solution)/shard_map/ppermute | solution.py:553
  57.2 0.6 copy-start.5
  57.8 33.8 %collective-permute-start.12 = (bf16[1376,512]{1,0:T(8,128)(2,1)}, bf16[1376,512]{1,0:T(8,128)(2,1)}, u32[]{:S(2)}, u32[]{:S(2)}) collective-permute-start(bf16[1376,512]{1,0:T(8,128)(2,1)} %get-tuple-element.80), channel_id=1, source_target_pairs={{0,8},{8,0},{16,24},{24,16},{1,9},{9,1},{17,25},{25,17},{2,10},{10... | collective-permute-start | bytes 4227080 | tf_op jit(solution)/shard_map/ppermute | solution.py:553
  59.3 32.3 %collective-permute-start.13 = (bf16[1376,512]{1,0:T(8,128)(2,1)}, bf16[1376,512]{1,0:T(8,128)(2,1)}, u32[]{:S(2)}, u32[]{:S(2)}) collective-permute-start(bf16[1376,512]{1,0:T(8,128)(2,1)} %get-tuple-element.81), channel_id=1, source_target_pairs={{0,16},{8,24},{16,0},{24,8},{1,17},{9,25},{17,1},{25,9},{2,18},{10... | collective-permute-start | bytes 4227080 | tf_op jit(solution)/shard_map/ppermute | solution.py:553
  59.8 6.0 %collective-permute-start.5 = (f32[8,4224]{1,0:T(8,128)S(1)}, f32[8,4224]{1,0:T(8,128)S(1)}, u32[]{:S(2)}, u32[]{:S(2)}) collective-permute-start(f32[8,4224]{1,0:T(8,128)S(1)} %get-tuple-element.61.refs_5_.refs_0_), channel_id=1, source_target_pairs={{0,1},{1,0},{2,3},{3,2},{4,5},{5,4},{6,7},{7,6},{8,9},{9,8},{10,11... | collective-permute-start | bytes 405512 | tf_op jit(solution)/shard_map/ppermute | solution.py:553
  65.9 9.8 %collective-permute-start.9 = (bf16[2,512,512]{2,1,0:T(8,128)(2,1)S(1)}, bf16[2,512,512]{2,1,0:T(8,128)(2,1)S(1)}, u32[]{:S(2)}, u32[]{:S(2)}) collective-permute-start(bf16[2,512,512]{2,1,0:T(8,128)(2,1)S(1)} %get-tuple-element.71), channel_id=1, source_target_pairs={{0,1},{1,0},{2,3},{3,2},{4,5},{5,4},{6,7},{7,6},{8,9},{9,8},{10,11... | collective-permute-start | bytes 3145736 | tf_op jit(solution)/shard_map/ppermute | solution.py:553
  66.5 6.4 %collective-permute-start.6 = (f32[8,4224]{1,0:T(8,128)S(1)}, f32[8,4224]{1,0:T(8,128)S(1)}, u32[]{:S(2)}, u32[]{:S(2)}) collective-permute-start(f32[8,4224]{1,0:T(8,128)S(1)} %get-tuple-element.65.refs_5_.refs_0_), channel_id=1, source_target_pairs={{0,2},{1,3},{2,0},{3,1},{4,6},{5,7},{6,4},{7,5},{8,10},{9,11},{10,... | collective-permute-start | bytes 405512 | tf_op jit(solution)/shard_map/ppermute | solution.py:553
  72.9 11.9 %collective-permute-start.7 = (bf16[2,512,512]{2,1,0:T(8,128)(2,1)S(1)}, bf16[2,512,512]{2,1,0:T(8,128)(2,1)S(1)}, u32[]{:S(2)}, u32[]{:S(2)}) collective-permute-start(bf16[2,512,512]{2,1,0:T(8,128)(2,1)S(1)} %get-tuple-element.69), channel_id=1, source_target_pairs={{0,1},{1,0},{2,3},{3,2},{4,5},{5,4},{6,7},{7,6},{8,9},{9,8},{10,11... | collective-permute-start | bytes 3145736 | tf_op jit(solution)/shard_map/ppermute | solution.py:553
  73.0 9.0 %collective-permute-start.8 = (f32[8,4224]{1,0:T(8,128)S(1)}, f32[8,4224]{1,0:T(8,128)S(1)}, u32[]{:S(2)}, u32[]{:S(2)}) collective-permute-start(f32[8,4224]{1,0:T(8,128)S(1)} %get-tuple-element.70.refs_6_.refs_0_), channel_id=1, source_target_pairs={{0,4},{1,5},{2,6},{3,7},{4,0},{5,1},{6,2},{7,3},{8,12},{9,13},{10,... | collective-permute-start | bytes 405512 | tf_op jit(solution)/shard_map/ppermute | solution.py:553
  82.0 15.5 %collective-permute-start.10 = (bf16[512,512]{1,0:T(8,128)(2,1)S(1)}, bf16[512,512]{1,0:T(8,128)(2,1)S(1)}, u32[]{:S(2)}, u32[]{:S(2)}) collective-permute-start(bf16[512,512]{1,0:T(8,128)(2,1)S(1)} %get-tuple-element.79), channel_id=1, source_target_pairs={{0,2},{1,3},{2,0},{3,1},{4,6},{5,7},{6,4},{7,5},{8,10},{9,11},{10,... | collective-permute-start | bytes 1572872 | tf_op jit(solution)/shard_map/ppermute | solution.py:553
  84.3 8.0 %collective-permute-start.11 = (f32[8,4224]{1,0:T(8,128)S(1)}, f32[8,4224]{1,0:T(8,128)S(1)}, u32[]{:S(2)}, u32[]{:S(2)}) collective-permute-start(f32[8,4224]{1,0:T(8,128)S(1)} %get-tuple-element.75.refs_6_.refs_0_), channel_id=1, source_target_pairs={{0,8},{8,0},{16,24},{24,16},{1,9},{9,1},{17,25},{25,17},{2,10},{10... | collective-permute-start | bytes 405512 | tf_op jit(solution)/shard_map/ppermute | solution.py:553
  92.4 5.1 %collective-permute-start.14 = (f32[8,4224]{1,0:T(8,128)S(1)}, f32[8,4224]{1,0:T(8,128)S(1)}, u32[]{:S(2)}, u32[]{:S(2)}) collective-permute-start(f32[8,4224]{1,0:T(8,128)S(1)} %get-tuple-element.83.refs_0_), channel_id=1, source_target_pairs={{0,16},{8,24},{16,0},{24,8},{1,17},{9,25},{17,1},{25,9},{2,18},{10... | collective-permute-start | bytes 405512 | tf_op jit(solution)/shard_map/ppermute | solution.py:553
  97.5 1.6 %copy-start.3 = (f32[8,4224]{1,0:T(8,128)}, f32[8,4224]{1,0:T(8,128)S(1)}, u32[]{:S(2)}) copy-start(f32[8,4224]{1,0:T(8,128)S(1)} %get-tuple-element.85.refs_2_.refs_0_) | copy-start | bytes 405508
  97.6 0.6 copy-start.1
  98.2 0.8 copy-start.6
  103.2 43.1 %collective-permute-start.17 = (bf16[1376,512]{1,0:T(8,128)(2,1)}, bf16[1376,512]{1,0:T(8,128)(2,1)}, u32[]{:S(2)}, u32[]{:S(2)}) collective-permute-start(bf16[1376,512]{1,0:T(8,128)(2,1)} %get-tuple-element.91.refs_7_), channel_id=1, source_target_pairs={{0,8},{8,0},{16,24},{24,16},{1,9},{9,1},{17,25},{25,17},{2,10},{10... | collective-permute-start | bytes 4227080 | tf_op jit(solution)/shard_map/ppermute | solution.py:553
  104.8 41.6 %collective-permute-start.18 = (bf16[1376,512]{1,0:T(8,128)(2,1)}, bf16[1376,512]{1,0:T(8,128)(2,1)}, u32[]{:S(2)}, u32[]{:S(2)}) collective-permute-start(bf16[1376,512]{1,0:T(8,128)(2,1)} %get-tuple-element.92.refs_6_), channel_id=1, source_target_pairs={{0,16},{8,24},{16,0},{24,8},{1,17},{9,25},{17,1},{25,9},{2,18},{10... | collective-permute-start | bytes 4227080 | tf_op jit(solution)/shard_map/ppermute | solution.py:553
  106.3 45.4 %collective-permute-start.16 = (bf16[512,512]{1,0:T(8,128)(2,1)}, bf16[512,512]{1,0:T(8,128)(2,1)S(1)}, u32[]{:S(2)}, u32[]{:S(2)}) collective-permute-start(bf16[512,512]{1,0:T(8,128)(2,1)} %get-tuple-element.88), channel_id=1, source_target_pairs={{0,2},{1,3},{2,0},{3,1},{4,6},{5,7},{6,4},{7,5},{8,10},{9,11},{10,... | collective-permute-start | bytes 1572872 | tf_op jit(solution)/shard_map/ppermute | solution.py:553
  106.6 45.1 %collective-permute-start.15 = (bf16[512,512]{1,0:T(8,128)(2,1)}, bf16[512,512]{1,0:T(8,128)(2,1)S(1)}, u32[]{:S(2)}, u32[]{:S(2)}) collective-permute-start(bf16[512,512]{1,0:T(8,128)(2,1)} %copy-done.6), channel_id=1, source_target_pairs={{0,4},{1,5},{2,6},{3,7},{4,0},{5,1},{6,2},{7,3},{8,12},{9,13},{10,... | collective-permute-start | bytes 1572872 | tf_op jit(solution)/shard_map/ppermute | solution.py:553
  151.7 0.7 copy-start.2

commit v8 on v6

--- a/solution.py
+++ b/solution.py
@@ -119,60 +119,103 @@
 
 
 def hidden_kernel(
-    replicas,
-    x_ref, wg_ref, wu_ref, wd_ref, err_ref, q_ref, dy_any,
-    hid_ref, dg_ref, du_ref, left_ref, dyq_ref,
-    dy_ref, q_terms, dyq_terms, sem,
+    replicas, units,
+    q_ref, x_any, dy_any, *refs,
 ):
-    fetch = pltpu.make_async_copy(dy_any, dy_ref, sem)
-
-    @pl.when(pl.program_id(0) == 0)
+    sources, refs = refs[:4], refs[4:]
+    (hid_ref, dg_ref, du_ref, left_ref, dyq_ref), refs = refs[:5], refs[5:]
+    (x_ref, dy_ref), slots, (q_terms, dyq_terms, once, sems) = refs[:2], refs[2:6], refs[6:]
+    step = pl.program_id(0)
+    tile = slots[0].shape[1]
+    last = pl.cdiv(units, tile) - 1
+    tail = units - last * tile
+    slot = lax.rem(step, 2)
+    fetch_x = pltpu.make_async_copy(x_any, x_ref, once.at[0])
+    fetch_dy = pltpu.make_async_copy(dy_any, dy_ref, once.at[1])
+
+    def move(act, at, which):
+        def each(rows):
+            for k in which:
+                source = sources[k].at[0] if len(sources[k].shape) == 3 else sources[k]
+                act(
+                    pltpu.make_async_copy(
+                        source.at[pl.ds(pl.multiple_of(at * tile, tile), rows)],
+                        slots[k].at[lax.rem(at, 2), pl.ds(0, rows)],
+                        sems.at[k, lax.rem(at, 2)],
+                    ),
+                    k % 2,
+                )
+
+        if tail == tile:
+            each(tile)
+        else:
+            pl.when(at < last)(lambda: each(tile))
+            pl.when(at == last)(lambda: each(tail))
+
+    def start(copy, queue):
+        copy.start(priority=queue)
+
+    def wait(copy, _):
+        copy.wait()
+
+    def finish(gate, up, both, dh):
+        sig = jax.nn.sigmoid(gate)
+        silu = gate * sig
+        hid = (silu * up).T.astype(BF16)
+        hid_ref[...] = hid
+        dg_ref[...] = (dh * up * sig * (1.0 + gate * (1.0 - sig))).astype(BF16)
+        du_ref[...] = (dh * silu).astype(BF16)
+        both += dot_nt(hid, dyq_terms[...])
+        left_ref[...] = gather_terms(both.T) / replicas
+
+    @pl.when(step == 0)
     def _():
-        fetch.start()
+        fetch_x.start()
+        move(start, step, (0, 1, 2))
+        fetch_dy.start()
+        move(start, step, (3,))
+
+    @pl.when(step < last)
+    def _():
+        move(start, step + 1, (0, 1, 2, 3))
+
+    @pl.when(step == 0)
+    def _():
         q_terms[...] = spread(q_ref[...])
-
-    gate = dot_nt(x_ref[...], wg_ref[...])
-    up = dot_nt(x_ref[...], wu_ref[...])
-    both = dot_nt(err_ref[0], q_terms[...])
-
-    @pl.when(pl.program_id(0) == 0)
-    def _():
-        fetch.wait()
+        fetch_x.wait()
+        move(wait, step, (0,))
+        gate = dot_nt(x_ref[...], slots[0][slot])
+        move(wait, step, (1,))
+        up = dot_nt(x_ref[...], slots[1][slot])
+        move(wait, step, (2,))
+        both = dot_nt(slots[2][slot], q_terms[...])
+        fetch_dy.wait()
         dyq = gather_terms(dot_nt(dy_ref[...], q_terms[...]).T)
         dyq_ref[...] = dyq
         dyq_terms[...] = spread(dyq)
-
-    dh = dot_nt(dy_ref[...], wd_ref[...])
-    sig = jax.nn.sigmoid(gate)
-    silu = gate * sig
-    hid = (silu * up).T.astype(BF16)
-    hid_ref[...] = hid
-    dg_ref[...] = (dh * up * sig * (1.0 + gate * (1.0 - sig))).astype(BF16)
-    du_ref[...] = (dh * silu).astype(BF16)
-    both += dot_nt(hid, dyq_terms[...])
-    left_ref[...] = gather_terms(both.T) / replicas
+        move(wait, step, (3,))
+        finish(gate, up, both, dot_nt(dy_ref[...], slots[3][slot]))
+
+    @pl.when(step > 0)
+    def _():
+        move(wait, step, (0, 1, 2, 3))
+        gate = dot_nt(x_ref[...], slots[0][slot])
+        up = dot_nt(x_ref[...], slots[1][slot])
+        both = dot_nt(slots[2][slot], q_terms[...])
+        finish(gate, up, both, dot_nt(dy_ref[...], slots[3][slot]))
 
 
 def hidden_call(x, dy, wg, wu, wd, err, q_t, replicas, **links):
     tok, depth = x.shape
     units = wg.shape[0]
     tile = unit_tile(units)
-    rows = pl.BlockSpec((tile, depth), lambda f: (f, 0))
     part = pl.BlockSpec((tok, tile), lambda f: (0, f))
     return launch(
-        functools.partial(hidden_kernel, replicas),
+        functools.partial(hidden_kernel, replicas, units),
         "hidden",
         (pl.cdiv(units, tile),),
-        [x, wg, wu, wd, err, q_t, dy],
-        [
-            whole((tok, depth)),
-            rows,
-            rows,
-            rows,
-            pl.BlockSpec((1, tile, depth), lambda f: (0, f, 0)),
-            whole(q_t.shape),
-            HELD,
-        ],
+        [q_t, x, dy, wg, wu, err, wd],
+        [whole(q_t.shape)] + [HELD] * 6,
         [
             pl.BlockSpec((tile, tok), lambda f: (f, 0)),
             part,
@@ -188,10 +231,12 @@
             shaped((R, tok), F32),
         ],
         scratch=[
-            pltpu.VMEM((tok, depth), BF16),
+            *[pltpu.VMEM((tok, depth), BF16)] * 2,
+            *[pltpu.VMEM((2, tile, depth), BF16)] * 4,
             pltpu.VMEM((SPLIT, depth), BF16),
             pltpu.VMEM((SPLIT, tok), BF16),
-            pltpu.SemaphoreType.DMA(()),
+            pltpu.SemaphoreType.DMA((2,)),
+            pltpu.SemaphoreType.DMA((4, 2)),
         ],
         **links,
     )

time: 152 us -> 153 us (level)
  no operation moved by 1% of the time
where the time goes in v8:
time: 153 us; the launch traced here: 151 us
  Pallas kernels  118 us (77%)
  starting transfers between devices  23 us (15%)
  waiting for transfers between devices  6.21 us (4%)
  local copies, waits for them, and re-layouts  2.6 us (2%)
    pallas_call x18, Pallas kernels, launch(): pl.pallas_call(inner, grid_spec=pltpu.PrefetchScalarGridSpec(num_scalar_p...  118 us
    ppermute x19, starting transfers between devices, exchange(): return lax.ppermute(value, axis, [(i, i ^ mask) for i in range(size)])  23 us
    ppermute x19, waiting for transfers between devices, exchange(): return lax.ppermute(value, axis, [(i, i ^ mask) for i in range(size)])  6.21 us
  transfers between devices with their start and end apart: 19, of which 4 were waited for; matrix products, arithmetic and copies ran while one was open for 1% of the time, Pallas kernels for 66%

profile of v8, /device:TPU:8, one launch (start us, length us, event | category | flops | bytes accessed | tf_op | source)
XLA Modules:
  0.0 151.3 jit_solution(10447493425983971173)
XLA Ops:
  0.6 4.0 %cast.1 = (bf16[1376,512]{1,0:T(8,128)(2,1)S(1)}, bf16[1376,512]{1,0:T(8,128)(2,1)S(1)}, bf16[1376,512]{1,0:T(8,128)(2,1)}, bf16[1376,512]{1,0:T(8,128)(2,1)}) custom-call(f32[1376,1024]{1,0:T(8,128)} %refs_1_.5), custom_call_target="tpu_custom_call" | custom-call | flops 1 | bytes 1 | tf_op jit(solution)/shard_map/cast/pallas_call | solution.py:36
  4.6 1.5 collective-permute-start.4
  6.1 1.5 %collective-permute-start.3 = (bf16[1376,512]{1,0:T(8,128)(2,1)S(1)}, bf16[1376,512]{1,0:T(8,128)(2,1)S(1)}, u32[]{:S(2)}, u32[]{:S(2)}) collective-permute-start(bf16[1376,512]{1,0:T(8,128)(2,1)S(1)} %get-tuple-element.52.refs_7_), channel_id=1, source_target_pairs={{0,16},{8,24},{16,0},{24,8},{1,17},{9,25},{17,1},{25,9},{2,18},{10... | collective-permute-start | bytes 4227080 | tf_op jit(solution)/shard_map/ppermute | solution.py:582
  7.6 36.2 %hidden.1 = (bf16[1376,512]{1,0:T(8,128)(2,1)S(1)}, bf16[512,1376]{1,0:T(8,128)(2,1)S(1)}, bf16[512,1376]{1,0:T(8,128)(2,1)S(1)}, f32[8,1376]{1,0:T(8,128)S(1)}, f32[8,512]{1,0:T(8,128)S(1)}) custom-call(f32[8,4096]{1,0:T(8,128)S(1)} %bitcast.13, bf16[512,4096]{1,0:T(8,128)(2,1)} %refs_1_.3, bf16[512,4096]{1,0:T(8,128)(2,1)} %refs_1_.4, ...), custom_call_target="tpu_custom_call" | custom-call | flops 1 | bytes 1 | tf_op jit(solution)/shard_map/hidden/pallas_call | solution.py:36
  43.9 0.5 collective-permute-start.2
  44.4 1.5 %collective-permute-start.1 = (f32[8,1376]{1,0:T(8,128)S(1)}, f32[8,1376]{1,0:T(8,128)S(1)}, u32[]{:S(2)}, u32[]{:S(2)}) collective-permute-start(f32[8,1376]{1,0:T(8,128)S(1)} %get-tuple-element.55.refs_0_), channel_id=1, source_target_pairs={{0,16},{8,24},{16,0},{24,8},{1,17},{9,25},{17,1},{25,9},{2,18},{10... | collective-permute-start | bytes 132104 | tf_op jit(solution)/shard_map/ppermute | solution.py:582
  46.0 1.5 collective-permute-start
  47.5 1.5 collective-permute-done.2.refs_3_
  49.0 1.0 collective-permute-done.refs_1_
  50.0 8.3 %right.1 = (f32[8,4224]{1,0:T(8,128)S(1)}, f32[8,1376]{1,0:T(8,128)S(1)}, f32[8,512]{1,0:T(8,128)S(1)}, bf16[1376,512]{1,0:T(8,128)(2,1)}, bf16[1376,512]{1,0:T(8,128)(2,1)}) custom-call(f32[8,1376]{1,0:T(8,128)S(1)} %get-tuple-element.55.refs_0_, ...), custom_call_target="tpu_custom_call", output_to_operand_aliasing={{2}: (11, {}), {3}: (12, {}), {4}: (13, {})} | custom-call | flops 1 | bytes 1 | tf_op jit(solution)/shard_map/right/pallas_call | solution.py:36
  58.3 0.0 copy-start.5
  58.4 0.6 copy-done.5
  59.0 1.5 collective-permute-start.12
  60.5 0.5 collective-permute-start.13
  61.0 0.0 collective-permute-start.5
  61.0 0.1 pad_add_fusion.1.refs_0_
  61.0 6.0 %blocks.4 = (bf16[2,512,512]{2,1,0:T(8,128)(2,1)S(1)}, f32[8,512]{1,0:T(8,128)S(1)}) custom-call(s32[2]{0:T(128)S(1)} %pad_add_fusion.1.refs_0_, bf16[512,1376]{1,0:T(8,128)(2,1)S(1)} %get-tuple-element.53.refs_1_, bf16[512,1376]{1,0:T(8,128)(2,1)S(1)} %get-tuple-element.54.refs_2_, bf16[1376,4096]{1,0:T(8,128)(2,1)} %bitcast.15, ...), custom_call_target="tpu_custom_call", output_to_operand_aliasing={{1}: (6, {})} | custom-call | flops 1 | bytes 1 | tf_op jit(solution)/shard_map/blocks/pallas_call | solution.py:36
  67.0 0.0 collective-permute-done.5.refs_1_
  67.0 0.6 collective-permute-start.9
  67.6 0.4 collective-permute-start.6
  68.1 6.1 %blocks.5 = (bf16[2,512,512]{2,1,0:T(8,128)(2,1)S(1)}, f32[8,512]{1,0:T(8,128)S(1)}) custom-call(s32[2]{0:T(128)S(1)} %pad_add_fusion.1.refs_0_, bf16[512,1376]{1,0:T(8,128)(2,1)S(1)} %get-tuple-element.53.refs_1_, bf16[512,1376]{1,0:T(8,128)(2,1)S(1)} %get-tuple-element.54.refs_2_, bf16[1376,4096]{1,0:T(8,128)(2,1)} %bitcast.16, ...), custom_call_target="tpu_custom_call", output_to_operand_aliasing={{1}: (6, {})} | custom-call | flops 1 | bytes 1 | tf_op jit(solution)/shard_map/blocks/pallas_call | solution.py:36
  74.2 0.0 collective-permute-done.6.refs_1_
  74.2 0.1 collective-permute-start.7
  74.3 2.7 %collective-permute-start.8 = (f32[8,4224]{1,0:T(8,128)S(1)}, f32[8,4224]{1,0:T(8,128)S(1)}, u32[]{:S(2)}, u32[]{:S(2)}) collective-permute-start(f32[8,4224]{1,0:T(8,128)S(1)} %get-tuple-element.70.refs_6_.refs_0_), channel_id=1, source_target_pairs={{0,4},{1,5},{2,6},{3,7},{4,0},{5,1},{6,2},{7,3},{8,12},{9,13},{10,... | collective-permute-start | bytes 405512 | tf_op jit(solution)/shard_map/ppermute | solution.py:582
  77.0 0.1 pad_add_fusion.refs_0_
  77.1 6.1 %blocks.6 = (bf16[512,512]{1,0:T(8,128)(2,1)S(1)}, bf16[512,512]{1,0:T(8,128)(2,1)S(1)}, f32[8,512]{1,0:T(8,128)S(1)}) custom-call(s32[2]{0:T(128)S(1)} %pad_add_fusion.refs_0_, bf16[512,1376]{1,0:T(8,128)(2,1)S(1)} %get-tuple-element.53.refs_1_, bf16[512,1376]{1,0:T(8,128)(2,1)S(1)} %get-tuple-element.54.refs_2_, ...), custom_call_target="tpu_custom_call", output_to_operand_aliasing={{2}: (7, {})} | custom-call | flops 1 | bytes 1 | tf_op jit(solution)/shard_map/blocks/pallas_call | solution.py:36
  83.1 0.2 collective-permute-done.8.refs_1_
  83.4 2.3 %collective-permute-start.10 = (bf16[512,512]{1,0:T(8,128)(2,1)S(1)}, bf16[512,512]{1,0:T(8,128)(2,1)S(1)}, u32[]{:S(2)}, u32[]{:S(2)}) collective-permute-start(bf16[512,512]{1,0:T(8,128)(2,1)S(1)} %get-tuple-element.79), channel_id=1, source_target_pairs={{0,2},{1,3},{2,0},{3,1},{4,6},{5,7},{6,4},{7,5},{8,10},{9,11},{10,... | collective-permute-start | bytes 1572872 | tf_op jit(solution)/shard_map/ppermute | solution.py:582
  85.7 0.5 collective-permute-start.11
  86.2 6.8 %blocks.7 = (bf16[512,512]{1,0:T(8,128)(2,1)S(1)}, bf16[512,512]{1,0:T(8,128)(2,1)}, f32[8,512]{1,0:T(8,128)S(1)}) custom-call(s32[2]{0:T(128)S(1)} %pad_add_fusion.refs_0_, bf16[512,1376]{1,0:T(8,128)(2,1)S(1)} %get-tuple-element.53.refs_1_, bf16[512,1376]{1,0:T(8,128)(2,1)S(1)} %get-tuple-element.54.refs_2_, ...), custom_call_target="tpu_custom_call", output_to_operand_aliasing={{2}: (7, {})} | custom-call | flops 1 | bytes 1 | tf_op jit(solution)/shard_map/blocks/pallas_call | solution.py:36
  93.0 0.0 collective-permute-done.12.refs_5_
  93.0 0.7 slice_add_fusion.refs_2_
  93.7 1.6 %collective-permute-start.14 = (f32[8,4224]{1,0:T(8,128)S(1)}, f32[8,4224]{1,0:T(8,128)S(1)}, u32[]{:S(2)}, u32[]{:S(2)}) collective-permute-start(f32[8,4224]{1,0:T(8,128)S(1)} %get-tuple-element.83.refs_0_), channel_id=1, source_target_pairs={{0,16},{8,24},{16,0},{24,8},{1,17},{9,25},{17,1},{25,9},{2,18},{10... | collective-permute-start | bytes 405512 | tf_op jit(solution)/shard_map/ppermute | solution.py:582
  95.3 3.4 %collective-permute-done.14.refs_1_ = f32[8,4224]{1,0:T(8,128)S(1)} collective-permute-done((f32[8,4224]{1,0:T(8,128)S(1)}, f32[8,4224]{1,0:T(8,128)S(1)}, u32[]{:S(2)}, u32[]{:S(2)}) %collective-permute-start.14) | collective-permute-done | bytes 135200 | tf_op jit(solution)/shard_map/ppermute | solution.py:582
  98.8 0.0 copy-start.3
  98.8 0.1 join.2
  99.0 0.6 copy-done.1
  99.6 4.3 %factors.1 = (bf16[1376,32]{1,0:T(8,128)(2,1)}, bf16[32,4096]{1,0:T(8,128)(2,1)}, bf16[1376,512]{1,0:T(8,128)(2,1)}, bf16[1376,512]{1,0:T(8,128)(2,1)}) custom-call(f32[8,4224]{1,0:T(8,128)} %copy-done.3, f32[8,1376]{1,0:T(8,128)} %copy-done.5, f32[8,512]{1,0:T(8,128)} %copy-done.1, ...), custom_call_target="tpu_custom_call", output_to_operand_aliasing={{2}: (3, {}), {3}: (4, {})} | custom-call | flops 1 | bytes 1 | tf_op jit(solution)/shard_map/factors/pallas_call | solution.py:36
  103.9 1.5 %collective-permute-start.17 = (bf16[1376,512]{1,0:T(8,128)(2,1)}, bf16[1376,512]{1,0:T(8,128)(2,1)}, u32[]{:S(2)}, u32[]{:S(2)}) collective-permute-start(bf16[1376,512]{1,0:T(8,128)(2,1)} %get-tuple-element.91.refs_7_), channel_id=1, source_target_pairs={{0,8},{8,0},{16,24},{24,16},{1,9},{9,1},{17,25},{25,17},{2,10},{10... | collective-permute-start | bytes 4227080 | tf_op jit(solution)/shard_map/ppermute | solution.py:582
  105.4 1.5 collective-permute-start.18
  106.9 0.3 collective-permute-start.16
  107.3 2.8 %collective-permute-start.15 = (bf16[512,512]{1,0:T(8,128)(2,1)}, bf16[512,512]{1,0:T(8,128)(2,1)S(1)}, u32[]{:S(2)}, u32[]{:S(2)}) collective-permute-start(bf16[512,512]{1,0:T(8,128)(2,1)} %copy-done.6), channel_id=1, source_target_pairs={{0,4},{1,5},{2,6},{3,7},{4,0},{5,1},{6,2},{7,3},{8,12},{9,13},{10,... | collective-permute-start | bytes 1572872 | tf_op jit(solution)/shard_map/ppermute | solution.py:582
  110.1 0.7 stack.54.refs_0_
  110.8 15.1 %error.1.refs_9_ = bf16[1,1376,4096]{2,1,0:T(8,128)(2,1)} custom-call(bf16[1376,512]{1,0:T(8,128)(2,1)} %copy-done, bf16[512,4096]{1,0:T(8,128)(2,1)} %refs_1_.4, bf16[1376,32]{1,0:T(8,128)(2,1)} %get-tuple-element.93.refs_2_.refs_4_, bf16[32,4096]{1,0:T(8,128)(2,1)} %get-tuple-element.94.refs_3_.refs_5_, bf16[1,1376,4096]{2,1,0:T(8,128)(2,1)} %refs_7_.3, ...), custom_call_target="tpu_custom_call" | custom-call | flops 1 | bytes 1 | tf_op jit(solution)/shard_map/error/pallas_call | solution.py:36
  125.9 18.3 %update.1 = (f32[1376,1024]{1,0:T(8,128)}, bf16[1376,4096]{1,0:T(8,128)(2,1)}, f32[8,512]{1,0:T(8,128)}) custom-call(s32[6]{0:T(128)} %stack.54.refs_0_, f32[1376,1024]{1,0:T(8,128)} %refs_1_.5, bf16[1376,32]{1,0:T(8,128)(2,1)} %get-tuple-element.93.refs_2_.refs_4_, ...), custom_call_target="tpu_custom_call", output_to_operand_aliasing={{2}: (10, {})} | custom-call | flops 1 | bytes 1 | tf_op jit(solution)/shard_map/update/pallas_call | solution.py:36
  144.2 5.4 %last.1 = (bf16[1376,4096]{1,0:T(8,128)(2,1)}, f32[8,512]{1,0:T(8,128)}) custom-call(s32[1]{0:T(128)} %bitcast.6.refs_0_, bf16[1376,512]{1,0:T(8,128)(2,1)} %collective-permute-done.17.refs_1_, bf16[1376,512]{1,0:T(8,128)(2,1)} %collective-permute-done.18.refs_2_, bf16[1376,4096]{1,0:T(8,128)(2,1)} %refs_3_.1, ...), custom_call_target="tpu_custom_call", output_to_operand_aliasing={{1}: (7, {}), {0}: (6, {})} | custom-call | flops 1 | bytes 1 | tf_op jit(solution)/shard_map/last/pallas_call | solution.py:36
  149.6 0.7 copy-done.2
  150.3 1.0 join.3
  (31 shorter events, 0.2 us)
Async XLA Ops:
  0.6 7.0 %copy-start.4 = (f32[4096,8]{0,1:T(8,128)S(1)}, f32[4096,8]{0,1:T(8,128)}, u32[]{:S(2)}) copy-start(f32[4096,8]{0,1:T(8,128)} %param.15) | copy-start | bytes 393220
  4.6 42.8 %collective-permute-start.4 = (bf16[1376,512]{1,0:T(8,128)(2,1)S(1)}, bf16[1376,512]{1,0:T(8,128)(2,1)S(1)}, u32[]{:S(2)}, u32[]{:S(2)}) collective-permute-start(bf16[1376,512]{1,0:T(8,128)(2,1)S(1)} %get-tuple-element.57), channel_id=1, source_target_pairs={{0,8},{8,0},{16,24},{24,16},{1,9},{9,1},{17,25},{25,17},{2,10},{10... | collective-permute-start | bytes 4227080 | tf_op jit(solution)/shard_map/ppermute | solution.py:582
  6.1 41.3 %collective-permute-start.3 = (bf16[1376,512]{1,0:T(8,128)(2,1)S(1)}, bf16[1376,512]{1,0:T(8,128)(2,1)S(1)}, u32[]{:S(2)}, u32[]{:S(2)}) collective-permute-start(bf16[1376,512]{1,0:T(8,128)(2,1)S(1)} %get-tuple-element.52.refs_7_), channel_id=1, source_target_pairs={{0,16},{8,24},{16,0},{24,8},{1,17},{9,25},{17,1},{25,9},{2,18},{10... | collective-permute-start | bytes 4227080 | tf_op jit(solution)/shard_map/ppermute | solution.py:582
  43.9 14.5 %copy-start = (bf16[1376,512]{1,0:T(8,128)(2,1)}, bf16[1376,512]{1,0:T(8,128)(2,1)S(1)}, u32[]{:S(2)}) copy-start(bf16[1376,512]{1,0:T(8,128)(2,1)S(1)} %get-tuple-element.56.refs_8_.refs_0_) | copy-start | bytes 4227076
  43.9 5.1 %collective-permute-start.2 = (f32[8,1376]{1,0:T(8,128)S(1)}, f32[8,1376]{1,0:T(8,128)S(1)}, u32[]{:S(2)}, u32[]{:S(2)}) collective-permute-start(f32[8,1376]{1,0:T(8,128)S(1)} %get-tuple-element.55.refs_0_), channel_id=1, source_target_pairs={{0,24},{8,16},{16,8},{24,0},{1,25},{9,17},{17,9},{25,1},{2,26},{10... | collective-permute-start | bytes 132104 | tf_op jit(solution)/shard_map/ppermute | solution.py:582
  44.4 4.5 %collective-permute-start.1 = (f32[8,1376]{1,0:T(8,128)S(1)}, f32[8,1376]{1,0:T(8,128)S(1)}, u32[]{:S(2)}, u32[]{:S(2)}) collective-permute-start(f32[8,1376]{1,0:T(8,128)S(1)} %get-tuple-element.55.refs_0_), channel_id=1, source_target_pairs={{0,16},{8,24},{16,0},{24,8},{1,17},{9,25},{17,1},{25,9},{2,18},{10... | collective-permute-start | bytes 132104 | tf_op jit(solution)/shard_map/ppermute | solution.py:582
  46.0 4.0 %collective-permute-start = (f32[8,1376]{1,0:T(8,128)S(1)}, f32[8,1376]{1,0:T(8,128)S(1)}, u32[]{:S(2)}, u32[]{:S(2)}) collective-permute-start(f32[8,1376]{1,0:T(8,128)S(1)} %get-tuple-element.55.refs_0_), channel_id=1, source_target_pairs={{0,8},{8,0},{16,24},{24,16},{1,9},{9,1},{17,25},{25,17},{2,10},{10... | collective-permute-start | bytes 132104 | tf_op jit(solution)/shard_map/ppermute | solution.py:582
  47.4 2.6 %copy-start.7 = (bf16[1376,512]{1,0:T(8,128)(2,1)}, bf16[1376,512]{1,0:T(8,128)(2,1)S(1)}, u32[]{:S(2)}) copy-start(bf16[1376,512]{1,0:T(8,128)(2,1)S(1)} %collective-permute-done.4.refs_4_) | copy-start | bytes 4227076
  47.5 10.9 %copy-start.8 = (bf16[1376,512]{1,0:T(8,128)(2,1)}, bf16[1376,512]{1,0:T(8,128)(2,1)S(1)}, u32[]{:S(2)}) copy-start(bf16[1376,512]{1,0:T(8,128)(2,1)S(1)} %collective-permute-done.3.refs_3_) | copy-start | bytes 4227076
  58.3 0.6 copy-start.5
  59.0 34.0 %collective-permute-start.12 = (bf16[1376,512]{1,0:T(8,128)(2,1)}, bf16[1376,512]{1,0:T(8,128)(2,1)}, u32[]{:S(2)}, u32[]{:S(2)}) collective-permute-start(bf16[1376,512]{1,0:T(8,128)(2,1)} %get-tuple-element.80), channel_id=1, source_target_pairs={{0,8},{8,0},{16,24},{24,16},{1,9},{9,1},{17,25},{25,17},{2,10},{10... | collective-permute-start | bytes 4227080 | tf_op jit(solution)/shard_map/ppermute | solution.py:582
  60.5 32.5 %collective-permute-start.13 = (bf16[1376,512]{1,0:T(8,128)(2,1)}, bf16[1376,512]{1,0:T(8,128)(2,1)}, u32[]{:S(2)}, u32[]{:S(2)}) collective-permute-start(bf16[1376,512]{1,0:T(8,128)(2,1)} %get-tuple-element.81), channel_id=1, source_target_pairs={{0,16},{8,24},{16,0},{24,8},{1,17},{9,25},{17,1},{25,9},{2,18},{10... | collective-permute-start | bytes 4227080 | tf_op jit(solution)/shard_map/ppermute | solution.py:582
  61.0 6.0 %collective-permute-start.5 = (f32[8,4224]{1,0:T(8,128)S(1)}, f32[8,4224]{1,0:T(8,128)S(1)}, u32[]{:S(2)}, u32[]{:S(2)}) collective-permute-start(f32[8,4224]{1,0:T(8,128)S(1)} %get-tuple-element.61.refs_5_.refs_0_), channel_id=1, source_target_pairs={{0,1},{1,0},{2,3},{3,2},{4,5},{5,4},{6,7},{7,6},{8,9},{9,8},{10,11... | collective-permute-start | bytes 405512 | tf_op jit(solution)/shard_map/ppermute | solution.py:582
  67.0 10.0 %collective-permute-start.9 = (bf16[2,512,512]{2,1,0:T(8,128)(2,1)S(1)}, bf16[2,512,512]{2,1,0:T(8,128)(2,1)S(1)}, u32[]{:S(2)}, u32[]{:S(2)}) collective-permute-start(bf16[2,512,512]{2,1,0:T(8,128)(2,1)S(1)} %get-tuple-element.71), channel_id=1, source_target_pairs={{0,1},{1,0},{2,3},{3,2},{4,5},{5,4},{6,7},{7,6},{8,9},{9,8},{10,11... | collective-permute-start | bytes 3145736 | tf_op jit(solution)/shard_map/ppermute | solution.py:582
  67.6 6.6 %collective-permute-start.6 = (f32[8,4224]{1,0:T(8,128)S(1)}, f32[8,4224]{1,0:T(8,128)S(1)}, u32[]{:S(2)}, u32[]{:S(2)}) collective-permute-start(f32[8,4224]{1,0:T(8,128)S(1)} %get-tuple-element.65.refs_5_.refs_0_), channel_id=1, source_target_pairs={{0,2},{1,3},{2,0},{3,1},{4,6},{5,7},{6,4},{7,5},{8,10},{9,11},{10,... | collective-permute-start | bytes 405512 | tf_op jit(solution)/shard_map/ppermute | solution.py:582
  74.2 11.9 %collective-permute-start.7 = (bf16[2,512,512]{2,1,0:T(8,128)(2,1)S(1)}, bf16[2,512,512]{2,1,0:T(8,128)(2,1)S(1)}, u32[]{:S(2)}, u32[]{:S(2)}) collective-permute-start(bf16[2,512,512]{2,1,0:T(8,128)(2,1)S(1)} %get-tuple-element.69), channel_id=1, source_target_pairs={{0,1},{1,0},{2,3},{3,2},{4,5},{5,4},{6,7},{7,6},{8,9},{9,8},{10,11... | collective-permute-start | bytes 3145736 | tf_op jit(solution)/shard_map/ppermute | solution.py:582
  74.3 9.0 %collective-permute-start.8 = (f32[8,4224]{1,0:T(8,128)S(1)}, f32[8,4224]{1,0:T(8,128)S(1)}, u32[]{:S(2)}, u32[]{:S(2)}) collective-permute-start(f32[8,4224]{1,0:T(8,128)S(1)} %get-tuple-element.70.refs_6_.refs_0_), channel_id=1, source_target_pairs={{0,4},{1,5},{2,6},{3,7},{4,0},{5,1},{6,2},{7,3},{8,12},{9,13},{10,... | collective-permute-start | bytes 405512 | tf_op jit(solution)/shard_map/ppermute | solution.py:582
  83.4 15.5 %collective-permute-start.10 = (bf16[512,512]{1,0:T(8,128)(2,1)S(1)}, bf16[512,512]{1,0:T(8,128)(2,1)S(1)}, u32[]{:S(2)}, u32[]{:S(2)}) collective-permute-start(bf16[512,512]{1,0:T(8,128)(2,1)S(1)} %get-tuple-element.79), channel_id=1, source_target_pairs={{0,2},{1,3},{2,0},{3,1},{4,6},{5,7},{6,4},{7,5},{8,10},{9,11},{10,... | collective-permute-start | bytes 1572872 | tf_op jit(solution)/shard_map/ppermute | solution.py:582
  85.7 8.0 %collective-permute-start.11 = (f32[8,4224]{1,0:T(8,128)S(1)}, f32[8,4224]{1,0:T(8,128)S(1)}, u32[]{:S(2)}, u32[]{:S(2)}) collective-permute-start(f32[8,4224]{1,0:T(8,128)S(1)} %get-tuple-element.75.refs_6_.refs_0_), channel_id=1, source_target_pairs={{0,8},{8,0},{16,24},{24,16},{1,9},{9,1},{17,25},{25,17},{2,10},{10... | collective-permute-start | bytes 405512 | tf_op jit(solution)/shard_map/ppermute | solution.py:582
  93.7 5.1 %collective-permute-start.14 = (f32[8,4224]{1,0:T(8,128)S(1)}, f32[8,4224]{1,0:T(8,128)S(1)}, u32[]{:S(2)}, u32[]{:S(2)}) collective-permute-start(f32[8,4224]{1,0:T(8,128)S(1)} %get-tuple-element.83.refs_0_), channel_id=1, source_target_pairs={{0,16},{8,24},{16,0},{24,8},{1,17},{9,25},{17,1},{25,9},{2,18},{10... | collective-permute-start | bytes 405512 | tf_op jit(solution)/shard_map/ppermute | solution.py:582
  98.8 0.8 copy-start.3
  99.0 0.6 copy-start.1
  99.6 4.3 %copy-start.6 = (bf16[512,512]{1,0:T(8,128)(2,1)}, bf16[512,512]{1,0:T(8,128)(2,1)S(1)}, u32[]{:S(2)}) copy-start(bf16[512,512]{1,0:T(8,128)(2,1)S(1)} %get-tuple-element.87) | copy-start | bytes 1572868
  103.9 40.3 %collective-permute-start.17 = (bf16[1376,512]{1,0:T(8,128)(2,1)}, bf16[1376,512]{1,0:T(8,128)(2,1)}, u32[]{:S(2)}, u32[]{:S(2)}) collective-permute-start(bf16[1376,512]{1,0:T(8,128)(2,1)} %get-tuple-element.91.refs_7_), channel_id=1, source_target_pairs={{0,8},{8,0},{16,24},{24,16},{1,9},{9,1},{17,25},{25,17},{2,10},{10... | collective-permute-start | bytes 4227080 | tf_op jit(solution)/shard_map/ppermute | solution.py:582
  105.4 38.8 %collective-permute-start.18 = (bf16[1376,512]{1,0:T(8,128)(2,1)}, bf16[1376,512]{1,0:T(8,128)(2,1)}, u32[]{:S(2)}, u32[]{:S(2)}) collective-permute-start(bf16[1376,512]{1,0:T(8,128)(2,1)} %get-tuple-element.92.refs_6_), channel_id=1, source_target_pairs={{0,16},{8,24},{16,0},{24,8},{1,17},{9,25},{17,1},{25,9},{2,18},{10... | collective-permute-start | bytes 4227080 | tf_op jit(solution)/shard_map/ppermute | solution.py:582
  106.9 42.7 %collective-permute-start.16 = (bf16[512,512]{1,0:T(8,128)(2,1)}, bf16[512,512]{1,0:T(8,128)(2,1)S(1)}, u32[]{:S(2)}, u32[]{:S(2)}) collective-permute-start(bf16[512,512]{1,0:T(8,128)(2,1)} %get-tuple-element.88), channel_id=1, source_target_pairs={{0,2},{1,3},{2,0},{3,1},{4,6},{5,7},{6,4},{7,5},{8,10},{9,11},{10,... | collective-permute-start | bytes 1572872 | tf_op jit(solution)/shard_map/ppermute | solution.py:582
  107.3 42.4 %collective-permute-start.15 = (bf16[512,512]{1,0:T(8,128)(2,1)}, bf16[512,512]{1,0:T(8,128)(2,1)S(1)}, u32[]{:S(2)}, u32[]{:S(2)}) collective-permute-start(bf16[512,512]{1,0:T(8,128)(2,1)} %copy-done.6), channel_id=1, source_target_pairs={{0,4},{1,5},{2,6},{3,7},{4,0},{5,1},{6,2},{7,3},{8,12},{9,13},{10,... | collective-permute-start | bytes 1572872 | tf_op jit(solution)/shard_map/ppermute | solution.py:582
  149.6 0.7 copy-start.2

commit v9 on v6

--- a/solution.py
+++ b/solution.py
@@ -408,90 +408,70 @@
     )
 
 
-def error_kernel(hid_ref, dy_ref, l_ref, r_ref, *refs):
-    errs, out_ref = refs[:-1], refs[-1]
-    width = errs[0].shape[2]
-    for part, err_ref in enumerate(errs):
-        at = slice(part * width, (part + 1) * width)
-        grown = dot(hid_ref[...], dy_ref[:, at]) + err_ref[0].astype(F32)
-        out_ref[0, :, at] = (grown - dot(l_ref[...], r_ref[:, at])).astype(BF16)
-
-
-def error_call(hid, dy, err, l, r, **links):
-    units, tok = hid.shape
-    depth = dy.shape[1]
-    tile = 352 if units > 512 else units
-    return launch(
-        error_kernel,
-        "error",
-        (pl.cdiv(units, tile),),
-        [hid, dy, l, r] + [err] * STREAMS,
-        [
-            pl.BlockSpec((tile, tok), lambda f: (f, 0)),
-            whole(dy.shape),
-            pl.BlockSpec((tile, SPLIT), lambda f: (f, 0)),
-            whole(r.shape),
-            *error_streams(tile, depth),
-        ],
-        [pl.BlockSpec((1, tile, depth), lambda f: (0, f, 0))],
-        [shaped(err.shape, BF16)],
-        vmem=LARGE,
-        **links,
-    )
-
-
 def updated(w, mom, approx):
     return (w.astype(F32) - 0.1 * (0.9 * mom.astype(F32) + approx)).astype(BF16)
 
 
-def update_kernel(own, at_ref, mom_ref, l_ref, r_ref, w_ref, *refs):
-    pieces, (mom_out, w_out) = refs[:-2], refs[-2:]
+def final_kernel(early, own, at_ref, hid_ref, dy_ref, err_ref, l_ref, r_ref, w_ref, mom_ref, *refs):
+    pieces, (err_out, w_out, mom_out) = refs[:-3], refs[-3:]
     step = pl.program_id(0)
-
-    @pl.when(step < own)
+    approx = dot(l_ref[...], r_ref[...])
+    grown = dot(hid_ref[...], dy_ref[...]) + err_ref[0].astype(F32)
+    err_out[0] = (grown - approx).astype(BF16)
+
+    @pl.when((step >= early) & (step < early + own))
     def _():
-        approx = dot(l_ref[...], r_ref[...])
         mom = mom_ref[...]
         mom_out[...] = 0.9 * mom + approx
         w_out[...] = updated(w_ref[...], mom.astype(BF16), approx)
 
     for slot, piece in enumerate(pieces):
 
-        @pl.when(step == own + slot)
+        @pl.when(step == early + own + slot)
         def _(piece=piece):
-            w_out[...] = updated(w_ref[...], piece[...], dot(l_ref[...], r_ref[...]))
-
-
-def update_call(at, mom, pieces, w, l, r, **links):
-    units, cols = mom.shape
+            w_out[...] = updated(w_ref[...], piece[...], approx)
+
+
+def final_call(at, early, hid, dy, err, l, r, w, mom, pieces, **links):
+    units, tok = hid.shape
+    cols = mom.shape[1]
     half = pieces[0].shape[1]
     own = cols // half
     tile = units // 2 if units % 32 == 0 and units > 512 else units
     tiles = units // tile
-
-    def during(low, high, column):
+    count = dy.shape[1] // half
+
+    def place(c, at):
+        return 2 * (at[0] ^ ((c // own + 3) % 4)) + c % own
+
+    def held_to(low, high, column):
         def index(c, f, at):
             row = jnp.where(c < low, 0, jnp.where(c > high, tiles - 1, f))
-            return row, column(jnp.clip(c, low, high))
+            return row, column(jnp.clip(c, low, high), at)
 
         return pl.BlockSpec((tile, half), index)
 
-    momenta = during(0, own - 1, lambda c: c)
-    weights = pl.BlockSpec((tile, half), lambda c, f, at: (f, at[c]))
-    return launch(
-        functools.partial(update_kernel, own),
-        "update",
-        (own + len(pieces), tiles),
-        [mom, l, r, w, *pieces],
+    weights = held_to(early, count - 1, place)
+    momenta = held_to(early, early + own - 1, lambda c, at: c - early)
+    arrived = [held_to(early + own + s, early + own + s, lambda c, at: 0) for s in range(len(pieces))]
+    error = pl.BlockSpec((1, tile, half), lambda c, f, at: (0, f, place(c, at)))
+    return launch(
+        functools.partial(final_kernel, early, own),
+        "final",
+        (count, tiles),
+        [hid, dy, err, l, r, w, mom, *pieces],
         [
+            pl.BlockSpec((tile, tok), lambda c, f, at: (f, 0)),
+            pl.BlockSpec((tok, half), lambda c, f, at: (0, place(c, at))),
+            error,
+            pl.BlockSpec((tile, SPLIT), lambda c, f, at: (f, 0)),
+            pl.BlockSpec((SPLIT, half), lambda c, f, at: (0, place(c, at))),
+            weights,
             momenta,
-            pl.BlockSpec((tile, SPLIT), lambda c, f, at: (f, 0)),
-            pl.BlockSpec((SPLIT, half), lambda c, f, at: (0, at[c])),
-            weights,
-            *[during(own + s, own + s, lambda c: 0) for s in range(len(pieces))],
-        ],
-        [momenta, weights],
-        [shaped(mom.shape, F32), shaped(w.shape, BF16)],
+            *arrived,
+        ],
+        [error, weights, momenta],
+        [shaped(err.shape, BF16), shaped(w.shape, BF16), shaped(mom.shape, F32)],
         places=[at],
         vmem=LARGE,
         **links,
@@ -626,17 +606,17 @@
     else:
         landed = [exchange(mine[slot], "mp", 2 * slot) for slot in range(1, count)]
 
-    (next_err,) = error_call(hid, out_grads, err_down, l, r)
-    keys = [(1, 0), (1, 1), (2, 0), (2, 1)]
-    at = jnp.stack([2 * (rank_dp ^ mask) + side for mask, side in [(0, 0), (0, 1)] + keys])
-    next_mom, new, order = update_call(
-        at.astype(jnp.int32),
-        mom_down,
-        [got[key] for key in keys],
-        w_down,
+    next_err, new, next_mom, order = final_call(
+        jnp.reshape(rank_dp, (1,)).astype(jnp.int32),
+        2,
+        hid,
+        out_grads,
+        err_down,
         l,
         r,
-        held=[next_err],
+        w_down,
+        mom_down,
+        [got[key] for key in [(1, 0), (1, 1), (2, 0), (2, 1)]],
         through=[order],
     )
     far = jnp.reshape(rank_dp ^ 3, (1,)).astype(jnp.int32)

time: 152 us -> 151 us (level)
    pallas_call x18 -> x17, Pallas kernels: 117 us -> 116 us  [launch(): pl.pallas_call(inner, grid_spec=pltpu.PrefetchScalarGridSpec(num_scalar_p...]
where the time goes in v9:
time: 151 us; the launch traced here: 150 us
  Pallas kernels  116 us (77%)
  starting transfers between devices  23 us (15%)
  waiting for transfers between devices  5.54 us (4%)
  local copies, waits for them, and re-layouts  2.74 us (2%)
  other arithmetic  1.53 us (1%)
    pallas_call x17, Pallas kernels, launch(): pl.pallas_call(inner, grid_spec=pltpu.PrefetchScalarGridSpec(num_scalar_p...  116 us
    ppermute x19, starting transfers between devices, exchange(): return lax.ppermute(value, axis, [(i, i ^ mask) for i in range(size)])  23 us
    ppermute x19, waiting for transfers between devices, exchange(): return lax.ppermute(value, axis, [(i, i ^ mask) for i in range(size)])  5.54 us
  transfers between devices with their start and end apart: 19, of which 4 were waited for; matrix products, arithmetic and copies ran while one was open for 1% of the time, Pallas kernels for 66%

profile of v9, /device:TPU:8, one launch (start us, length us, event | category | flops | bytes accessed | tf_op | source)
XLA Modules:
  0.0 149.6 jit_solution(4470940536275233430)
XLA Ops:
  0.6 4.0 %cast.1 = (bf16[1376,512]{1,0:T(8,128)(2,1)S(1)}, bf16[1376,512]{1,0:T(8,128)(2,1)S(1)}, bf16[1376,512]{1,0:T(8,128)(2,1)}, bf16[1376,512]{1,0:T(8,128)(2,1)}) custom-call(f32[1376,1024]{1,0:T(8,128)} %refs_7_.3), custom_call_target="tpu_custom_call" | custom-call | flops 1 | bytes 1 | tf_op jit(solution)/shard_map/cast/pallas_call | solution.py:36
  4.6 1.5 collective-permute-start.4
  6.1 1.5 %collective-permute-start.3 = (bf16[1376,512]{1,0:T(8,128)(2,1)S(1)}, bf16[1376,512]{1,0:T(8,128)(2,1)}, u32[]{:S(2)}, u32[]{:S(2)}) collective-permute-start(bf16[1376,512]{1,0:T(8,128)(2,1)S(1)} %get-tuple-element.53.refs_7_), channel_id=1, source_target_pairs={{0,16},{8,24},{16,0},{24,8},{1,17},{9,25},{17,1},{25,9},{2,18},{10... | collective-permute-start | bytes 4227080 | tf_op jit(solution)/shard_map/ppermute | solution.py:517
  7.6 35.1 %hidden.1 = (bf16[1376,512]{1,0:T(8,128)(2,1)S(1)}, bf16[512,1376]{1,0:T(8,128)(2,1)S(1)}, bf16[512,1376]{1,0:T(8,128)(2,1)S(1)}, f32[8,1376]{1,0:T(8,128)S(1)}, f32[8,512]{1,0:T(8,128)S(1)}) custom-call(bf16[512,4096]{1,0:T(8,128)(2,1)} %refs_0_.3, bf16[1376,4096]{1,0:T(8,128)(2,1)} %bitcast.9, bf16[1376,4096]{1,0:T(8,128)(2,1)} %bitcast.14, ...), custom_call_target="tpu_custom_call" | custom-call | flops 1 | bytes 1 | tf_op jit(solution)/shard_map/hidden/pallas_call | solution.py:36
  42.8 0.6 collective-permute-start.2
  43.3 1.5 %collective-permute-start.1 = (f32[8,1376]{1,0:T(8,128)S(1)}, f32[8,1376]{1,0:T(8,128)S(1)}, u32[]{:S(2)}, u32[]{:S(2)}) collective-permute-start(f32[8,1376]{1,0:T(8,128)S(1)} %get-tuple-element.56.refs_0_), channel_id=1, source_target_pairs={{0,16},{8,24},{16,0},{24,8},{1,17},{9,25},{17,1},{25,9},{2,18},{10... | collective-permute-start | bytes 132104 | tf_op jit(solution)/shard_map/ppermute | solution.py:517
  44.8 1.5 collective-permute-start
  46.3 0.0 collective-permute-done.4.refs_4_
  46.3 0.0 collective-permute-done.3.refs_3_
  46.3 0.7 slice_add_fusion.1.refs_10_
  47.0 0.8 collective-permute-done.2.refs_3_
  47.8 0.0 collective-permute-done.1.refs_2_
  47.8 1.0 collective-permute-done.refs_1_
  48.9 8.3 %right.1 = (f32[8,4224]{1,0:T(8,128)S(1)}, f32[8,1376]{1,0:T(8,128)S(1)}, f32[8,512]{1,0:T(8,128)S(1)}, bf16[1376,512]{1,0:T(8,128)(2,1)}, bf16[1376,512]{1,0:T(8,128)(2,1)}) custom-call(f32[8,1376]{1,0:T(8,128)S(1)} %get-tuple-element.56.refs_0_, ...), custom_call_target="tpu_custom_call", output_to_operand_aliasing={{2}: (11, {}), {3}: (12, {}), {4}: (13, {})} | custom-call | flops 1 | bytes 1 | tf_op jit(solution)/shard_map/right/pallas_call | solution.py:36
  57.2 0.0 copy-start.5
  57.2 0.6 copy-done.5
  57.8 1.5 collective-permute-start.12
  59.3 0.5 collective-permute-start.13
  59.8 0.0 collective-permute-start.5
  59.8 0.1 pad_add_fusion.1.refs_0_
  59.9 6.0 %blocks.4 = (bf16[2,512,512]{2,1,0:T(8,128)(2,1)S(1)}, f32[8,512]{1,0:T(8,128)S(1)}) custom-call(s32[2]{0:T(128)S(1)} %pad_add_fusion.1.refs_0_, bf16[512,1376]{1,0:T(8,128)(2,1)S(1)} %get-tuple-element.54.refs_1_, bf16[512,1376]{1,0:T(8,128)(2,1)S(1)} %get-tuple-element.55.refs_2_, bf16[1376,4096]{1,0:T(8,128)(2,1)} %bitcast.10, ...), custom_call_target="tpu_custom_call", output_to_operand_aliasing={{1}: (6, {})} | custom-call | flops 1 | bytes 1 | tf_op jit(solution)/shard_map/blocks/pallas_call | solution.py:36
  65.9 0.6 collective-permute-start.9
  66.5 0.4 collective-permute-start.6
  66.9 6.0 %blocks.5 = (bf16[2,512,512]{2,1,0:T(8,128)(2,1)S(1)}, f32[8,512]{1,0:T(8,128)S(1)}) custom-call(s32[2]{0:T(128)S(1)} %pad_add_fusion.1.refs_0_, bf16[512,1376]{1,0:T(8,128)(2,1)S(1)} %get-tuple-element.54.refs_1_, bf16[512,1376]{1,0:T(8,128)(2,1)S(1)} %get-tuple-element.55.refs_2_, bf16[1376,4096]{1,0:T(8,128)(2,1)} %bitcast.11, ...), custom_call_target="tpu_custom_call", output_to_operand_aliasing={{1}: (6, {})} | custom-call | flops 1 | bytes 1 | tf_op jit(solution)/shard_map/blocks/pallas_call | solution.py:36
  72.9 0.1 collective-permute-start.7
  73.0 2.7 %collective-permute-start.8 = (f32[8,4224]{1,0:T(8,128)S(1)}, f32[8,4224]{1,0:T(8,128)S(1)}, u32[]{:S(2)}, u32[]{:S(2)}) collective-permute-start(f32[8,4224]{1,0:T(8,128)S(1)} %get-tuple-element.71.refs_6_.refs_0_), channel_id=1, source_target_pairs={{0,4},{1,5},{2,6},{3,7},{4,0},{5,1},{6,2},{7,3},{8,12},{9,13},{10,... | collective-permute-start | bytes 405512 | tf_op jit(solution)/shard_map/ppermute | solution.py:517
  75.7 0.1 pad_add_fusion.refs_0_
  75.7 6.1 %blocks.6 = (bf16[512,512]{1,0:T(8,128)(2,1)S(1)}, bf16[512,512]{1,0:T(8,128)(2,1)S(1)}, f32[8,512]{1,0:T(8,128)S(1)}) custom-call(s32[2]{0:T(128)S(1)} %pad_add_fusion.refs_0_, bf16[512,1376]{1,0:T(8,128)(2,1)S(1)} %get-tuple-element.54.refs_1_, bf16[512,1376]{1,0:T(8,128)(2,1)S(1)} %get-tuple-element.55.refs_2_, ...), custom_call_target="tpu_custom_call", output_to_operand_aliasing={{2}: (7, {})} | custom-call | flops 1 | bytes 1 | tf_op jit(solution)/shard_map/blocks/pallas_call | solution.py:36
  81.8 0.2 collective-permute-done.8.refs_1_
  82.0 2.3 %collective-permute-start.10 = (bf16[512,512]{1,0:T(8,128)(2,1)S(1)}, bf16[512,512]{1,0:T(8,128)(2,1)S(1)}, u32[]{:S(2)}, u32[]{:S(2)}) collective-permute-start(bf16[512,512]{1,0:T(8,128)(2,1)S(1)} %get-tuple-element.80), channel_id=1, source_target_pairs={{0,2},{1,3},{2,0},{3,1},{4,6},{5,7},{6,4},{7,5},{8,10},{9,11},{10,... | collective-permute-start | bytes 1572872 | tf_op jit(solution)/shard_map/ppermute | solution.py:517
  84.3 0.5 collective-permute-start.11
  84.8 6.8 %blocks.7 = (bf16[512,512]{1,0:T(8,128)(2,1)S(1)}, bf16[512,512]{1,0:T(8,128)(2,1)}, f32[8,512]{1,0:T(8,128)S(1)}) custom-call(s32[2]{0:T(128)S(1)} %pad_add_fusion.refs_0_, bf16[512,1376]{1,0:T(8,128)(2,1)S(1)} %get-tuple-element.54.refs_1_, bf16[512,1376]{1,0:T(8,128)(2,1)S(1)} %get-tuple-element.55.refs_2_, ...), custom_call_target="tpu_custom_call", output_to_operand_aliasing={{2}: (7, {})} | custom-call | flops 1 | bytes 1 | tf_op jit(solution)/shard_map/blocks/pallas_call | solution.py:36
  91.7 0.7 slice_add_fusion.refs_2_
  92.4 1.6 %collective-permute-start.14 = (f32[8,4224]{1,0:T(8,128)S(1)}, f32[8,4224]{1,0:T(8,128)S(1)}, u32[]{:S(2)}, u32[]{:S(2)}) collective-permute-start(f32[8,4224]{1,0:T(8,128)S(1)} %get-tuple-element.84.refs_0_), channel_id=1, source_target_pairs={{0,16},{8,24},{16,0},{24,8},{1,17},{9,25},{17,1},{25,9},{2,18},{10... | collective-permute-start | bytes 405512 | tf_op jit(solution)/shard_map/ppermute | solution.py:517
  94.0 3.4 %collective-permute-done.14.refs_1_ = f32[8,4224]{1,0:T(8,128)S(1)} collective-permute-done((f32[8,4224]{1,0:T(8,128)S(1)}, f32[8,4224]{1,0:T(8,128)S(1)}, u32[]{:S(2)}, u32[]{:S(2)}) %collective-permute-start.14) | collective-permute-done | bytes 135200 | tf_op jit(solution)/shard_map/ppermute | solution.py:517
  97.5 0.0 copy-start.3
  97.5 0.1 join.2
  97.6 0.6 copy-done.1
  98.2 0.8 copy-done.6
  99.0 4.2 %factors.1 = (bf16[1376,32]{1,0:T(8,128)(2,1)}, bf16[32,4096]{1,0:T(8,128)(2,1)}, bf16[1376,512]{1,0:T(8,128)(2,1)}, bf16[1376,512]{1,0:T(8,128)(2,1)}) custom-call(f32[8,4224]{1,0:T(8,128)} %copy-done.3, f32[8,1376]{1,0:T(8,128)} %copy-done.5, f32[8,512]{1,0:T(8,128)} %copy-done.1, ...), custom_call_target="tpu_custom_call", output_to_operand_aliasing={{2}: (3, {}), {3}: (4, {})} | custom-call | flops 1 | bytes 1 | tf_op jit(solution)/shard_map/factors/pallas_call | solution.py:36
  103.2 1.6 %collective-permute-start.17 = (bf16[1376,512]{1,0:T(8,128)(2,1)}, bf16[1376,512]{1,0:T(8,128)(2,1)}, u32[]{:S(2)}, u32[]{:S(2)}) collective-permute-start(bf16[1376,512]{1,0:T(8,128)(2,1)} %get-tuple-element.92.refs_10_), channel_id=1, source_target_pairs={{0,8},{8,0},{16,24},{24,16},{1,9},{9,1},{17,25},{25,17},{2,10},{10... | collective-permute-start | bytes 4227080 | tf_op jit(solution)/shard_map/ppermute | solution.py:517
  104.8 1.5 %collective-permute-start.18 = (bf16[1376,512]{1,0:T(8,128)(2,1)}, bf16[1376,512]{1,0:T(8,128)(2,1)}, u32[]{:S(2)}, u32[]{:S(2)}) collective-permute-start(bf16[1376,512]{1,0:T(8,128)(2,1)} %get-tuple-element.93.refs_9_), channel_id=1, source_target_pairs={{0,16},{8,24},{16,0},{24,8},{1,17},{9,25},{17,1},{25,9},{2,18},{10... | collective-permute-start | bytes 4227080 | tf_op jit(solution)/shard_map/ppermute | solution.py:517
  106.3 0.3 collective-permute-start.16
  106.6 2.8 %collective-permute-start.15 = (bf16[512,512]{1,0:T(8,128)(2,1)}, bf16[512,512]{1,0:T(8,128)(2,1)S(1)}, u32[]{:S(2)}, u32[]{:S(2)}) collective-permute-start(bf16[512,512]{1,0:T(8,128)(2,1)} %copy-done.6), channel_id=1, source_target_pairs={{0,4},{1,5},{2,6},{3,7},{4,0},{5,1},{6,2},{7,3},{8,12},{9,13},{10,... | collective-permute-start | bytes 1572872 | tf_op jit(solution)/shard_map/ppermute | solution.py:517
  109.4 33.1 %final.1 = (bf16[1,1376,4096]{2,1,0:T(8,128)(2,1)}, bf16[1376,4096]{1,0:T(8,128)(2,1)}, f32[1376,1024]{1,0:T(8,128)}, f32[8,512]{1,0:T(8,128)}) custom-call(s32[1]{0:T(128)} %bitcast.7.refs_0_, bf16[1376,512]{1,0:T(8,128)(2,1)} %copy-done, bf16[512,4096]{1,0:T(8,128)(2,1)} %refs_2_.1, ...), custom_call_target="tpu_custom_call", output_to_operand_aliasing={{3}: (12, {})} | custom-call | flops 1 | bytes 1 | tf_op jit(solution)/shard_map/final/pallas_call | solution.py:36
  142.5 5.4 %last.1 = (bf16[1376,4096]{1,0:T(8,128)(2,1)}, f32[8,512]{1,0:T(8,128)}) custom-call(s32[1]{0:T(128)} %bitcast.6.refs_0_, bf16[1376,512]{1,0:T(8,128)(2,1)} %collective-permute-done.17.refs_1_, bf16[1376,512]{1,0:T(8,128)(2,1)} %collective-permute-done.18.refs_2_, bf16[1376,4096]{1,0:T(8,128)(2,1)} %refs_3_.5, ...), custom_call_target="tpu_custom_call", output_to_operand_aliasing={{1}: (7, {}), {0}: (6, {})} | custom-call | flops 1 | bytes 1 | tf_op jit(solution)/shard_map/last/pallas_call | solution.py:36
  147.9 0.7 copy-done.2
  148.6 1.0 join.3
  (25 shorter events, 0.1 us)
Async XLA Ops:
  0.6 7.0 %copy-start.4 = (f32[4096,8]{0,1:T(8,128)S(1)}, f32[4096,8]{0,1:T(8,128)}, u32[]{:S(2)}) copy-start(f32[4096,8]{0,1:T(8,128)} %param.15) | copy-start | bytes 393220
  4.6 41.7 %collective-permute-start.4 = (bf16[1376,512]{1,0:T(8,128)(2,1)S(1)}, bf16[1376,512]{1,0:T(8,128)(2,1)}, u32[]{:S(2)}, u32[]{:S(2)}) collective-permute-start(bf16[1376,512]{1,0:T(8,128)(2,1)S(1)} %get-tuple-element.58), channel_id=1, source_target_pairs={{0,8},{8,0},{16,24},{24,16},{1,9},{9,1},{17,25},{25,17},{2,10},{10... | collective-permute-start | bytes 4227080 | tf_op jit(solution)/shard_map/ppermute | solution.py:517
  6.1 40.2 %collective-permute-start.3 = (bf16[1376,512]{1,0:T(8,128)(2,1)S(1)}, bf16[1376,512]{1,0:T(8,128)(2,1)}, u32[]{:S(2)}, u32[]{:S(2)}) collective-permute-start(bf16[1376,512]{1,0:T(8,128)(2,1)S(1)} %get-tuple-element.53.refs_7_), channel_id=1, source_target_pairs={{0,16},{8,24},{16,0},{24,8},{1,17},{9,25},{17,1},{25,9},{2,18},{10... | collective-permute-start | bytes 4227080 | tf_op jit(solution)/shard_map/ppermute | solution.py:517
  42.7 14.4 %copy-start = (bf16[1376,512]{1,0:T(8,128)(2,1)}, bf16[1376,512]{1,0:T(8,128)(2,1)S(1)}, u32[]{:S(2)}) copy-start(bf16[1376,512]{1,0:T(8,128)(2,1)S(1)} %get-tuple-element.57.refs_8_.refs_1_) | copy-start | bytes 4227076
  42.8 5.1 %collective-permute-start.2 = (f32[8,1376]{1,0:T(8,128)S(1)}, f32[8,1376]{1,0:T(8,128)S(1)}, u32[]{:S(2)}, u32[]{:S(2)}) collective-permute-start(f32[8,1376]{1,0:T(8,128)S(1)} %get-tuple-element.56.refs_0_), channel_id=1, source_target_pairs={{0,24},{8,16},{16,8},{24,0},{1,25},{9,17},{17,9},{25,1},{2,26},{10... | collective-permute-start | bytes 132104 | tf_op jit(solution)/shard_map/ppermute | solution.py:517
  43.3 4.5 %collective-permute-start.1 = (f32[8,1376]{1,0:T(8,128)S(1)}, f32[8,1376]{1,0:T(8,128)S(1)}, u32[]{:S(2)}, u32[]{:S(2)}) collective-permute-start(f32[8,1376]{1,0:T(8,128)S(1)} %get-tuple-element.56.refs_0_), channel_id=1, source_target_pairs={{0,16},{8,24},{16,0},{24,8},{1,17},{9,25},{17,1},{25,9},{2,18},{10... | collective-permute-start | bytes 132104 | tf_op jit(solution)/shard_map/ppermute | solution.py:517
  44.8 4.0 %collective-permute-start = (f32[8,1376]{1,0:T(8,128)S(1)}, f32[8,1376]{1,0:T(8,128)S(1)}, u32[]{:S(2)}, u32[]{:S(2)}) collective-permute-start(f32[8,1376]{1,0:T(8,128)S(1)} %get-tuple-element.56.refs_0_), channel_id=1, source_target_pairs={{0,8},{8,0},{16,24},{24,16},{1,9},{9,1},{17,25},{25,17},{2,10},{10... | collective-permute-start | bytes 132104 | tf_op jit(solution)/shard_map/ppermute | solution.py:517
  57.2 0.6 copy-start.5
  57.8 33.8 %collective-permute-start.12 = (bf16[1376,512]{1,0:T(8,128)(2,1)}, bf16[1376,512]{1,0:T(8,128)(2,1)}, u32[]{:S(2)}, u32[]{:S(2)}) collective-permute-start(bf16[1376,512]{1,0:T(8,128)(2,1)} %get-tuple-element.81), channel_id=1, source_target_pairs={{0,8},{8,0},{16,24},{24,16},{1,9},{9,1},{17,25},{25,17},{2,10},{10... | collective-permute-start | bytes 4227080 | tf_op jit(solution)/shard_map/ppermute | solution.py:517
  59.3 32.3 %collective-permute-start.13 = (bf16[1376,512]{1,0:T(8,128)(2,1)}, bf16[1376,512]{1,0:T(8,128)(2,1)}, u32[]{:S(2)}, u32[]{:S(2)}) collective-permute-start(bf16[1376,512]{1,0:T(8,128)(2,1)} %get-tuple-element.82), channel_id=1, source_target_pairs={{0,16},{8,24},{16,0},{24,8},{1,17},{9,25},{17,1},{25,9},{2,18},{10... | collective-permute-start | bytes 4227080 | tf_op jit(solution)/shard_map/ppermute | solution.py:517
  59.8 6.0 %collective-permute-start.5 = (f32[8,4224]{1,0:T(8,128)S(1)}, f32[8,4224]{1,0:T(8,128)S(1)}, u32[]{:S(2)}, u32[]{:S(2)}) collective-permute-start(f32[8,4224]{1,0:T(8,128)S(1)} %get-tuple-element.62.refs_5_.refs_0_), channel_id=1, source_target_pairs={{0,1},{1,0},{2,3},{3,2},{4,5},{5,4},{6,7},{7,6},{8,9},{9,8},{10,11... | collective-permute-start | bytes 405512 | tf_op jit(solution)/shard_map/ppermute | solution.py:517
  65.9 9.8 %collective-permute-start.9 = (bf16[2,512,512]{2,1,0:T(8,128)(2,1)S(1)}, bf16[2,512,512]{2,1,0:T(8,128)(2,1)S(1)}, u32[]{:S(2)}, u32[]{:S(2)}) collective-permute-start(bf16[2,512,512]{2,1,0:T(8,128)(2,1)S(1)} %get-tuple-element.72), channel_id=1, source_target_pairs={{0,1},{1,0},{2,3},{3,2},{4,5},{5,4},{6,7},{7,6},{8,9},{9,8},{10,11... | collective-permute-start | bytes 3145736 | tf_op jit(solution)/shard_map/ppermute | solution.py:517
  66.5 6.4 %collective-permute-start.6 = (f32[8,4224]{1,0:T(8,128)S(1)}, f32[8,4224]{1,0:T(8,128)S(1)}, u32[]{:S(2)}, u32[]{:S(2)}) collective-permute-start(f32[8,4224]{1,0:T(8,128)S(1)} %get-tuple-element.66.refs_5_.refs_0_), channel_id=1, source_target_pairs={{0,2},{1,3},{2,0},{3,1},{4,6},{5,7},{6,4},{7,5},{8,10},{9,11},{10,... | collective-permute-start | bytes 405512 | tf_op jit(solution)/shard_map/ppermute | solution.py:517
  72.9 11.9 %collective-permute-start.7 = (bf16[2,512,512]{2,1,0:T(8,128)(2,1)S(1)}, bf16[2,512,512]{2,1,0:T(8,128)(2,1)S(1)}, u32[]{:S(2)}, u32[]{:S(2)}) collective-permute-start(bf16[2,512,512]{2,1,0:T(8,128)(2,1)S(1)} %get-tuple-element.70), channel_id=1, source_target_pairs={{0,1},{1,0},{2,3},{3,2},{4,5},{5,4},{6,7},{7,6},{8,9},{9,8},{10,11... | collective-permute-start | bytes 3145736 | tf_op jit(solution)/shard_map/ppermute | solution.py:517
  73.0 9.0 %collective-permute-start.8 = (f32[8,4224]{1,0:T(8,128)S(1)}, f32[8,4224]{1,0:T(8,128)S(1)}, u32[]{:S(2)}, u32[]{:S(2)}) collective-permute-start(f32[8,4224]{1,0:T(8,128)S(1)} %get-tuple-element.71.refs_6_.refs_0_), channel_id=1, source_target_pairs={{0,4},{1,5},{2,6},{3,7},{4,0},{5,1},{6,2},{7,3},{8,12},{9,13},{10,... | collective-permute-start | bytes 405512 | tf_op jit(solution)/shard_map/ppermute | solution.py:517
  82.0 15.5 %collective-permute-start.10 = (bf16[512,512]{1,0:T(8,128)(2,1)S(1)}, bf16[512,512]{1,0:T(8,128)(2,1)S(1)}, u32[]{:S(2)}, u32[]{:S(2)}) collective-permute-start(bf16[512,512]{1,0:T(8,128)(2,1)S(1)} %get-tuple-element.80), channel_id=1, source_target_pairs={{0,2},{1,3},{2,0},{3,1},{4,6},{5,7},{6,4},{7,5},{8,10},{9,11},{10,... | collective-permute-start | bytes 1572872 | tf_op jit(solution)/shard_map/ppermute | solution.py:517
  84.3 8.0 %collective-permute-start.11 = (f32[8,4224]{1,0:T(8,128)S(1)}, f32[8,4224]{1,0:T(8,128)S(1)}, u32[]{:S(2)}, u32[]{:S(2)}) collective-permute-start(f32[8,4224]{1,0:T(8,128)S(1)} %get-tuple-element.76.refs_6_.refs_0_), channel_id=1, source_target_pairs={{0,8},{8,0},{16,24},{24,16},{1,9},{9,1},{17,25},{25,17},{2,10},{10... | collective-permute-start | bytes 405512 | tf_op jit(solution)/shard_map/ppermute | solution.py:517
  92.4 5.1 %collective-permute-start.14 = (f32[8,4224]{1,0:T(8,128)S(1)}, f32[8,4224]{1,0:T(8,128)S(1)}, u32[]{:S(2)}, u32[]{:S(2)}) collective-permute-start(f32[8,4224]{1,0:T(8,128)S(1)} %get-tuple-element.84.refs_0_), channel_id=1, source_target_pairs={{0,16},{8,24},{16,0},{24,8},{1,17},{9,25},{17,1},{25,9},{2,18},{10... | collective-permute-start | bytes 405512 | tf_op jit(solution)/shard_map/ppermute | solution.py:517
  97.5 1.6 %copy-start.3 = (f32[8,4224]{1,0:T(8,128)}, f32[8,4224]{1,0:T(8,128)S(1)}, u32[]{:S(2)}) copy-start(f32[8,4224]{1,0:T(8,128)S(1)} %get-tuple-element.86.refs_2_.refs_0_) | copy-start | bytes 405508
  97.6 0.6 copy-start.1
  98.2 0.8 copy-start.6
  103.2 39.3 %collective-permute-start.17 = (bf16[1376,512]{1,0:T(8,128)(2,1)}, bf16[1376,512]{1,0:T(8,128)(2,1)}, u32[]{:S(2)}, u32[]{:S(2)}) collective-permute-start(bf16[1376,512]{1,0:T(8,128)(2,1)} %get-tuple-element.92.refs_10_), channel_id=1, source_target_pairs={{0,8},{8,0},{16,24},{24,16},{1,9},{9,1},{17,25},{25,17},{2,10},{10... | collective-permute-start | bytes 4227080 | tf_op jit(solution)/shard_map/ppermute | solution.py:517
  104.8 37.7 %collective-permute-start.18 = (bf16[1376,512]{1,0:T(8,128)(2,1)}, bf16[1376,512]{1,0:T(8,128)(2,1)}, u32[]{:S(2)}, u32[]{:S(2)}) collective-permute-start(bf16[1376,512]{1,0:T(8,128)(2,1)} %get-tuple-element.93.refs_9_), channel_id=1, source_target_pairs={{0,16},{8,24},{16,0},{24,8},{1,17},{9,25},{17,1},{25,9},{2,18},{10... | collective-permute-start | bytes 4227080 | tf_op jit(solution)/shard_map/ppermute | solution.py:517
  106.3 41.6 %collective-permute-start.16 = (bf16[512,512]{1,0:T(8,128)(2,1)}, bf16[512,512]{1,0:T(8,128)(2,1)S(1)}, u32[]{:S(2)}, u32[]{:S(2)}) collective-permute-start(bf16[512,512]{1,0:T(8,128)(2,1)} %get-tuple-element.89), channel_id=1, source_target_pairs={{0,2},{1,3},{2,0},{3,1},{4,6},{5,7},{6,4},{7,5},{8,10},{9,11},{10,... | collective-permute-start | bytes 1572872 | tf_op jit(solution)/shard_map/ppermute | solution.py:517
  106.6 41.3 %collective-permute-start.15 = (bf16[512,512]{1,0:T(8,128)(2,1)}, bf16[512,512]{1,0:T(8,128)(2,1)S(1)}, u32[]{:S(2)}, u32[]{:S(2)}) collective-permute-start(bf16[512,512]{1,0:T(8,128)(2,1)} %copy-done.6), channel_id=1, source_target_pairs={{0,4},{1,5},{2,6},{3,7},{4,0},{5,1},{6,2},{7,3},{8,12},{9,13},{10,... | collective-permute-start | bytes 1572872 | tf_op jit(solution)/shard_map/ppermute | solution.py:517
  147.9 0.7 copy-start.2
